TPU v7x, 32 devices: a whole 2x2x4 slice. The times are simulated.
32 devices in a mesh: sx: 4 (over y, core), sy: 8 (over z, x).
Axes of the slice: x: 2, y: 2, z: 4, core: 2. Of those that a mesh axis runs over, the one named last changes fastest.
Arguments:
- loads: float32 [4, 8, 1536, 256], P('sx', 'sy')
- schur_flex: float32 [4, 8, 1536, 1536], P('sx', 'sy'), as said below
- dirichlet: float32 [4, 8, 1536, 1536], P('sx', 'sy'), as said below
- coupling: float32 [4, 8, 16, 1536], P('sx', 'sy'), may hold values from -0.3125 to 0.3125
- corner_index: int32 [4, 8, 16], P('sx', 'sy'), may hold values from 0 to 128, as said below
- face_lists: int32 [4, 8, 4, 384], P('sx', 'sy'), may hold values from 0 to 383, as said below
- coarse_inverse: float32 [128, 128], P(('sx', 'sy')), as said below
Outputs:
- multipliers: float32 [4, 8, 1536, 256], P('sx', 'sy')
- residual: float32 [4, 8, 1536, 256], P('sx', 'sy')
Inputs may be any that keep to these rules, and one draw needn't show every extreme that they name: `corner_index`: each subdomain lists 4 coarse dofs for each of its four corners; 128 marks a corner on the clamped edges of the panel, which has no coarse dof; every coarse dof below 128 is named by some subdomain. `face_lists`: each face's list is a permutation of the 384 dofs of the facing face; the facing lists of two neighbouring subdomains are inverse permutations. `schur_flex`: symmetric positive definite for every subdomain. `dirichlet`: symmetric positive definite for every subdomain. `coarse_inverse`: symmetric positive definite.
All inputs are finite; a program needn't handle non-finite values.
Results may differ from a plain program's by a relative error of at most 0.00017.
Values sent between devices are 32-bit elements; how exact they have to be, the bound alone decides.
No kernel may reach another device: no remote copies, remote signals or barrier semaphores. Data moves between devices by JAX's collectives and lax.ppermute only.
A program may use at most 128 MiB of HBM per device.

v0:
```python
import functools

import jax
import jax.numpy as jnp
from jax import lax
from jax.experimental import pallas as pl
from jax.experimental.pallas import tpu as pltpu
from jax.sharding import PartitionSpec as P

HIGHEST = lax.Precision.HIGHEST
F32 = jnp.float32
BF16 = jnp.bfloat16
LIMIT = 8 * 1024 * 1024
CRIT_FLOPS = 8 * 10**9
FAR_ROWS = 8


def swapped(block, axis, bit):
    return lax.ppermute(block, axis, [(i, i ^ bit) for i in range(lax.axis_size(axis))])


def swapped_between(block, axis):
    route = []
    for i in range(1, lax.axis_size(axis) - 1, 2):
        route += [(i, i + 1), (i + 1, i)]
    return lax.ppermute(block, axis, route)


def exchanged(slots, axis):
    between = swapped_between(slots[1], axis)
    return swapped(slots[0], axis, 1), between


def bits_of(axis):
    return [1 << i for i in range((lax.axis_size(axis) - 1).bit_length())]


def steps_of():
    return [("sx", bit) for bit in bits_of("sx")] + [("sy", bit) for bit in bits_of("sy")[:0:-1]] + [("sy", 1)]


def stacked_rows(parts):
    count = parts[0].shape[0]
    total = count * len(parts)
    return sum(jnp.pad(p, ((at * count, total - (at + 1) * count), (0, 0))) for at, p in enumerate(parts))


def doubled(rows, steps):
    for axis, bit in steps:
        rows = stacked_rows([rows, swapped(rows, axis, bit)])
    return rows


def block_of(other):
    return sum(1 << at for at, (axis, bit) in enumerate(steps_of()) if axis == "sy" and other & bit)


def split(x):
    high = x.astype(BF16)
    return high, (x - high.astype(F32)).astype(BF16)


def dot(a, b):
    return jnp.dot(a, b, preferred_element_type=F32)


def product(a, b_high, b_low):
    a_high, a_low = split(a)
    return dot(a_high, b_high) + (dot(a_high, b_low) + dot(a_low, b_high))


def thirds(x):
    high = x.astype(BF16)
    rest = x - high.astype(F32)
    mid = rest.astype(BF16)
    return high, mid, (rest - mid.astype(F32)).astype(BF16)


def permuted(select, rows):
    high, mid, low = thirds(rows)
    return dot(select, high) + (dot(select, mid) + dot(select, low))


def pair(flag, first, second):
    return jnp.where(flag == 1.0, second, first), jnp.where(flag == 1.0, first, second)


def faces_of(flags, slots):
    return (*pair(flags[4], slots[0], slots[1]), *pair(flags[5], slots[2], slots[3]))


def pack_kernel(corners, load, coupling, *refs):
    outs, sems = refs[:4], refs[4]
    face = load.shape[0] // 4
    width = load.shape[1]
    ncl = coupling.shape[0]
    even = [1 - lax.axis_index("sx") % 2, 1 - lax.axis_index("sy") % 2]
    faces = [even[0], 1 - even[0], 2 + even[1], 3 - even[1]]
    copies = []

    def copy(source, target):
        copies.append(pltpu.make_async_copy(source, target, sems.at[len(copies)]))
        copies[-1].start()

    for slot in (3, 2, 0, 1):
        first = pl.multiple_of(faces[slot] * face, 128)
        out = outs[slot]
        copy(load.at[pl.ds(first, face)], out.at[pl.ds(0, face)])
        for block, at in enumerate(range(0, face, width)):
            wide = min(width, face - at)
            source = coupling.at[:, pl.ds(pl.multiple_of(first + at, 128), wide)]
            copy(source, out.at[pl.ds(face + block * ncl, ncl), pl.ds(0, wide)])
    start = face + (face // width) * ncl
    for out in outs:
        for k in range(ncl):
            listed = jnp.full((1, width - face % width), corners[k].astype(F32))
            out[start + k : start + k + 1, face % width :] = listed
    for started in copies:
        started.wait()


def lift_kernel(flags, near0, near1, near2, near3, select, coupling, sent, out):
    face = out.shape[0] // 4
    ncoarse = out.shape[1]
    ncl = coupling.shape[0]
    ids = lax.broadcasted_iota(jnp.int32, (ncl, ncoarse), 1).astype(F32)
    own_pick = (sent[sent.shape[0] - ncl :, sent.shape[1] - 1 :] == ids).astype(F32)
    nears = faces_of(flags, [near[face:] for near in (near0, near1, near2, near3)])
    for f, near in enumerate(nears):
        columns = jnp.concatenate([near[at : at + ncl] for at in range(0, near.shape[0], ncl)], axis=1)
        near_pick = (columns[:, columns.shape[1] - 1 :] == ids).astype(F32)
        own = jnp.dot(coupling[:, f * face : (f + 1) * face].T, own_pick, precision=HIGHEST)
        theirs = jnp.dot(columns[:, :face].T, near_pick, precision=HIGHEST)
        out[f * face : (f + 1) * face] = own - permuted(select[f], theirs)


def field_into(at, owns, nears, select, flags, coef, bases, lifts, outs, images, high, low):
    size = outs[0].shape[0]
    if lifts:
        lift, sol = lifts
        corrections = product(lift[at * size : (at + 2) * size], *split(sol[...]))
    owns = pair(flags[4 + at // 2], *(own[:size] for own in owns))
    nears = pair(flags[4 + at // 2], *(near[:size] for near in nears))
    for f in range(2):
        image = owns[f] - permuted(select[at + f], nears[f])
        rows = slice(f * size, (f + 1) * size)
        if lifts:
            image = image + corrections[rows]
        if images:
            images[f][...] = image
        value = coef[0:1] * image
        if bases:
            value = bases[f][...] + value
        outs[f][...] = value
        high[rows], low[rows] = split(flags[at + f] * value)


def take(refs, *counts):
    groups = []
    for count in counts:
        groups.append(refs[:count])
        refs = refs[count:]
    return (*groups, refs)


def early_kernel(based, lifted, *refs):
    (flags, mat), owns, nears, (select, coef), bases, lifts, outs, images, rest = take(
        refs, 2, 2, 2, 2, 2 * based, 2 * lifted, 2, 2 * lifted
    )
    partial, high, low = rest
    field_into(0, owns, nears, select, flags, coef, bases, lifts, outs, images, high, low)
    half = high.shape[0]
    for rows in (slice(0, half), slice(half, 2 * half)):
        partial[rows] = product(mat[rows, :half], high[...], low[...])


def crit_kernel(based, lifted, *refs):
    (flags, mat), owns, nears, (select, coef, partial), bases, lifts, outs, images, rest = take(
        refs, 2, 2, 2, 3, 2 * based, 2 * lifted, 2, 2 * lifted
    )
    slot2, slot3, high, low = rest
    field_into(2, owns, nears, select, flags, coef, bases, lifts, outs, images, high, low)
    half = high.shape[0]
    size = half // 2
    value = partial[half:] + product(mat[half:, half:], high[...], low[...])
    slot3[:size], slot2[:size] = pair(flags[5], value[size:], value[:size])
    for slot in (slot2, slot3):
        slot[size:] = jnp.zeros((slot.shape[0] - size, slot.shape[1]), F32)


def late_rows(flags, mat, values, partial, high, low, slots):
    size = values[0].shape[0]
    for f in (2, 3):
        rows = slice((f - 2) * size, (f - 1) * size)
        high[rows], low[rows] = split(flags[f] * values[f][...])
    value = partial[: 2 * size] + product(mat[: 2 * size, 2 * size :], high[...], low[...])
    slots[1][...], slots[0][...] = pair(flags[4], value[size:], value[:size])
    return faces_of(flags, [slot[:size] for slot in slots])


def inner(flags, values, others):
    return sum(jnp.sum(flags[f] * values[f][...] * others[f], axis=0, keepdims=True) for f in range(4))


def prec_late_kernel(*refs):
    (flags, mat), values, applied, (partial, slot0, slot1, dots, high, low) = take(refs, 2, 4, 2)
    dots[...] = inner(flags, values, late_rows(flags, mat, values, partial, high, low, (slot0, slot1, *applied)))


def flex_late_kernel(others, *refs):
    (flags, mat), values, applied, other, rest = take(refs, 2, 4, 2, 4 * others)
    partial, coupling, carried, slot0, slot1, sums, high, low = rest
    size = slot0.shape[0]
    ncl = coupling.shape[0]
    coarse = None
    for f in range(4):
        term = product(coupling[:, f * size : (f + 1) * size], *split(flags[f] * values[f][...]))
        coarse = term if coarse is None else coarse + term
    faces = late_rows(flags, mat, values, partial, high, low, (slot0, slot1, *applied))
    rows = [inner(flags, values, faces), carried[...]]
    if others:
        rows.append(inner(flags, values, faces_of(flags, [slot[:size] for slot in other])))
    sums[:ncl] = coarse
    for at, row in enumerate(rows):
        sums[ncl + at : ncl + at + 1] = row
    end = ncl + len(rows)
    sums[end:] = jnp.zeros((sums.shape[0] - end, sums.shape[1]), F32)


def spread_kernel(ncl, rows, origins, table, *refs):
    parts, out = refs[:-1], refs[-1]
    ncoarse = out.shape[0] - 8
    ids = lax.broadcasted_iota(jnp.int32, (ncoarse, ncl), 0).astype(F32)
    size = ncl + 8
    each = parts[0].shape[0] // size
    coarse, dots = None, None
    for at, origin in enumerate(origins):
        start = origin * rows + rows - 8
        pick = (ids == table[start : start + 1, :ncl]).astype(BF16)
        values = parts[at // each][at % each * size : (at % each + 1) * size]
        term = permuted(pick, values[:ncl])
        coarse = term if coarse is None else coarse + term
        dots = values[ncl:] if dots is None else dots + values[ncl:]
    out[:ncoarse] = coarse
    out[ncoarse:] = dots


def inverse_from(table, rows, matrix):
    own = rows - 8
    for at in range(table.shape[0] // rows):
        matrix[at * own : (at + 1) * own] = table[at * rows : at * rows + own]


def first_step_kernel(rows, total, table, order, out, matrix):
    ncoarse = matrix.shape[0]
    inverse_from(table, rows, matrix)
    rhs = total[:ncoarse]
    sol = permuted(order[...], jnp.dot(matrix[...], rhs, precision=HIGHEST))
    fine_dot = total[ncoarse : ncoarse + 1]
    rho = 0.5 * total[ncoarse + 1 : ncoarse + 2]
    curve = fine_dot + jnp.sum(rhs * sol, axis=0, keepdims=True)
    out[:ncoarse] = sol
    out[ncoarse : ncoarse + 1] = -rho / curve
    out[ncoarse + 1 : ncoarse + 2] = rho
    out[ncoarse + 2 : ncoarse + 3] = fine_dot
    out[ncoarse + 3 :] = jnp.zeros((out.shape[0] - ncoarse - 3, out.shape[1]), F32)


def second_step_kernel(rows, total, table, order, total0, out0, out, matrix):
    ncoarse = matrix.shape[0]
    inverse_from(table, rows, matrix)
    rhs = total[:ncoarse]
    sol = permuted(order[...], jnp.dot(matrix[...], rhs, precision=HIGHEST))
    dot11, rho1, dot10 = (total[ncoarse + row : ncoarse + row + 1] for row in range(3))
    minus_step0, rho0, dot00 = (out0[ncoarse + row : ncoarse + row + 1] for row in range(3))
    rho1 = 0.5 * rho1
    beta = rho1 / rho0
    coarse = jnp.sum((rhs + beta * total0[:ncoarse]) * (sol + beta * out0[:ncoarse]), axis=0, keepdims=True)
    step1 = rho1 / (dot11 + 2.0 * beta * dot10 + beta * beta * dot00 + coarse)
    out[:ncoarse] = sol
    out[ncoarse : ncoarse + 1] = -step1
    out[ncoarse + 1 : ncoarse + 2] = -step1 * beta
    out[ncoarse + 2 : ncoarse + 3] = step1 * beta - minus_step0
    out[ncoarse + 3 : ncoarse + 4] = step1
    out[ncoarse + 4 :] = jnp.zeros((out.shape[0] - ncoarse - 4, out.shape[1]), F32)


def stored(values, out, sems):
    size = values.shape[1]
    return [
        pltpu.make_async_copy(values.at[f], out.at[pl.ds(f * size, size)], sems.at[f]) for f in range(4)
    ]


def tail_kernel(*refs):
    (flags,), owns, nears, residuals, images, (select, lift, sol, steps, out, values, sems) = take(
        refs, 1, 4, 4, 4, 4
    )
    stores = stored(values, out, sems)
    parts = split(sol[...])
    size = values.shape[1]
    owns = faces_of(flags, [own[:size] for own in owns])
    nears = faces_of(flags, [near[:size] for near in nears])
    for f in range(4):
        image = owns[f] - permuted(select[f], nears[f]) + product(lift[f * size : (f + 1) * size], *parts)
        values[f] = residuals[f][...] + steps[0:1] * image + steps[1:2] * images[f][...]
        stores[f].start()
    for copy in stores:
        copy.wait()


def weighted_kernel(*refs):
    firsts, seconds, (steps, out, values, sems) = take(refs, 4, 4)
    stores = stored(values, out, sems)
    for f in range(4):
        values[f] = steps[2:3] * firsts[f][...] + steps[3:4] * seconds[f][...]
        stores[f].start()
    for copy in stores:
        copy.wait()


VMEM_SPEC = pl.BlockSpec(memory_space=pltpu.VMEM)
SMEM_SPEC = pl.BlockSpec(memory_space=pltpu.SMEM)
ANY_SPEC = pl.BlockSpec(memory_space=pl.ANY)


def call(kernel, operands, shapes, scratch=(), smem=0, anywhere=(), out_spec=VMEM_SPEC, flops=1024, limit=LIMIT):
    return pl.pallas_call(
        kernel,
        in_specs=[SMEM_SPEC if i < smem else ANY_SPEC if i in anywhere else VMEM_SPEC for i in range(len(operands))],
        out_specs=[out_spec] * len(shapes),
        out_shape=[jax.ShapeDtypeStruct(s, F32) for s in shapes],
        scratch_shapes=list(scratch),
        compiler_params=pltpu.CompilerParams(vmem_limit_bytes=limit),
        cost_estimate=pl.CostEstimate(flops=flops, bytes_accessed=1024, transcendentals=0),
    )(*operands)


def shards(loads, schur_flex, dirichlet, coupling, corner_index, face_lists, coarse_inverse):
    flex_mat = schur_flex[0, 0]
    prec_mat = dirichlet[0, 0]
    coupling_mat = coupling[0, 0]
    corners = corner_index[0, 0]
    face_index = face_lists[0, 0]
    load = loads[0, 0]
    ncoarse = coarse_inverse.shape[1]
    ncl, ni = coupling_mat.shape
    width = load.shape[1]
    face, half = ni // 4, ni // 2
    n_sx, n_sy = lax.axis_size("sx"), lax.axis_size("sy")
    at_x, at_y = lax.axis_index("sx"), lax.axis_index("sy")
    count = n_sx * n_sy

    has = jnp.stack([at_x > 0, at_x < n_sx - 1, at_y > 0, at_y < n_sy - 1])
    even = jnp.stack([at_x, at_y]) % 2 == 0
    flags = jnp.concatenate([jnp.where(has, 2.0, 1.0), jnp.where(even, 1.0, 0.0)]).astype(F32)
    select = (face_index[:, :, None] == jnp.arange(face, dtype=jnp.int32)).astype(BF16)
    coarse_ids = jnp.arange(ncoarse, dtype=jnp.int32)
    block = coarse_ids // (ncoarse // (n_sx * n_sy))
    origin = jnp.zeros_like(block)
    for at, (axis, bit) in enumerate(steps_of()):
        weight = bit * n_sy if axis == "sx" else bit
        origin = origin + ((block >> at) & 1) * weight
    origin = origin ^ (at_x * n_sy + at_y)
    within = coarse_ids % (ncoarse // (n_sx * n_sy))
    order = (origin * (ncoarse // (n_sx * n_sy)) + within)[None, :] == coarse_ids[:, None]
    order = order.astype(BF16)
    one_face, far_face = (face, width), (face + FAR_ROWS, width)
    parts = [pltpu.VMEM((half, width), BF16)] * 2
    one, select, order, flags = lax.optimization_barrier((jnp.ones((1, width), F32), select, order, flags))
    half_one = jnp.full((1, width), 0.5, F32)

    def early(matrix, owns, nears, coef, bases, lifts):
        operands = [flags, matrix, *owns, *nears, select, coef, *bases, *lifts]
        shapes = [one_face] * (4 if lifts else 2) + [(ni, width)]
        kernel = functools.partial(early_kernel, bool(bases), bool(lifts))
        *fields, partial = call(kernel, operands, shapes, parts, smem=1)
        return fields[:2], fields[2:], partial

    def crit(matrix, owns, nears, coef, partial, bases, lifts):
        operands = [flags, matrix, *owns, *nears, select, coef, partial, *bases, *lifts]
        shapes = [one_face] * (4 if lifts else 2) + [far_face] * 2
        kernel = functools.partial(crit_kernel, bool(bases), bool(lifts))
        *fields, a2, a3 = call(kernel, operands, shapes, parts, smem=1, flops=CRIT_FLOPS)
        return fields[:2], fields[2:], (a2, a3)

    def fields_of(matrix, owns, nears, coef, bases=(), lifts=(), beside=None):
        v01, q01, partial = early(matrix, owns[:2], nears[:2], coef, bases[:2], lifts)
        if beside is not None:
            partial, coef, made = beside(partial, coef)
        v23, q23, a23 = crit(matrix, owns[2:], nears[2:], coef, partial, bases[2:], lifts)
        fields = (*v01, *v23), (*q01, *q23), a23, partial
        return fields if beside is None else (*fields, made)

    def prec_late(values, a23, partial):
        operands = [flags, prec_mat, *values, *a23, partial]
        a0, a1, dots = call(prec_late_kernel, operands, [one_face, one_face, (1, width)], parts, smem=1)
        return (a0, a1, *a23), dots

    def flex_late(values, a23, partial, carried, other=()):
        operands = [flags, flex_mat, *values, *a23, *other, partial, coupling_mat, carried]
        kernel = functools.partial(flex_late_kernel, int(bool(other)))
        a0, a1, sums = call(kernel, operands, [one_face, one_face, (ncl + 8, width)], parts, smem=1)
        return (a0, a1, *a23), sums

    def solved(kernel, sums, faces, others):
        other, *far = lax.optimization_barrier((swapped(sums, "sy", 1), *faces[2:]))
        far = exchanged(far, "sy")
        close = faces[:2]
        parts, origins = [sums, other], [0, 1]
        for bit in bits_of("sy")[:0:-1]:
            rows = stacked_rows(parts)
            other, *close = lax.optimization_barrier((swapped(rows, "sy", bit), *close))
            parts = [rows, other]
            origins = origins + [at ^ bit for at in origins]
        origins = [block_of(at) for at in origins]
        spread = functools.partial(spread_kernel, ncl, table_rows, origins)
        (total,) = call(spread, [table, *parts], [step_shape])
        for bit in bits_of("sx"):
            total = total + swapped(total, "sx", bit)
        scratch = [pltpu.VMEM((ncoarse, ncoarse), F32)]
        kernel = functools.partial(kernel, table_rows)
        (result,) = call(kernel, [total, table, order, *others], [step_shape], scratch)
        return (*exchanged(close, "sx"), *far), total, result

    step_shape = (ncoarse + 8, width)
    extra = -(-face // width) * ncl
    copies = 4 * (1 + -(-face // width))
    sent = call(
        pack_kernel,
        [corners, load, coupling_mat],
        [(face + extra, width)] * 4,
        [pltpu.SemaphoreType.DMA((copies,))],
        smem=1,
        anywhere=(1, 2),
        limit=7 * LIMIT,
    )
    near = (*exchanged(sent[:2], "sx"), *exchanged(sent[2:], "sy"))

    own = coarse_inverse.shape[0]
    table_rows = own + 8
    listed = jnp.pad(corners.astype(F32)[None], ((own, 7), (0, ncoarse - ncl)))
    own_rows = jnp.pad(coarse_inverse, ((0, 8), (0, 0))) + listed
    own_rows, _ = lax.optimization_barrier((own_rows, sent[0]))
    most_rows = doubled(own_rows, steps_of()[:-1])

    def last_step(partial, coef):
        partial, rows = lax.optimization_barrier((partial, most_rows))
        table, coef = lax.optimization_barrier((doubled(rows, steps_of()[-1:]), coef))
        return partial, coef, table

    residual0, _, a23, partial, table = fields_of(prec_mat, sent, near, one, beside=last_step)
    applied0, rho0 = prec_late(residual0, a23, partial)
    (lift,) = call(
        lift_kernel, [flags, *near, select, coupling_mat, sent[0]], [(ni, ncoarse)], smem=1
    )
    lift, half_one = lax.optimization_barrier((lift, half_one))
    near = (*exchanged(applied0[:2], "sx"), *exchanged(applied0[2:], "sy"))

    direction0, _, a23, partial = fields_of(flex_mat, applied0, near, half_one)
    fine0, sums = flex_late(direction0, a23, partial, rho0)
    near, total0, result0 = solved(first_step_kernel, sums, fine0, [])
    lifts = (lift, result0[:ncoarse])
    residual1, image0, a23, partial = fields_of(prec_mat, fine0, near, result0[ncoarse:], residual0, lifts)
    applied1, rho1 = prec_late(residual1, a23, partial)
    near = (*exchanged(applied1[:2], "sx"), *exchanged(applied1[2:], "sy"))

    precond, _, a23, partial = fields_of(flex_mat, applied1, near, half_one)
    fine1, sums = flex_late(precond, a23, partial, rho1, fine0)
    near, _, result1 = solved(second_step_kernel, sums, fine1, [total0, result0])
    sol1, steps1 = result1[:ncoarse], result1[ncoarse:]

    def final(kernel, operands, smem=0):
        ends = [pltpu.VMEM((4, face, width), F32), pltpu.SemaphoreType.DMA((4,))]
        return call(kernel, operands, [(ni, width)], ends, smem=smem, out_spec=ANY_SPEC)[0]

    multipliers = final(weighted_kernel, [*direction0, *precond, steps1])
    operands = [flags, *fine1, *near, *residual1, *image0, select, lift, sol1, steps1]
    residual2 = final(tail_kernel, operands, smem=1)
    return multipliers[None, None], residual2[None, None]


def solution(mesh):
    return jax.shard_map(
        shards,
        mesh=mesh,
        in_specs=(
            P("sx", "sy", None, None),
            P("sx", "sy", None, None),
            P("sx", "sy", None, None),
            P("sx", "sy", None, None),
            P("sx", "sy", None),
            P("sx", "sy", None, None),
            P(("sx", "sy"), None),
        ),
        out_specs=(P("sx", "sy", None, None), P("sx", "sy", None, None)),
        check_vma=False,
    )
```

profile of v0, /device:TPU:0, one launch (start us, length us, event | category | flops | bytes accessed | tf_op | source)
XLA Modules:
  0.0 159.5 jit_solution(593484745076913520)
XLA Ops:
  0.7 3.5 %shard_map.86 = (f32[416,256]{1,0:T(8,128)}, f32[416,256]{1,0:T(8,128)}, f32[416,256]{1,0:T(8,128)}, f32[416,256]{1,0:T(8,128)}) custom-call(s32[16]{0:T(128)} %bitcast.38, f32[1536,256]{1,0:T(8,128)} %bitcast.34, f32[16,1536]{1,0:T(8,128)} %bitcast.30), custom_call_target="tpu_custom_call" | custom-call | flops 1024 | bytes 1024 | tf_op jit(solution)/shard_map/pallas_call | solution.py:328
  5.6 3.0 %collective-permute-start.2 = (f32[416,256]{1,0:T(8,128)}, f32[416,256]{1,0:T(8,128)S(1)}, u32[]{:S(2)}, u32[]{:S(2)}) collective-permute-start(f32[416,256]{1,0:T(8,128)} %get-tuple-element.86.refs_2_), channel_id=1, source_target_pairs={{0,1},{1,0},{2,3},{3,2},{4,5},{5,4},{6,7},{7,6},{8,9},{9,8},{10,11... | collective-permute-start | bytes 1277960 | tf_op jit(solution)/shard_map/ppermute | solution.py:19
  9.6 3.0 %collective-permute-start.5 = (f32[24,128]{1,0:T(8,128)S(1)}, f32[24,128]{1,0:T(8,128)S(1)}, u32[]{:S(2)}, u32[]{:S(2)}) collective-permute-start(f32[24,128]{1,0:T(8,128)S(1)} %pad_add_fusion.8), channel_id=1, source_target_pairs={{0,16},{8,24},{16,0},{24,8},{1,17},{9,25},{17,1},{25,9},{2,18},{10... | collective-permute-start | bytes 36872 | tf_op jit(solution)/shard_map/ppermute | solution.py:19
  12.7 3.7 %collective-permute-done.5 = f32[24,128]{1,0:T(8,128)S(1)} collective-permute-done((f32[24,128]{1,0:T(8,128)S(1)}, f32[24,128]{1,0:T(8,128)S(1)}, u32[]{:S(2)}, u32[]{:S(2)}) %collective-permute-start.5) | collective-permute-done | bytes 12320 | tf_op jit(solution)/shard_map/ppermute | solution.py:19
  16.3 2.6 %collective-permute-start.6 = (f32[48,128]{1,0:T(8,128)S(1)}, f32[48,128]{1,0:T(8,128)S(1)}, u32[]{:S(2)}, u32[]{:S(2)}) collective-permute-start(f32[48,128]{1,0:T(8,128)S(1)} %pad_add_fusion.7), channel_id=1, source_target_pairs={{0,4},{1,5},{2,6},{3,7},{4,0},{5,1},{6,2},{7,3},{8,12},{9,13},{10,... | collective-permute-start | bytes 73736 | tf_op jit(solution)/shard_map/ppermute | solution.py:19
  19.0 4.2 %collective-permute-done.6 = f32[48,128]{1,0:T(8,128)S(1)} collective-permute-done((f32[48,128]{1,0:T(8,128)S(1)}, f32[48,128]{1,0:T(8,128)S(1)}, u32[]{:S(2)}, u32[]{:S(2)}) %collective-permute-start.6) | collective-permute-done | bytes 24608 | tf_op jit(solution)/shard_map/ppermute | solution.py:19
  23.3 1.6 collective-permute-start.7
  24.9 2.4 %collective-permute-done.7 = f32[96,128]{1,0:T(8,128)S(1)} collective-permute-done((f32[96,128]{1,0:T(8,128)S(1)}, f32[96,128]{1,0:T(8,128)S(1)}, u32[]{:S(2)}, u32[]{:S(2)}) %collective-permute-start.7) | collective-permute-done | bytes 49184 | tf_op jit(solution)/shard_map/ppermute | solution.py:19
  27.4 3.7 %copy-done = f32[1,1,1536,1536]{3,2,1,0:T(8,128)S(1)} copy-done((f32[1,1,1536,1536]{3,2,1,0:T(8,128)S(1)}, f32[1,1,1536,1536]{3,2,1,0:T(8,128)}, u32[]{:S(2)}) %copy-start) | copy-done | bytes 9437208
  31.1 1.0 copy-done.4
  32.1 3.4 %shard_map.87 = (f32[384,256]{1,0:T(8,128)S(1)}, f32[384,256]{1,0:T(8,128)S(1)}, f32[1536,256]{1,0:T(8,128)S(1)}) custom-call(f32[6]{0:T(128)S(1)} %pad_maximum_fusion.refs_0_.flags, f32[1536,1536]{1,0:T(8,128)S(1)} %bitcast.16, f32[416,256]{1,0:T(8,128)S(1)} %copy-done.2, f32[416,256]{1,0:T(8,128)S(1)} %copy-done.4, ...), custom_call_target="tpu_custom_call" | custom-call | flops 1024 | bytes 1024 | tf_op jit(solution)/shard_map/pallas_call | solution.py:328
  35.6 5.2 %collective-permute-done.8 = f32[192,128]{1,0:T(8,128)S(1)} collective-permute-done((f32[192,128]{1,0:T(8,128)S(1)}, f32[192,128]{1,0:T(8,128)S(1)}, u32[]{:S(2)}, u32[]{:S(2)}) %collective-permute-start.8) | collective-permute-done | bytes 98336 | tf_op jit(solution)/shard_map/ppermute | solution.py:19
  40.9 2.7 %shard_map.88 = (f32[384,256]{1,0:T(8,128)S(1)}, f32[384,256]{1,0:T(8,128)S(1)}, f32[392,256]{1,0:T(8,128)S(1)}, f32[392,256]{1,0:T(8,128)S(1)}) custom-call(f32[6]{0:T(128)S(1)} %pad_maximum_fusion.refs_0_.flags, f32[1536,1536]{1,0:T(8,128)S(1)} %bitcast.17, f32[416,256]{1,0:T(8,128)S(1)} %copy-done.5, f32[416,256]{1,0:T(8,128)S(1)} %copy-done.6, ...), custom_call_target="tpu_custom_call" | custom-call | flops 8000000000 | bytes 1024 | tf_op jit(solution)/shard_map/pallas_call | solution.py:328
  44.7 2.0 %shard_map.89 = (f32[384,256]{1,0:T(8,128)S(1)}, f32[384,256]{1,0:T(8,128)S(1)}, f32[1,256]{1,0:T(1,128)S(1)}) custom-call(f32[6]{0:T(128)S(1)} %pad_maximum_fusion.refs_0_.flags, f32[1536,1536]{1,0:T(8,128)S(1)} %bitcast.18, f32[384,256]{1,0:T(8,128)S(1)} %get-tuple-element.84.refs_2_.refs_8_, f32[384,256]{1,0:T(8,128)S(1)} %get-tuple-element.85.refs_3_.refs_9_, ...), custom_call_target="tpu_custom_call" | custom-call | flops 1024 | bytes 1024 | tf_op jit(solution)/shard_map/pallas_call | solution.py:328
  46.8 1.0 collective-permute-start.10
  47.8 3.5 %shard_map.90.refs_10_.refs_11_.refs_18_ = f32[1536,128]{1,0:T(8,128)S(1)} custom-call(f32[6]{0:T(128)S(1)} %pad_maximum_fusion.refs_0_.flags, f32[416,256]{1,0:T(8,128)S(1)} %collective-permute-done.refs_4_.near0, f32[416,256]{1,0:T(8,128)S(1)} %collective-permute-done.1.refs_5_.near1, f32[416,256]{1,0:T(8,128)S(1)} %collective-permute-done.2.refs_4_.near2, ...), custom_call_target="tpu_custom_call" | custom-call | flops 1024 | bytes 1024 | tf_op jit(solution)/shard_map/pallas_call | solution.py:328
  51.4 3.4 %shard_map.91 = (f32[384,256]{1,0:T(8,128)S(1)}, f32[384,256]{1,0:T(8,128)S(1)}, f32[1536,256]{1,0:T(8,128)S(1)}) custom-call(f32[6]{0:T(128)S(1)} %pad_maximum_fusion.refs_0_.flags, f32[1536,1536]{1,0:T(8,128)S(1)} %bitcast.24, f32[384,256]{1,0:T(8,128)S(1)} %get-tuple-element.97.refs_2_, f32[384,256]{1,0:T(8,128)S(1)} %get-tuple-element.98.refs_3_, ...), custom_call_target="tpu_custom_call" | custom-call | flops 1024 | bytes 1024 | tf_op jit(solution)/shard_map/pallas_call | solution.py:328
  54.8 6.5 %collective-permute-done.11.refs_4_ = f32[392,256]{1,0:T(8,128)S(1)} collective-permute-done((f32[392,256]{1,0:T(8,128)S(1)}, f32[392,256]{1,0:T(8,128)S(1)}, u32[]{:S(2)}, u32[]{:S(2)}) %collective-permute-start.11) | collective-permute-done | bytes 401440 | tf_op jit(solution)/shard_map/ppermute | solution.py:19
  61.3 2.7 %shard_map.92 = (f32[384,256]{1,0:T(8,128)S(1)}, f32[384,256]{1,0:T(8,128)S(1)}, f32[392,256]{1,0:T(8,128)S(1)}, f32[392,256]{1,0:T(8,128)S(1)}) custom-call(f32[6]{0:T(128)S(1)} %pad_maximum_fusion.refs_0_.flags, f32[1536,1536]{1,0:T(8,128)S(1)} %bitcast.25, f32[392,256]{1,0:T(8,128)S(1)} %get-tuple-element.95.refs_6_.refs_2_, ...), custom_call_target="tpu_custom_call" | custom-call | flops 8000000000 | bytes 1024 | tf_op jit(solution)/shard_map/pallas_call | solution.py:328
  64.0 2.3 %shard_map.93 = (f32[384,256]{1,0:T(8,128)S(1)}, f32[384,256]{1,0:T(8,128)S(1)}, f32[24,256]{1,0:T(8,128)S(1)}) custom-call(f32[6]{0:T(128)S(1)} %pad_maximum_fusion.refs_0_.flags, f32[1536,1536]{1,0:T(8,128)S(1)} %bitcast.26, f32[384,256]{1,0:T(8,128)S(1)} %get-tuple-element.100.refs_2_.refs_0_, f32[384,256]{1,0:T(8,128)S(1)} %get-tuple-element.101.refs_3_.refs_1_, ...), custom_call_target="tpu_custom_call" | custom-call | flops 1024 | bytes 1024 | tf_op jit(solution)/shard_map/pallas_call | solution.py:328
  66.3 2.5 %collective-permute-start.13 = (f32[24,256]{1,0:T(8,128)S(1)}, f32[24,256]{1,0:T(8,128)S(1)}, u32[]{:S(2)}, u32[]{:S(2)}) collective-permute-start(f32[24,256]{1,0:T(8,128)S(1)} %get-tuple-element.110), channel_id=1, source_target_pairs={{0,1},{1,0},{2,3},{3,2},{4,5},{5,4},{6,7},{7,6},{8,9},{9,8},{10,11... | collective-permute-start | bytes 73736 | tf_op jit(solution)/shard_map/ppermute | solution.py:19
  68.9 2.0 %collective-permute-done.13 = f32[24,256]{1,0:T(8,128)S(1)} collective-permute-done((f32[24,256]{1,0:T(8,128)S(1)}, f32[24,256]{1,0:T(8,128)S(1)}, u32[]{:S(2)}, u32[]{:S(2)}) %collective-permute-start.13) | collective-permute-done | bytes 24608 | tf_op jit(solution)/shard_map/ppermute | solution.py:19
  70.8 3.3 %collective-permute-start.14 = (f32[48,256]{1,0:T(8,128)S(1)}, f32[48,256]{1,0:T(8,128)S(1)}, u32[]{:S(2)}, u32[]{:S(2)}) collective-permute-start(f32[48,256]{1,0:T(8,128)S(1)} %pad_add_fusion.5), channel_id=1, source_target_pairs={{0,4},{1,5},{2,6},{3,7},{4,0},{5,1},{6,2},{7,3},{8,12},{9,13},{10,... | collective-permute-start | bytes 147464 | tf_op jit(solution)/shard_map/ppermute | solution.py:19
  74.1 2.3 %collective-permute-done.14 = f32[48,256]{1,0:T(8,128)S(1)} collective-permute-done((f32[48,256]{1,0:T(8,128)S(1)}, f32[48,256]{1,0:T(8,128)S(1)}, u32[]{:S(2)}, u32[]{:S(2)}) %collective-permute-start.14) | collective-permute-done | bytes 49184 | tf_op jit(solution)/shard_map/ppermute | solution.py:19
  76.5 1.8 %collective-permute-start.15 = (f32[96,256]{1,0:T(8,128)S(1)}, f32[96,256]{1,0:T(8,128)S(1)}, u32[]{:S(2)}, u32[]{:S(2)}) collective-permute-start(f32[96,256]{1,0:T(8,128)S(1)} %pad_add_fusion.2.refs_0_), channel_id=1, source_target_pairs={{0,2},{1,3},{2,0},{3,1},{4,6},{5,7},{6,4},{7,5},{8,10},{9,11},{10,... | collective-permute-start | bytes 294920 | tf_op jit(solution)/shard_map/ppermute | solution.py:19
  78.3 1.5 collective-permute-start.20
  82.6 3.6 %collective-permute-start.18 = (f32[136,256]{1,0:T(8,128)S(1)}, f32[136,256]{1,0:T(8,128)S(1)}, u32[]{:S(2)}, u32[]{:S(2)}) collective-permute-start(f32[136,256]{1,0:T(8,128)S(1)} %shard_map.94), channel_id=1, source_target_pairs={{0,8},{8,0},{16,24},{24,16},{1,9},{9,1},{17,25},{25,17},{2,10},{10... | collective-permute-start | bytes 417800 | tf_op jit(solution)/shard_map/ppermute | solution.py:19
  86.3 1.0 collective-permute-done.18
  87.6 6.4 %collective-permute-done.19 = f32[136,256]{1,0:T(8,128)S(1)} collective-permute-done((f32[136,256]{1,0:T(8,128)S(1)}, f32[136,256]{1,0:T(8,128)S(1)}, u32[]{:S(2)}, u32[]{:S(2)}) %collective-permute-start.19) | collective-permute-done | bytes 139296 | tf_op jit(solution)/shard_map/ppermute | solution.py:19
  94.6 3.7 %shard_map.96 = (f32[384,256]{1,0:T(8,128)S(1)}, f32[384,256]{1,0:T(8,128)S(1)}, f32[384,256]{1,0:T(8,128)S(1)}, f32[384,256]{1,0:T(8,128)S(1)}, f32[1536,256]{1,0:T(8,128)S(1)}) custom-call(f32[6]{0:T(128)S(1)} %pad_maximum_fusion.refs_0_.flags, f32[1536,1536]{1,0:T(8,128)S(1)} %bitcast.19, f32[384,256]{1,0:T(8,128)S(1)} %get-tuple-element.115.refs_2_.refs_8_, ...), custom_call_target="tpu_custom_call" | custom-call | flops 1024 | bytes 1024 | tf_op jit(solution)/shard_map/pallas_call | solution.py:328
  98.4 3.2 %shard_map.97 = (f32[384,256]{1,0:T(8,128)S(1)}, f32[384,256]{1,0:T(8,128)S(1)}, f32[384,256]{1,0:T(8,128)S(1)}, f32[384,256]{1,0:T(8,128)S(1)}, f32[392,256]{1,0:T(8,128)S(1)}, /*index=5*/f32[392,256]{1,0:T(8,128)S(1)}) custom-call(f32[6]{0:T(128)S(1)} %pad_maximum_fusion.refs_0_.flags, f32[1536,1536]{1,0:T(8,128)S(1)} %bitcast.20, ...), custom_call_target="tpu_custom_call" | custom-call | flops 8000000000 | bytes 1024 | tf_op jit(solution)/shard_map/pallas_call | solution.py:328
  101.6 2.8 %collective-permute-start.24 = (f32[392,256]{1,0:T(8,128)S(1)}, f32[392,256]{1,0:T(8,128)S(1)}, u32[]{:S(2)}, u32[]{:S(2)}) collective-permute-start(f32[392,256]{1,0:T(8,128)S(1)} %get-tuple-element.128.refs_6_.refs_2_), channel_id=1, source_target_pairs={{0,1},{1,0},{2,3},{3,2},{4,5},{5,4},{6,7},{7,6},{8,9},{9,8},{10,11... | collective-permute-start | bytes 1204232 | tf_op jit(solution)/shard_map/ppermute | solution.py:19
  105.1 2.0 %shard_map.98 = (f32[384,256]{1,0:T(8,128)S(1)}, f32[384,256]{1,0:T(8,128)S(1)}, f32[1,256]{1,0:T(1,128)S(1)}) custom-call(f32[6]{0:T(128)S(1)} %pad_maximum_fusion.refs_0_.flags, f32[1536,1536]{1,0:T(8,128)S(1)} %bitcast.21, f32[384,256]{1,0:T(8,128)S(1)} %get-tuple-element.121.refs_2_.refs_9_, f32[384,256]{1,0:T(8,128)S(1)} %get-tuple-element.122.refs_3_.refs_10_, ...), custom_call_target="tpu_custom_call" | custom-call | flops 1024 | bytes 1024 | tf_op jit(solution)/shard_map/pallas_call | solution.py:328
  108.9 3.4 %shard_map.99 = (f32[384,256]{1,0:T(8,128)S(1)}, f32[384,256]{1,0:T(8,128)S(1)}, f32[1536,256]{1,0:T(8,128)S(1)}) custom-call(f32[6]{0:T(128)S(1)} %pad_maximum_fusion.refs_0_.flags, f32[1536,1536]{1,0:T(8,128)S(1)} %bitcast.27, f32[384,256]{1,0:T(8,128)S(1)} %get-tuple-element.130.refs_2_, f32[384,256]{1,0:T(8,128)S(1)} %get-tuple-element.131.refs_3_, ...), custom_call_target="tpu_custom_call" | custom-call | flops 1024 | bytes 1024 | tf_op jit(solution)/shard_map/pallas_call | solution.py:328
  112.3 7.6 %collective-permute-done.24.refs_4_ = f32[392,256]{1,0:T(8,128)S(1)} collective-permute-done((f32[392,256]{1,0:T(8,128)S(1)}, f32[392,256]{1,0:T(8,128)S(1)}, u32[]{:S(2)}, u32[]{:S(2)}) %collective-permute-start.24) | collective-permute-done | bytes 401440 | tf_op jit(solution)/shard_map/ppermute | solution.py:19
  119.9 2.7 %shard_map.100 = (f32[384,256]{1,0:T(8,128)S(1)}, f32[384,256]{1,0:T(8,128)S(1)}, f32[392,256]{1,0:T(8,128)S(1)}, f32[392,256]{1,0:T(8,128)S(1)}) custom-call(f32[6]{0:T(128)S(1)} %pad_maximum_fusion.refs_0_.flags, f32[1536,1536]{1,0:T(8,128)S(1)} %bitcast.28, f32[392,256]{1,0:T(8,128)S(1)} %get-tuple-element.128.refs_6_.refs_2_, ...), custom_call_target="tpu_custom_call" | custom-call | flops 8000000000 | bytes 1024 | tf_op jit(solution)/shard_map/pallas_call | solution.py:328
  122.6 2.5 %shard_map.101 = (f32[384,256]{1,0:T(8,128)S(1)}, f32[384,256]{1,0:T(8,128)S(1)}, f32[24,256]{1,0:T(8,128)S(1)}) custom-call(f32[6]{0:T(128)S(1)} %pad_maximum_fusion.refs_0_.flags, f32[1536,1536]{1,0:T(8,128)S(1)} %bitcast.29, f32[384,256]{1,0:T(8,128)S(1)} %get-tuple-element.132.refs_2_.refs_4_, f32[384,256]{1,0:T(8,128)S(1)} %get-tuple-element.133.refs_3_.refs_5_, ...), custom_call_target="tpu_custom_call" | custom-call | flops 1024 | bytes 1024 | tf_op jit(solution)/shard_map/pallas_call | solution.py:328
  125.2 2.5 %collective-permute-start.26 = (f32[24,256]{1,0:T(8,128)S(1)}, f32[24,256]{1,0:T(8,128)S(1)}, u32[]{:S(2)}, u32[]{:S(2)}) collective-permute-start(f32[24,256]{1,0:T(8,128)S(1)} %get-tuple-element.140), channel_id=1, source_target_pairs={{0,1},{1,0},{2,3},{3,2},{4,5},{5,4},{6,7},{7,6},{8,9},{9,8},{10,11... | collective-permute-start | bytes 73736 | tf_op jit(solution)/shard_map/ppermute | solution.py:19
  127.7 1.8 %collective-permute-done.26 = f32[24,256]{1,0:T(8,128)S(1)} collective-permute-done((f32[24,256]{1,0:T(8,128)S(1)}, f32[24,256]{1,0:T(8,128)S(1)}, u32[]{:S(2)}, u32[]{:S(2)}) %collective-permute-start.26) | collective-permute-done | bytes 24608 | tf_op jit(solution)/shard_map/ppermute | solution.py:19
  129.5 3.7 %collective-permute-start.27 = (f32[48,256]{1,0:T(8,128)S(1)}, f32[48,256]{1,0:T(8,128)S(1)}, u32[]{:S(2)}, u32[]{:S(2)}) collective-permute-start(f32[48,256]{1,0:T(8,128)S(1)} %pad_add_fusion.4), channel_id=1, source_target_pairs={{0,4},{1,5},{2,6},{3,7},{4,0},{5,1},{6,2},{7,3},{8,12},{9,13},{10,... | collective-permute-start | bytes 147464 | tf_op jit(solution)/shard_map/ppermute | solution.py:19
  133.2 2.1 %collective-permute-done.27 = f32[48,256]{1,0:T(8,128)S(1)} collective-permute-done((f32[48,256]{1,0:T(8,128)S(1)}, f32[48,256]{1,0:T(8,128)S(1)}, u32[]{:S(2)}, u32[]{:S(2)}) %collective-permute-start.27) | collective-permute-done | bytes 49184 | tf_op jit(solution)/shard_map/ppermute | solution.py:19
  135.3 1.8 %collective-permute-start.28 = (f32[96,256]{1,0:T(8,128)S(1)}, f32[96,256]{1,0:T(8,128)S(1)}, u32[]{:S(2)}, u32[]{:S(2)}) collective-permute-start(f32[96,256]{1,0:T(8,128)S(1)} %pad_add_fusion.1.refs_0_), channel_id=1, source_target_pairs={{0,2},{1,3},{2,0},{3,1},{4,6},{5,7},{6,4},{7,5},{8,10},{9,11},{10,... | collective-permute-start | bytes 294920 | tf_op jit(solution)/shard_map/ppermute | solution.py:19
  137.0 1.7 %collective-permute-start.33 = (f32[392,256]{1,0:T(8,128)S(1)}, f32[392,256]{1,0:T(8,128)S(1)}, u32[]{:S(2)}, u32[]{:S(2)}) collective-permute-start(f32[392,256]{1,0:T(8,128)S(1)} %get-tuple-element.150.refs_6_.refs_3_), channel_id=1, source_target_pairs={{0,1},{1,0},{2,3},{3,2},{4,5},{5,4},{6,7},{7,6},{8,9},{9,8},{10,11... | collective-permute-start | bytes 1204232 | tf_op jit(solution)/shard_map/ppermute | solution.py:19
  141.2 3.0 %collective-permute-start.29 = (f32[136,256]{1,0:T(8,128)S(1)}, f32[136,256]{1,0:T(8,128)S(1)}, u32[]{:S(2)}, u32[]{:S(2)}) collective-permute-start(f32[136,256]{1,0:T(8,128)S(1)} %shard_map.102), channel_id=1, source_target_pairs={{0,8},{8,0},{16,24},{24,16},{1,9},{9,1},{17,25},{25,17},{2,10},{10... | collective-permute-start | bytes 417800 | tf_op jit(solution)/shard_map/ppermute | solution.py:19
  146.1 6.6 %collective-permute-done.30 = f32[136,256]{1,0:T(8,128)S(1)} collective-permute-done((f32[136,256]{1,0:T(8,128)S(1)}, f32[136,256]{1,0:T(8,128)S(1)}, u32[]{:S(2)}, u32[]{:S(2)}) %collective-permute-start.30) | collective-permute-done | bytes 139296 | tf_op jit(solution)/shard_map/ppermute | solution.py:19
  153.3 1.2 shard_map.104
  154.6 1.1 collective-permute-done.33.refs_7_
  155.6 3.7 %shard_map.105 = f32[1536,256]{1,0:T(8,128)} custom-call(f32[6]{0:T(128)S(1)} %pad_maximum_fusion.refs_0_.flags, f32[384,256]{1,0:T(8,128)S(1)} %get-tuple-element.148.refs_1_, f32[384,256]{1,0:T(8,128)S(1)} %get-tuple-element.149.refs_2_, f32[392,256]{1,0:T(8,128)S(1)} %get-tuple-element.150.refs_6_.refs_3_, ...), custom_call_target="tpu_custom_call" | custom-call | flops 1024 | bytes 1024 | tf_op jit(solution)/shard_map/pallas_call | solution.py:328
  (96 shorter events, 14.9 us)
Async XLA Ops:
  0.6 4.1 %copy-start.9 = (s32[1,1,16]{2,1,0:T(1,128)S(1)}, s32[1,1,16]{2,1,0:T(1,128)}, u32[]{:S(2)}) copy-start(s32[1,1,16]{2,1,0:T(1,128)} %param.11) | copy-start | bytes 196
  0.6 4.1 %copy-start.8 = (f32[4,128]{1,0:T(4,128)S(1)}, f32[4,128]{1,0:T(4,128)}, u32[]{:S(2)}) copy-start(f32[4,128]{1,0:T(4,128)} %param.13) | copy-start | bytes 6148
  0.7 8.6 %copy-start.7 = (s32[1,1,4,384]{3,2,1,0:T(4,128)S(1)}, s32[1,1,4,384]{3,2,1,0:T(4,128)}, u32[]{:S(2)}) copy-start(s32[1,1,4,384]{3,2,1,0:T(4,128)} %param.12) | copy-start | bytes 18436
  4.2 23.2 %copy-start.2 = (f32[416,256]{1,0:T(8,128)S(1)}, f32[416,256]{1,0:T(8,128)}, u32[]{:S(2)}) copy-start(f32[416,256]{1,0:T(8,128)} %get-tuple-element.80.refs_2_.sent) | copy-start | bytes 1277956
  4.2 23.2 %collective-permute-start = (f32[416,256]{1,0:T(8,128)}, f32[416,256]{1,0:T(8,128)S(1)}, u32[]{:S(2)}, u32[]{:S(2)}) collective-permute-start(f32[416,256]{1,0:T(8,128)} %get-tuple-element.80.refs_2_.sent), channel_id=1, source_target_pairs={{0,8},{8,0},{16,24},{24,16},{1,9},{9,1},{17,25},{25,17},{2,10},{10... | collective-permute-start | bytes 1277960 | tf_op jit(solution)/shard_map/ppermute | solution.py:19
  4.8 4.8 %collective-permute-start.4 = (f32[12,128]{1,0:T(8,128)S(1)}, f32[12,128]{1,0:T(8,128)S(1)}, u32[]{:S(2)}, u32[]{:S(2)}) collective-permute-start(f32[12,128]{1,0:T(8,128)S(1)} %pad_add_fusion.9), channel_id=1, source_target_pairs={{0,8},{8,0},{16,24},{24,16},{1,9},{9,1},{17,25},{25,17},{2,10},{10... | collective-permute-start | bytes 18440 | tf_op jit(solution)/shard_map/ppermute | solution.py:19
  4.9 22.5 %collective-permute-start.1 = (f32[416,256]{1,0:T(8,128)}, f32[416,256]{1,0:T(8,128)S(1)}, u32[]{:S(2)}, u32[]{:S(2)}) collective-permute-start(f32[416,256]{1,0:T(8,128)} %get-tuple-element.81.refs_3_), channel_id=1, source_target_pairs={{8,16},{16,8},{9,17},{17,9},{10,18},{18,10},{11,19},{19,11},{12,20... | collective-permute-start | bytes 1277960 | tf_op jit(solution)/shard_map/ppermute | solution.py:26
  5.6 35.3 %collective-permute-start.2 = (f32[416,256]{1,0:T(8,128)}, f32[416,256]{1,0:T(8,128)S(1)}, u32[]{:S(2)}, u32[]{:S(2)}) collective-permute-start(f32[416,256]{1,0:T(8,128)} %get-tuple-element.86.refs_2_), channel_id=1, source_target_pairs={{0,1},{1,0},{2,3},{3,2},{4,5},{5,4},{6,7},{7,6},{8,9},{9,8},{10,11... | collective-permute-start | bytes 1277960 | tf_op jit(solution)/shard_map/ppermute | solution.py:19
  8.6 32.3 %collective-permute-start.3 = (f32[416,256]{1,0:T(8,128)}, f32[416,256]{1,0:T(8,128)S(1)}, u32[]{:S(2)}, u32[]{:S(2)}) collective-permute-start(f32[416,256]{1,0:T(8,128)} %get-tuple-element.87.refs_3_), channel_id=1, source_target_pairs={{1,2},{2,1},{3,4},{4,3},{5,6},{6,5},{9,10},{10,9},{11,12},{12,11},... | collective-permute-start | bytes 1277960 | tf_op jit(solution)/shard_map/ppermute | solution.py:26
  9.6 6.7 %collective-permute-start.5 = (f32[24,128]{1,0:T(8,128)S(1)}, f32[24,128]{1,0:T(8,128)S(1)}, u32[]{:S(2)}, u32[]{:S(2)}) collective-permute-start(f32[24,128]{1,0:T(8,128)S(1)} %pad_add_fusion.8), channel_id=1, source_target_pairs={{0,16},{8,24},{16,0},{24,8},{1,17},{9,25},{17,1},{25,9},{2,18},{10... | collective-permute-start | bytes 36872 | tf_op jit(solution)/shard_map/ppermute | solution.py:19
  16.3 7.0 %collective-permute-start.6 = (f32[48,128]{1,0:T(8,128)S(1)}, f32[48,128]{1,0:T(8,128)S(1)}, u32[]{:S(2)}, u32[]{:S(2)}) collective-permute-start(f32[48,128]{1,0:T(8,128)S(1)} %pad_add_fusion.7), channel_id=1, source_target_pairs={{0,4},{1,5},{2,6},{3,7},{4,0},{5,1},{6,2},{7,3},{8,12},{9,13},{10,... | collective-permute-start | bytes 73736 | tf_op jit(solution)/shard_map/ppermute | solution.py:19
  23.3 4.1 %collective-permute-start.7 = (f32[96,128]{1,0:T(8,128)S(1)}, f32[96,128]{1,0:T(8,128)S(1)}, u32[]{:S(2)}, u32[]{:S(2)}) collective-permute-start(f32[96,128]{1,0:T(8,128)S(1)} %pad_add_fusion.6), channel_id=1, source_target_pairs={{0,2},{1,3},{2,0},{3,1},{4,6},{5,7},{6,4},{7,5},{8,10},{9,11},{10,... | collective-permute-start | bytes 147464 | tf_op jit(solution)/shard_map/ppermute | solution.py:19
  27.4 3.7 %copy-start = (f32[1,1,1536,1536]{3,2,1,0:T(8,128)S(1)}, f32[1,1,1536,1536]{3,2,1,0:T(8,128)}, u32[]{:S(2)}) copy-start(f32[1,1,1536,1536]{3,2,1,0:T(8,128)} %param.9) | copy-start | bytes 28311556
  31.1 1.0 copy-start.4
  32.1 8.8 %copy-start.1 = (f32[1,1,1536,1536]{3,2,1,0:T(8,128)S(1)}, f32[1,1,1536,1536]{3,2,1,0:T(8,128)}, u32[]{:S(2)}) copy-start(f32[1,1,1536,1536]{3,2,1,0:T(8,128)} %param.9) | copy-start | bytes 28311556
  32.1 8.8 %copy-start.5 = (f32[416,256]{1,0:T(8,128)S(1)}, f32[416,256]{1,0:T(8,128)}, u32[]{:S(2)}) copy-start(f32[416,256]{1,0:T(8,128)} %get-tuple-element.86.refs_2_) | copy-start | bytes 1277956
  32.1 8.8 %copy-start.6 = (f32[416,256]{1,0:T(8,128)S(1)}, f32[416,256]{1,0:T(8,128)}, u32[]{:S(2)}) copy-start(f32[416,256]{1,0:T(8,128)} %get-tuple-element.87.refs_3_) | copy-start | bytes 1277956
  35.6 5.3 %collective-permute-start.8 = (f32[192,128]{1,0:T(8,128)S(1)}, f32[192,128]{1,0:T(8,128)S(1)}, u32[]{:S(2)}, u32[]{:S(2)}) collective-permute-start(f32[192,128]{1,0:T(8,128)S(1)} %pad_add_fusion.3), channel_id=1, source_target_pairs={{0,1},{1,0},{2,3},{3,2},{4,5},{5,4},{6,7},{7,6},{8,9},{9,8},{10,11... | collective-permute-start | bytes 294920 | tf_op jit(solution)/shard_map/ppermute | solution.py:19
  43.6 17.6 %collective-permute-start.11 = (f32[392,256]{1,0:T(8,128)S(1)}, f32[392,256]{1,0:T(8,128)S(1)}, u32[]{:S(2)}, u32[]{:S(2)}) collective-permute-start(f32[392,256]{1,0:T(8,128)S(1)} %get-tuple-element.95.refs_6_.refs_2_), channel_id=1, source_target_pairs={{0,1},{1,0},{2,3},{3,2},{4,5},{5,4},{6,7},{7,6},{8,9},{9,8},{10,11... | collective-permute-start | bytes 1204232 | tf_op jit(solution)/shard_map/ppermute | solution.py:19
  44.0 17.3 %collective-permute-start.12 = (f32[392,256]{1,0:T(8,128)S(1)}, f32[392,256]{1,0:T(8,128)S(1)}, u32[]{:S(2)}, u32[]{:S(2)}) collective-permute-start(f32[392,256]{1,0:T(8,128)S(1)} %get-tuple-element.96.refs_7_.refs_3_), channel_id=1, source_target_pairs={{1,2},{2,1},{3,4},{4,3},{5,6},{6,5},{9,10},{10,9},{11,12},{12,11},... | collective-permute-start | bytes 1204232 | tf_op jit(solution)/shard_map/ppermute | solution.py:26
  44.7 6.7 %slice-start = ((s8[9437184]{0:T(1024)(128)(4,1)}), s8[4194304]{0:T(1024)(128)(4,1)S(1)}, s32[]{:S(2)}) async-start(s8[9437184]{0:T(1024)(128)(4,1)} %bitcast.22), calls=%async_computation | async-start | bytes 8388608
  44.7 3.1 %copy-start.3 = (f32[1,1,16,1536]{3,2,1,0:T(8,128)S(1)}, f32[1,1,16,1536]{3,2,1,0:T(8,128)}, u32[]{:S(2)}) copy-start(f32[1,1,16,1536]{3,2,1,0:T(8,128)} %param.10) | copy-start | bytes 294916
  44.7 6.7 %slice-start.1 = ((s8[9437184]{0:T(1024)(128)(4,1)}), s8[4194304]{0:T(1024)(128)(4,1)S(1)}, s32[]{:S(2)}) async-start(s8[9437184]{0:T(1024)(128)(4,1)} %bitcast.22), calls=%async_computation.1 | async-start | bytes 8388608
  44.7 6.7 %slice-start.2 = ((s8[9437184]{0:T(1024)(128)(4,1)}), s8[1048576]{0:T(1024)(128)(4,1)S(1)}, s32[]{:S(2)}) async-start(s8[9437184]{0:T(1024)(128)(4,1)} %bitcast.22), calls=%async_computation.2 | async-start | bytes 2097152
  46.7 4.6 %collective-permute-start.9 = (f32[384,256]{1,0:T(8,128)S(1)}, f32[384,256]{1,0:T(8,128)S(1)}, u32[]{:S(2)}, u32[]{:S(2)}) collective-permute-start(f32[384,256]{1,0:T(8,128)S(1)} %get-tuple-element.97.refs_2_), channel_id=1, source_target_pairs={{0,8},{8,0},{16,24},{24,16},{1,9},{9,1},{17,25},{25,17},{2,10},{10... | collective-permute-start | bytes 1179656 | tf_op jit(solution)/shard_map/ppermute | solution.py:19
  46.8 4.6 %collective-permute-start.10 = (f32[384,256]{1,0:T(8,128)S(1)}, f32[384,256]{1,0:T(8,128)S(1)}, u32[]{:S(2)}, u32[]{:S(2)}) collective-permute-start(f32[384,256]{1,0:T(8,128)S(1)} %get-tuple-element.98.refs_3_), channel_id=1, source_target_pairs={{8,16},{16,8},{9,17},{17,9},{10,18},{18,10},{11,19},{19,11},{12,20... | collective-permute-start | bytes 1179656 | tf_op jit(solution)/shard_map/ppermute | solution.py:26
  66.3 4.5 %collective-permute-start.13 = (f32[24,256]{1,0:T(8,128)S(1)}, f32[24,256]{1,0:T(8,128)S(1)}, u32[]{:S(2)}, u32[]{:S(2)}) collective-permute-start(f32[24,256]{1,0:T(8,128)S(1)} %get-tuple-element.110), channel_id=1, source_target_pairs={{0,1},{1,0},{2,3},{3,2},{4,5},{5,4},{6,7},{7,6},{8,9},{9,8},{10,11... | collective-permute-start | bytes 73736 | tf_op jit(solution)/shard_map/ppermute | solution.py:19
  70.8 5.6 %collective-permute-start.14 = (f32[48,256]{1,0:T(8,128)S(1)}, f32[48,256]{1,0:T(8,128)S(1)}, u32[]{:S(2)}, u32[]{:S(2)}) collective-permute-start(f32[48,256]{1,0:T(8,128)S(1)} %pad_add_fusion.5), channel_id=1, source_target_pairs={{0,4},{1,5},{2,6},{3,7},{4,0},{5,1},{6,2},{7,3},{8,12},{9,13},{10,... | collective-permute-start | bytes 147464 | tf_op jit(solution)/shard_map/ppermute | solution.py:19
  76.5 4.7 %collective-permute-start.15 = (f32[96,256]{1,0:T(8,128)S(1)}, f32[96,256]{1,0:T(8,128)S(1)}, u32[]{:S(2)}, u32[]{:S(2)}) collective-permute-start(f32[96,256]{1,0:T(8,128)S(1)} %pad_add_fusion.2.refs_0_), channel_id=1, source_target_pairs={{0,2},{1,3},{2,0},{3,1},{4,6},{5,7},{6,4},{7,5},{8,10},{9,11},{10,... | collective-permute-start | bytes 294920 | tf_op jit(solution)/shard_map/ppermute | solution.py:19
  78.3 20.1 %collective-permute-start.20 = (f32[392,256]{1,0:T(8,128)S(1)}, f32[392,256]{1,0:T(8,128)S(1)}, u32[]{:S(2)}, u32[]{:S(2)}) collective-permute-start(f32[392,256]{1,0:T(8,128)S(1)} %get-tuple-element.123.refs_6_.refs_2_.refs_10_), channel_id=1, source_target_pairs={{0,1},{1,0},{2,3},{3,2},{4,5},{5,4},{6,7},{7,6},{8,9},{9,8},{10,11... | collective-permute-start | bytes 1204232 | tf_op jit(solution)/shard_map/ppermute | solution.py:19
  79.7 18.6 %collective-permute-start.21 = (f32[392,256]{1,0:T(8,128)S(1)}, f32[392,256]{1,0:T(8,128)S(1)}, u32[]{:S(2)}, u32[]{:S(2)}) collective-permute-start(f32[392,256]{1,0:T(8,128)S(1)} %get-tuple-element.124.refs_7_.refs_3_.refs_11_), channel_id=1, source_target_pairs={{1,2},{2,1},{3,4},{4,3},{5,6},{6,5},{9,10},{10,9},{11,12},{12,11},... | collective-permute-start | bytes 1204232 | tf_op jit(solution)/shard_map/ppermute | solution.py:26
  81.2 13.4 %collective-permute-start.16 = (f32[384,256]{1,0:T(8,128)S(1)}, f32[384,256]{1,0:T(8,128)S(1)}, u32[]{:S(2)}, u32[]{:S(2)}) collective-permute-start(f32[384,256]{1,0:T(8,128)S(1)} %get-tuple-element.115.refs_2_.refs_8_), channel_id=1, source_target_pairs={{0,8},{8,0},{16,24},{24,16},{1,9},{9,1},{17,25},{25,17},{2,10},{10... | collective-permute-start | bytes 1179656 | tf_op jit(solution)/shard_map/ppermute | solution.py:19
  81.2 13.5 %collective-permute-start.17 = (f32[384,256]{1,0:T(8,128)S(1)}, f32[384,256]{1,0:T(8,128)S(1)}, u32[]{:S(2)}, u32[]{:S(2)}) collective-permute-start(f32[384,256]{1,0:T(8,128)S(1)} %get-tuple-element.116.refs_3_.refs_9_), channel_id=1, source_target_pairs={{8,16},{16,8},{9,17},{17,9},{10,18},{18,10},{11,19},{19,11},{12,20... | collective-permute-start | bytes 1179656 | tf_op jit(solution)/shard_map/ppermute | solution.py:26
  82.6 4.6 %collective-permute-start.18 = (f32[136,256]{1,0:T(8,128)S(1)}, f32[136,256]{1,0:T(8,128)S(1)}, u32[]{:S(2)}, u32[]{:S(2)}) collective-permute-start(f32[136,256]{1,0:T(8,128)S(1)} %shard_map.94), channel_id=1, source_target_pairs={{0,8},{8,0},{16,24},{24,16},{1,9},{9,1},{17,25},{25,17},{2,10},{10... | collective-permute-start | bytes 417800 | tf_op jit(solution)/shard_map/ppermute | solution.py:19
  87.3 6.7 %collective-permute-start.19 = (f32[136,256]{1,0:T(8,128)S(1)}, f32[136,256]{1,0:T(8,128)S(1)}, u32[]{:S(2)}, u32[]{:S(2)}) collective-permute-start(f32[136,256]{1,0:T(8,128)S(1)} %add.157), channel_id=1, source_target_pairs={{0,16},{8,24},{16,0},{24,8},{1,17},{9,25},{17,1},{25,9},{2,18},{10... | collective-permute-start | bytes 417800 | tf_op jit(solution)/shard_map/ppermute | solution.py:19
  101.6 18.3 %collective-permute-start.24 = (f32[392,256]{1,0:T(8,128)S(1)}, f32[392,256]{1,0:T(8,128)S(1)}, u32[]{:S(2)}, u32[]{:S(2)}) collective-permute-start(f32[392,256]{1,0:T(8,128)S(1)} %get-tuple-element.128.refs_6_.refs_2_), channel_id=1, source_target_pairs={{0,1},{1,0},{2,3},{3,2},{4,5},{5,4},{6,7},{7,6},{8,9},{9,8},{10,11... | collective-permute-start | bytes 1204232 | tf_op jit(solution)/shard_map/ppermute | solution.py:19
  104.4 15.5 %collective-permute-start.25 = (f32[392,256]{1,0:T(8,128)S(1)}, f32[392,256]{1,0:T(8,128)S(1)}, u32[]{:S(2)}, u32[]{:S(2)}) collective-permute-start(f32[392,256]{1,0:T(8,128)S(1)} %get-tuple-element.129.refs_7_.refs_3_), channel_id=1, source_target_pairs={{1,2},{2,1},{3,4},{4,3},{5,6},{6,5},{9,10},{10,9},{11,12},{12,11},... | collective-permute-start | bytes 1204232 | tf_op jit(solution)/shard_map/ppermute | solution.py:26
  107.1 1.8 %collective-permute-start.22 = (f32[384,256]{1,0:T(8,128)S(1)}, f32[384,256]{1,0:T(8,128)S(1)}, u32[]{:S(2)}, u32[]{:S(2)}) collective-permute-start(f32[384,256]{1,0:T(8,128)S(1)} %get-tuple-element.130.refs_2_), channel_id=1, source_target_pairs={{0,8},{8,0},{16,24},{24,16},{1,9},{9,1},{17,25},{25,17},{2,10},{10... | collective-permute-start | bytes 1179656 | tf_op jit(solution)/shard_map/ppermute | solution.py:19
  107.2 1.7 %collective-permute-start.23 = (f32[384,256]{1,0:T(8,128)S(1)}, f32[384,256]{1,0:T(8,128)S(1)}, u32[]{:S(2)}, u32[]{:S(2)}) collective-permute-start(f32[384,256]{1,0:T(8,128)S(1)} %get-tuple-element.131.refs_3_), channel_id=1, source_target_pairs={{8,16},{16,8},{9,17},{17,9},{10,18},{18,10},{11,19},{19,11},{12,20... | collective-permute-start | bytes 1179656 | tf_op jit(solution)/shard_map/ppermute | solution.py:26
  125.2 4.4 %collective-permute-start.26 = (f32[24,256]{1,0:T(8,128)S(1)}, f32[24,256]{1,0:T(8,128)S(1)}, u32[]{:S(2)}, u32[]{:S(2)}) collective-permute-start(f32[24,256]{1,0:T(8,128)S(1)} %get-tuple-element.140), channel_id=1, source_target_pairs={{0,1},{1,0},{2,3},{3,2},{4,5},{5,4},{6,7},{7,6},{8,9},{9,8},{10,11... | collective-permute-start | bytes 73736 | tf_op jit(solution)/shard_map/ppermute | solution.py:19
  129.5 5.8 %collective-permute-start.27 = (f32[48,256]{1,0:T(8,128)S(1)}, f32[48,256]{1,0:T(8,128)S(1)}, u32[]{:S(2)}, u32[]{:S(2)}) collective-permute-start(f32[48,256]{1,0:T(8,128)S(1)} %pad_add_fusion.4), channel_id=1, source_target_pairs={{0,4},{1,5},{2,6},{3,7},{4,0},{5,1},{6,2},{7,3},{8,12},{9,13},{10,... | collective-permute-start | bytes 147464 | tf_op jit(solution)/shard_map/ppermute | solution.py:19
  135.3 4.7 %collective-permute-start.28 = (f32[96,256]{1,0:T(8,128)S(1)}, f32[96,256]{1,0:T(8,128)S(1)}, u32[]{:S(2)}, u32[]{:S(2)}) collective-permute-start(f32[96,256]{1,0:T(8,128)S(1)} %pad_add_fusion.1.refs_0_), channel_id=1, source_target_pairs={{0,2},{1,3},{2,0},{3,1},{4,6},{5,7},{6,4},{7,5},{8,10},{9,11},{10,... | collective-permute-start | bytes 294920 | tf_op jit(solution)/shard_map/ppermute | solution.py:19
  137.0 18.6 %collective-permute-start.33 = (f32[392,256]{1,0:T(8,128)S(1)}, f32[392,256]{1,0:T(8,128)S(1)}, u32[]{:S(2)}, u32[]{:S(2)}) collective-permute-start(f32[392,256]{1,0:T(8,128)S(1)} %get-tuple-element.150.refs_6_.refs_3_), channel_id=1, source_target_pairs={{0,1},{1,0},{2,3},{3,2},{4,5},{5,4},{6,7},{7,6},{8,9},{9,8},{10,11... | collective-permute-start | bytes 1204232 | tf_op jit(solution)/shard_map/ppermute | solution.py:19
  138.8 16.9 %collective-permute-start.34 = (f32[392,256]{1,0:T(8,128)S(1)}, f32[392,256]{1,0:T(8,128)S(1)}, u32[]{:S(2)}, u32[]{:S(2)}) collective-permute-start(f32[392,256]{1,0:T(8,128)S(1)} %get-tuple-element.151.refs_7_.refs_4_), channel_id=1, source_target_pairs={{1,2},{2,1},{3,4},{4,3},{5,6},{6,5},{9,10},{10,9},{11,12},{12,11},... | collective-permute-start | bytes 1204232 | tf_op jit(solution)/shard_map/ppermute | solution.py:26
  140.0 15.7 %collective-permute-start.31 = (f32[384,256]{1,0:T(8,128)S(1)}, f32[384,256]{1,0:T(8,128)S(1)}, u32[]{:S(2)}, u32[]{:S(2)}) collective-permute-start(f32[384,256]{1,0:T(8,128)S(1)} %get-tuple-element.148.refs_1_), channel_id=1, source_target_pairs={{0,8},{8,0},{16,24},{24,16},{1,9},{9,1},{17,25},{25,17},{2,10},{10... | collective-permute-start | bytes 1179656 | tf_op jit(solution)/shard_map/ppermute | solution.py:19
  140.0 15.7 %collective-permute-start.32 = (f32[384,256]{1,0:T(8,128)S(1)}, f32[384,256]{1,0:T(8,128)S(1)}, u32[]{:S(2)}, u32[]{:S(2)}) collective-permute-start(f32[384,256]{1,0:T(8,128)S(1)} %get-tuple-element.149.refs_2_), channel_id=1, source_target_pairs={{8,16},{16,8},{9,17},{17,9},{10,18},{18,10},{11,19},{19,11},{12,20... | collective-permute-start | bytes 1179656 | tf_op jit(solution)/shard_map/ppermute | solution.py:26
  141.2 4.0 %collective-permute-start.29 = (f32[136,256]{1,0:T(8,128)S(1)}, f32[136,256]{1,0:T(8,128)S(1)}, u32[]{:S(2)}, u32[]{:S(2)}) collective-permute-start(f32[136,256]{1,0:T(8,128)S(1)} %shard_map.102), channel_id=1, source_target_pairs={{0,8},{8,0},{16,24},{24,16},{1,9},{9,1},{17,25},{25,17},{2,10},{10... | collective-permute-start | bytes 417800 | tf_op jit(solution)/shard_map/ppermute | solution.py:19
  145.3 7.5 %collective-permute-start.30 = (f32[136,256]{1,0:T(8,128)S(1)}, f32[136,256]{1,0:T(8,128)S(1)}, u32[]{:S(2)}, u32[]{:S(2)}) collective-permute-start(f32[136,256]{1,0:T(8,128)S(1)} %add.161), channel_id=1, source_target_pairs={{0,16},{8,24},{16,0},{24,8},{1,17},{9,25},{17,1},{25,9},{2,18},{10... | collective-permute-start | bytes 417800 | tf_op jit(solution)/shard_map/ppermute | solution.py:19
where the time goes:
time: 160 us
  waiting for transfers between devices  56 us (35%)
  starting transfers between devices  48.4 us (30%)
  Pallas kernels  48.3 us (30%)
  local copies, waits for them, and re-layouts  4.77 us (3%)
    ppermute x25, waiting for transfers between devices, swapped(): lax.ppermute(block, axis, [(i, i ^ bit) for i in range(lax.axis_size(axis...  56 us
    pallas_call x20, Pallas kernels, call(): pl.pallas_call(kernel, in_specs=[SMEM_SPEC if i < smem else ANY_SPEC if i...  48.3 us
    ppermute x25, starting transfers between devices, swapped(): lax.ppermute(block, axis, [(i, i ^ bit) for i in range(lax.axis_size(axis...  40.8 us
    ppermute x10, starting transfers between devices, swapped_between(): return lax.ppermute(block, axis, route)  7.56 us
    unnamed x26, local copies, waits for them, and re-layouts  4.74 us
  transfers between devices with their start and end apart: 35, of which 18 were waited for; matrix products, arithmetic and copies ran while one was open for 0% of the time, Pallas kernels for 16%

commit v1 on v0

--- a/solution.py
+++ b/solution.py
@@ -36,7 +36,7 @@
 
 
 def steps_of():
-    return [("sx", bit) for bit in bits_of("sx")] + [("sy", bit) for bit in bits_of("sy")[:0:-1]] + [("sy", 1)]
+    return [("sy", 1)] + [("sx", bit) for bit in bits_of("sx")] + [("sy", bit) for bit in bits_of("sy")[:0:-1]]
 
 
 def stacked_rows(parts):
@@ -90,7 +90,7 @@
 
 
 def pack_kernel(corners, load, coupling, *refs):
-    outs, sems = refs[:4], refs[4]
+    outs, (lists, sems) = refs[:4], refs[4:]
     face = load.shape[0] // 4
     width = load.shape[1]
     ncl = coupling.shape[0]
@@ -111,10 +111,10 @@
             source = coupling.at[:, pl.ds(pl.multiple_of(first + at, 128), wide)]
             copy(source, out.at[pl.ds(face + block * ncl, ncl), pl.ds(0, wide)])
     start = face + (face // width) * ncl
+    for k in range(ncl):
+        lists[k : k + 1] = jnp.full((1, lists.shape[1]), corners[k].astype(F32))
     for out in outs:
-        for k in range(ncl):
-            listed = jnp.full((1, width - face % width), corners[k].astype(F32))
-            out[start + k : start + k + 1, face % width :] = listed
+        copy(lists, out.at[pl.ds(start, ncl), pl.ds(face % width, lists.shape[1])])
     for started in copies:
         started.wait()
 
@@ -292,17 +292,22 @@
     ]
 
 
+def moved_kernel(*refs):
+    (flags,), owns, nears, (select,), outs = take(refs, 1, 4, 4, 1)
+    size = outs[0].shape[0]
+    owns = faces_of(flags, [own[:size] for own in owns])
+    nears = faces_of(flags, [near[:size] for near in nears])
+    for f, out in enumerate(outs):
+        out[...] = owns[f] - permuted(select[f], nears[f])
+
+
 def tail_kernel(*refs):
-    (flags,), owns, nears, residuals, images, (select, lift, sol, steps, out, values, sems) = take(
-        refs, 1, 4, 4, 4, 4
-    )
+    moved, residuals, images, (lift, sol, steps, out, values, sems) = take(refs, 4, 4, 4)
     stores = stored(values, out, sems)
     parts = split(sol[...])
     size = values.shape[1]
-    owns = faces_of(flags, [own[:size] for own in owns])
-    nears = faces_of(flags, [near[:size] for near in nears])
     for f in range(4):
-        image = owns[f] - permuted(select[f], nears[f]) + product(lift[f * size : (f + 1) * size], *parts)
+        image = moved[f][...] + product(lift[f * size : (f + 1) * size], *parts)
         values[f] = residuals[f][...] + steps[0:1] * image + steps[1:2] * images[f][...]
         stores[f].start()
     for copy in stores:
@@ -403,36 +408,35 @@
         a0, a1, sums = call(kernel, operands, [one_face, one_face, (ncl + 8, width)], parts, smem=1)
         return (a0, a1, *a23), sums
 
-    def solved(kernel, sums, faces, others):
-        other, *far = lax.optimization_barrier((swapped(sums, "sy", 1), *faces[2:]))
-        far = exchanged(far, "sy")
-        close = faces[:2]
-        parts, origins = [sums, other], [0, 1]
-        for bit in bits_of("sy")[:0:-1]:
-            rows = stacked_rows(parts)
-            other, *close = lax.optimization_barrier((swapped(rows, "sy", bit), *close))
-            parts = [rows, other]
-            origins = origins + [at ^ bit for at in origins]
-        origins = [block_of(at) for at in origins]
+    def solved(kernel, sums, faces, more, before=None):
+        both = stacked_rows([sums, swapped(sums, "sy", 1)])
+        others = [swapped(both, "sy", at) for at in range(2, n_sy, 2)]
+        others, faces = lax.optimization_barrier((others, faces))
+        near = (*exchanged(faces[:2], "sx"), *exchanged(faces[2:], "sy"))
+        parts = [both, *others]
+        origins = [block_of(at) for at in range(n_sy)]
         spread = functools.partial(spread_kernel, ncl, table_rows, origins)
         (total,) = call(spread, [table, *parts], [step_shape])
         for bit in bits_of("sx"):
             total = total + swapped(total, "sx", bit)
         scratch = [pltpu.VMEM((ncoarse, ncoarse), F32)]
         kernel = functools.partial(kernel, table_rows)
-        (result,) = call(kernel, [total, table, order, *others], [step_shape], scratch)
-        return (*exchanged(close, "sx"), *far), total, result
+        if before is not None:
+            total, near = before(total, near)
+        (result,) = call(kernel, [total, table, order, *more], [step_shape], scratch)
+        return near, total, result
 
     step_shape = (ncoarse + 8, width)
     extra = -(-face // width) * ncl
-    copies = 4 * (1 + -(-face // width))
+    copies = 4 * (2 + -(-face // width))
     sent = call(
         pack_kernel,
         [corners, load, coupling_mat],
         [(face + extra, width)] * 4,
-        [pltpu.SemaphoreType.DMA((copies,))],
+        [pltpu.VMEM((ncl, width - face % width), F32), pltpu.SemaphoreType.DMA((copies,))],
         smem=1,
         anywhere=(1, 2),
+        out_spec=ANY_SPEC,
         limit=7 * LIMIT,
     )
     near = (*exchanged(sent[:2], "sx"), *exchanged(sent[2:], "sy"))
@@ -442,19 +446,17 @@
     listed = jnp.pad(corners.astype(F32)[None], ((own, 7), (0, ncoarse - ncl)))
     own_rows = jnp.pad(coarse_inverse, ((0, 8), (0, 0))) + listed
     own_rows, _ = lax.optimization_barrier((own_rows, sent[0]))
-    most_rows = doubled(own_rows, steps_of()[:-1])
-
-    def last_step(partial, coef):
-        partial, rows = lax.optimization_barrier((partial, most_rows))
-        table, coef = lax.optimization_barrier((doubled(rows, steps_of()[-1:]), coef))
-        return partial, coef, table
-
-    residual0, _, a23, partial, table = fields_of(prec_mat, sent, near, one, beside=last_step)
+
+    def most_steps(partial, coef):
+        rows, coef = lax.optimization_barrier((doubled(own_rows, steps_of()[:-1]), coef))
+        return partial, coef, rows
+
+    residual0, _, a23, partial, most_rows = fields_of(prec_mat, sent, near, one, beside=most_steps)
     applied0, rho0 = prec_late(residual0, a23, partial)
     (lift,) = call(
         lift_kernel, [flags, *near, select, coupling_mat, sent[0]], [(ni, ncoarse)], smem=1
     )
-    lift, half_one = lax.optimization_barrier((lift, half_one))
+    table, half_one = lax.optimization_barrier((doubled(most_rows, steps_of()[-1:]), half_one))
     near = (*exchanged(applied0[:2], "sx"), *exchanged(applied0[2:], "sy"))
 
     direction0, _, a23, partial = fields_of(flex_mat, applied0, near, half_one)
@@ -467,16 +469,20 @@
 
     precond, _, a23, partial = fields_of(flex_mat, applied1, near, half_one)
     fine1, sums = flex_late(precond, a23, partial, rho1, fine0)
-    near, _, result1 = solved(second_step_kernel, sums, fine1, [total0, result0])
+
+    def jump_first(total, near):
+        moved = call(moved_kernel, [flags, *fine1, *near, select], [one_face] * 4, smem=1)
+        return lax.optimization_barrier((total, moved))
+
+    moved, _, result1 = solved(second_step_kernel, sums, fine1, [total0, result0], jump_first)
     sol1, steps1 = result1[:ncoarse], result1[ncoarse:]
 
-    def final(kernel, operands, smem=0):
+    def final(kernel, operands):
         ends = [pltpu.VMEM((4, face, width), F32), pltpu.SemaphoreType.DMA((4,))]
-        return call(kernel, operands, [(ni, width)], ends, smem=smem, out_spec=ANY_SPEC)[0]
+        return call(kernel, operands, [(ni, width)], ends, out_spec=ANY_SPEC)[0]
 
     multipliers = final(weighted_kernel, [*direction0, *precond, steps1])
-    operands = [flags, *fine1, *near, *residual1, *image0, select, lift, sol1, steps1]
-    residual2 = final(tail_kernel, operands, smem=1)
+    residual2 = final(tail_kernel, [*moved, *residual1, *image0, lift, sol1, steps1])
     return multipliers[None, None], residual2[None, None]
 
 

time: 160 us -> 207 us (1.29)
  Pallas kernels: 48.3 us -> 97.6 us
  waiting for transfers between devices: 56 us -> 51.5 us
  starting transfers between devices: 48.4 us -> 50.6 us
    pallas_call x20 -> x21, Pallas kernels: 48.3 us -> 97.6 us  [call(): pl.pallas_call(kernel, in_specs=[SMEM_SPEC if i < smem else ANY_SPEC if i...]
    ppermute x25 -> x27, waiting for transfers between devices: 56 us -> 51.5 us  [swapped(): lax.ppermute(block, axis, [(i, i ^ bit) for i in range(lax.axis_size(axis...]
    ppermute x25 -> x27, starting transfers between devices: 40.8 us -> 43 us  [swapped(): lax.ppermute(block, axis, [(i, i ^ bit) for i in range(lax.axis_size(axis...]
    unnamed x26 -> x30, local copies, waits for them, and re-layouts: 4.74 us -> 4.82 us
  transfers between devices with their start and end apart: 35 -> 37, of which waited for: 18 -> 17; matrix products, arithmetic and copies ran while one was open for 0% -> 0% of each run, Pallas kernels for 16% -> 11%
where the time goes in v1:
time: 207 us
  Pallas kernels  97.6 us (47%)
  waiting for transfers between devices  51.5 us (25%)
  starting transfers between devices  50.6 us (24%)
  local copies, waits for them, and re-layouts  4.86 us (2%)
    pallas_call x21, Pallas kernels, call(): pl.pallas_call(kernel, in_specs=[SMEM_SPEC if i < smem else ANY_SPEC if i...  97.6 us
    ppermute x27, waiting for transfers between devices, swapped(): lax.ppermute(block, axis, [(i, i ^ bit) for i in range(lax.axis_size(axis...  51.5 us
    ppermute x27, starting transfers between devices, swapped(): lax.ppermute(block, axis, [(i, i ^ bit) for i in range(lax.axis_size(axis...  43 us
    ppermute x10, starting transfers between devices, swapped_between(): return lax.ppermute(block, axis, route)  7.57 us
    unnamed x30, local copies, waits for them, and re-layouts  4.82 us
  transfers between devices with their start and end apart: 37, of which 17 were waited for; matrix products, arithmetic and copies ran while one was open for 0% of the time, Pallas kernels for 11%

profile of v1, /device:TPU:0, one launch (start us, length us, event | category | flops | bytes accessed | tf_op | source)
XLA Modules:
  0.0 206.7 jit_solution(12725536525959201374)
XLA Ops:
  0.7 52.7 %shard_map.86 = (f32[416,256]{1,0:T(8,128)}, f32[416,256]{1,0:T(8,128)}, f32[416,256]{1,0:T(8,128)}, f32[416,256]{1,0:T(8,128)}) custom-call(s32[16]{0:T(128)} %bitcast.40, f32[1536,256]{1,0:T(8,128)} %bitcast.36, f32[16,1536]{1,0:T(8,128)} %bitcast.32), custom_call_target="tpu_custom_call" | custom-call | flops 1024 | bytes 1024 | tf_op jit(solution)/shard_map/pallas_call | solution.py:333
  53.9 2.6 %collective-permute-start.4 = (f32[12,128]{1,0:T(8,128)S(1)}, f32[12,128]{1,0:T(8,128)S(1)}, u32[]{:S(2)}, u32[]{:S(2)}) collective-permute-start(f32[12,128]{1,0:T(8,128)S(1)} %pad_add_fusion.7), channel_id=1, source_target_pairs={{0,1},{1,0},{2,3},{3,2},{4,5},{5,4},{6,7},{7,6},{8,9},{9,8},{10,11... | collective-permute-start | bytes 18440 | tf_op jit(solution)/shard_map/ppermute | solution.py:19
  58.3 3.1 %collective-permute-start.5 = (f32[24,128]{1,0:T(8,128)S(1)}, f32[24,128]{1,0:T(8,128)S(1)}, u32[]{:S(2)}, u32[]{:S(2)}) collective-permute-start(f32[24,128]{1,0:T(8,128)S(1)} %pad_add_fusion.6), channel_id=1, source_target_pairs={{0,8},{8,0},{16,24},{24,16},{1,9},{9,1},{17,25},{25,17},{2,10},{10... | collective-permute-start | bytes 36872 | tf_op jit(solution)/shard_map/ppermute | solution.py:19
  63.0 4.1 %collective-permute-done.6 = f32[48,128]{1,0:T(8,128)S(1)} collective-permute-done((f32[48,128]{1,0:T(8,128)S(1)}, f32[48,128]{1,0:T(8,128)S(1)}, u32[]{:S(2)}, u32[]{:S(2)}) %collective-permute-start.6) | collective-permute-done | bytes 24608 | tf_op jit(solution)/shard_map/ppermute | solution.py:19
  67.0 4.0 %collective-permute-start.7 = (f32[96,128]{1,0:T(8,128)S(1)}, f32[96,128]{1,0:T(8,128)S(1)}, u32[]{:S(2)}, u32[]{:S(2)}) collective-permute-start(f32[96,128]{1,0:T(8,128)S(1)} %pad_add_fusion.4), channel_id=1, source_target_pairs={{0,4},{1,5},{2,6},{3,7},{4,0},{5,1},{6,2},{7,3},{8,12},{9,13},{10,... | collective-permute-start | bytes 147464 | tf_op jit(solution)/shard_map/ppermute | solution.py:19
  71.1 2.9 %collective-permute-done.7 = f32[96,128]{1,0:T(8,128)S(1)} collective-permute-done((f32[96,128]{1,0:T(8,128)S(1)}, f32[96,128]{1,0:T(8,128)S(1)}, u32[]{:S(2)}, u32[]{:S(2)}) %collective-permute-start.7) | collective-permute-done | bytes 49184 | tf_op jit(solution)/shard_map/ppermute | solution.py:19
  74.1 3.7 %copy-done = f32[1,1,1536,1536]{3,2,1,0:T(8,128)S(1)} copy-done((f32[1,1,1536,1536]{3,2,1,0:T(8,128)S(1)}, f32[1,1,1536,1536]{3,2,1,0:T(8,128)}, u32[]{:S(2)}) %copy-start) | copy-done | bytes 9437208
  78.8 3.4 %shard_map.87 = (f32[384,256]{1,0:T(8,128)S(1)}, f32[384,256]{1,0:T(8,128)S(1)}, f32[1536,256]{1,0:T(8,128)S(1)}) custom-call(f32[6]{0:T(128)S(1)} %pad_maximum_fusion.refs_0_.flags, f32[1536,1536]{1,0:T(8,128)S(1)} %bitcast.16, f32[416,256]{1,0:T(8,128)S(1)} %copy-done.1, f32[416,256]{1,0:T(8,128)S(1)} %copy-done.3, ...), custom_call_target="tpu_custom_call" | custom-call | flops 1024 | bytes 1024 | tf_op jit(solution)/shard_map/pallas_call | solution.py:333
  82.3 2.7 %shard_map.88 = (f32[384,256]{1,0:T(8,128)S(1)}, f32[384,256]{1,0:T(8,128)S(1)}, f32[392,256]{1,0:T(8,128)S(1)}, f32[392,256]{1,0:T(8,128)S(1)}) custom-call(f32[6]{0:T(128)S(1)} %pad_maximum_fusion.refs_0_.flags, f32[1536,1536]{1,0:T(8,128)S(1)} %bitcast.17, f32[416,256]{1,0:T(8,128)S(1)} %copy-done.4, f32[416,256]{1,0:T(8,128)S(1)} %copy-done.5, ...), custom_call_target="tpu_custom_call" | custom-call | flops 8000000000 | bytes 1024 | tf_op jit(solution)/shard_map/pallas_call | solution.py:333
  85.0 1.2 collective-permute-start.11
  87.1 2.0 shard_map.89
  89.1 2.0 collective-permute-start.8
  91.9 2.9 %collective-permute-start.10 = (f32[192,128]{1,0:T(8,128)S(1)}, f32[192,128]{1,0:T(8,128)S(1)}, u32[]{:S(2)}, u32[]{:S(2)}) collective-permute-start(f32[192,128]{1,0:T(8,128)S(1)} %pad_add_fusion.1), channel_id=1, source_target_pairs={{0,2},{1,3},{2,0},{3,1},{4,6},{5,7},{6,4},{7,5},{8,10},{9,11},{10,... | collective-permute-start | bytes 294920 | tf_op jit(solution)/shard_map/ppermute | solution.py:19
  94.8 7.8 %collective-permute-done.10 = f32[192,128]{1,0:T(8,128)S(1)} collective-permute-done((f32[192,128]{1,0:T(8,128)S(1)}, f32[192,128]{1,0:T(8,128)S(1)}, u32[]{:S(2)}, u32[]{:S(2)}) %collective-permute-start.10) | collective-permute-done | bytes 98336 | tf_op jit(solution)/shard_map/ppermute | solution.py:19
  102.7 3.4 %shard_map.90 = (f32[384,256]{1,0:T(8,128)S(1)}, f32[384,256]{1,0:T(8,128)S(1)}, f32[1536,256]{1,0:T(8,128)S(1)}) custom-call(f32[6]{0:T(128)S(1)} %pad_maximum_fusion.refs_0_.flags, f32[1536,1536]{1,0:T(8,128)S(1)} %bitcast.26, f32[384,256]{1,0:T(8,128)S(1)} %get-tuple-element.98.refs_2_, f32[384,256]{1,0:T(8,128)S(1)} %get-tuple-element.99.refs_3_, ...), custom_call_target="tpu_custom_call" | custom-call | flops 1024 | bytes 1024 | tf_op jit(solution)/shard_map/pallas_call | solution.py:333
  106.2 2.7 %shard_map.91 = (f32[384,256]{1,0:T(8,128)S(1)}, f32[384,256]{1,0:T(8,128)S(1)}, f32[392,256]{1,0:T(8,128)S(1)}, f32[392,256]{1,0:T(8,128)S(1)}) custom-call(f32[6]{0:T(128)S(1)} %pad_maximum_fusion.refs_0_.flags, f32[1536,1536]{1,0:T(8,128)S(1)} %bitcast.27, f32[392,256]{1,0:T(8,128)S(1)} %get-tuple-element.96.refs_6_.refs_2_, ...), custom_call_target="tpu_custom_call" | custom-call | flops 8000000000 | bytes 1024 | tf_op jit(solution)/shard_map/pallas_call | solution.py:333
  108.9 2.3 %shard_map.92 = (f32[384,256]{1,0:T(8,128)S(1)}, f32[384,256]{1,0:T(8,128)S(1)}, f32[24,256]{1,0:T(8,128)S(1)}) custom-call(f32[6]{0:T(128)S(1)} %pad_maximum_fusion.refs_0_.flags, f32[1536,1536]{1,0:T(8,128)S(1)} %bitcast.28, f32[384,256]{1,0:T(8,128)S(1)} %get-tuple-element.102.refs_2_.refs_0_, f32[384,256]{1,0:T(8,128)S(1)} %get-tuple-element.103.refs_3_.refs_1_, ...), custom_call_target="tpu_custom_call" | custom-call | flops 1024 | bytes 1024 | tf_op jit(solution)/shard_map/pallas_call | solution.py:333
  111.9 3.2 %collective-permute-done.13 = f32[24,256]{1,0:T(8,128)S(1)} collective-permute-done((f32[24,256]{1,0:T(8,128)S(1)}, f32[24,256]{1,0:T(8,128)S(1)}, u32[]{:S(2)}, u32[]{:S(2)}) %collective-permute-start.13) | collective-permute-done | bytes 24608 | tf_op jit(solution)/shard_map/ppermute | solution.py:19
  115.1 2.4 %collective-permute-start.16 = (f32[48,256]{1,0:T(8,128)S(1)}, f32[48,256]{1,0:T(8,128)S(1)}, u32[]{:S(2)}, u32[]{:S(2)}) collective-permute-start(f32[48,256]{1,0:T(8,128)S(1)} %pad_add_fusion.3.refs_0_), channel_id=1, source_target_pairs={{0,6},{1,7},{2,4},{3,5},{4,2},{5,3},{6,0},{7,1},{8,14},{9,15},{10,... | collective-permute-start | bytes 147464 | tf_op jit(solution)/shard_map/ppermute | solution.py:19
  117.5 2.0 collective-permute-start.14
  119.5 1.8 collective-permute-done.16.refs_3_
  121.3 1.2 collective-permute-done.15.refs_2_
  122.5 1.3 collective-permute-start.21
  126.0 1.8 collective-permute-start.19
  128.9 2.0 collective-permute-start.20
  130.9 3.5 %shard_map.95.refs_10_.refs_11_.refs_12_ = f32[1536,128]{1,0:T(8,128)S(1)} custom-call(f32[6]{0:T(128)S(1)} %pad_maximum_fusion.refs_0_.flags, f32[416,256]{1,0:T(8,128)S(1)} %collective-permute-done.refs_4_.near0, f32[416,256]{1,0:T(8,128)S(1)} %collective-permute-done.1.refs_5_.near1, f32[416,256]{1,0:T(8,128)S(1)} %collective-permute-done.2.refs_4_.near2, ...), custom_call_target="tpu_custom_call" | custom-call | flops 1024 | bytes 1024 | tf_op jit(solution)/shard_map/pallas_call | solution.py:333
  134.4 2.9 %collective-permute-done.20 = f32[136,256]{1,0:T(8,128)S(1)} collective-permute-done((f32[136,256]{1,0:T(8,128)S(1)}, f32[136,256]{1,0:T(8,128)S(1)}, u32[]{:S(2)}, u32[]{:S(2)}) %collective-permute-start.20) | collective-permute-done | bytes 139296 | tf_op jit(solution)/shard_map/ppermute | solution.py:19
  137.9 3.7 %shard_map.96 = (f32[384,256]{1,0:T(8,128)S(1)}, f32[384,256]{1,0:T(8,128)S(1)}, f32[384,256]{1,0:T(8,128)S(1)}, f32[384,256]{1,0:T(8,128)S(1)}, f32[1536,256]{1,0:T(8,128)S(1)}) custom-call(f32[6]{0:T(128)S(1)} %pad_maximum_fusion.refs_0_.flags, f32[1536,1536]{1,0:T(8,128)S(1)} %bitcast.21, f32[384,256]{1,0:T(8,128)S(1)} %get-tuple-element.113.refs_2_.refs_8_, ...), custom_call_target="tpu_custom_call" | custom-call | flops 1024 | bytes 1024 | tf_op jit(solution)/shard_map/pallas_call | solution.py:333
  141.7 3.2 %shard_map.97 = (f32[384,256]{1,0:T(8,128)S(1)}, f32[384,256]{1,0:T(8,128)S(1)}, f32[384,256]{1,0:T(8,128)S(1)}, f32[384,256]{1,0:T(8,128)S(1)}, f32[392,256]{1,0:T(8,128)S(1)}, /*index=5*/f32[392,256]{1,0:T(8,128)S(1)}) custom-call(f32[6]{0:T(128)S(1)} %pad_maximum_fusion.refs_0_.flags, f32[1536,1536]{1,0:T(8,128)S(1)} %bitcast.22, ...), custom_call_target="tpu_custom_call" | custom-call | flops 8000000000 | bytes 1024 | tf_op jit(solution)/shard_map/pallas_call | solution.py:333
  144.9 3.2 %collective-permute-start.25 = (f32[392,256]{1,0:T(8,128)S(1)}, f32[392,256]{1,0:T(8,128)S(1)}, u32[]{:S(2)}, u32[]{:S(2)}) collective-permute-start(f32[392,256]{1,0:T(8,128)S(1)} %get-tuple-element.127.refs_6_.refs_2_), channel_id=1, source_target_pairs={{0,1},{1,0},{2,3},{3,2},{4,5},{5,4},{6,7},{7,6},{8,9},{9,8},{10,11... | collective-permute-start | bytes 1204232 | tf_op jit(solution)/shard_map/ppermute | solution.py:19
  148.8 2.0 shard_map.98
  152.6 3.4 %shard_map.99 = (f32[384,256]{1,0:T(8,128)S(1)}, f32[384,256]{1,0:T(8,128)S(1)}, f32[1536,256]{1,0:T(8,128)S(1)}) custom-call(f32[6]{0:T(128)S(1)} %pad_maximum_fusion.refs_0_.flags, f32[1536,1536]{1,0:T(8,128)S(1)} %bitcast.29, f32[384,256]{1,0:T(8,128)S(1)} %get-tuple-element.129.refs_2_, f32[384,256]{1,0:T(8,128)S(1)} %get-tuple-element.130.refs_3_, ...), custom_call_target="tpu_custom_call" | custom-call | flops 1024 | bytes 1024 | tf_op jit(solution)/shard_map/pallas_call | solution.py:333
  156.0 7.4 %collective-permute-done.25.refs_4_ = f32[392,256]{1,0:T(8,128)S(1)} collective-permute-done((f32[392,256]{1,0:T(8,128)S(1)}, f32[392,256]{1,0:T(8,128)S(1)}, u32[]{:S(2)}, u32[]{:S(2)}) %collective-permute-start.25) | collective-permute-done | bytes 401440 | tf_op jit(solution)/shard_map/ppermute | solution.py:19
  163.4 2.7 %shard_map.100 = (f32[384,256]{1,0:T(8,128)S(1)}, f32[384,256]{1,0:T(8,128)S(1)}, f32[392,256]{1,0:T(8,128)S(1)}, f32[392,256]{1,0:T(8,128)S(1)}) custom-call(f32[6]{0:T(128)S(1)} %pad_maximum_fusion.refs_0_.flags, f32[1536,1536]{1,0:T(8,128)S(1)} %bitcast.30, f32[392,256]{1,0:T(8,128)S(1)} %get-tuple-element.127.refs_6_.refs_2_, ...), custom_call_target="tpu_custom_call" | custom-call | flops 8000000000 | bytes 1024 | tf_op jit(solution)/shard_map/pallas_call | solution.py:333
  166.1 2.5 %shard_map.101 = (f32[384,256]{1,0:T(8,128)S(1)}, f32[384,256]{1,0:T(8,128)S(1)}, f32[24,256]{1,0:T(8,128)S(1)}) custom-call(f32[6]{0:T(128)S(1)} %pad_maximum_fusion.refs_0_.flags, f32[1536,1536]{1,0:T(8,128)S(1)} %bitcast.31, f32[384,256]{1,0:T(8,128)S(1)} %get-tuple-element.131.refs_2_.refs_4_, f32[384,256]{1,0:T(8,128)S(1)} %get-tuple-element.132.refs_3_.refs_5_, ...), custom_call_target="tpu_custom_call" | custom-call | flops 1024 | bytes 1024 | tf_op jit(solution)/shard_map/pallas_call | solution.py:333
  168.6 2.5 %collective-permute-start.27 = (f32[24,256]{1,0:T(8,128)S(1)}, f32[24,256]{1,0:T(8,128)S(1)}, u32[]{:S(2)}, u32[]{:S(2)}) collective-permute-start(f32[24,256]{1,0:T(8,128)S(1)} %get-tuple-element.139), channel_id=1, source_target_pairs={{0,1},{1,0},{2,3},{3,2},{4,5},{5,4},{6,7},{7,6},{8,9},{9,8},{10,11... | collective-permute-start | bytes 73736 | tf_op jit(solution)/shard_map/ppermute | solution.py:19
  171.1 1.8 collective-permute-done.27
  173.0 3.8 %collective-permute-start.30 = (f32[48,256]{1,0:T(8,128)S(1)}, f32[48,256]{1,0:T(8,128)S(1)}, u32[]{:S(2)}, u32[]{:S(2)}) collective-permute-start(f32[48,256]{1,0:T(8,128)S(1)} %pad_add_fusion.2.refs_0_), channel_id=1, source_target_pairs={{0,6},{1,7},{2,4},{3,5},{4,2},{5,3},{6,0},{7,1},{8,14},{9,15},{10,... | collective-permute-start | bytes 147464 | tf_op jit(solution)/shard_map/ppermute | solution.py:19
  177.4 1.6 collective-permute-done.30.refs_3_
  179.0 3.0 %collective-permute-done.29.refs_2_ = f32[48,256]{1,0:T(8,128)S(1)} collective-permute-done((f32[48,256]{1,0:T(8,128)S(1)}, f32[48,256]{1,0:T(8,128)S(1)}, u32[]{:S(2)}, u32[]{:S(2)}) %collective-permute-start.29) | collective-permute-done | bytes 49184 | tf_op jit(solution)/shard_map/ppermute | solution.py:19
  182.0 1.6 collective-permute-start.35
  185.5 2.0 collective-permute-start.31
  188.6 1.8 collective-permute-start.32
  190.4 6.6 %collective-permute-done.32 = f32[136,256]{1,0:T(8,128)S(1)} collective-permute-done((f32[136,256]{1,0:T(8,128)S(1)}, f32[136,256]{1,0:T(8,128)S(1)}, u32[]{:S(2)}, u32[]{:S(2)}) %collective-permute-start.32) | collective-permute-done | bytes 139296 | tf_op jit(solution)/shard_map/ppermute | solution.py:19
  197.1 3.7 %collective-permute-done.35.refs_7_ = f32[392,256]{1,0:T(8,128)S(1)} collective-permute-done((f32[392,256]{1,0:T(8,128)S(1)}, f32[392,256]{1,0:T(8,128)S(1)}, u32[]{:S(2)}, u32[]{:S(2)}) %collective-permute-start.35) | collective-permute-done | bytes 401440 | tf_op jit(solution)/shard_map/ppermute | solution.py:19
  200.8 2.0 shard_map.103
  203.4 1.2 shard_map.105
  204.6 1.9 shard_map.106
  (104 shorter events, 17.9 us)
Async XLA Ops:
  0.6 53.3 %copy-start.8 = (s32[1,1,16]{2,1,0:T(1,128)S(1)}, s32[1,1,16]{2,1,0:T(1,128)}, u32[]{:S(2)}) copy-start(s32[1,1,16]{2,1,0:T(1,128)} %param.11) | copy-start | bytes 196
  0.6 53.2 %copy-start.7 = (f32[4,128]{1,0:T(4,128)S(1)}, f32[4,128]{1,0:T(4,128)}, u32[]{:S(2)}) copy-start(f32[4,128]{1,0:T(4,128)} %param.13) | copy-start | bytes 6148
  0.7 57.3 %copy-start.6 = (s32[1,1,4,384]{3,2,1,0:T(4,128)S(1)}, s32[1,1,4,384]{3,2,1,0:T(4,128)}, u32[]{:S(2)}) copy-start(s32[1,1,4,384]{3,2,1,0:T(4,128)} %param.12) | copy-start | bytes 18436
  53.4 20.7 %copy-start.1 = (f32[416,256]{1,0:T(8,128)S(1)}, f32[416,256]{1,0:T(8,128)}, u32[]{:S(2)}) copy-start(f32[416,256]{1,0:T(8,128)} %get-tuple-element.83.refs_2_.sent) | copy-start | bytes 1277956
  53.4 20.7 %collective-permute-start = (f32[416,256]{1,0:T(8,128)}, f32[416,256]{1,0:T(8,128)S(1)}, u32[]{:S(2)}, u32[]{:S(2)}) collective-permute-start(f32[416,256]{1,0:T(8,128)} %get-tuple-element.83.refs_2_.sent), channel_id=1, source_target_pairs={{0,8},{8,0},{16,24},{24,16},{1,9},{9,1},{17,25},{25,17},{2,10},{10... | collective-permute-start | bytes 1277960 | tf_op jit(solution)/shard_map/ppermute | solution.py:19
  53.9 4.4 %collective-permute-start.4 = (f32[12,128]{1,0:T(8,128)S(1)}, f32[12,128]{1,0:T(8,128)S(1)}, u32[]{:S(2)}, u32[]{:S(2)}) collective-permute-start(f32[12,128]{1,0:T(8,128)S(1)} %pad_add_fusion.7), channel_id=1, source_target_pairs={{0,1},{1,0},{2,3},{3,2},{4,5},{5,4},{6,7},{7,6},{8,9},{9,8},{10,11... | collective-permute-start | bytes 18440 | tf_op jit(solution)/shard_map/ppermute | solution.py:19
  56.5 17.5 %collective-permute-start.1 = (f32[416,256]{1,0:T(8,128)}, f32[416,256]{1,0:T(8,128)S(1)}, u32[]{:S(2)}, u32[]{:S(2)}) collective-permute-start(f32[416,256]{1,0:T(8,128)} %get-tuple-element.84.refs_3_), channel_id=1, source_target_pairs={{8,16},{16,8},{9,17},{17,9},{10,18},{18,10},{11,19},{19,11},{12,20... | collective-permute-start | bytes 1277960 | tf_op jit(solution)/shard_map/ppermute | solution.py:26
  57.2 25.0 %collective-permute-start.2 = (f32[416,256]{1,0:T(8,128)}, f32[416,256]{1,0:T(8,128)S(1)}, u32[]{:S(2)}, u32[]{:S(2)}) collective-permute-start(f32[416,256]{1,0:T(8,128)} %get-tuple-element.89.refs_2_), channel_id=1, source_target_pairs={{0,1},{1,0},{2,3},{3,2},{4,5},{5,4},{6,7},{7,6},{8,9},{9,8},{10,11... | collective-permute-start | bytes 1277960 | tf_op jit(solution)/shard_map/ppermute | solution.py:19
  57.3 24.9 %collective-permute-start.3 = (f32[416,256]{1,0:T(8,128)}, f32[416,256]{1,0:T(8,128)S(1)}, u32[]{:S(2)}, u32[]{:S(2)}) collective-permute-start(f32[416,256]{1,0:T(8,128)} %get-tuple-element.90.refs_3_), channel_id=1, source_target_pairs={{1,2},{2,1},{3,4},{4,3},{5,6},{6,5},{9,10},{10,9},{11,12},{12,11},... | collective-permute-start | bytes 1277960 | tf_op jit(solution)/shard_map/ppermute | solution.py:26
  58.3 4.0 %collective-permute-start.5 = (f32[24,128]{1,0:T(8,128)S(1)}, f32[24,128]{1,0:T(8,128)S(1)}, u32[]{:S(2)}, u32[]{:S(2)}) collective-permute-start(f32[24,128]{1,0:T(8,128)S(1)} %pad_add_fusion.6), channel_id=1, source_target_pairs={{0,8},{8,0},{16,24},{24,16},{1,9},{9,1},{17,25},{25,17},{2,10},{10... | collective-permute-start | bytes 36872 | tf_op jit(solution)/shard_map/ppermute | solution.py:19
  62.3 4.7 %collective-permute-start.6 = (f32[48,128]{1,0:T(8,128)S(1)}, f32[48,128]{1,0:T(8,128)S(1)}, u32[]{:S(2)}, u32[]{:S(2)}) collective-permute-start(f32[48,128]{1,0:T(8,128)S(1)} %pad_add_fusion.5), channel_id=1, source_target_pairs={{0,16},{8,24},{16,0},{24,8},{1,17},{9,25},{17,1},{25,9},{2,18},{10... | collective-permute-start | bytes 73736 | tf_op jit(solution)/shard_map/ppermute | solution.py:19
  67.0 7.0 %collective-permute-start.7 = (f32[96,128]{1,0:T(8,128)S(1)}, f32[96,128]{1,0:T(8,128)S(1)}, u32[]{:S(2)}, u32[]{:S(2)}) collective-permute-start(f32[96,128]{1,0:T(8,128)S(1)} %pad_add_fusion.4), channel_id=1, source_target_pairs={{0,4},{1,5},{2,6},{3,7},{4,0},{5,1},{6,2},{7,3},{8,12},{9,13},{10,... | collective-permute-start | bytes 147464 | tf_op jit(solution)/shard_map/ppermute | solution.py:19
  74.1 3.7 %copy-start = (f32[1,1,1536,1536]{3,2,1,0:T(8,128)S(1)}, f32[1,1,1536,1536]{3,2,1,0:T(8,128)}, u32[]{:S(2)}) copy-start(f32[1,1,1536,1536]{3,2,1,0:T(8,128)} %param.9) | copy-start | bytes 28311556
  82.2 4.8 %slice-start = ((s8[9437184]{0:T(1024)(128)(4,1)}), s8[4194304]{0:T(1024)(128)(4,1)S(1)}, s32[]{:S(2)}) async-start(s8[9437184]{0:T(1024)(128)(4,1)} %bitcast.18), calls=%async_computation | async-start | bytes 8388608
  82.2 20.4 %slice-start.3 = ((s8[9437184]{0:T(1024)(128)(4,1)}), s8[4194304]{0:T(1024)(128)(4,1)S(1)}, s32[]{:S(2)}) async-start(s8[9437184]{0:T(1024)(128)(4,1)} %bitcast.24), calls=%async_computation.3 | async-start | bytes 8388608
  82.2 4.8 %slice-start.1 = ((s8[9437184]{0:T(1024)(128)(4,1)}), s8[4194304]{0:T(1024)(128)(4,1)S(1)}, s32[]{:S(2)}) async-start(s8[9437184]{0:T(1024)(128)(4,1)} %bitcast.18), calls=%async_computation.1 | async-start | bytes 8388608
  82.3 4.8 %slice-start.2 = ((s8[9437184]{0:T(1024)(128)(4,1)}), s8[1048576]{0:T(1024)(128)(4,1)S(1)}, s32[]{:S(2)}) async-start(s8[9437184]{0:T(1024)(128)(4,1)} %bitcast.18), calls=%async_computation.2 | async-start | bytes 2097152
  82.3 20.4 %slice-start.4 = ((s8[9437184]{0:T(1024)(128)(4,1)}), s8[4194304]{0:T(1024)(128)(4,1)S(1)}, s32[]{:S(2)}) async-start(s8[9437184]{0:T(1024)(128)(4,1)} %bitcast.24), calls=%async_computation.4 | async-start | bytes 8388608
  82.3 20.4 %slice-start.5 = ((s8[9437184]{0:T(1024)(128)(4,1)}), s8[1048576]{0:T(1024)(128)(4,1)S(1)}, s32[]{:S(2)}) async-start(s8[9437184]{0:T(1024)(128)(4,1)} %bitcast.24), calls=%async_computation.5 | async-start | bytes 2097152
  85.0 21.2 %collective-permute-start.11 = (f32[392,256]{1,0:T(8,128)S(1)}, f32[392,256]{1,0:T(8,128)S(1)}, u32[]{:S(2)}, u32[]{:S(2)}) collective-permute-start(f32[392,256]{1,0:T(8,128)S(1)} %get-tuple-element.96.refs_6_.refs_2_), channel_id=1, source_target_pairs={{0,1},{1,0},{2,3},{3,2},{4,5},{5,4},{6,7},{7,6},{8,9},{9,8},{10,11... | collective-permute-start | bytes 1204232 | tf_op jit(solution)/shard_map/ppermute | solution.py:19
  86.2 20.0 %collective-permute-start.12 = (f32[392,256]{1,0:T(8,128)S(1)}, f32[392,256]{1,0:T(8,128)S(1)}, u32[]{:S(2)}, u32[]{:S(2)}) collective-permute-start(f32[392,256]{1,0:T(8,128)S(1)} %get-tuple-element.97.refs_7_.refs_3_), channel_id=1, source_target_pairs={{1,2},{2,1},{3,4},{4,3},{5,6},{6,5},{9,10},{10,9},{11,12},{12,11},... | collective-permute-start | bytes 1204232 | tf_op jit(solution)/shard_map/ppermute | solution.py:26
  89.1 13.5 %collective-permute-start.8 = (f32[384,256]{1,0:T(8,128)S(1)}, f32[384,256]{1,0:T(8,128)S(1)}, u32[]{:S(2)}, u32[]{:S(2)}) collective-permute-start(f32[384,256]{1,0:T(8,128)S(1)} %get-tuple-element.98.refs_2_), channel_id=1, source_target_pairs={{0,8},{8,0},{16,24},{24,16},{1,9},{9,1},{17,25},{25,17},{2,10},{10... | collective-permute-start | bytes 1179656 | tf_op jit(solution)/shard_map/ppermute | solution.py:19
  91.1 11.5 %collective-permute-start.9 = (f32[384,256]{1,0:T(8,128)S(1)}, f32[384,256]{1,0:T(8,128)S(1)}, u32[]{:S(2)}, u32[]{:S(2)}) collective-permute-start(f32[384,256]{1,0:T(8,128)S(1)} %get-tuple-element.99.refs_3_), channel_id=1, source_target_pairs={{8,16},{16,8},{9,17},{17,9},{10,18},{18,10},{11,19},{19,11},{12,20... | collective-permute-start | bytes 1179656 | tf_op jit(solution)/shard_map/ppermute | solution.py:26
  91.9 10.6 %collective-permute-start.10 = (f32[192,128]{1,0:T(8,128)S(1)}, f32[192,128]{1,0:T(8,128)S(1)}, u32[]{:S(2)}, u32[]{:S(2)}) collective-permute-start(f32[192,128]{1,0:T(8,128)S(1)} %pad_add_fusion.1), channel_id=1, source_target_pairs={{0,2},{1,3},{2,0},{3,1},{4,6},{5,7},{6,4},{7,5},{8,10},{9,11},{10,... | collective-permute-start | bytes 294920 | tf_op jit(solution)/shard_map/ppermute | solution.py:19
  111.2 3.9 %collective-permute-start.13 = (f32[24,256]{1,0:T(8,128)S(1)}, f32[24,256]{1,0:T(8,128)S(1)}, u32[]{:S(2)}, u32[]{:S(2)}) collective-permute-start(f32[24,256]{1,0:T(8,128)S(1)} %get-tuple-element.112), channel_id=1, source_target_pairs={{0,1},{1,0},{2,3},{3,2},{4,5},{5,4},{6,7},{7,6},{8,9},{9,8},{10,11... | collective-permute-start | bytes 73736 | tf_op jit(solution)/shard_map/ppermute | solution.py:19
  115.1 6.2 %collective-permute-start.16 = (f32[48,256]{1,0:T(8,128)S(1)}, f32[48,256]{1,0:T(8,128)S(1)}, u32[]{:S(2)}, u32[]{:S(2)}) collective-permute-start(f32[48,256]{1,0:T(8,128)S(1)} %pad_add_fusion.3.refs_0_), channel_id=1, source_target_pairs={{0,6},{1,7},{2,4},{3,5},{4,2},{5,3},{6,0},{7,1},{8,14},{9,15},{10,... | collective-permute-start | bytes 147464 | tf_op jit(solution)/shard_map/ppermute | solution.py:19
  117.5 5.0 %collective-permute-start.15 = (f32[48,256]{1,0:T(8,128)S(1)}, f32[48,256]{1,0:T(8,128)S(1)}, u32[]{:S(2)}, u32[]{:S(2)}) collective-permute-start(f32[48,256]{1,0:T(8,128)S(1)} %pad_add_fusion.3.refs_0_), channel_id=1, source_target_pairs={{0,4},{1,5},{2,6},{3,7},{4,0},{5,1},{6,2},{7,3},{8,12},{9,13},{10,... | collective-permute-start | bytes 147464 | tf_op jit(solution)/shard_map/ppermute | solution.py:19
  117.5 5.0 %collective-permute-start.14 = (f32[48,256]{1,0:T(8,128)S(1)}, f32[48,256]{1,0:T(8,128)S(1)}, u32[]{:S(2)}, u32[]{:S(2)}) collective-permute-start(f32[48,256]{1,0:T(8,128)S(1)} %pad_add_fusion.3.refs_0_), channel_id=1, source_target_pairs={{0,2},{1,3},{2,0},{3,1},{4,6},{5,7},{6,4},{7,5},{8,10},{9,11},{10,... | collective-permute-start | bytes 147464 | tf_op jit(solution)/shard_map/ppermute | solution.py:19
  122.5 19.2 %collective-permute-start.21 = (f32[392,256]{1,0:T(8,128)S(1)}, f32[392,256]{1,0:T(8,128)S(1)}, u32[]{:S(2)}, u32[]{:S(2)}) collective-permute-start(f32[392,256]{1,0:T(8,128)S(1)} %get-tuple-element.122.refs_6_.refs_2_.refs_10_), channel_id=1, source_target_pairs={{0,1},{1,0},{2,3},{3,2},{4,5},{5,4},{6,7},{7,6},{8,9},{9,8},{10,11... | collective-permute-start | bytes 1204232 | tf_op jit(solution)/shard_map/ppermute | solution.py:19
  123.8 17.9 %collective-permute-start.22 = (f32[392,256]{1,0:T(8,128)S(1)}, f32[392,256]{1,0:T(8,128)S(1)}, u32[]{:S(2)}, u32[]{:S(2)}) collective-permute-start(f32[392,256]{1,0:T(8,128)S(1)} %get-tuple-element.123.refs_7_.refs_3_.refs_11_), channel_id=1, source_target_pairs={{1,2},{2,1},{3,4},{4,3},{5,6},{6,5},{9,10},{10,9},{11,12},{12,11},... | collective-permute-start | bytes 1204232 | tf_op jit(solution)/shard_map/ppermute | solution.py:26
  124.5 13.4 %collective-permute-start.17 = (f32[384,256]{1,0:T(8,128)S(1)}, f32[384,256]{1,0:T(8,128)S(1)}, u32[]{:S(2)}, u32[]{:S(2)}) collective-permute-start(f32[384,256]{1,0:T(8,128)S(1)} %get-tuple-element.113.refs_2_.refs_8_), channel_id=1, source_target_pairs={{0,8},{8,0},{16,24},{24,16},{1,9},{9,1},{17,25},{25,17},{2,10},{10... | collective-permute-start | bytes 1179656 | tf_op jit(solution)/shard_map/ppermute | solution.py:19
  124.6 13.4 %collective-permute-start.18 = (f32[384,256]{1,0:T(8,128)S(1)}, f32[384,256]{1,0:T(8,128)S(1)}, u32[]{:S(2)}, u32[]{:S(2)}) collective-permute-start(f32[384,256]{1,0:T(8,128)S(1)} %get-tuple-element.114.refs_3_.refs_9_), channel_id=1, source_target_pairs={{8,16},{16,8},{9,17},{17,9},{10,18},{18,10},{11,19},{19,11},{12,20... | collective-permute-start | bytes 1179656 | tf_op jit(solution)/shard_map/ppermute | solution.py:26
  126.0 2.8 %collective-permute-start.19 = (f32[136,256]{1,0:T(8,128)S(1)}, f32[136,256]{1,0:T(8,128)S(1)}, u32[]{:S(2)}, u32[]{:S(2)}) collective-permute-start(f32[136,256]{1,0:T(8,128)S(1)} %shard_map.93), channel_id=1, source_target_pairs={{0,8},{8,0},{16,24},{24,16},{1,9},{9,1},{17,25},{25,17},{2,10},{10... | collective-permute-start | bytes 417800 | tf_op jit(solution)/shard_map/ppermute | solution.py:19
  128.9 8.5 %collective-permute-start.20 = (f32[136,256]{1,0:T(8,128)S(1)}, f32[136,256]{1,0:T(8,128)S(1)}, u32[]{:S(2)}, u32[]{:S(2)}) collective-permute-start(f32[136,256]{1,0:T(8,128)S(1)} %add.142), channel_id=1, source_target_pairs={{0,16},{8,24},{16,0},{24,8},{1,17},{9,25},{17,1},{25,9},{2,18},{10... | collective-permute-start | bytes 417800 | tf_op jit(solution)/shard_map/ppermute | solution.py:19
  144.9 18.5 %collective-permute-start.25 = (f32[392,256]{1,0:T(8,128)S(1)}, f32[392,256]{1,0:T(8,128)S(1)}, u32[]{:S(2)}, u32[]{:S(2)}) collective-permute-start(f32[392,256]{1,0:T(8,128)S(1)} %get-tuple-element.127.refs_6_.refs_2_), channel_id=1, source_target_pairs={{0,1},{1,0},{2,3},{3,2},{4,5},{5,4},{6,7},{7,6},{8,9},{9,8},{10,11... | collective-permute-start | bytes 1204232 | tf_op jit(solution)/shard_map/ppermute | solution.py:19
  148.1 15.3 %collective-permute-start.26 = (f32[392,256]{1,0:T(8,128)S(1)}, f32[392,256]{1,0:T(8,128)S(1)}, u32[]{:S(2)}, u32[]{:S(2)}) collective-permute-start(f32[392,256]{1,0:T(8,128)S(1)} %get-tuple-element.128.refs_7_.refs_3_), channel_id=1, source_target_pairs={{1,2},{2,1},{3,4},{4,3},{5,6},{6,5},{9,10},{10,9},{11,12},{12,11},... | collective-permute-start | bytes 1204232 | tf_op jit(solution)/shard_map/ppermute | solution.py:26
  150.8 1.8 collective-permute-start.23
  150.9 1.7 collective-permute-start.24
  168.6 4.4 %collective-permute-start.27 = (f32[24,256]{1,0:T(8,128)S(1)}, f32[24,256]{1,0:T(8,128)S(1)}, u32[]{:S(2)}, u32[]{:S(2)}) collective-permute-start(f32[24,256]{1,0:T(8,128)S(1)} %get-tuple-element.139), channel_id=1, source_target_pairs={{0,1},{1,0},{2,3},{3,2},{4,5},{5,4},{6,7},{7,6},{8,9},{9,8},{10,11... | collective-permute-start | bytes 73736 | tf_op jit(solution)/shard_map/ppermute | solution.py:19
  173.0 6.0 %collective-permute-start.30 = (f32[48,256]{1,0:T(8,128)S(1)}, f32[48,256]{1,0:T(8,128)S(1)}, u32[]{:S(2)}, u32[]{:S(2)}) collective-permute-start(f32[48,256]{1,0:T(8,128)S(1)} %pad_add_fusion.2.refs_0_), channel_id=1, source_target_pairs={{0,6},{1,7},{2,4},{3,5},{4,2},{5,3},{6,0},{7,1},{8,14},{9,15},{10,... | collective-permute-start | bytes 147464 | tf_op jit(solution)/shard_map/ppermute | solution.py:19
  176.7 5.2 %collective-permute-start.29 = (f32[48,256]{1,0:T(8,128)S(1)}, f32[48,256]{1,0:T(8,128)S(1)}, u32[]{:S(2)}, u32[]{:S(2)}) collective-permute-start(f32[48,256]{1,0:T(8,128)S(1)} %pad_add_fusion.2.refs_0_), channel_id=1, source_target_pairs={{0,4},{1,5},{2,6},{3,7},{4,0},{5,1},{6,2},{7,3},{8,12},{9,13},{10,... | collective-permute-start | bytes 147464 | tf_op jit(solution)/shard_map/ppermute | solution.py:19
  176.7 5.2 %collective-permute-start.28 = (f32[48,256]{1,0:T(8,128)S(1)}, f32[48,256]{1,0:T(8,128)S(1)}, u32[]{:S(2)}, u32[]{:S(2)}) collective-permute-start(f32[48,256]{1,0:T(8,128)S(1)} %pad_add_fusion.2.refs_0_), channel_id=1, source_target_pairs={{0,2},{1,3},{2,0},{3,1},{4,6},{5,7},{6,4},{7,5},{8,10},{9,11},{10,... | collective-permute-start | bytes 147464 | tf_op jit(solution)/shard_map/ppermute | solution.py:19
  182.0 18.8 %collective-permute-start.35 = (f32[392,256]{1,0:T(8,128)S(1)}, f32[392,256]{1,0:T(8,128)S(1)}, u32[]{:S(2)}, u32[]{:S(2)}) collective-permute-start(f32[392,256]{1,0:T(8,128)S(1)} %get-tuple-element.147.refs_6_.refs_3_), channel_id=1, source_target_pairs={{0,1},{1,0},{2,3},{3,2},{4,5},{5,4},{6,7},{7,6},{8,9},{9,8},{10,11... | collective-permute-start | bytes 1204232 | tf_op jit(solution)/shard_map/ppermute | solution.py:19
  183.5 17.3 %collective-permute-start.36 = (f32[392,256]{1,0:T(8,128)S(1)}, f32[392,256]{1,0:T(8,128)S(1)}, u32[]{:S(2)}, u32[]{:S(2)}) collective-permute-start(f32[392,256]{1,0:T(8,128)S(1)} %get-tuple-element.148.refs_7_.refs_4_), channel_id=1, source_target_pairs={{1,2},{2,1},{3,4},{4,3},{5,6},{6,5},{9,10},{10,9},{11,12},{12,11},... | collective-permute-start | bytes 1204232 | tf_op jit(solution)/shard_map/ppermute | solution.py:26
  184.2 12.8 %collective-permute-start.33 = (f32[384,256]{1,0:T(8,128)S(1)}, f32[384,256]{1,0:T(8,128)S(1)}, u32[]{:S(2)}, u32[]{:S(2)}) collective-permute-start(f32[384,256]{1,0:T(8,128)S(1)} %get-tuple-element.145.refs_1_), channel_id=1, source_target_pairs={{0,8},{8,0},{16,24},{24,16},{1,9},{9,1},{17,25},{25,17},{2,10},{10... | collective-permute-start | bytes 1179656 | tf_op jit(solution)/shard_map/ppermute | solution.py:19
  184.3 12.8 %collective-permute-start.34 = (f32[384,256]{1,0:T(8,128)S(1)}, f32[384,256]{1,0:T(8,128)S(1)}, u32[]{:S(2)}, u32[]{:S(2)}) collective-permute-start(f32[384,256]{1,0:T(8,128)S(1)} %get-tuple-element.146.refs_2_), channel_id=1, source_target_pairs={{8,16},{16,8},{9,17},{17,9},{10,18},{18,10},{11,19},{19,11},{12,20... | collective-permute-start | bytes 1179656 | tf_op jit(solution)/shard_map/ppermute | solution.py:26
  185.5 3.0 %collective-permute-start.31 = (f32[136,256]{1,0:T(8,128)S(1)}, f32[136,256]{1,0:T(8,128)S(1)}, u32[]{:S(2)}, u32[]{:S(2)}) collective-permute-start(f32[136,256]{1,0:T(8,128)S(1)} %shard_map.102), channel_id=1, source_target_pairs={{0,8},{8,0},{16,24},{24,16},{1,9},{9,1},{17,25},{25,17},{2,10},{10... | collective-permute-start | bytes 417800 | tf_op jit(solution)/shard_map/ppermute | solution.py:19
  188.6 8.4 %collective-permute-start.32 = (f32[136,256]{1,0:T(8,128)S(1)}, f32[136,256]{1,0:T(8,128)S(1)}, u32[]{:S(2)}, u32[]{:S(2)}) collective-permute-start(f32[136,256]{1,0:T(8,128)S(1)} %add.145), channel_id=1, source_target_pairs={{0,16},{8,24},{16,0},{24,8},{1,17},{9,25},{17,1},{25,9},{2,18},{10... | collective-permute-start | bytes 417800 | tf_op jit(solution)/shard_map/ppermute | solution.py:19
  (4 other events, 10.7 us)

commit v2 on v1

--- a/solution.py
+++ b/solution.py
@@ -90,7 +90,7 @@
 
 
 def pack_kernel(corners, load, coupling, *refs):
-    outs, (lists, sems) = refs[:4], refs[4:]
+    outs, sems = refs[:4], refs[4]
     face = load.shape[0] // 4
     width = load.shape[1]
     ncl = coupling.shape[0]
@@ -111,12 +111,23 @@
             source = coupling.at[:, pl.ds(pl.multiple_of(first + at, 128), wide)]
             copy(source, out.at[pl.ds(face + block * ncl, ncl), pl.ds(0, wide)])
     start = face + (face // width) * ncl
-    for k in range(ncl):
-        lists[k : k + 1] = jnp.full((1, lists.shape[1]), corners[k].astype(F32))
     for out in outs:
-        copy(lists, out.at[pl.ds(start, ncl), pl.ds(face % width, lists.shape[1])])
+        for k in range(ncl):
+            listed = jnp.full((1, width - face % width), corners[k].astype(F32))
+            out[start + k : start + k + 1, face % width :] = listed
     for started in copies:
         started.wait()
+
+
+def rows_kernel(corners, inverse, out):
+    own = inverse.shape[0]
+    out[:own] = inverse[...]
+    out[own:] = jnp.zeros((out.shape[0] - own, out.shape[1]), F32)
+    columns = lax.broadcasted_iota(jnp.int32, (1, out.shape[1]), 1)
+    listed = jnp.zeros((1, out.shape[1]), F32)
+    for k in range(corners.shape[0]):
+        listed = jnp.where(columns == k, corners[k].astype(F32), listed)
+    out[own : own + 1] = listed
 
 
 def lift_kernel(flags, near0, near1, near2, near3, select, coupling, sent, out):
@@ -428,35 +439,32 @@
 
     step_shape = (ncoarse + 8, width)
     extra = -(-face // width) * ncl
-    copies = 4 * (2 + -(-face // width))
+    copies = 4 * (1 + -(-face // width))
     sent = call(
         pack_kernel,
         [corners, load, coupling_mat],
         [(face + extra, width)] * 4,
-        [pltpu.VMEM((ncl, width - face % width), F32), pltpu.SemaphoreType.DMA((copies,))],
+        [pltpu.SemaphoreType.DMA((copies,))],
         smem=1,
         anywhere=(1, 2),
-        out_spec=ANY_SPEC,
         limit=7 * LIMIT,
     )
     near = (*exchanged(sent[:2], "sx"), *exchanged(sent[2:], "sy"))
 
     own = coarse_inverse.shape[0]
     table_rows = own + 8
-    listed = jnp.pad(corners.astype(F32)[None], ((own, 7), (0, ncoarse - ncl)))
-    own_rows = jnp.pad(coarse_inverse, ((0, 8), (0, 0))) + listed
-    own_rows, _ = lax.optimization_barrier((own_rows, sent[0]))
-
-    def most_steps(partial, coef):
-        rows, coef = lax.optimization_barrier((doubled(own_rows, steps_of()[:-1]), coef))
-        return partial, coef, rows
-
-    residual0, _, a23, partial, most_rows = fields_of(prec_mat, sent, near, one, beside=most_steps)
+    inverse, _ = lax.optimization_barrier((coarse_inverse, sent[0]))
+    (own_rows,) = call(rows_kernel, [corners, inverse], [(table_rows, ncoarse)], smem=1, flops=CRIT_FLOPS)
+
+    def gather(partial, coef):
+        table, coef = lax.optimization_barrier((doubled(own_rows, steps_of()), coef))
+        return partial, coef, table
+
+    residual0, _, a23, partial, table = fields_of(prec_mat, sent, near, one, beside=gather)
     applied0, rho0 = prec_late(residual0, a23, partial)
     (lift,) = call(
         lift_kernel, [flags, *near, select, coupling_mat, sent[0]], [(ni, ncoarse)], smem=1
     )
-    table, half_one = lax.optimization_barrier((doubled(most_rows, steps_of()[-1:]), half_one))
     near = (*exchanged(applied0[:2], "sx"), *exchanged(applied0[2:], "sy"))
 
     direction0, _, a23, partial = fields_of(flex_mat, applied0, near, half_one)

time: 207 us -> 163 us (0.79)
  Pallas kernels: 97.6 us -> 50.3 us
  waiting for transfers between devices: 51.5 us -> 57.5 us
    pallas_call x21 -> x22, Pallas kernels: 97.6 us -> 50.3 us  [call(): pl.pallas_call(kernel, in_specs=[SMEM_SPEC if i < smem else ANY_SPEC if i...]
    ppermute x27, waiting for transfers between devices: 51.5 us -> 57.5 us  [swapped(): lax.ppermute(block, axis, [(i, i ^ bit) for i in range(lax.axis_size(axis...]
    unnamed x30 -> x24, local copies, waits for them, and re-layouts: 4.82 us -> 3.73 us
  transfers between devices with their start and end apart: 37 -> 37, of which waited for: 17 -> 20; matrix products, arithmetic and copies ran while one was open for 0% -> 0% of each run, Pallas kernels for 11% -> 15%
where the time goes in v2:
time: 163 us
  waiting for transfers between devices  57.5 us (35%)
  Pallas kernels  50.3 us (31%)
  starting transfers between devices  49.2 us (30%)
  local copies, waits for them, and re-layouts  3.76 us (2%)
    ppermute x27, waiting for transfers between devices, swapped(): lax.ppermute(block, axis, [(i, i ^ bit) for i in range(lax.axis_size(axis...  57.5 us
    pallas_call x22, Pallas kernels, call(): pl.pallas_call(kernel, in_specs=[SMEM_SPEC if i < smem else ANY_SPEC if i...  50.3 us
    ppermute x27, starting transfers between devices, swapped(): lax.ppermute(block, axis, [(i, i ^ bit) for i in range(lax.axis_size(axis...  41.8 us
    ppermute x10, starting transfers between devices, swapped_between(): return lax.ppermute(block, axis, route)  7.45 us
    unnamed x24, local copies, waits for them, and re-layouts  3.73 us
  transfers between devices with their start and end apart: 37, of which 20 were waited for; matrix products, arithmetic and copies ran while one was open for 0% of the time, Pallas kernels for 15%

profile of v2, /device:TPU:0, one launch (start us, length us, event | category | flops | bytes accessed | tf_op | source)
XLA Modules:
  0.0 162.9 jit_solution(1704184846279947037)
XLA Ops:
  0.6 3.5 %shard_map.86 = (f32[416,256]{1,0:T(8,128)}, f32[416,256]{1,0:T(8,128)}, f32[416,256]{1,0:T(8,128)}, f32[416,256]{1,0:T(8,128)}) custom-call(s32[16]{0:T(128)} %bitcast.34, f32[1536,256]{1,0:T(8,128)} %bitcast.36, f32[16,1536]{1,0:T(8,128)} %bitcast.30), custom_call_target="tpu_custom_call" | custom-call | flops 1024 | bytes 1024 | tf_op jit(solution)/shard_map/pallas_call | solution.py:344
  5.3 2.6 %collective-permute-start.4 = (f32[12,128]{1,0:T(8,128)S(1)}, f32[12,128]{1,0:T(8,128)S(1)}, u32[]{:S(2)}, u32[]{:S(2)}) collective-permute-start(f32[12,128]{1,0:T(8,128)S(1)} %shard_map.88), channel_id=1, source_target_pairs={{0,1},{1,0},{2,3},{3,2},{4,5},{5,4},{6,7},{7,6},{8,9},{9,8},{10,11... | collective-permute-start | bytes 18440 | tf_op jit(solution)/shard_map/ppermute | solution.py:19
  9.8 3.0 %collective-permute-start.5 = (f32[24,128]{1,0:T(8,128)S(1)}, f32[24,128]{1,0:T(8,128)S(1)}, u32[]{:S(2)}, u32[]{:S(2)}) collective-permute-start(f32[24,128]{1,0:T(8,128)S(1)} %pad_add_fusion.6), channel_id=1, source_target_pairs={{0,8},{8,0},{16,24},{24,16},{1,9},{9,1},{17,25},{25,17},{2,10},{10... | collective-permute-start | bytes 36872 | tf_op jit(solution)/shard_map/ppermute | solution.py:19
  14.5 4.0 %collective-permute-done.6 = f32[48,128]{1,0:T(8,128)S(1)} collective-permute-done((f32[48,128]{1,0:T(8,128)S(1)}, f32[48,128]{1,0:T(8,128)S(1)}, u32[]{:S(2)}, u32[]{:S(2)}) %collective-permute-start.6) | collective-permute-done | bytes 24608 | tf_op jit(solution)/shard_map/ppermute | solution.py:19
  18.4 4.0 %collective-permute-start.7 = (f32[96,128]{1,0:T(8,128)S(1)}, f32[96,128]{1,0:T(8,128)S(1)}, u32[]{:S(2)}, u32[]{:S(2)}) collective-permute-start(f32[96,128]{1,0:T(8,128)S(1)} %pad_add_fusion.4), channel_id=1, source_target_pairs={{0,4},{1,5},{2,6},{3,7},{4,0},{5,1},{6,2},{7,3},{8,12},{9,13},{10,... | collective-permute-start | bytes 147464 | tf_op jit(solution)/shard_map/ppermute | solution.py:19
  22.5 2.9 %collective-permute-done.7 = f32[96,128]{1,0:T(8,128)S(1)} collective-permute-done((f32[96,128]{1,0:T(8,128)S(1)}, f32[96,128]{1,0:T(8,128)S(1)}, u32[]{:S(2)}, u32[]{:S(2)}) %collective-permute-start.7) | collective-permute-done | bytes 49184 | tf_op jit(solution)/shard_map/ppermute | solution.py:19
  25.4 1.6 collective-permute-start.8
  27.1 3.1 %collective-permute-done.8 = f32[192,128]{1,0:T(8,128)S(1)} collective-permute-done((f32[192,128]{1,0:T(8,128)S(1)}, f32[192,128]{1,0:T(8,128)S(1)}, u32[]{:S(2)}, u32[]{:S(2)}) %collective-permute-start.8) | collective-permute-done | bytes 98336 | tf_op jit(solution)/shard_map/ppermute | solution.py:19
  30.2 3.7 %copy-done = f32[1,1,1536,1536]{3,2,1,0:T(8,128)S(1)} copy-done((f32[1,1,1536,1536]{3,2,1,0:T(8,128)S(1)}, f32[1,1,1536,1536]{3,2,1,0:T(8,128)}, u32[]{:S(2)}) %copy-start) | copy-done | bytes 9437208
  33.9 4.0 %shard_map.87 = (f32[384,256]{1,0:T(8,128)S(1)}, f32[384,256]{1,0:T(8,128)S(1)}, f32[1536,256]{1,0:T(8,128)S(1)}) custom-call(f32[6]{0:T(128)S(1)} %pad_maximum_fusion.refs_0_.flags, f32[1536,1536]{1,0:T(8,128)S(1)} %bitcast.14, f32[416,256]{1,0:T(8,128)S(1)} %copy-done.1, f32[416,256]{1,0:T(8,128)} %get-tuple-element.82.refs_3_, ...), custom_call_target="tpu_custom_call" | custom-call | flops 1024 | bytes 1024 | tf_op jit(solution)/shard_map/pallas_call | solution.py:344
  38.0 3.4 %shard_map.89 = (f32[384,256]{1,0:T(8,128)S(1)}, f32[384,256]{1,0:T(8,128)S(1)}, f32[392,256]{1,0:T(8,128)S(1)}, f32[392,256]{1,0:T(8,128)S(1)}) custom-call(f32[6]{0:T(128)S(1)} %pad_maximum_fusion.refs_0_.flags, f32[1536,1536]{1,0:T(8,128)S(1)} %bitcast.15, f32[416,256]{1,0:T(8,128)} %get-tuple-element.87.refs_2_, f32[416,256]{1,0:T(8,128)} %get-tuple-element.88.refs_3_, ...), custom_call_target="tpu_custom_call" | custom-call | flops 8000000000 | bytes 1024 | tf_op jit(solution)/shard_map/pallas_call | solution.py:344
  41.4 1.2 collective-permute-start.11
  43.4 2.0 %shard_map.90 = (f32[384,256]{1,0:T(8,128)S(1)}, f32[384,256]{1,0:T(8,128)S(1)}, f32[1,256]{1,0:T(1,128)S(1)}) custom-call(f32[6]{0:T(128)S(1)} %pad_maximum_fusion.refs_0_.flags, f32[1536,1536]{1,0:T(8,128)S(1)} %bitcast.18, f32[384,256]{1,0:T(8,128)S(1)} %get-tuple-element.85.refs_2_.refs_8_, f32[384,256]{1,0:T(8,128)S(1)} %get-tuple-element.86.refs_3_.refs_9_, ...), custom_call_target="tpu_custom_call" | custom-call | flops 1024 | bytes 1024 | tf_op jit(solution)/shard_map/pallas_call | solution.py:344
  47.2 3.4 %shard_map.91 = (f32[384,256]{1,0:T(8,128)S(1)}, f32[384,256]{1,0:T(8,128)S(1)}, f32[1536,256]{1,0:T(8,128)S(1)}) custom-call(f32[6]{0:T(128)S(1)} %pad_maximum_fusion.refs_0_.flags, f32[1536,1536]{1,0:T(8,128)S(1)} %bitcast.24, f32[384,256]{1,0:T(8,128)S(1)} %get-tuple-element.96.refs_2_, f32[384,256]{1,0:T(8,128)S(1)} %get-tuple-element.97.refs_3_, ...), custom_call_target="tpu_custom_call" | custom-call | flops 1024 | bytes 1024 | tf_op jit(solution)/shard_map/pallas_call | solution.py:344
  50.6 9.3 %collective-permute-done.11.refs_4_ = f32[392,256]{1,0:T(8,128)S(1)} collective-permute-done((f32[392,256]{1,0:T(8,128)S(1)}, f32[392,256]{1,0:T(8,128)S(1)}, u32[]{:S(2)}, u32[]{:S(2)}) %collective-permute-start.11) | collective-permute-done | bytes 401440 | tf_op jit(solution)/shard_map/ppermute | solution.py:19
  59.9 2.7 %shard_map.92 = (f32[384,256]{1,0:T(8,128)S(1)}, f32[384,256]{1,0:T(8,128)S(1)}, f32[392,256]{1,0:T(8,128)S(1)}, f32[392,256]{1,0:T(8,128)S(1)}) custom-call(f32[6]{0:T(128)S(1)} %pad_maximum_fusion.refs_0_.flags, f32[1536,1536]{1,0:T(8,128)S(1)} %bitcast.25, f32[392,256]{1,0:T(8,128)S(1)} %get-tuple-element.94.refs_6_.refs_2_, ...), custom_call_target="tpu_custom_call" | custom-call | flops 8000000000 | bytes 1024 | tf_op jit(solution)/shard_map/pallas_call | solution.py:344
  62.6 2.3 %shard_map.93 = (f32[384,256]{1,0:T(8,128)S(1)}, f32[384,256]{1,0:T(8,128)S(1)}, f32[24,256]{1,0:T(8,128)S(1)}) custom-call(f32[6]{0:T(128)S(1)} %pad_maximum_fusion.refs_0_.flags, f32[1536,1536]{1,0:T(8,128)S(1)} %bitcast.26, f32[384,256]{1,0:T(8,128)S(1)} %get-tuple-element.98.refs_2_.refs_0_, f32[384,256]{1,0:T(8,128)S(1)} %get-tuple-element.99.refs_3_.refs_1_, ...), custom_call_target="tpu_custom_call" | custom-call | flops 1024 | bytes 1024 | tf_op jit(solution)/shard_map/pallas_call | solution.py:344
  64.9 2.5 %collective-permute-start.13 = (f32[24,256]{1,0:T(8,128)S(1)}, f32[24,256]{1,0:T(8,128)S(1)}, u32[]{:S(2)}, u32[]{:S(2)}) collective-permute-start(f32[24,256]{1,0:T(8,128)S(1)} %get-tuple-element.108), channel_id=1, source_target_pairs={{0,1},{1,0},{2,3},{3,2},{4,5},{5,4},{6,7},{7,6},{8,9},{9,8},{10,11... | collective-permute-start | bytes 73736 | tf_op jit(solution)/shard_map/ppermute | solution.py:19
  67.5 1.8 %collective-permute-done.13 = f32[24,256]{1,0:T(8,128)S(1)} collective-permute-done((f32[24,256]{1,0:T(8,128)S(1)}, f32[24,256]{1,0:T(8,128)S(1)}, u32[]{:S(2)}, u32[]{:S(2)}) %collective-permute-start.13) | collective-permute-done | bytes 24608 | tf_op jit(solution)/shard_map/ppermute | solution.py:19
  69.3 3.4 %collective-permute-start.16 = (f32[48,256]{1,0:T(8,128)S(1)}, f32[48,256]{1,0:T(8,128)S(1)}, u32[]{:S(2)}, u32[]{:S(2)}) collective-permute-start(f32[48,256]{1,0:T(8,128)S(1)} %pad_add_fusion.3.refs_0_), channel_id=1, source_target_pairs={{0,6},{1,7},{2,4},{3,5},{4,2},{5,3},{6,0},{7,1},{8,14},{9,15},{10,... | collective-permute-start | bytes 147464 | tf_op jit(solution)/shard_map/ppermute | solution.py:19
  72.7 1.3 collective-permute-start.15
  74.0 1.5 collective-permute-done.16.refs_3_
  75.5 2.7 %collective-permute-done.15.refs_2_ = f32[48,256]{1,0:T(8,128)S(1)} collective-permute-done((f32[48,256]{1,0:T(8,128)S(1)}, f32[48,256]{1,0:T(8,128)S(1)}, u32[]{:S(2)}, u32[]{:S(2)}) %collective-permute-start.15) | collective-permute-done | bytes 49184 | tf_op jit(solution)/shard_map/ppermute | solution.py:19
  81.8 1.8 %collective-permute-start.19 = (f32[136,256]{1,0:T(8,128)S(1)}, f32[136,256]{1,0:T(8,128)S(1)}, u32[]{:S(2)}, u32[]{:S(2)}) collective-permute-start(f32[136,256]{1,0:T(8,128)S(1)} %shard_map.94), channel_id=1, source_target_pairs={{0,8},{8,0},{16,24},{24,16},{1,9},{9,1},{17,25},{25,17},{2,10},{10... | collective-permute-start | bytes 417800 | tf_op jit(solution)/shard_map/ppermute | solution.py:19
  84.6 2.0 %collective-permute-start.20 = (f32[136,256]{1,0:T(8,128)S(1)}, f32[136,256]{1,0:T(8,128)S(1)}, u32[]{:S(2)}, u32[]{:S(2)}) collective-permute-start(f32[136,256]{1,0:T(8,128)S(1)} %add.134), channel_id=1, source_target_pairs={{0,16},{8,24},{16,0},{24,8},{1,17},{9,25},{17,1},{25,9},{2,18},{10... | collective-permute-start | bytes 417800 | tf_op jit(solution)/shard_map/ppermute | solution.py:19
  86.7 3.5 %shard_map.96.refs_10_.refs_11_.refs_12_ = f32[1536,128]{1,0:T(8,128)S(1)} custom-call(f32[6]{0:T(128)S(1)} %pad_maximum_fusion.refs_0_.flags, f32[416,256]{1,0:T(8,128)S(1)} %collective-permute-done.refs_4_.near0, f32[416,256]{1,0:T(8,128)S(1)} %collective-permute-done.1.refs_5_.near1, f32[416,256]{1,0:T(8,128)S(1)} %collective-permute-done.2.refs_4_.near2, ...), custom_call_target="tpu_custom_call" | custom-call | flops 1024 | bytes 1024 | tf_op jit(solution)/shard_map/pallas_call | solution.py:344
  90.2 2.9 %collective-permute-done.20 = f32[136,256]{1,0:T(8,128)S(1)} collective-permute-done((f32[136,256]{1,0:T(8,128)S(1)}, f32[136,256]{1,0:T(8,128)S(1)}, u32[]{:S(2)}, u32[]{:S(2)}) %collective-permute-start.20) | collective-permute-done | bytes 139296 | tf_op jit(solution)/shard_map/ppermute | solution.py:19
  93.7 3.8 %shard_map.97 = (f32[384,256]{1,0:T(8,128)S(1)}, f32[384,256]{1,0:T(8,128)S(1)}, f32[384,256]{1,0:T(8,128)S(1)}, f32[384,256]{1,0:T(8,128)S(1)}, f32[1536,256]{1,0:T(8,128)S(1)}) custom-call(f32[6]{0:T(128)S(1)} %pad_maximum_fusion.refs_0_.flags, f32[1536,1536]{1,0:T(8,128)S(1)} %bitcast.19, f32[384,256]{1,0:T(8,128)S(1)} %get-tuple-element.109.refs_2_.refs_8_, ...), custom_call_target="tpu_custom_call" | custom-call | flops 1024 | bytes 1024 | tf_op jit(solution)/shard_map/pallas_call | solution.py:344
  97.5 3.2 %shard_map.98 = (f32[384,256]{1,0:T(8,128)S(1)}, f32[384,256]{1,0:T(8,128)S(1)}, f32[384,256]{1,0:T(8,128)S(1)}, f32[384,256]{1,0:T(8,128)S(1)}, f32[392,256]{1,0:T(8,128)S(1)}, /*index=5*/f32[392,256]{1,0:T(8,128)S(1)}) custom-call(f32[6]{0:T(128)S(1)} %pad_maximum_fusion.refs_0_.flags, f32[1536,1536]{1,0:T(8,128)S(1)} %bitcast.20, ...), custom_call_target="tpu_custom_call" | custom-call | flops 8000000000 | bytes 1024 | tf_op jit(solution)/shard_map/pallas_call | solution.py:344
  100.7 3.2 %collective-permute-start.25 = (f32[392,256]{1,0:T(8,128)S(1)}, f32[392,256]{1,0:T(8,128)S(1)}, u32[]{:S(2)}, u32[]{:S(2)}) collective-permute-start(f32[392,256]{1,0:T(8,128)S(1)} %get-tuple-element.123.refs_6_.refs_2_), channel_id=1, source_target_pairs={{0,1},{1,0},{2,3},{3,2},{4,5},{5,4},{6,7},{7,6},{8,9},{9,8},{10,11... | collective-permute-start | bytes 1204232 | tf_op jit(solution)/shard_map/ppermute | solution.py:19
  104.6 2.0 %shard_map.99 = (f32[384,256]{1,0:T(8,128)S(1)}, f32[384,256]{1,0:T(8,128)S(1)}, f32[1,256]{1,0:T(1,128)S(1)}) custom-call(f32[6]{0:T(128)S(1)} %pad_maximum_fusion.refs_0_.flags, f32[1536,1536]{1,0:T(8,128)S(1)} %bitcast.21, f32[384,256]{1,0:T(8,128)S(1)} %get-tuple-element.116.refs_2_.refs_4_, f32[384,256]{1,0:T(8,128)S(1)} %get-tuple-element.117.refs_3_.refs_5_, ...), custom_call_target="tpu_custom_call" | custom-call | flops 1024 | bytes 1024 | tf_op jit(solution)/shard_map/pallas_call | solution.py:344
  108.4 3.4 %shard_map.100 = (f32[384,256]{1,0:T(8,128)S(1)}, f32[384,256]{1,0:T(8,128)S(1)}, f32[1536,256]{1,0:T(8,128)S(1)}) custom-call(f32[6]{0:T(128)S(1)} %pad_maximum_fusion.refs_0_.flags, f32[1536,1536]{1,0:T(8,128)S(1)} %bitcast.27, f32[384,256]{1,0:T(8,128)S(1)} %get-tuple-element.125.refs_2_, f32[384,256]{1,0:T(8,128)S(1)} %get-tuple-element.126.refs_3_, ...), custom_call_target="tpu_custom_call" | custom-call | flops 1024 | bytes 1024 | tf_op jit(solution)/shard_map/pallas_call | solution.py:344
  111.8 8.2 %collective-permute-done.25.refs_4_ = f32[392,256]{1,0:T(8,128)S(1)} collective-permute-done((f32[392,256]{1,0:T(8,128)S(1)}, f32[392,256]{1,0:T(8,128)S(1)}, u32[]{:S(2)}, u32[]{:S(2)}) %collective-permute-start.25) | collective-permute-done | bytes 401440 | tf_op jit(solution)/shard_map/ppermute | solution.py:19
  120.0 2.7 %shard_map.101 = (f32[384,256]{1,0:T(8,128)S(1)}, f32[384,256]{1,0:T(8,128)S(1)}, f32[392,256]{1,0:T(8,128)S(1)}, f32[392,256]{1,0:T(8,128)S(1)}) custom-call(f32[6]{0:T(128)S(1)} %pad_maximum_fusion.refs_0_.flags, f32[1536,1536]{1,0:T(8,128)S(1)} %bitcast.28, f32[392,256]{1,0:T(8,128)S(1)} %get-tuple-element.123.refs_6_.refs_2_, ...), custom_call_target="tpu_custom_call" | custom-call | flops 8000000000 | bytes 1024 | tf_op jit(solution)/shard_map/pallas_call | solution.py:344
  122.7 2.5 %shard_map.102 = (f32[384,256]{1,0:T(8,128)S(1)}, f32[384,256]{1,0:T(8,128)S(1)}, f32[24,256]{1,0:T(8,128)S(1)}) custom-call(f32[6]{0:T(128)S(1)} %pad_maximum_fusion.refs_0_.flags, f32[1536,1536]{1,0:T(8,128)S(1)} %bitcast.29, f32[384,256]{1,0:T(8,128)S(1)} %get-tuple-element.127.refs_2_.refs_4_, f32[384,256]{1,0:T(8,128)S(1)} %get-tuple-element.128.refs_3_.refs_5_, ...), custom_call_target="tpu_custom_call" | custom-call | flops 1024 | bytes 1024 | tf_op jit(solution)/shard_map/pallas_call | solution.py:344
  125.2 2.5 %collective-permute-start.27 = (f32[24,256]{1,0:T(8,128)S(1)}, f32[24,256]{1,0:T(8,128)S(1)}, u32[]{:S(2)}, u32[]{:S(2)}) collective-permute-start(f32[24,256]{1,0:T(8,128)S(1)} %get-tuple-element.135), channel_id=1, source_target_pairs={{0,1},{1,0},{2,3},{3,2},{4,5},{5,4},{6,7},{7,6},{8,9},{9,8},{10,11... | collective-permute-start | bytes 73736 | tf_op jit(solution)/shard_map/ppermute | solution.py:19
  127.7 1.8 %collective-permute-done.27 = f32[24,256]{1,0:T(8,128)S(1)} collective-permute-done((f32[24,256]{1,0:T(8,128)S(1)}, f32[24,256]{1,0:T(8,128)S(1)}, u32[]{:S(2)}, u32[]{:S(2)}) %collective-permute-start.27) | collective-permute-done | bytes 24608 | tf_op jit(solution)/shard_map/ppermute | solution.py:19
  129.5 2.6 %collective-permute-start.30 = (f32[48,256]{1,0:T(8,128)S(1)}, f32[48,256]{1,0:T(8,128)S(1)}, u32[]{:S(2)}, u32[]{:S(2)}) collective-permute-start(f32[48,256]{1,0:T(8,128)S(1)} %pad_add_fusion.2.refs_0_), channel_id=1, source_target_pairs={{0,6},{1,7},{2,4},{3,5},{4,2},{5,3},{6,0},{7,1},{8,14},{9,15},{10,... | collective-permute-start | bytes 147464 | tf_op jit(solution)/shard_map/ppermute | solution.py:19
  133.9 1.7 %collective-permute-done.30.refs_3_ = f32[48,256]{1,0:T(8,128)S(1)} collective-permute-done((f32[48,256]{1,0:T(8,128)S(1)}, f32[48,256]{1,0:T(8,128)S(1)}, u32[]{:S(2)}, u32[]{:S(2)}) %collective-permute-start.30) | collective-permute-done | bytes 49184 | tf_op jit(solution)/shard_map/ppermute | solution.py:19
  135.6 2.5 %collective-permute-done.29.refs_2_ = f32[48,256]{1,0:T(8,128)S(1)} collective-permute-done((f32[48,256]{1,0:T(8,128)S(1)}, f32[48,256]{1,0:T(8,128)S(1)}, u32[]{:S(2)}, u32[]{:S(2)}) %collective-permute-start.29) | collective-permute-done | bytes 49184 | tf_op jit(solution)/shard_map/ppermute | solution.py:19
  138.1 1.6 collective-permute-start.35
  141.7 2.0 %collective-permute-start.31 = (f32[136,256]{1,0:T(8,128)S(1)}, f32[136,256]{1,0:T(8,128)S(1)}, u32[]{:S(2)}, u32[]{:S(2)}) collective-permute-start(f32[136,256]{1,0:T(8,128)S(1)} %shard_map.103), channel_id=1, source_target_pairs={{0,8},{8,0},{16,24},{24,16},{1,9},{9,1},{17,25},{25,17},{2,10},{10... | collective-permute-start | bytes 417800 | tf_op jit(solution)/shard_map/ppermute | solution.py:19
  144.7 1.9 %collective-permute-start.32 = (f32[136,256]{1,0:T(8,128)S(1)}, f32[136,256]{1,0:T(8,128)S(1)}, u32[]{:S(2)}, u32[]{:S(2)}) collective-permute-start(f32[136,256]{1,0:T(8,128)S(1)} %add.137), channel_id=1, source_target_pairs={{0,16},{8,24},{16,0},{24,8},{1,17},{9,25},{17,1},{25,9},{2,18},{10... | collective-permute-start | bytes 417800 | tf_op jit(solution)/shard_map/ppermute | solution.py:19
  146.6 6.6 %collective-permute-done.32 = f32[136,256]{1,0:T(8,128)S(1)} collective-permute-done((f32[136,256]{1,0:T(8,128)S(1)}, f32[136,256]{1,0:T(8,128)S(1)}, u32[]{:S(2)}, u32[]{:S(2)}) %collective-permute-start.32) | collective-permute-done | bytes 139296 | tf_op jit(solution)/shard_map/ppermute | solution.py:19
  153.3 3.7 %collective-permute-done.35.refs_7_ = f32[392,256]{1,0:T(8,128)S(1)} collective-permute-done((f32[392,256]{1,0:T(8,128)S(1)}, f32[392,256]{1,0:T(8,128)S(1)}, u32[]{:S(2)}, u32[]{:S(2)}) %collective-permute-start.35) | collective-permute-done | bytes 401440 | tf_op jit(solution)/shard_map/ppermute | solution.py:19
  156.9 2.0 %shard_map.104 = (f32[384,256]{1,0:T(8,128)S(1)}, f32[384,256]{1,0:T(8,128)S(1)}, f32[384,256]{1,0:T(8,128)S(1)}, f32[384,256]{1,0:T(8,128)S(1)}) custom-call(f32[6]{0:T(128)S(1)} %pad_maximum_fusion.refs_0_.flags, f32[384,256]{1,0:T(8,128)S(1)} %get-tuple-element.141.refs_1_, f32[384,256]{1,0:T(8,128)S(1)} %get-tuple-element.142.refs_2_, ...), custom_call_target="tpu_custom_call" | custom-call | flops 1024 | bytes 1024 | tf_op jit(solution)/shard_map/pallas_call | solution.py:344
  159.6 1.2 shard_map.106
  160.8 1.9 %shard_map.107 = f32[1536,256]{1,0:T(8,128)} custom-call(f32[384,256]{1,0:T(8,128)S(1)} %get-tuple-element.150.refs_0_, f32[384,256]{1,0:T(8,128)S(1)} %get-tuple-element.151.refs_1_, f32[384,256]{1,0:T(8,128)S(1)} %get-tuple-element.152.refs_2_, f32[384,256]{1,0:T(8,128)S(1)} %get-tuple-element.153.refs_3_, ...), custom_call_target="tpu_custom_call" | custom-call | flops 1024 | bytes 1024 | tf_op jit(solution)/shard_map/pallas_call | solution.py:344
  (97 shorter events, 20.3 us)
Async XLA Ops:
  0.6 4.1 %copy-start.3 = (s32[1,1,16]{2,1,0:T(1,128)S(1)}, s32[1,1,16]{2,1,0:T(1,128)}, u32[]{:S(2)}) copy-start(s32[1,1,16]{2,1,0:T(1,128)} %param.11) | copy-start | bytes 196
  0.6 4.1 %copy-start.4 = (f32[4,128]{1,0:T(4,128)S(1)}, f32[4,128]{1,0:T(4,128)}, u32[]{:S(2)}) copy-start(f32[4,128]{1,0:T(4,128)} %inverse) | copy-start | bytes 6148
  4.2 5.3 %copy-start.5 = (s32[1,1,4,384]{3,2,1,0:T(4,128)S(1)}, s32[1,1,4,384]{3,2,1,0:T(4,128)}, u32[]{:S(2)}) copy-start(s32[1,1,4,384]{3,2,1,0:T(4,128)} %param.12) | copy-start | bytes 18436
  4.2 26.0 %collective-permute-start = (f32[416,256]{1,0:T(8,128)}, f32[416,256]{1,0:T(8,128)S(1)}, u32[]{:S(2)}, u32[]{:S(2)}) collective-permute-start(f32[416,256]{1,0:T(8,128)} %get-tuple-element.81.refs_2_.sent), channel_id=1, source_target_pairs={{0,8},{8,0},{16,24},{24,16},{1,9},{9,1},{17,25},{25,17},{2,10},{10... | collective-permute-start | bytes 1277960 | tf_op jit(solution)/shard_map/ppermute | solution.py:19
  5.3 24.9 %copy-start.1 = (f32[416,256]{1,0:T(8,128)S(1)}, f32[416,256]{1,0:T(8,128)}, u32[]{:S(2)}) copy-start(f32[416,256]{1,0:T(8,128)} %get-tuple-element.81.refs_2_.sent) | copy-start | bytes 1277956
  5.3 4.5 %collective-permute-start.4 = (f32[12,128]{1,0:T(8,128)S(1)}, f32[12,128]{1,0:T(8,128)S(1)}, u32[]{:S(2)}, u32[]{:S(2)}) collective-permute-start(f32[12,128]{1,0:T(8,128)S(1)} %shard_map.88), channel_id=1, source_target_pairs={{0,1},{1,0},{2,3},{3,2},{4,5},{5,4},{6,7},{7,6},{8,9},{9,8},{10,11... | collective-permute-start | bytes 18440 | tf_op jit(solution)/shard_map/ppermute | solution.py:19
  7.9 22.3 %collective-permute-start.1 = (f32[416,256]{1,0:T(8,128)}, f32[416,256]{1,0:T(8,128)S(1)}, u32[]{:S(2)}, u32[]{:S(2)}) collective-permute-start(f32[416,256]{1,0:T(8,128)} %get-tuple-element.82.refs_3_), channel_id=1, source_target_pairs={{8,16},{16,8},{9,17},{17,9},{10,18},{18,10},{11,19},{19,11},{12,20... | collective-permute-start | bytes 1277960 | tf_op jit(solution)/shard_map/ppermute | solution.py:26
  8.6 29.4 %collective-permute-start.2 = (f32[416,256]{1,0:T(8,128)}, f32[416,256]{1,0:T(8,128)S(1)}, u32[]{:S(2)}, u32[]{:S(2)}) collective-permute-start(f32[416,256]{1,0:T(8,128)} %get-tuple-element.87.refs_2_), channel_id=1, source_target_pairs={{0,1},{1,0},{2,3},{3,2},{4,5},{5,4},{6,7},{7,6},{8,9},{9,8},{10,11... | collective-permute-start | bytes 1277960 | tf_op jit(solution)/shard_map/ppermute | solution.py:19
  8.8 29.2 %collective-permute-start.3 = (f32[416,256]{1,0:T(8,128)}, f32[416,256]{1,0:T(8,128)S(1)}, u32[]{:S(2)}, u32[]{:S(2)}) collective-permute-start(f32[416,256]{1,0:T(8,128)} %get-tuple-element.88.refs_3_), channel_id=1, source_target_pairs={{1,2},{2,1},{3,4},{4,3},{5,6},{6,5},{9,10},{10,9},{11,12},{12,11},... | collective-permute-start | bytes 1277960 | tf_op jit(solution)/shard_map/ppermute | solution.py:26
  9.8 3.9 %collective-permute-start.5 = (f32[24,128]{1,0:T(8,128)S(1)}, f32[24,128]{1,0:T(8,128)S(1)}, u32[]{:S(2)}, u32[]{:S(2)}) collective-permute-start(f32[24,128]{1,0:T(8,128)S(1)} %pad_add_fusion.6), channel_id=1, source_target_pairs={{0,8},{8,0},{16,24},{24,16},{1,9},{9,1},{17,25},{25,17},{2,10},{10... | collective-permute-start | bytes 36872 | tf_op jit(solution)/shard_map/ppermute | solution.py:19
  13.7 4.8 %collective-permute-start.6 = (f32[48,128]{1,0:T(8,128)S(1)}, f32[48,128]{1,0:T(8,128)S(1)}, u32[]{:S(2)}, u32[]{:S(2)}) collective-permute-start(f32[48,128]{1,0:T(8,128)S(1)} %pad_add_fusion.5), channel_id=1, source_target_pairs={{0,16},{8,24},{16,0},{24,8},{1,17},{9,25},{17,1},{25,9},{2,18},{10... | collective-permute-start | bytes 73736 | tf_op jit(solution)/shard_map/ppermute | solution.py:19
  18.4 7.0 %collective-permute-start.7 = (f32[96,128]{1,0:T(8,128)S(1)}, f32[96,128]{1,0:T(8,128)S(1)}, u32[]{:S(2)}, u32[]{:S(2)}) collective-permute-start(f32[96,128]{1,0:T(8,128)S(1)} %pad_add_fusion.4), channel_id=1, source_target_pairs={{0,4},{1,5},{2,6},{3,7},{4,0},{5,1},{6,2},{7,3},{8,12},{9,13},{10,... | collective-permute-start | bytes 147464 | tf_op jit(solution)/shard_map/ppermute | solution.py:19
  25.4 4.8 %collective-permute-start.8 = (f32[192,128]{1,0:T(8,128)S(1)}, f32[192,128]{1,0:T(8,128)S(1)}, u32[]{:S(2)}, u32[]{:S(2)}) collective-permute-start(f32[192,128]{1,0:T(8,128)S(1)} %pad_add_fusion.1), channel_id=1, source_target_pairs={{0,2},{1,3},{2,0},{3,1},{4,6},{5,7},{6,4},{7,5},{8,10},{9,11},{10,... | collective-permute-start | bytes 294920 | tf_op jit(solution)/shard_map/ppermute | solution.py:19
  30.2 3.7 %copy-start = (f32[1,1,1536,1536]{3,2,1,0:T(8,128)S(1)}, f32[1,1,1536,1536]{3,2,1,0:T(8,128)}, u32[]{:S(2)}) copy-start(f32[1,1,1536,1536]{3,2,1,0:T(8,128)} %param.9) | copy-start | bytes 28311556
  33.9 13.3 %slice-start.3 = ((s8[9437184]{0:T(1024)(128)(4,1)}), s8[4194304]{0:T(1024)(128)(4,1)S(1)}, s32[]{:S(2)}) async-start(s8[9437184]{0:T(1024)(128)(4,1)} %bitcast.22), calls=%async_computation.3 | async-start | bytes 8388608
  38.0 5.4 %slice-start = ((s8[9437184]{0:T(1024)(128)(4,1)}), s8[4194304]{0:T(1024)(128)(4,1)S(1)}, s32[]{:S(2)}) async-start(s8[9437184]{0:T(1024)(128)(4,1)} %bitcast.16), calls=%async_computation | async-start | bytes 8388608
  38.0 5.4 %slice-start.1 = ((s8[9437184]{0:T(1024)(128)(4,1)}), s8[4194304]{0:T(1024)(128)(4,1)S(1)}, s32[]{:S(2)}) async-start(s8[9437184]{0:T(1024)(128)(4,1)} %bitcast.16), calls=%async_computation.1 | async-start | bytes 8388608
  38.0 5.4 %slice-start.2 = ((s8[9437184]{0:T(1024)(128)(4,1)}), s8[1048576]{0:T(1024)(128)(4,1)S(1)}, s32[]{:S(2)}) async-start(s8[9437184]{0:T(1024)(128)(4,1)} %bitcast.16), calls=%async_computation.2 | async-start | bytes 2097152
  38.0 9.2 %slice-start.4 = ((s8[9437184]{0:T(1024)(128)(4,1)}), s8[4194304]{0:T(1024)(128)(4,1)S(1)}, s32[]{:S(2)}) async-start(s8[9437184]{0:T(1024)(128)(4,1)} %bitcast.22), calls=%async_computation.4 | async-start | bytes 8388608
  38.0 9.2 %slice-start.5 = ((s8[9437184]{0:T(1024)(128)(4,1)}), s8[1048576]{0:T(1024)(128)(4,1)S(1)}, s32[]{:S(2)}) async-start(s8[9437184]{0:T(1024)(128)(4,1)} %bitcast.22), calls=%async_computation.5 | async-start | bytes 2097152
  41.4 18.5 %collective-permute-start.11 = (f32[392,256]{1,0:T(8,128)S(1)}, f32[392,256]{1,0:T(8,128)S(1)}, u32[]{:S(2)}, u32[]{:S(2)}) collective-permute-start(f32[392,256]{1,0:T(8,128)S(1)} %get-tuple-element.94.refs_6_.refs_2_), channel_id=1, source_target_pairs={{0,1},{1,0},{2,3},{3,2},{4,5},{5,4},{6,7},{7,6},{8,9},{9,8},{10,11... | collective-permute-start | bytes 1204232 | tf_op jit(solution)/shard_map/ppermute | solution.py:19
  42.7 17.2 %collective-permute-start.12 = (f32[392,256]{1,0:T(8,128)S(1)}, f32[392,256]{1,0:T(8,128)S(1)}, u32[]{:S(2)}, u32[]{:S(2)}) collective-permute-start(f32[392,256]{1,0:T(8,128)S(1)} %get-tuple-element.95.refs_7_.refs_3_), channel_id=1, source_target_pairs={{1,2},{2,1},{3,4},{4,3},{5,6},{6,5},{9,10},{10,9},{11,12},{12,11},... | collective-permute-start | bytes 1204232 | tf_op jit(solution)/shard_map/ppermute | solution.py:26
  45.4 1.8 %collective-permute-start.9 = (f32[384,256]{1,0:T(8,128)S(1)}, f32[384,256]{1,0:T(8,128)S(1)}, u32[]{:S(2)}, u32[]{:S(2)}) collective-permute-start(f32[384,256]{1,0:T(8,128)S(1)} %get-tuple-element.96.refs_2_), channel_id=1, source_target_pairs={{0,8},{8,0},{16,24},{24,16},{1,9},{9,1},{17,25},{25,17},{2,10},{10... | collective-permute-start | bytes 1179656 | tf_op jit(solution)/shard_map/ppermute | solution.py:19
  45.5 1.7 %collective-permute-start.10 = (f32[384,256]{1,0:T(8,128)S(1)}, f32[384,256]{1,0:T(8,128)S(1)}, u32[]{:S(2)}, u32[]{:S(2)}) collective-permute-start(f32[384,256]{1,0:T(8,128)S(1)} %get-tuple-element.97.refs_3_), channel_id=1, source_target_pairs={{8,16},{16,8},{9,17},{17,9},{10,18},{18,10},{11,19},{19,11},{12,20... | collective-permute-start | bytes 1179656 | tf_op jit(solution)/shard_map/ppermute | solution.py:26
  64.9 4.4 %collective-permute-start.13 = (f32[24,256]{1,0:T(8,128)S(1)}, f32[24,256]{1,0:T(8,128)S(1)}, u32[]{:S(2)}, u32[]{:S(2)}) collective-permute-start(f32[24,256]{1,0:T(8,128)S(1)} %get-tuple-element.108), channel_id=1, source_target_pairs={{0,1},{1,0},{2,3},{3,2},{4,5},{5,4},{6,7},{7,6},{8,9},{9,8},{10,11... | collective-permute-start | bytes 73736 | tf_op jit(solution)/shard_map/ppermute | solution.py:19
  69.3 6.2 %collective-permute-start.16 = (f32[48,256]{1,0:T(8,128)S(1)}, f32[48,256]{1,0:T(8,128)S(1)}, u32[]{:S(2)}, u32[]{:S(2)}) collective-permute-start(f32[48,256]{1,0:T(8,128)S(1)} %pad_add_fusion.3.refs_0_), channel_id=1, source_target_pairs={{0,6},{1,7},{2,4},{3,5},{4,2},{5,3},{6,0},{7,1},{8,14},{9,15},{10,... | collective-permute-start | bytes 147464 | tf_op jit(solution)/shard_map/ppermute | solution.py:19
  72.7 5.5 %collective-permute-start.15 = (f32[48,256]{1,0:T(8,128)S(1)}, f32[48,256]{1,0:T(8,128)S(1)}, u32[]{:S(2)}, u32[]{:S(2)}) collective-permute-start(f32[48,256]{1,0:T(8,128)S(1)} %pad_add_fusion.3.refs_0_), channel_id=1, source_target_pairs={{0,4},{1,5},{2,6},{3,7},{4,0},{5,1},{6,2},{7,3},{8,12},{9,13},{10,... | collective-permute-start | bytes 147464 | tf_op jit(solution)/shard_map/ppermute | solution.py:19
  74.0 4.6 %collective-permute-start.14 = (f32[48,256]{1,0:T(8,128)S(1)}, f32[48,256]{1,0:T(8,128)S(1)}, u32[]{:S(2)}, u32[]{:S(2)}) collective-permute-start(f32[48,256]{1,0:T(8,128)S(1)} %pad_add_fusion.3.refs_0_), channel_id=1, source_target_pairs={{0,2},{1,3},{2,0},{3,1},{4,6},{5,7},{6,4},{7,5},{8,10},{9,11},{10,... | collective-permute-start | bytes 147464 | tf_op jit(solution)/shard_map/ppermute | solution.py:19
  78.6 18.9 %collective-permute-start.21 = (f32[392,256]{1,0:T(8,128)S(1)}, f32[392,256]{1,0:T(8,128)S(1)}, u32[]{:S(2)}, u32[]{:S(2)}) collective-permute-start(f32[392,256]{1,0:T(8,128)S(1)} %get-tuple-element.118.refs_6_.refs_2_.refs_10_), channel_id=1, source_target_pairs={{0,1},{1,0},{2,3},{3,2},{4,5},{5,4},{6,7},{7,6},{8,9},{9,8},{10,11... | collective-permute-start | bytes 1204232 | tf_op jit(solution)/shard_map/ppermute | solution.py:19
  79.6 17.9 %collective-permute-start.22 = (f32[392,256]{1,0:T(8,128)S(1)}, f32[392,256]{1,0:T(8,128)S(1)}, u32[]{:S(2)}, u32[]{:S(2)}) collective-permute-start(f32[392,256]{1,0:T(8,128)S(1)} %get-tuple-element.119.refs_7_.refs_3_.refs_11_), channel_id=1, source_target_pairs={{1,2},{2,1},{3,4},{4,3},{5,6},{6,5},{9,10},{10,9},{11,12},{12,11},... | collective-permute-start | bytes 1204232 | tf_op jit(solution)/shard_map/ppermute | solution.py:26
  80.3 13.4 %collective-permute-start.17 = (f32[384,256]{1,0:T(8,128)S(1)}, f32[384,256]{1,0:T(8,128)S(1)}, u32[]{:S(2)}, u32[]{:S(2)}) collective-permute-start(f32[384,256]{1,0:T(8,128)S(1)} %get-tuple-element.109.refs_2_.refs_8_), channel_id=1, source_target_pairs={{0,8},{8,0},{16,24},{24,16},{1,9},{9,1},{17,25},{25,17},{2,10},{10... | collective-permute-start | bytes 1179656 | tf_op jit(solution)/shard_map/ppermute | solution.py:19
  80.3 13.4 %collective-permute-start.18 = (f32[384,256]{1,0:T(8,128)S(1)}, f32[384,256]{1,0:T(8,128)S(1)}, u32[]{:S(2)}, u32[]{:S(2)}) collective-permute-start(f32[384,256]{1,0:T(8,128)S(1)} %get-tuple-element.110.refs_3_.refs_9_), channel_id=1, source_target_pairs={{8,16},{16,8},{9,17},{17,9},{10,18},{18,10},{11,19},{19,11},{12,20... | collective-permute-start | bytes 1179656 | tf_op jit(solution)/shard_map/ppermute | solution.py:26
  81.8 2.8 %collective-permute-start.19 = (f32[136,256]{1,0:T(8,128)S(1)}, f32[136,256]{1,0:T(8,128)S(1)}, u32[]{:S(2)}, u32[]{:S(2)}) collective-permute-start(f32[136,256]{1,0:T(8,128)S(1)} %shard_map.94), channel_id=1, source_target_pairs={{0,8},{8,0},{16,24},{24,16},{1,9},{9,1},{17,25},{25,17},{2,10},{10... | collective-permute-start | bytes 417800 | tf_op jit(solution)/shard_map/ppermute | solution.py:19
  84.6 8.5 %collective-permute-start.20 = (f32[136,256]{1,0:T(8,128)S(1)}, f32[136,256]{1,0:T(8,128)S(1)}, u32[]{:S(2)}, u32[]{:S(2)}) collective-permute-start(f32[136,256]{1,0:T(8,128)S(1)} %add.134), channel_id=1, source_target_pairs={{0,16},{8,24},{16,0},{24,8},{1,17},{9,25},{17,1},{25,9},{2,18},{10... | collective-permute-start | bytes 417800 | tf_op jit(solution)/shard_map/ppermute | solution.py:19
  100.7 19.3 %collective-permute-start.25 = (f32[392,256]{1,0:T(8,128)S(1)}, f32[392,256]{1,0:T(8,128)S(1)}, u32[]{:S(2)}, u32[]{:S(2)}) collective-permute-start(f32[392,256]{1,0:T(8,128)S(1)} %get-tuple-element.123.refs_6_.refs_2_), channel_id=1, source_target_pairs={{0,1},{1,0},{2,3},{3,2},{4,5},{5,4},{6,7},{7,6},{8,9},{9,8},{10,11... | collective-permute-start | bytes 1204232 | tf_op jit(solution)/shard_map/ppermute | solution.py:19
  103.9 16.1 %collective-permute-start.26 = (f32[392,256]{1,0:T(8,128)S(1)}, f32[392,256]{1,0:T(8,128)S(1)}, u32[]{:S(2)}, u32[]{:S(2)}) collective-permute-start(f32[392,256]{1,0:T(8,128)S(1)} %get-tuple-element.124.refs_7_.refs_3_), channel_id=1, source_target_pairs={{1,2},{2,1},{3,4},{4,3},{5,6},{6,5},{9,10},{10,9},{11,12},{12,11},... | collective-permute-start | bytes 1204232 | tf_op jit(solution)/shard_map/ppermute | solution.py:26
  106.6 1.8 %collective-permute-start.23 = (f32[384,256]{1,0:T(8,128)S(1)}, f32[384,256]{1,0:T(8,128)S(1)}, u32[]{:S(2)}, u32[]{:S(2)}) collective-permute-start(f32[384,256]{1,0:T(8,128)S(1)} %get-tuple-element.125.refs_2_), channel_id=1, source_target_pairs={{0,8},{8,0},{16,24},{24,16},{1,9},{9,1},{17,25},{25,17},{2,10},{10... | collective-permute-start | bytes 1179656 | tf_op jit(solution)/shard_map/ppermute | solution.py:19
  106.7 1.7 %collective-permute-start.24 = (f32[384,256]{1,0:T(8,128)S(1)}, f32[384,256]{1,0:T(8,128)S(1)}, u32[]{:S(2)}, u32[]{:S(2)}) collective-permute-start(f32[384,256]{1,0:T(8,128)S(1)} %get-tuple-element.126.refs_3_), channel_id=1, source_target_pairs={{8,16},{16,8},{9,17},{17,9},{10,18},{18,10},{11,19},{19,11},{12,20... | collective-permute-start | bytes 1179656 | tf_op jit(solution)/shard_map/ppermute | solution.py:26
  125.2 4.4 %collective-permute-start.27 = (f32[24,256]{1,0:T(8,128)S(1)}, f32[24,256]{1,0:T(8,128)S(1)}, u32[]{:S(2)}, u32[]{:S(2)}) collective-permute-start(f32[24,256]{1,0:T(8,128)S(1)} %get-tuple-element.135), channel_id=1, source_target_pairs={{0,1},{1,0},{2,3},{3,2},{4,5},{5,4},{6,7},{7,6},{8,9},{9,8},{10,11... | collective-permute-start | bytes 73736 | tf_op jit(solution)/shard_map/ppermute | solution.py:19
  129.5 6.0 %collective-permute-start.30 = (f32[48,256]{1,0:T(8,128)S(1)}, f32[48,256]{1,0:T(8,128)S(1)}, u32[]{:S(2)}, u32[]{:S(2)}) collective-permute-start(f32[48,256]{1,0:T(8,128)S(1)} %pad_add_fusion.2.refs_0_), channel_id=1, source_target_pairs={{0,6},{1,7},{2,4},{3,5},{4,2},{5,3},{6,0},{7,1},{8,14},{9,15},{10,... | collective-permute-start | bytes 147464 | tf_op jit(solution)/shard_map/ppermute | solution.py:19
  132.1 6.0 %collective-permute-start.29 = (f32[48,256]{1,0:T(8,128)S(1)}, f32[48,256]{1,0:T(8,128)S(1)}, u32[]{:S(2)}, u32[]{:S(2)}) collective-permute-start(f32[48,256]{1,0:T(8,128)S(1)} %pad_add_fusion.2.refs_0_), channel_id=1, source_target_pairs={{0,4},{1,5},{2,6},{3,7},{4,0},{5,1},{6,2},{7,3},{8,12},{9,13},{10,... | collective-permute-start | bytes 147464 | tf_op jit(solution)/shard_map/ppermute | solution.py:19
  132.9 5.2 %collective-permute-start.28 = (f32[48,256]{1,0:T(8,128)S(1)}, f32[48,256]{1,0:T(8,128)S(1)}, u32[]{:S(2)}, u32[]{:S(2)}) collective-permute-start(f32[48,256]{1,0:T(8,128)S(1)} %pad_add_fusion.2.refs_0_), channel_id=1, source_target_pairs={{0,2},{1,3},{2,0},{3,1},{4,6},{5,7},{6,4},{7,5},{8,10},{9,11},{10,... | collective-permute-start | bytes 147464 | tf_op jit(solution)/shard_map/ppermute | solution.py:19
  138.1 18.8 %collective-permute-start.35 = (f32[392,256]{1,0:T(8,128)S(1)}, f32[392,256]{1,0:T(8,128)S(1)}, u32[]{:S(2)}, u32[]{:S(2)}) collective-permute-start(f32[392,256]{1,0:T(8,128)S(1)} %get-tuple-element.143.refs_6_.refs_3_), channel_id=1, source_target_pairs={{0,1},{1,0},{2,3},{3,2},{4,5},{5,4},{6,7},{7,6},{8,9},{9,8},{10,11... | collective-permute-start | bytes 1204232 | tf_op jit(solution)/shard_map/ppermute | solution.py:19
  139.7 17.2 %collective-permute-start.36 = (f32[392,256]{1,0:T(8,128)S(1)}, f32[392,256]{1,0:T(8,128)S(1)}, u32[]{:S(2)}, u32[]{:S(2)}) collective-permute-start(f32[392,256]{1,0:T(8,128)S(1)} %get-tuple-element.144.refs_7_.refs_4_), channel_id=1, source_target_pairs={{1,2},{2,1},{3,4},{4,3},{5,6},{6,5},{9,10},{10,9},{11,12},{12,11},... | collective-permute-start | bytes 1204232 | tf_op jit(solution)/shard_map/ppermute | solution.py:26
  140.4 12.8 %collective-permute-start.33 = (f32[384,256]{1,0:T(8,128)S(1)}, f32[384,256]{1,0:T(8,128)S(1)}, u32[]{:S(2)}, u32[]{:S(2)}) collective-permute-start(f32[384,256]{1,0:T(8,128)S(1)} %get-tuple-element.141.refs_1_), channel_id=1, source_target_pairs={{0,8},{8,0},{16,24},{24,16},{1,9},{9,1},{17,25},{25,17},{2,10},{10... | collective-permute-start | bytes 1179656 | tf_op jit(solution)/shard_map/ppermute | solution.py:19
  140.5 12.8 %collective-permute-start.34 = (f32[384,256]{1,0:T(8,128)S(1)}, f32[384,256]{1,0:T(8,128)S(1)}, u32[]{:S(2)}, u32[]{:S(2)}) collective-permute-start(f32[384,256]{1,0:T(8,128)S(1)} %get-tuple-element.142.refs_2_), channel_id=1, source_target_pairs={{8,16},{16,8},{9,17},{17,9},{10,18},{18,10},{11,19},{19,11},{12,20... | collective-permute-start | bytes 1179656 | tf_op jit(solution)/shard_map/ppermute | solution.py:26
  141.7 3.0 %collective-permute-start.31 = (f32[136,256]{1,0:T(8,128)S(1)}, f32[136,256]{1,0:T(8,128)S(1)}, u32[]{:S(2)}, u32[]{:S(2)}) collective-permute-start(f32[136,256]{1,0:T(8,128)S(1)} %shard_map.103), channel_id=1, source_target_pairs={{0,8},{8,0},{16,24},{24,16},{1,9},{9,1},{17,25},{25,17},{2,10},{10... | collective-permute-start | bytes 417800 | tf_op jit(solution)/shard_map/ppermute | solution.py:19
  144.7 8.5 %collective-permute-start.32 = (f32[136,256]{1,0:T(8,128)S(1)}, f32[136,256]{1,0:T(8,128)S(1)}, u32[]{:S(2)}, u32[]{:S(2)}) collective-permute-start(f32[136,256]{1,0:T(8,128)S(1)} %add.137), channel_id=1, source_target_pairs={{0,16},{8,24},{16,0},{24,8},{1,17},{9,25},{17,1},{25,9},{2,18},{10... | collective-permute-start | bytes 417800 | tf_op jit(solution)/shard_map/ppermute | solution.py:19
  (1 other events, 2.7 us)

commit v3 on v0

--- a/solution.py
+++ b/solution.py
@@ -36,7 +36,8 @@
 
 
 def steps_of():
-    return [("sx", bit) for bit in bits_of("sx")] + [("sy", bit) for bit in bits_of("sy")[:0:-1]] + [("sy", 1)]
+    sx, sy = ([(axis, bit) for bit in bits_of(axis)[::-1]] for axis in ("sx", "sy"))
+    return sy[-1:] + sy[:-1] + sx
 
 
 def stacked_rows(parts):
@@ -117,6 +118,17 @@
             out[start + k : start + k + 1, face % width :] = listed
     for started in copies:
         started.wait()
+
+
+def rows_kernel(corners, inverse, out):
+    own = inverse.shape[0]
+    out[:own] = inverse[...]
+    out[own:] = jnp.zeros((out.shape[0] - own, out.shape[1]), F32)
+    columns = lax.broadcasted_iota(jnp.int32, (1, out.shape[1]), 1)
+    listed = jnp.zeros((1, out.shape[1]), F32)
+    for k in range(corners.shape[0]):
+        listed = jnp.where(columns == k, corners[k].astype(F32), listed)
+    out[own : own + 1] = listed
 
 
 def lift_kernel(flags, near0, near1, near2, near3, select, coupling, sent, out):
@@ -403,7 +415,7 @@
         a0, a1, sums = call(kernel, operands, [one_face, one_face, (ncl + 8, width)], parts, smem=1)
         return (a0, a1, *a23), sums
 
-    def solved(kernel, sums, faces, others):
+    def solved(kernel, sums, faces, more):
         other, *far = lax.optimization_barrier((swapped(sums, "sy", 1), *faces[2:]))
         far = exchanged(far, "sy")
         close = faces[:2]
@@ -420,7 +432,7 @@
             total = total + swapped(total, "sx", bit)
         scratch = [pltpu.VMEM((ncoarse, ncoarse), F32)]
         kernel = functools.partial(kernel, table_rows)
-        (result,) = call(kernel, [total, table, order, *others], [step_shape], scratch)
+        (result,) = call(kernel, [total, table, order, *more], [step_shape], scratch)
         return (*exchanged(close, "sx"), *far), total, result
 
     step_shape = (ncoarse + 8, width)
@@ -439,22 +451,19 @@
 
     own = coarse_inverse.shape[0]
     table_rows = own + 8
-    listed = jnp.pad(corners.astype(F32)[None], ((own, 7), (0, ncoarse - ncl)))
-    own_rows = jnp.pad(coarse_inverse, ((0, 8), (0, 0))) + listed
-    own_rows, _ = lax.optimization_barrier((own_rows, sent[0]))
-    most_rows = doubled(own_rows, steps_of()[:-1])
-
-    def last_step(partial, coef):
-        partial, rows = lax.optimization_barrier((partial, most_rows))
-        table, coef = lax.optimization_barrier((doubled(rows, steps_of()[-1:]), coef))
-        return partial, coef, table
-
-    residual0, _, a23, partial, table = fields_of(prec_mat, sent, near, one, beside=last_step)
+    inverse, _ = lax.optimization_barrier((coarse_inverse, sent[0]))
+    (own_rows,) = call(rows_kernel, [corners, inverse], [(table_rows, ncoarse)], smem=1, flops=CRIT_FLOPS)
+
+    def gather(partial, coef):
+        rows, coef = lax.optimization_barrier((doubled(own_rows, steps_of()[:-1]), coef))
+        return partial, coef, rows
+
+    residual0, _, a23, partial, rows = fields_of(prec_mat, sent, near, one, beside=gather)
     applied0, rho0 = prec_late(residual0, a23, partial)
     (lift,) = call(
         lift_kernel, [flags, *near, select, coupling_mat, sent[0]], [(ni, ncoarse)], smem=1
     )
-    lift, half_one = lax.optimization_barrier((lift, half_one))
+    table, half_one = lax.optimization_barrier((doubled(rows, steps_of()[-1:]), half_one))
     near = (*exchanged(applied0[:2], "sx"), *exchanged(applied0[2:], "sy"))
 
     direction0, _, a23, partial = fields_of(flex_mat, applied0, near, half_one)

time: 160 us -> 160 us (level)
  waiting for transfers between devices: 56 us -> 52.1 us
  starting transfers between devices: 48.4 us -> 50.3 us
  Pallas kernels: 48.3 us -> 50 us
    ppermute x25, waiting for transfers between devices: 56 us -> 52.1 us  [swapped(): lax.ppermute(block, axis, [(i, i ^ bit) for i in range(lax.axis_size(axis...]
    ppermute x25, starting transfers between devices: 40.8 us -> 42.7 us  [swapped(): lax.ppermute(block, axis, [(i, i ^ bit) for i in range(lax.axis_size(axis...]
    pallas_call x20 -> x21, Pallas kernels: 48.3 us -> 50 us  [call(): pl.pallas_call(kernel, in_specs=[SMEM_SPEC if i < smem else ANY_SPEC if i...]
    unnamed x26 -> x24, local copies, waits for them, and re-layouts: 4.74 us -> 4.48 us
  transfers between devices with their start and end apart: 35 -> 35, of which waited for: 18 -> 17; matrix products, arithmetic and copies ran while one was open for 0% -> 0% of each run, Pallas kernels for 16% -> 16%
where the time goes in v3:
time: 160 us; the launch traced here: 159 us
  waiting for transfers between devices  52.1 us (33%)
  starting transfers between devices  50.3 us (31%)
  Pallas kernels  50 us (31%)
  local copies, waits for them, and re-layouts  4.51 us (3%)
    ppermute x25, waiting for transfers between devices, swapped(): lax.ppermute(block, axis, [(i, i ^ bit) for i in range(lax.axis_size(axis...  52.1 us
    pallas_call x21, Pallas kernels, call(): pl.pallas_call(kernel, in_specs=[SMEM_SPEC if i < smem else ANY_SPEC if i...  50 us
    ppermute x25, starting transfers between devices, swapped(): lax.ppermute(block, axis, [(i, i ^ bit) for i in range(lax.axis_size(axis...  42.7 us
    ppermute x10, starting transfers between devices, swapped_between(): return lax.ppermute(block, axis, route)  7.57 us
    unnamed x24, local copies, waits for them, and re-layouts  4.48 us
  transfers between devices with their start and end apart: 35, of which 17 were waited for; matrix products, arithmetic and copies ran while one was open for 0% of the time, Pallas kernels for 16%

profile of v3, /device:TPU:0, one launch (start us, length us, event | category | flops | bytes accessed | tf_op | source)
XLA Modules:
  0.0 159.0 jit_solution(337832208884001928)
XLA Ops:
  0.6 3.5 %shard_map.86 = (f32[416,256]{1,0:T(8,128)}, f32[416,256]{1,0:T(8,128)}, f32[416,256]{1,0:T(8,128)}, f32[416,256]{1,0:T(8,128)}) custom-call(s32[16]{0:T(128)} %bitcast.34, f32[1536,256]{1,0:T(8,128)} %bitcast.36, f32[16,1536]{1,0:T(8,128)} %bitcast.30), custom_call_target="tpu_custom_call" | custom-call | flops 1024 | bytes 1024 | tf_op jit(solution)/shard_map/pallas_call | solution.py:340
  5.3 2.6 %collective-permute-start.4 = (f32[12,128]{1,0:T(8,128)S(1)}, f32[12,128]{1,0:T(8,128)S(1)}, u32[]{:S(2)}, u32[]{:S(2)}) collective-permute-start(f32[12,128]{1,0:T(8,128)S(1)} %shard_map.88), channel_id=1, source_target_pairs={{0,1},{1,0},{2,3},{3,2},{4,5},{5,4},{6,7},{7,6},{8,9},{9,8},{10,11... | collective-permute-start | bytes 18440 | tf_op jit(solution)/shard_map/ppermute | solution.py:19
  9.8 5.6 %collective-permute-start.5 = (f32[24,128]{1,0:T(8,128)S(1)}, f32[24,128]{1,0:T(8,128)S(1)}, u32[]{:S(2)}, u32[]{:S(2)}) collective-permute-start(f32[24,128]{1,0:T(8,128)S(1)} %pad_add_fusion.8), channel_id=1, source_target_pairs={{0,4},{1,5},{2,6},{3,7},{4,0},{5,1},{6,2},{7,3},{8,12},{9,13},{10,... | collective-permute-start | bytes 36872 | tf_op jit(solution)/shard_map/ppermute | solution.py:19
  15.5 9.0 %collective-permute-done.5 = f32[24,128]{1,0:T(8,128)S(1)} collective-permute-done((f32[24,128]{1,0:T(8,128)S(1)}, f32[24,128]{1,0:T(8,128)S(1)}, u32[]{:S(2)}, u32[]{:S(2)}) %collective-permute-start.5) | collective-permute-done | bytes 12320 | tf_op jit(solution)/shard_map/ppermute | solution.py:19
  24.6 1.6 collective-permute-start.6
  26.2 2.2 %collective-permute-done.6 = f32[48,128]{1,0:T(8,128)S(1)} collective-permute-done((f32[48,128]{1,0:T(8,128)S(1)}, f32[48,128]{1,0:T(8,128)S(1)}, u32[]{:S(2)}, u32[]{:S(2)}) %collective-permute-start.6) | collective-permute-done | bytes 24608 | tf_op jit(solution)/shard_map/ppermute | solution.py:19
  28.4 2.3 %collective-permute-start.7 = (f32[96,128]{1,0:T(8,128)S(1)}, f32[96,128]{1,0:T(8,128)S(1)}, u32[]{:S(2)}, u32[]{:S(2)}) collective-permute-start(f32[96,128]{1,0:T(8,128)S(1)} %pad_add_fusion.6), channel_id=1, source_target_pairs={{0,16},{8,24},{16,0},{24,8},{1,17},{9,25},{17,1},{25,9},{2,18},{10... | collective-permute-start | bytes 147464 | tf_op jit(solution)/shard_map/ppermute | solution.py:19
  30.8 2.0 %collective-permute-done.7 = f32[96,128]{1,0:T(8,128)S(1)} collective-permute-done((f32[96,128]{1,0:T(8,128)S(1)}, f32[96,128]{1,0:T(8,128)S(1)}, u32[]{:S(2)}, u32[]{:S(2)}) %collective-permute-start.7) | collective-permute-done | bytes 49184 | tf_op jit(solution)/shard_map/ppermute | solution.py:19
  32.9 3.7 %copy-done = f32[1,1,1536,1536]{3,2,1,0:T(8,128)S(1)} copy-done((f32[1,1,1536,1536]{3,2,1,0:T(8,128)S(1)}, f32[1,1,1536,1536]{3,2,1,0:T(8,128)}, u32[]{:S(2)}) %copy-start) | copy-done | bytes 9437208
  36.5 3.9 %shard_map.87 = (f32[384,256]{1,0:T(8,128)S(1)}, f32[384,256]{1,0:T(8,128)S(1)}, f32[1536,256]{1,0:T(8,128)S(1)}) custom-call(f32[6]{0:T(128)S(1)} %pad_maximum_fusion.refs_0_.flags, f32[1536,1536]{1,0:T(8,128)S(1)} %bitcast.14, f32[416,256]{1,0:T(8,128)S(1)} %copy-done.1, f32[416,256]{1,0:T(8,128)} %get-tuple-element.79.refs_3_, ...), custom_call_target="tpu_custom_call" | custom-call | flops 1024 | bytes 1024 | tf_op jit(solution)/shard_map/pallas_call | solution.py:340
  40.5 3.4 %shard_map.89 = (f32[384,256]{1,0:T(8,128)S(1)}, f32[384,256]{1,0:T(8,128)S(1)}, f32[392,256]{1,0:T(8,128)S(1)}, f32[392,256]{1,0:T(8,128)S(1)}) custom-call(f32[6]{0:T(128)S(1)} %pad_maximum_fusion.refs_0_.flags, f32[1536,1536]{1,0:T(8,128)S(1)} %bitcast.15, f32[416,256]{1,0:T(8,128)} %get-tuple-element.84.refs_2_, f32[416,256]{1,0:T(8,128)} %get-tuple-element.85.refs_3_, ...), custom_call_target="tpu_custom_call" | custom-call | flops 8000000000 | bytes 1024 | tf_op jit(solution)/shard_map/pallas_call | solution.py:340
  45.6 2.0 %shard_map.90 = (f32[384,256]{1,0:T(8,128)S(1)}, f32[384,256]{1,0:T(8,128)S(1)}, f32[1,256]{1,0:T(1,128)S(1)}) custom-call(f32[6]{0:T(128)S(1)} %pad_maximum_fusion.refs_0_.flags, f32[1536,1536]{1,0:T(8,128)S(1)} %bitcast.18, f32[384,256]{1,0:T(8,128)S(1)} %get-tuple-element.82.refs_2_.refs_8_, f32[384,256]{1,0:T(8,128)S(1)} %get-tuple-element.83.refs_3_.refs_9_, ...), custom_call_target="tpu_custom_call" | custom-call | flops 1024 | bytes 1024 | tf_op jit(solution)/shard_map/pallas_call | solution.py:340
  48.5 3.4 %collective-permute-start.10 = (f32[192,128]{1,0:T(8,128)S(1)}, f32[192,128]{1,0:T(8,128)S(1)}, u32[]{:S(2)}, u32[]{:S(2)}) collective-permute-start(f32[192,128]{1,0:T(8,128)S(1)} %pad_add_fusion.3), channel_id=1, source_target_pairs={{0,8},{8,0},{16,24},{24,16},{1,9},{9,1},{17,25},{25,17},{2,10},{10... | collective-permute-start | bytes 294920 | tf_op jit(solution)/shard_map/ppermute | solution.py:19
  51.9 0.9 collective-permute-done.10
  53.0 3.4 %shard_map.91 = (f32[384,256]{1,0:T(8,128)S(1)}, f32[384,256]{1,0:T(8,128)S(1)}, f32[1536,256]{1,0:T(8,128)S(1)}) custom-call(f32[6]{0:T(128)S(1)} %pad_maximum_fusion.refs_0_.flags, f32[1536,1536]{1,0:T(8,128)S(1)} %bitcast.24, f32[384,256]{1,0:T(8,128)S(1)} %get-tuple-element.93.refs_2_, f32[384,256]{1,0:T(8,128)S(1)} %get-tuple-element.94.refs_3_, ...), custom_call_target="tpu_custom_call" | custom-call | flops 1024 | bytes 1024 | tf_op jit(solution)/shard_map/pallas_call | solution.py:340
  56.4 4.2 %collective-permute-done.11.refs_4_ = f32[392,256]{1,0:T(8,128)S(1)} collective-permute-done((f32[392,256]{1,0:T(8,128)S(1)}, f32[392,256]{1,0:T(8,128)S(1)}, u32[]{:S(2)}, u32[]{:S(2)}) %collective-permute-start.11) | collective-permute-done | bytes 401440 | tf_op jit(solution)/shard_map/ppermute | solution.py:19
  60.6 2.7 %shard_map.92 = (f32[384,256]{1,0:T(8,128)S(1)}, f32[384,256]{1,0:T(8,128)S(1)}, f32[392,256]{1,0:T(8,128)S(1)}, f32[392,256]{1,0:T(8,128)S(1)}) custom-call(f32[6]{0:T(128)S(1)} %pad_maximum_fusion.refs_0_.flags, f32[1536,1536]{1,0:T(8,128)S(1)} %bitcast.25, f32[392,256]{1,0:T(8,128)S(1)} %get-tuple-element.91.refs_6_.refs_2_, ...), custom_call_target="tpu_custom_call" | custom-call | flops 8000000000 | bytes 1024 | tf_op jit(solution)/shard_map/pallas_call | solution.py:340
  63.3 2.3 %shard_map.93 = (f32[384,256]{1,0:T(8,128)S(1)}, f32[384,256]{1,0:T(8,128)S(1)}, f32[24,256]{1,0:T(8,128)S(1)}) custom-call(f32[6]{0:T(128)S(1)} %pad_maximum_fusion.refs_0_.flags, f32[1536,1536]{1,0:T(8,128)S(1)} %bitcast.26, f32[384,256]{1,0:T(8,128)S(1)} %get-tuple-element.97.refs_2_.refs_0_, f32[384,256]{1,0:T(8,128)S(1)} %get-tuple-element.98.refs_3_.refs_1_, ...), custom_call_target="tpu_custom_call" | custom-call | flops 1024 | bytes 1024 | tf_op jit(solution)/shard_map/pallas_call | solution.py:340
  65.6 2.5 %collective-permute-start.13 = (f32[24,256]{1,0:T(8,128)S(1)}, f32[24,256]{1,0:T(8,128)S(1)}, u32[]{:S(2)}, u32[]{:S(2)}) collective-permute-start(f32[24,256]{1,0:T(8,128)S(1)} %get-tuple-element.107), channel_id=1, source_target_pairs={{0,1},{1,0},{2,3},{3,2},{4,5},{5,4},{6,7},{7,6},{8,9},{9,8},{10,11... | collective-permute-start | bytes 73736 | tf_op jit(solution)/shard_map/ppermute | solution.py:19
  68.2 1.8 %collective-permute-done.13 = f32[24,256]{1,0:T(8,128)S(1)} collective-permute-done((f32[24,256]{1,0:T(8,128)S(1)}, f32[24,256]{1,0:T(8,128)S(1)}, u32[]{:S(2)}, u32[]{:S(2)}) %collective-permute-start.13) | collective-permute-done | bytes 24608 | tf_op jit(solution)/shard_map/ppermute | solution.py:19
  70.0 2.5 %collective-permute-start.14 = (f32[48,256]{1,0:T(8,128)S(1)}, f32[48,256]{1,0:T(8,128)S(1)}, u32[]{:S(2)}, u32[]{:S(2)}) collective-permute-start(f32[48,256]{1,0:T(8,128)S(1)} %pad_add_fusion.5), channel_id=1, source_target_pairs={{0,4},{1,5},{2,6},{3,7},{4,0},{5,1},{6,2},{7,3},{8,12},{9,13},{10,... | collective-permute-start | bytes 147464 | tf_op jit(solution)/shard_map/ppermute | solution.py:19
  72.5 2.9 %collective-permute-done.14 = f32[48,256]{1,0:T(8,128)S(1)} collective-permute-done((f32[48,256]{1,0:T(8,128)S(1)}, f32[48,256]{1,0:T(8,128)S(1)}, u32[]{:S(2)}, u32[]{:S(2)}) %collective-permute-start.14) | collective-permute-done | bytes 49184 | tf_op jit(solution)/shard_map/ppermute | solution.py:19
  75.4 2.9 %collective-permute-start.15 = (f32[96,256]{1,0:T(8,128)S(1)}, f32[96,256]{1,0:T(8,128)S(1)}, u32[]{:S(2)}, u32[]{:S(2)}) collective-permute-start(f32[96,256]{1,0:T(8,128)S(1)} %pad_add_fusion.2.refs_0_), channel_id=1, source_target_pairs={{0,2},{1,3},{2,0},{3,1},{4,6},{5,7},{6,4},{7,5},{8,10},{9,11},{10,... | collective-permute-start | bytes 294920 | tf_op jit(solution)/shard_map/ppermute | solution.py:19
  79.5 1.5 collective-permute-done.15.refs_1_
  82.4 4.4 %collective-permute-start.18 = (f32[136,256]{1,0:T(8,128)S(1)}, f32[136,256]{1,0:T(8,128)S(1)}, u32[]{:S(2)}, u32[]{:S(2)}) collective-permute-start(f32[136,256]{1,0:T(8,128)S(1)} %shard_map.94), channel_id=1, source_target_pairs={{0,8},{8,0},{16,24},{24,16},{1,9},{9,1},{17,25},{25,17},{2,10},{10... | collective-permute-start | bytes 417800 | tf_op jit(solution)/shard_map/ppermute | solution.py:19
  86.8 1.0 collective-permute-done.18
  88.1 3.5 %shard_map.96.refs_10_.refs_11_.refs_18_ = f32[1536,128]{1,0:T(8,128)S(1)} custom-call(f32[6]{0:T(128)S(1)} %pad_maximum_fusion.refs_0_.flags, f32[416,256]{1,0:T(8,128)S(1)} %collective-permute-done.refs_4_.near0, f32[416,256]{1,0:T(8,128)S(1)} %collective-permute-done.1.refs_5_.near1, f32[416,256]{1,0:T(8,128)S(1)} %collective-permute-done.2.refs_4_.near2, ...), custom_call_target="tpu_custom_call" | custom-call | flops 1024 | bytes 1024 | tf_op jit(solution)/shard_map/pallas_call | solution.py:340
  91.7 2.9 %collective-permute-done.19 = f32[136,256]{1,0:T(8,128)S(1)} collective-permute-done((f32[136,256]{1,0:T(8,128)S(1)}, f32[136,256]{1,0:T(8,128)S(1)}, u32[]{:S(2)}, u32[]{:S(2)}) %collective-permute-start.19) | collective-permute-done | bytes 139296 | tf_op jit(solution)/shard_map/ppermute | solution.py:19
  95.2 3.7 %shard_map.97 = (f32[384,256]{1,0:T(8,128)S(1)}, f32[384,256]{1,0:T(8,128)S(1)}, f32[384,256]{1,0:T(8,128)S(1)}, f32[384,256]{1,0:T(8,128)S(1)}, f32[1536,256]{1,0:T(8,128)S(1)}) custom-call(f32[6]{0:T(128)S(1)} %pad_maximum_fusion.refs_0_.flags, f32[1536,1536]{1,0:T(8,128)S(1)} %bitcast.19, f32[384,256]{1,0:T(8,128)S(1)} %get-tuple-element.112.refs_2_.refs_8_, ...), custom_call_target="tpu_custom_call" | custom-call | flops 1024 | bytes 1024 | tf_op jit(solution)/shard_map/pallas_call | solution.py:340
  98.9 3.2 %shard_map.98 = (f32[384,256]{1,0:T(8,128)S(1)}, f32[384,256]{1,0:T(8,128)S(1)}, f32[384,256]{1,0:T(8,128)S(1)}, f32[384,256]{1,0:T(8,128)S(1)}, f32[392,256]{1,0:T(8,128)S(1)}, /*index=5*/f32[392,256]{1,0:T(8,128)S(1)}) custom-call(f32[6]{0:T(128)S(1)} %pad_maximum_fusion.refs_0_.flags, f32[1536,1536]{1,0:T(8,128)S(1)} %bitcast.20, ...), custom_call_target="tpu_custom_call" | custom-call | flops 8000000000 | bytes 1024 | tf_op jit(solution)/shard_map/pallas_call | solution.py:340
  102.2 2.1 %collective-permute-start.24 = (f32[392,256]{1,0:T(8,128)S(1)}, f32[392,256]{1,0:T(8,128)S(1)}, u32[]{:S(2)}, u32[]{:S(2)}) collective-permute-start(f32[392,256]{1,0:T(8,128)S(1)} %get-tuple-element.124.refs_6_.refs_2_), channel_id=1, source_target_pairs={{0,1},{1,0},{2,3},{3,2},{4,5},{5,4},{6,7},{7,6},{8,9},{9,8},{10,11... | collective-permute-start | bytes 1204232 | tf_op jit(solution)/shard_map/ppermute | solution.py:19
  105.0 2.0 %shard_map.99 = (f32[384,256]{1,0:T(8,128)S(1)}, f32[384,256]{1,0:T(8,128)S(1)}, f32[1,256]{1,0:T(1,128)S(1)}) custom-call(f32[6]{0:T(128)S(1)} %pad_maximum_fusion.refs_0_.flags, f32[1536,1536]{1,0:T(8,128)S(1)} %bitcast.21, f32[384,256]{1,0:T(8,128)S(1)} %get-tuple-element.117.refs_2_.refs_9_, f32[384,256]{1,0:T(8,128)S(1)} %get-tuple-element.118.refs_3_.refs_10_, ...), custom_call_target="tpu_custom_call" | custom-call | flops 1024 | bytes 1024 | tf_op jit(solution)/shard_map/pallas_call | solution.py:340
  107.0 0.9 collective-permute-start.23
  108.8 3.4 %shard_map.100 = (f32[384,256]{1,0:T(8,128)S(1)}, f32[384,256]{1,0:T(8,128)S(1)}, f32[1536,256]{1,0:T(8,128)S(1)}) custom-call(f32[6]{0:T(128)S(1)} %pad_maximum_fusion.refs_0_.flags, f32[1536,1536]{1,0:T(8,128)S(1)} %bitcast.27, f32[384,256]{1,0:T(8,128)S(1)} %get-tuple-element.126.refs_2_, f32[384,256]{1,0:T(8,128)S(1)} %get-tuple-element.127.refs_3_, ...), custom_call_target="tpu_custom_call" | custom-call | flops 1024 | bytes 1024 | tf_op jit(solution)/shard_map/pallas_call | solution.py:340
  112.2 8.9 %collective-permute-done.24.refs_4_ = f32[392,256]{1,0:T(8,128)S(1)} collective-permute-done((f32[392,256]{1,0:T(8,128)S(1)}, f32[392,256]{1,0:T(8,128)S(1)}, u32[]{:S(2)}, u32[]{:S(2)}) %collective-permute-start.24) | collective-permute-done | bytes 401440 | tf_op jit(solution)/shard_map/ppermute | solution.py:19
  121.0 2.7 %shard_map.101 = (f32[384,256]{1,0:T(8,128)S(1)}, f32[384,256]{1,0:T(8,128)S(1)}, f32[392,256]{1,0:T(8,128)S(1)}, f32[392,256]{1,0:T(8,128)S(1)}) custom-call(f32[6]{0:T(128)S(1)} %pad_maximum_fusion.refs_0_.flags, f32[1536,1536]{1,0:T(8,128)S(1)} %bitcast.28, f32[392,256]{1,0:T(8,128)S(1)} %get-tuple-element.124.refs_6_.refs_2_, ...), custom_call_target="tpu_custom_call" | custom-call | flops 8000000000 | bytes 1024 | tf_op jit(solution)/shard_map/pallas_call | solution.py:340
  123.7 2.5 %shard_map.102 = (f32[384,256]{1,0:T(8,128)S(1)}, f32[384,256]{1,0:T(8,128)S(1)}, f32[24,256]{1,0:T(8,128)S(1)}) custom-call(f32[6]{0:T(128)S(1)} %pad_maximum_fusion.refs_0_.flags, f32[1536,1536]{1,0:T(8,128)S(1)} %bitcast.29, f32[384,256]{1,0:T(8,128)S(1)} %get-tuple-element.128.refs_2_.refs_4_, f32[384,256]{1,0:T(8,128)S(1)} %get-tuple-element.129.refs_3_.refs_5_, ...), custom_call_target="tpu_custom_call" | custom-call | flops 1024 | bytes 1024 | tf_op jit(solution)/shard_map/pallas_call | solution.py:340
  126.3 2.5 %collective-permute-start.26 = (f32[24,256]{1,0:T(8,128)S(1)}, f32[24,256]{1,0:T(8,128)S(1)}, u32[]{:S(2)}, u32[]{:S(2)}) collective-permute-start(f32[24,256]{1,0:T(8,128)S(1)} %get-tuple-element.136), channel_id=1, source_target_pairs={{0,1},{1,0},{2,3},{3,2},{4,5},{5,4},{6,7},{7,6},{8,9},{9,8},{10,11... | collective-permute-start | bytes 73736 | tf_op jit(solution)/shard_map/ppermute | solution.py:19
  128.8 1.8 %collective-permute-done.26 = f32[24,256]{1,0:T(8,128)S(1)} collective-permute-done((f32[24,256]{1,0:T(8,128)S(1)}, f32[24,256]{1,0:T(8,128)S(1)}, u32[]{:S(2)}, u32[]{:S(2)}) %collective-permute-start.26) | collective-permute-done | bytes 24608 | tf_op jit(solution)/shard_map/ppermute | solution.py:19
  130.6 1.9 %collective-permute-start.27 = (f32[48,256]{1,0:T(8,128)S(1)}, f32[48,256]{1,0:T(8,128)S(1)}, u32[]{:S(2)}, u32[]{:S(2)}) collective-permute-start(f32[48,256]{1,0:T(8,128)S(1)} %pad_add_fusion.4), channel_id=1, source_target_pairs={{0,4},{1,5},{2,6},{3,7},{4,0},{5,1},{6,2},{7,3},{8,12},{9,13},{10,... | collective-permute-start | bytes 147464 | tf_op jit(solution)/shard_map/ppermute | solution.py:19
  132.6 3.1 %collective-permute-done.27 = f32[48,256]{1,0:T(8,128)S(1)} collective-permute-done((f32[48,256]{1,0:T(8,128)S(1)}, f32[48,256]{1,0:T(8,128)S(1)}, u32[]{:S(2)}, u32[]{:S(2)}) %collective-permute-start.27) | collective-permute-done | bytes 49184 | tf_op jit(solution)/shard_map/ppermute | solution.py:19
  135.6 2.2 %collective-permute-start.28 = (f32[96,256]{1,0:T(8,128)S(1)}, f32[96,256]{1,0:T(8,128)S(1)}, u32[]{:S(2)}, u32[]{:S(2)}) collective-permute-start(f32[96,256]{1,0:T(8,128)S(1)} %pad_add_fusion.1.refs_0_), channel_id=1, source_target_pairs={{0,2},{1,3},{2,0},{3,1},{4,6},{5,7},{6,4},{7,5},{8,10},{9,11},{10,... | collective-permute-start | bytes 294920 | tf_op jit(solution)/shard_map/ppermute | solution.py:19
  138.9 1.6 collective-permute-done.28.refs_1_
  141.7 3.0 %collective-permute-start.29 = (f32[136,256]{1,0:T(8,128)S(1)}, f32[136,256]{1,0:T(8,128)S(1)}, u32[]{:S(2)}, u32[]{:S(2)}) collective-permute-start(f32[136,256]{1,0:T(8,128)S(1)} %shard_map.103), channel_id=1, source_target_pairs={{0,8},{8,0},{16,24},{24,16},{1,9},{9,1},{17,25},{25,17},{2,10},{10... | collective-permute-start | bytes 417800 | tf_op jit(solution)/shard_map/ppermute | solution.py:19
  144.7 1.0 collective-permute-done.29
  146.6 6.6 %collective-permute-done.30 = f32[136,256]{1,0:T(8,128)S(1)} collective-permute-done((f32[136,256]{1,0:T(8,128)S(1)}, f32[136,256]{1,0:T(8,128)S(1)}, u32[]{:S(2)}, u32[]{:S(2)}) %collective-permute-start.30) | collective-permute-done | bytes 139296 | tf_op jit(solution)/shard_map/ppermute | solution.py:19
  153.8 1.2 shard_map.105
  155.1 3.7 %shard_map.106 = f32[1536,256]{1,0:T(8,128)} custom-call(f32[6]{0:T(128)S(1)} %pad_maximum_fusion.refs_0_.flags, f32[384,256]{1,0:T(8,128)S(1)} %get-tuple-element.144.refs_1_, f32[384,256]{1,0:T(8,128)S(1)} %get-tuple-element.145.refs_2_, f32[392,256]{1,0:T(8,128)S(1)} %get-tuple-element.146.refs_6_.refs_3_, ...), custom_call_target="tpu_custom_call" | custom-call | flops 1024 | bytes 1024 | tf_op jit(solution)/shard_map/pallas_call | solution.py:340
  (94 shorter events, 14.6 us)
Async XLA Ops:
  0.6 4.1 %copy-start.3 = (s32[1,1,16]{2,1,0:T(1,128)S(1)}, s32[1,1,16]{2,1,0:T(1,128)}, u32[]{:S(2)}) copy-start(s32[1,1,16]{2,1,0:T(1,128)} %param.11) | copy-start | bytes 196
  0.6 4.1 %copy-start.4 = (f32[4,128]{1,0:T(4,128)S(1)}, f32[4,128]{1,0:T(4,128)}, u32[]{:S(2)}) copy-start(f32[4,128]{1,0:T(4,128)} %inverse) | copy-start | bytes 6148
  4.2 5.3 %copy-start.5 = (s32[1,1,4,384]{3,2,1,0:T(4,128)S(1)}, s32[1,1,4,384]{3,2,1,0:T(4,128)}, u32[]{:S(2)}) copy-start(s32[1,1,4,384]{3,2,1,0:T(4,128)} %param.12) | copy-start | bytes 18436
  4.2 28.6 %collective-permute-start = (f32[416,256]{1,0:T(8,128)}, f32[416,256]{1,0:T(8,128)S(1)}, u32[]{:S(2)}, u32[]{:S(2)}) collective-permute-start(f32[416,256]{1,0:T(8,128)} %get-tuple-element.78.refs_2_.sent), channel_id=1, source_target_pairs={{0,8},{8,0},{16,24},{24,16},{1,9},{9,1},{17,25},{25,17},{2,10},{10... | collective-permute-start | bytes 1277960 | tf_op jit(solution)/shard_map/ppermute | solution.py:19
  5.3 27.6 %copy-start.1 = (f32[416,256]{1,0:T(8,128)S(1)}, f32[416,256]{1,0:T(8,128)}, u32[]{:S(2)}) copy-start(f32[416,256]{1,0:T(8,128)} %get-tuple-element.78.refs_2_.sent) | copy-start | bytes 1277956
  5.3 4.5 %collective-permute-start.4 = (f32[12,128]{1,0:T(8,128)S(1)}, f32[12,128]{1,0:T(8,128)S(1)}, u32[]{:S(2)}, u32[]{:S(2)}) collective-permute-start(f32[12,128]{1,0:T(8,128)S(1)} %shard_map.88), channel_id=1, source_target_pairs={{0,1},{1,0},{2,3},{3,2},{4,5},{5,4},{6,7},{7,6},{8,9},{9,8},{10,11... | collective-permute-start | bytes 18440 | tf_op jit(solution)/shard_map/ppermute | solution.py:19
  7.9 24.9 %collective-permute-start.1 = (f32[416,256]{1,0:T(8,128)}, f32[416,256]{1,0:T(8,128)S(1)}, u32[]{:S(2)}, u32[]{:S(2)}) collective-permute-start(f32[416,256]{1,0:T(8,128)} %get-tuple-element.79.refs_3_), channel_id=1, source_target_pairs={{8,16},{16,8},{9,17},{17,9},{10,18},{18,10},{11,19},{19,11},{12,20... | collective-permute-start | bytes 1277960 | tf_op jit(solution)/shard_map/ppermute | solution.py:26
  8.6 31.9 %collective-permute-start.2 = (f32[416,256]{1,0:T(8,128)}, f32[416,256]{1,0:T(8,128)S(1)}, u32[]{:S(2)}, u32[]{:S(2)}) collective-permute-start(f32[416,256]{1,0:T(8,128)} %get-tuple-element.84.refs_2_), channel_id=1, source_target_pairs={{0,1},{1,0},{2,3},{3,2},{4,5},{5,4},{6,7},{7,6},{8,9},{9,8},{10,11... | collective-permute-start | bytes 1277960 | tf_op jit(solution)/shard_map/ppermute | solution.py:19
  8.8 31.7 %collective-permute-start.3 = (f32[416,256]{1,0:T(8,128)}, f32[416,256]{1,0:T(8,128)S(1)}, u32[]{:S(2)}, u32[]{:S(2)}) collective-permute-start(f32[416,256]{1,0:T(8,128)} %get-tuple-element.85.refs_3_), channel_id=1, source_target_pairs={{1,2},{2,1},{3,4},{4,3},{5,6},{6,5},{9,10},{10,9},{11,12},{12,11},... | collective-permute-start | bytes 1277960 | tf_op jit(solution)/shard_map/ppermute | solution.py:26
  9.8 14.7 %collective-permute-start.5 = (f32[24,128]{1,0:T(8,128)S(1)}, f32[24,128]{1,0:T(8,128)S(1)}, u32[]{:S(2)}, u32[]{:S(2)}) collective-permute-start(f32[24,128]{1,0:T(8,128)S(1)} %pad_add_fusion.8), channel_id=1, source_target_pairs={{0,4},{1,5},{2,6},{3,7},{4,0},{5,1},{6,2},{7,3},{8,12},{9,13},{10,... | collective-permute-start | bytes 36872 | tf_op jit(solution)/shard_map/ppermute | solution.py:19
  24.6 3.8 %collective-permute-start.6 = (f32[48,128]{1,0:T(8,128)S(1)}, f32[48,128]{1,0:T(8,128)S(1)}, u32[]{:S(2)}, u32[]{:S(2)}) collective-permute-start(f32[48,128]{1,0:T(8,128)S(1)} %pad_add_fusion.7), channel_id=1, source_target_pairs={{0,2},{1,3},{2,0},{3,1},{4,6},{5,7},{6,4},{7,5},{8,10},{9,11},{10,... | collective-permute-start | bytes 73736 | tf_op jit(solution)/shard_map/ppermute | solution.py:19
  28.4 4.4 %collective-permute-start.7 = (f32[96,128]{1,0:T(8,128)S(1)}, f32[96,128]{1,0:T(8,128)S(1)}, u32[]{:S(2)}, u32[]{:S(2)}) collective-permute-start(f32[96,128]{1,0:T(8,128)S(1)} %pad_add_fusion.6), channel_id=1, source_target_pairs={{0,16},{8,24},{16,0},{24,8},{1,17},{9,25},{17,1},{25,9},{2,18},{10... | collective-permute-start | bytes 147464 | tf_op jit(solution)/shard_map/ppermute | solution.py:19
  32.9 3.7 %copy-start = (f32[1,1,1536,1536]{3,2,1,0:T(8,128)S(1)}, f32[1,1,1536,1536]{3,2,1,0:T(8,128)}, u32[]{:S(2)}) copy-start(f32[1,1,1536,1536]{3,2,1,0:T(8,128)} %param.9) | copy-start | bytes 28311556
  40.5 4.4 %slice-start = ((s8[9437184]{0:T(1024)(128)(4,1)}), s8[4194304]{0:T(1024)(128)(4,1)S(1)}, s32[]{:S(2)}) async-start(s8[9437184]{0:T(1024)(128)(4,1)} %bitcast.16), calls=%async_computation | async-start | bytes 8388608
  40.5 12.5 %slice-start.3 = ((s8[9437184]{0:T(1024)(128)(4,1)}), s8[4194304]{0:T(1024)(128)(4,1)S(1)}, s32[]{:S(2)}) async-start(s8[9437184]{0:T(1024)(128)(4,1)} %bitcast.22), calls=%async_computation.3 | async-start | bytes 8388608
  40.5 4.9 %slice-start.1 = ((s8[9437184]{0:T(1024)(128)(4,1)}), s8[4194304]{0:T(1024)(128)(4,1)S(1)}, s32[]{:S(2)}) async-start(s8[9437184]{0:T(1024)(128)(4,1)} %bitcast.16), calls=%async_computation.1 | async-start | bytes 8388608
  40.5 5.1 %slice-start.2 = ((s8[9437184]{0:T(1024)(128)(4,1)}), s8[1048576]{0:T(1024)(128)(4,1)S(1)}, s32[]{:S(2)}) async-start(s8[9437184]{0:T(1024)(128)(4,1)} %bitcast.16), calls=%async_computation.2 | async-start | bytes 2097152
  40.5 12.4 %slice-start.4 = ((s8[9437184]{0:T(1024)(128)(4,1)}), s8[4194304]{0:T(1024)(128)(4,1)S(1)}, s32[]{:S(2)}) async-start(s8[9437184]{0:T(1024)(128)(4,1)} %bitcast.22), calls=%async_computation.4 | async-start | bytes 8388608
  40.5 12.4 %slice-start.5 = ((s8[9437184]{0:T(1024)(128)(4,1)}), s8[1048576]{0:T(1024)(128)(4,1)S(1)}, s32[]{:S(2)}) async-start(s8[9437184]{0:T(1024)(128)(4,1)} %bitcast.22), calls=%async_computation.5 | async-start | bytes 2097152
  43.9 16.7 %collective-permute-start.11 = (f32[392,256]{1,0:T(8,128)S(1)}, f32[392,256]{1,0:T(8,128)S(1)}, u32[]{:S(2)}, u32[]{:S(2)}) collective-permute-start(f32[392,256]{1,0:T(8,128)S(1)} %get-tuple-element.91.refs_6_.refs_2_), channel_id=1, source_target_pairs={{0,1},{1,0},{2,3},{3,2},{4,5},{5,4},{6,7},{7,6},{8,9},{9,8},{10,11... | collective-permute-start | bytes 1204232 | tf_op jit(solution)/shard_map/ppermute | solution.py:19
  44.0 16.6 %collective-permute-start.12 = (f32[392,256]{1,0:T(8,128)S(1)}, f32[392,256]{1,0:T(8,128)S(1)}, u32[]{:S(2)}, u32[]{:S(2)}) collective-permute-start(f32[392,256]{1,0:T(8,128)S(1)} %get-tuple-element.92.refs_7_.refs_3_), channel_id=1, source_target_pairs={{1,2},{2,1},{3,4},{4,3},{5,6},{6,5},{9,10},{10,9},{11,12},{12,11},... | collective-permute-start | bytes 1204232 | tf_op jit(solution)/shard_map/ppermute | solution.py:26
  47.6 5.3 %collective-permute-start.8 = (f32[384,256]{1,0:T(8,128)S(1)}, f32[384,256]{1,0:T(8,128)S(1)}, u32[]{:S(2)}, u32[]{:S(2)}) collective-permute-start(f32[384,256]{1,0:T(8,128)S(1)} %get-tuple-element.93.refs_2_), channel_id=1, source_target_pairs={{0,8},{8,0},{16,24},{24,16},{1,9},{9,1},{17,25},{25,17},{2,10},{10... | collective-permute-start | bytes 1179656 | tf_op jit(solution)/shard_map/ppermute | solution.py:19
  47.7 5.3 %collective-permute-start.9 = (f32[384,256]{1,0:T(8,128)S(1)}, f32[384,256]{1,0:T(8,128)S(1)}, u32[]{:S(2)}, u32[]{:S(2)}) collective-permute-start(f32[384,256]{1,0:T(8,128)S(1)} %get-tuple-element.94.refs_3_), channel_id=1, source_target_pairs={{8,16},{16,8},{9,17},{17,9},{10,18},{18,10},{11,19},{19,11},{12,20... | collective-permute-start | bytes 1179656 | tf_op jit(solution)/shard_map/ppermute | solution.py:26
  48.5 4.4 %collective-permute-start.10 = (f32[192,128]{1,0:T(8,128)S(1)}, f32[192,128]{1,0:T(8,128)S(1)}, u32[]{:S(2)}, u32[]{:S(2)}) collective-permute-start(f32[192,128]{1,0:T(8,128)S(1)} %pad_add_fusion.3), channel_id=1, source_target_pairs={{0,8},{8,0},{16,24},{24,16},{1,9},{9,1},{17,25},{25,17},{2,10},{10... | collective-permute-start | bytes 294920 | tf_op jit(solution)/shard_map/ppermute | solution.py:19
  60.6 2.7 %copy-start.2 = (f32[1,1,16,1536]{3,2,1,0:T(8,128)S(1)}, f32[1,1,16,1536]{3,2,1,0:T(8,128)}, u32[]{:S(2)}) copy-start(f32[1,1,16,1536]{3,2,1,0:T(8,128)} %param.10) | copy-start | bytes 294916
  65.6 4.4 %collective-permute-start.13 = (f32[24,256]{1,0:T(8,128)S(1)}, f32[24,256]{1,0:T(8,128)S(1)}, u32[]{:S(2)}, u32[]{:S(2)}) collective-permute-start(f32[24,256]{1,0:T(8,128)S(1)} %get-tuple-element.107), channel_id=1, source_target_pairs={{0,1},{1,0},{2,3},{3,2},{4,5},{5,4},{6,7},{7,6},{8,9},{9,8},{10,11... | collective-permute-start | bytes 73736 | tf_op jit(solution)/shard_map/ppermute | solution.py:19
  70.0 5.4 %collective-permute-start.14 = (f32[48,256]{1,0:T(8,128)S(1)}, f32[48,256]{1,0:T(8,128)S(1)}, u32[]{:S(2)}, u32[]{:S(2)}) collective-permute-start(f32[48,256]{1,0:T(8,128)S(1)} %pad_add_fusion.5), channel_id=1, source_target_pairs={{0,4},{1,5},{2,6},{3,7},{4,0},{5,1},{6,2},{7,3},{8,12},{9,13},{10,... | collective-permute-start | bytes 147464 | tf_op jit(solution)/shard_map/ppermute | solution.py:19
  75.4 5.5 %collective-permute-start.15 = (f32[96,256]{1,0:T(8,128)S(1)}, f32[96,256]{1,0:T(8,128)S(1)}, u32[]{:S(2)}, u32[]{:S(2)}) collective-permute-start(f32[96,256]{1,0:T(8,128)S(1)} %pad_add_fusion.2.refs_0_), channel_id=1, source_target_pairs={{0,2},{1,3},{2,0},{3,1},{4,6},{5,7},{6,4},{7,5},{8,10},{9,11},{10,... | collective-permute-start | bytes 294920 | tf_op jit(solution)/shard_map/ppermute | solution.py:19
  78.3 20.6 %collective-permute-start.20 = (f32[392,256]{1,0:T(8,128)S(1)}, f32[392,256]{1,0:T(8,128)S(1)}, u32[]{:S(2)}, u32[]{:S(2)}) collective-permute-start(f32[392,256]{1,0:T(8,128)S(1)} %get-tuple-element.119.refs_6_.refs_2_.refs_10_), channel_id=1, source_target_pairs={{0,1},{1,0},{2,3},{3,2},{4,5},{5,4},{6,7},{7,6},{8,9},{9,8},{10,11... | collective-permute-start | bytes 1204232 | tf_op jit(solution)/shard_map/ppermute | solution.py:19
  78.8 20.1 %collective-permute-start.21 = (f32[392,256]{1,0:T(8,128)S(1)}, f32[392,256]{1,0:T(8,128)S(1)}, u32[]{:S(2)}, u32[]{:S(2)}) collective-permute-start(f32[392,256]{1,0:T(8,128)S(1)} %get-tuple-element.120.refs_7_.refs_3_.refs_11_), channel_id=1, source_target_pairs={{1,2},{2,1},{3,4},{4,3},{5,6},{6,5},{9,10},{10,9},{11,12},{12,11},... | collective-permute-start | bytes 1204232 | tf_op jit(solution)/shard_map/ppermute | solution.py:26
  80.9 14.2 %collective-permute-start.16 = (f32[384,256]{1,0:T(8,128)S(1)}, f32[384,256]{1,0:T(8,128)S(1)}, u32[]{:S(2)}, u32[]{:S(2)}) collective-permute-start(f32[384,256]{1,0:T(8,128)S(1)} %get-tuple-element.112.refs_2_.refs_8_), channel_id=1, source_target_pairs={{0,8},{8,0},{16,24},{24,16},{1,9},{9,1},{17,25},{25,17},{2,10},{10... | collective-permute-start | bytes 1179656 | tf_op jit(solution)/shard_map/ppermute | solution.py:19
  80.9 14.2 %collective-permute-start.17 = (f32[384,256]{1,0:T(8,128)S(1)}, f32[384,256]{1,0:T(8,128)S(1)}, u32[]{:S(2)}, u32[]{:S(2)}) collective-permute-start(f32[384,256]{1,0:T(8,128)S(1)} %get-tuple-element.113.refs_3_.refs_9_), channel_id=1, source_target_pairs={{8,16},{16,8},{9,17},{17,9},{10,18},{18,10},{11,19},{19,11},{12,20... | collective-permute-start | bytes 1179656 | tf_op jit(solution)/shard_map/ppermute | solution.py:26
  82.4 5.4 %collective-permute-start.18 = (f32[136,256]{1,0:T(8,128)S(1)}, f32[136,256]{1,0:T(8,128)S(1)}, u32[]{:S(2)}, u32[]{:S(2)}) collective-permute-start(f32[136,256]{1,0:T(8,128)S(1)} %shard_map.94), channel_id=1, source_target_pairs={{0,8},{8,0},{16,24},{24,16},{1,9},{9,1},{17,25},{25,17},{2,10},{10... | collective-permute-start | bytes 417800 | tf_op jit(solution)/shard_map/ppermute | solution.py:19
  87.8 6.7 %collective-permute-start.19 = (f32[136,256]{1,0:T(8,128)S(1)}, f32[136,256]{1,0:T(8,128)S(1)}, u32[]{:S(2)}, u32[]{:S(2)}) collective-permute-start(f32[136,256]{1,0:T(8,128)S(1)} %add.149), channel_id=1, source_target_pairs={{0,16},{8,24},{16,0},{24,8},{1,17},{9,25},{17,1},{25,9},{2,18},{10... | collective-permute-start | bytes 417800 | tf_op jit(solution)/shard_map/ppermute | solution.py:19
  102.2 18.9 %collective-permute-start.24 = (f32[392,256]{1,0:T(8,128)S(1)}, f32[392,256]{1,0:T(8,128)S(1)}, u32[]{:S(2)}, u32[]{:S(2)}) collective-permute-start(f32[392,256]{1,0:T(8,128)S(1)} %get-tuple-element.124.refs_6_.refs_2_), channel_id=1, source_target_pairs={{0,1},{1,0},{2,3},{3,2},{4,5},{5,4},{6,7},{7,6},{8,9},{9,8},{10,11... | collective-permute-start | bytes 1204232 | tf_op jit(solution)/shard_map/ppermute | solution.py:19
  104.3 16.8 %collective-permute-start.25 = (f32[392,256]{1,0:T(8,128)S(1)}, f32[392,256]{1,0:T(8,128)S(1)}, u32[]{:S(2)}, u32[]{:S(2)}) collective-permute-start(f32[392,256]{1,0:T(8,128)S(1)} %get-tuple-element.125.refs_7_.refs_3_), channel_id=1, source_target_pairs={{1,2},{2,1},{3,4},{4,3},{5,6},{6,5},{9,10},{10,9},{11,12},{12,11},... | collective-permute-start | bytes 1204232 | tf_op jit(solution)/shard_map/ppermute | solution.py:26
  107.0 1.8 %collective-permute-start.22 = (f32[384,256]{1,0:T(8,128)S(1)}, f32[384,256]{1,0:T(8,128)S(1)}, u32[]{:S(2)}, u32[]{:S(2)}) collective-permute-start(f32[384,256]{1,0:T(8,128)S(1)} %get-tuple-element.126.refs_2_), channel_id=1, source_target_pairs={{0,8},{8,0},{16,24},{24,16},{1,9},{9,1},{17,25},{25,17},{2,10},{10... | collective-permute-start | bytes 1179656 | tf_op jit(solution)/shard_map/ppermute | solution.py:19
  107.0 1.7 %collective-permute-start.23 = (f32[384,256]{1,0:T(8,128)S(1)}, f32[384,256]{1,0:T(8,128)S(1)}, u32[]{:S(2)}, u32[]{:S(2)}) collective-permute-start(f32[384,256]{1,0:T(8,128)S(1)} %get-tuple-element.127.refs_3_), channel_id=1, source_target_pairs={{8,16},{16,8},{9,17},{17,9},{10,18},{18,10},{11,19},{19,11},{12,20... | collective-permute-start | bytes 1179656 | tf_op jit(solution)/shard_map/ppermute | solution.py:26
  126.3 4.4 %collective-permute-start.26 = (f32[24,256]{1,0:T(8,128)S(1)}, f32[24,256]{1,0:T(8,128)S(1)}, u32[]{:S(2)}, u32[]{:S(2)}) collective-permute-start(f32[24,256]{1,0:T(8,128)S(1)} %get-tuple-element.136), channel_id=1, source_target_pairs={{0,1},{1,0},{2,3},{3,2},{4,5},{5,4},{6,7},{7,6},{8,9},{9,8},{10,11... | collective-permute-start | bytes 73736 | tf_op jit(solution)/shard_map/ppermute | solution.py:19
  130.6 5.0 %collective-permute-start.27 = (f32[48,256]{1,0:T(8,128)S(1)}, f32[48,256]{1,0:T(8,128)S(1)}, u32[]{:S(2)}, u32[]{:S(2)}) collective-permute-start(f32[48,256]{1,0:T(8,128)S(1)} %pad_add_fusion.4), channel_id=1, source_target_pairs={{0,4},{1,5},{2,6},{3,7},{4,0},{5,1},{6,2},{7,3},{8,12},{9,13},{10,... | collective-permute-start | bytes 147464 | tf_op jit(solution)/shard_map/ppermute | solution.py:19
  135.6 4.8 %collective-permute-start.28 = (f32[96,256]{1,0:T(8,128)S(1)}, f32[96,256]{1,0:T(8,128)S(1)}, u32[]{:S(2)}, u32[]{:S(2)}) collective-permute-start(f32[96,256]{1,0:T(8,128)S(1)} %pad_add_fusion.1.refs_0_), channel_id=1, source_target_pairs={{0,2},{1,3},{2,0},{3,1},{4,6},{5,7},{6,4},{7,5},{8,10},{9,11},{10,... | collective-permute-start | bytes 294920 | tf_op jit(solution)/shard_map/ppermute | solution.py:19
  137.9 17.2 %collective-permute-start.33 = (f32[392,256]{1,0:T(8,128)S(1)}, f32[392,256]{1,0:T(8,128)S(1)}, u32[]{:S(2)}, u32[]{:S(2)}) collective-permute-start(f32[392,256]{1,0:T(8,128)S(1)} %get-tuple-element.146.refs_6_.refs_3_), channel_id=1, source_target_pairs={{0,1},{1,0},{2,3},{3,2},{4,5},{5,4},{6,7},{7,6},{8,9},{9,8},{10,11... | collective-permute-start | bytes 1204232 | tf_op jit(solution)/shard_map/ppermute | solution.py:19
  138.2 16.9 %collective-permute-start.34 = (f32[392,256]{1,0:T(8,128)S(1)}, f32[392,256]{1,0:T(8,128)S(1)}, u32[]{:S(2)}, u32[]{:S(2)}) collective-permute-start(f32[392,256]{1,0:T(8,128)S(1)} %get-tuple-element.147.refs_7_.refs_4_), channel_id=1, source_target_pairs={{1,2},{2,1},{3,4},{4,3},{5,6},{6,5},{9,10},{10,9},{11,12},{12,11},... | collective-permute-start | bytes 1204232 | tf_op jit(solution)/shard_map/ppermute | solution.py:26
  140.5 14.6 %collective-permute-start.31 = (f32[384,256]{1,0:T(8,128)S(1)}, f32[384,256]{1,0:T(8,128)S(1)}, u32[]{:S(2)}, u32[]{:S(2)}) collective-permute-start(f32[384,256]{1,0:T(8,128)S(1)} %get-tuple-element.144.refs_1_), channel_id=1, source_target_pairs={{0,8},{8,0},{16,24},{24,16},{1,9},{9,1},{17,25},{25,17},{2,10},{10... | collective-permute-start | bytes 1179656 | tf_op jit(solution)/shard_map/ppermute | solution.py:19
  140.5 14.6 %collective-permute-start.32 = (f32[384,256]{1,0:T(8,128)S(1)}, f32[384,256]{1,0:T(8,128)S(1)}, u32[]{:S(2)}, u32[]{:S(2)}) collective-permute-start(f32[384,256]{1,0:T(8,128)S(1)} %get-tuple-element.145.refs_2_), channel_id=1, source_target_pairs={{8,16},{16,8},{9,17},{17,9},{10,18},{18,10},{11,19},{19,11},{12,20... | collective-permute-start | bytes 1179656 | tf_op jit(solution)/shard_map/ppermute | solution.py:26
  141.7 4.0 %collective-permute-start.29 = (f32[136,256]{1,0:T(8,128)S(1)}, f32[136,256]{1,0:T(8,128)S(1)}, u32[]{:S(2)}, u32[]{:S(2)}) collective-permute-start(f32[136,256]{1,0:T(8,128)S(1)} %shard_map.103), channel_id=1, source_target_pairs={{0,8},{8,0},{16,24},{24,16},{1,9},{9,1},{17,25},{25,17},{2,10},{10... | collective-permute-start | bytes 417800 | tf_op jit(solution)/shard_map/ppermute | solution.py:19
  145.8 7.5 %collective-permute-start.30 = (f32[136,256]{1,0:T(8,128)S(1)}, f32[136,256]{1,0:T(8,128)S(1)}, u32[]{:S(2)}, u32[]{:S(2)}) collective-permute-start(f32[136,256]{1,0:T(8,128)S(1)} %add.153), channel_id=1, source_target_pairs={{0,16},{8,24},{16,0},{24,8},{1,17},{9,25},{17,1},{25,9},{2,18},{10... | collective-permute-start | bytes 417800 | tf_op jit(solution)/shard_map/ppermute | solution.py:19

commit v4 on v3

--- a/solution.py
+++ b/solution.py
@@ -36,8 +36,7 @@
 
 
 def steps_of():
-    sx, sy = ([(axis, bit) for bit in bits_of(axis)[::-1]] for axis in ("sx", "sy"))
-    return sy[-1:] + sy[:-1] + sx
+    return [("sy", 1)] + [("sx", bit) for bit in bits_of("sx")] + [("sy", bit) for bit in bits_of("sy")[:0:-1]]
 
 
 def stacked_rows(parts):
@@ -116,6 +115,8 @@
         for k in range(ncl):
             listed = jnp.full((1, width - face % width), corners[k].astype(F32))
             out[start + k : start + k + 1, face % width :] = listed
+        if out.shape[0] > start + ncl:
+            out[start + ncl :] = jnp.zeros((out.shape[0] - start - ncl, width), F32)
     for started in copies:
         started.wait()
 
@@ -137,7 +138,8 @@
     ncl = coupling.shape[0]
     ids = lax.broadcasted_iota(jnp.int32, (ncl, ncoarse), 1).astype(F32)
     own_pick = (sent[sent.shape[0] - ncl :, sent.shape[1] - 1 :] == ids).astype(F32)
-    nears = faces_of(flags, [near[face:] for near in (near0, near1, near2, near3)])
+    end = near0.shape[0]
+    nears = faces_of(flags, [near[face:end] for near in (near0, near1, near2, near3)])
     for f, near in enumerate(nears):
         columns = jnp.concatenate([near[at : at + ncl] for at in range(0, near.shape[0], ncl)], axis=1)
         near_pick = (columns[:, columns.shape[1] - 1 :] == ids).astype(F32)
@@ -441,7 +443,7 @@
     sent = call(
         pack_kernel,
         [corners, load, coupling_mat],
-        [(face + extra, width)] * 4,
+        [(face + extra, width)] * 2 + [(face + extra + FAR_ROWS, width)] * 2,
         [pltpu.SemaphoreType.DMA((copies,))],
         smem=1,
         anywhere=(1, 2),
@@ -451,7 +453,7 @@
 
     own = coarse_inverse.shape[0]
     table_rows = own + 8
-    inverse, _ = lax.optimization_barrier((coarse_inverse, sent[0]))
+    inverse, flags, order, _ = lax.optimization_barrier((coarse_inverse, flags, order, sent[0]))
     (own_rows,) = call(rows_kernel, [corners, inverse], [(table_rows, ncoarse)], smem=1, flops=CRIT_FLOPS)
 
     def gather(partial, coef):

time: 160 us -> 151 us (0.944)
  waiting for transfers between devices: 52.1 us -> 46.8 us
  local copies, waits for them, and re-layouts: 4.51 us -> 0.1 us
  starting transfers between devices: 50.3 us -> 51.9 us
    ppermute x25, waiting for transfers between devices: 52.1 us -> 46.8 us  [swapped(): lax.ppermute(block, axis, [(i, i ^ bit) for i in range(lax.axis_size(axis...]
    unnamed x24 -> x26, local copies, waits for them, and re-layouts: 4.48 us -> 0.07 us
    ppermute x25, starting transfers between devices: 42.7 us -> 44.5 us  [swapped(): lax.ppermute(block, axis, [(i, i ^ bit) for i in range(lax.axis_size(axis...]
  transfers between devices with their start and end apart: 35 -> 35, of which waited for: 17 -> 17; matrix products, arithmetic and copies ran while one was open for 0% -> 0% of each run, Pallas kernels for 16% -> 17%
where the time goes in v4:
time: 151 us; the launch traced here: 150 us
  starting transfers between devices  51.9 us (34%)
  Pallas kernels  48.7 us (32%)
  waiting for transfers between devices  46.8 us (31%)
    pallas_call x21, Pallas kernels, call(): pl.pallas_call(kernel, in_specs=[SMEM_SPEC if i < smem else ANY_SPEC if i...  48.7 us
    ppermute x25, waiting for transfers between devices, swapped(): lax.ppermute(block, axis, [(i, i ^ bit) for i in range(lax.axis_size(axis...  46.8 us
    ppermute x25, starting transfers between devices, swapped(): lax.ppermute(block, axis, [(i, i ^ bit) for i in range(lax.axis_size(axis...  44.5 us
    ppermute x10, starting transfers between devices, swapped_between(): return lax.ppermute(block, axis, route)  7.44 us
  transfers between devices with their start and end apart: 35, of which 17 were waited for; matrix products, arithmetic and copies ran while one was open for 0% of the time, Pallas kernels for 17%

profile of v4, /device:TPU:0, one launch (start us, length us, event | category | flops | bytes accessed | tf_op | source)
XLA Modules:
  0.0 150.3 jit_solution(3907234204135739865)
XLA Ops:
  0.7 1.0 fusion.refs_6_.select.refs_17_
  1.9 3.4 %shard_map.86 = (f32[416,256]{1,0:T(8,128)}, f32[416,256]{1,0:T(8,128)}, f32[424,256]{1,0:T(8,128)}, f32[424,256]{1,0:T(8,128)}) custom-call(s32[16]{0:T(128)} %bitcast.34, f32[1536,256]{1,0:T(8,128)} %bitcast.36, f32[16,1536]{1,0:T(8,128)} %bitcast.30), custom_call_target="tpu_custom_call" | custom-call | flops 1024 | bytes 1024 | tf_op jit(solution)/shard_map/pallas_call | solution.py:342
  6.0 3.0 %collective-permute-start.4 = (f32[12,128]{1,0:T(8,128)S(1)}, f32[12,128]{1,0:T(8,128)S(1)}, u32[]{:S(2)}, u32[]{:S(2)}) collective-permute-start(f32[12,128]{1,0:T(8,128)S(1)} %shard_map.88), channel_id=1, source_target_pairs={{0,1},{1,0},{2,3},{3,2},{4,5},{5,4},{6,7},{7,6},{8,9},{9,8},{10,11... | collective-permute-start | bytes 18440 | tf_op jit(solution)/shard_map/ppermute | solution.py:19
  11.4 3.5 %collective-permute-start = (f32[416,256]{1,0:T(8,128)S(1)}, f32[416,256]{1,0:T(8,128)S(1)}, u32[]{:S(2)}, u32[]{:S(2)}) collective-permute-start(f32[416,256]{1,0:T(8,128)S(1)} %copy-done), channel_id=1, source_target_pairs={{0,8},{8,0},{16,24},{24,16},{1,9},{9,1},{17,25},{25,17},{2,10},{10... | collective-permute-start | bytes 1277960 | tf_op jit(solution)/shard_map/ppermute | solution.py:19
  14.9 6.4 %collective-permute-done.6 = f32[48,128]{1,0:T(8,128)S(1)} collective-permute-done((f32[48,128]{1,0:T(8,128)S(1)}, f32[48,128]{1,0:T(8,128)S(1)}, u32[]{:S(2)}, u32[]{:S(2)}) %collective-permute-start.6) | collective-permute-done | bytes 24608 | tf_op jit(solution)/shard_map/ppermute | solution.py:19
  21.3 5.0 %collective-permute-start.7 = (f32[96,128]{1,0:T(8,128)S(1)}, f32[96,128]{1,0:T(8,128)S(1)}, u32[]{:S(2)}, u32[]{:S(2)}) collective-permute-start(f32[96,128]{1,0:T(8,128)S(1)} %pad_add_fusion.6), channel_id=1, source_target_pairs={{0,4},{1,5},{2,6},{3,7},{4,0},{5,1},{6,2},{7,3},{8,12},{9,13},{10,... | collective-permute-start | bytes 147464 | tf_op jit(solution)/shard_map/ppermute | solution.py:19
  26.3 2.1 %collective-permute-done.7 = f32[96,128]{1,0:T(8,128)S(1)} collective-permute-done((f32[96,128]{1,0:T(8,128)S(1)}, f32[96,128]{1,0:T(8,128)S(1)}, u32[]{:S(2)}, u32[]{:S(2)}) %collective-permute-start.7) | collective-permute-done | bytes 49184 | tf_op jit(solution)/shard_map/ppermute | solution.py:19
  28.4 3.4 %shard_map.87 = (f32[384,256]{1,0:T(8,128)S(1)}, f32[384,256]{1,0:T(8,128)S(1)}, f32[1536,256]{1,0:T(8,128)S(1)}) custom-call(f32[6]{0:T(128)S(1)} %pad_maximum_fusion.refs_0_.flags, f32[1536,1536]{1,0:T(8,128)S(1)} %bitcast.16, f32[416,256]{1,0:T(8,128)S(1)} %copy-done, f32[416,256]{1,0:T(8,128)S(1)} %copy-done.2, ...), custom_call_target="tpu_custom_call" | custom-call | flops 1024 | bytes 1024 | tf_op jit(solution)/shard_map/pallas_call | solution.py:342
  31.9 2.7 %shard_map.89 = (f32[384,256]{1,0:T(8,128)S(1)}, f32[384,256]{1,0:T(8,128)S(1)}, f32[392,256]{1,0:T(8,128)S(1)}, f32[392,256]{1,0:T(8,128)S(1)}) custom-call(f32[6]{0:T(128)S(1)} %pad_maximum_fusion.refs_0_.flags, f32[1536,1536]{1,0:T(8,128)S(1)} %bitcast.17, f32[424,256]{1,0:T(8,128)S(1)} %copy-done.4, f32[424,256]{1,0:T(8,128)S(1)} %copy-done.5, ...), custom_call_target="tpu_custom_call" | custom-call | flops 8000000000 | bytes 1024 | tf_op jit(solution)/shard_map/pallas_call | solution.py:342
  34.6 2.1 %collective-permute-start.11 = (f32[392,256]{1,0:T(8,128)S(1)}, f32[392,256]{1,0:T(8,128)S(1)}, u32[]{:S(2)}, u32[]{:S(2)}) collective-permute-start(f32[392,256]{1,0:T(8,128)S(1)} %get-tuple-element.95.refs_6_.refs_2_), channel_id=1, source_target_pairs={{0,1},{1,0},{2,3},{3,2},{4,5},{5,4},{6,7},{7,6},{8,9},{9,8},{10,11... | collective-permute-start | bytes 1204232 | tf_op jit(solution)/shard_map/ppermute | solution.py:19
  37.4 2.0 %shard_map.90 = (f32[384,256]{1,0:T(8,128)S(1)}, f32[384,256]{1,0:T(8,128)S(1)}, f32[1,256]{1,0:T(1,128)S(1)}) custom-call(f32[6]{0:T(128)S(1)} %pad_maximum_fusion.refs_0_.flags, f32[1536,1536]{1,0:T(8,128)S(1)} %bitcast.18, f32[384,256]{1,0:T(8,128)S(1)} %get-tuple-element.86.refs_2_.refs_8_, f32[384,256]{1,0:T(8,128)S(1)} %get-tuple-element.87.refs_3_.refs_9_, ...), custom_call_target="tpu_custom_call" | custom-call | flops 1024 | bytes 1024 | tf_op jit(solution)/shard_map/pallas_call | solution.py:342
  40.3 2.9 %collective-permute-start.10 = (f32[192,128]{1,0:T(8,128)S(1)}, f32[192,128]{1,0:T(8,128)S(1)}, u32[]{:S(2)}, u32[]{:S(2)}) collective-permute-start(f32[192,128]{1,0:T(8,128)S(1)} %pad_add_fusion.3), channel_id=1, source_target_pairs={{0,2},{1,3},{2,0},{3,1},{4,6},{5,7},{6,4},{7,5},{8,10},{9,11},{10,... | collective-permute-start | bytes 294920 | tf_op jit(solution)/shard_map/ppermute | solution.py:19
  43.2 5.7 %collective-permute-done.10 = f32[192,128]{1,0:T(8,128)S(1)} collective-permute-done((f32[192,128]{1,0:T(8,128)S(1)}, f32[192,128]{1,0:T(8,128)S(1)}, u32[]{:S(2)}, u32[]{:S(2)}) %collective-permute-start.10) | collective-permute-done | bytes 98336 | tf_op jit(solution)/shard_map/ppermute | solution.py:19
  48.9 3.4 %shard_map.91 = (f32[384,256]{1,0:T(8,128)S(1)}, f32[384,256]{1,0:T(8,128)S(1)}, f32[1536,256]{1,0:T(8,128)S(1)}) custom-call(f32[6]{0:T(128)S(1)} %pad_maximum_fusion.refs_0_.flags, f32[1536,1536]{1,0:T(8,128)S(1)} %bitcast.24, f32[384,256]{1,0:T(8,128)S(1)} %get-tuple-element.97.refs_2_, f32[384,256]{1,0:T(8,128)S(1)} %get-tuple-element.98.refs_3_, ...), custom_call_target="tpu_custom_call" | custom-call | flops 1024 | bytes 1024 | tf_op jit(solution)/shard_map/pallas_call | solution.py:342
  52.4 2.7 %shard_map.92 = (f32[384,256]{1,0:T(8,128)S(1)}, f32[384,256]{1,0:T(8,128)S(1)}, f32[392,256]{1,0:T(8,128)S(1)}, f32[392,256]{1,0:T(8,128)S(1)}) custom-call(f32[6]{0:T(128)S(1)} %pad_maximum_fusion.refs_0_.flags, f32[1536,1536]{1,0:T(8,128)S(1)} %bitcast.25, f32[392,256]{1,0:T(8,128)S(1)} %get-tuple-element.95.refs_6_.refs_2_, ...), custom_call_target="tpu_custom_call" | custom-call | flops 8000000000 | bytes 1024 | tf_op jit(solution)/shard_map/pallas_call | solution.py:342
  55.1 2.3 %shard_map.93 = (f32[384,256]{1,0:T(8,128)S(1)}, f32[384,256]{1,0:T(8,128)S(1)}, f32[24,256]{1,0:T(8,128)S(1)}) custom-call(f32[6]{0:T(128)S(1)} %pad_maximum_fusion.refs_0_.flags, f32[1536,1536]{1,0:T(8,128)S(1)} %bitcast.26, f32[384,256]{1,0:T(8,128)S(1)} %get-tuple-element.101.refs_2_.refs_0_, f32[384,256]{1,0:T(8,128)S(1)} %get-tuple-element.102.refs_3_.refs_1_, ...), custom_call_target="tpu_custom_call" | custom-call | flops 1024 | bytes 1024 | tf_op jit(solution)/shard_map/pallas_call | solution.py:342
  57.4 1.5 %collective-permute-start.13 = (f32[24,256]{1,0:T(8,128)S(1)}, f32[24,256]{1,0:T(8,128)S(1)}, u32[]{:S(2)}, u32[]{:S(2)}) collective-permute-start(f32[24,256]{1,0:T(8,128)S(1)} %get-tuple-element.111), channel_id=1, source_target_pairs={{0,1},{1,0},{2,3},{3,2},{4,5},{5,4},{6,7},{7,6},{8,9},{9,8},{10,11... | collective-permute-start | bytes 73736 | tf_op jit(solution)/shard_map/ppermute | solution.py:19
  58.9 2.4 %collective-permute-done.13 = f32[24,256]{1,0:T(8,128)S(1)} collective-permute-done((f32[24,256]{1,0:T(8,128)S(1)}, f32[24,256]{1,0:T(8,128)S(1)}, u32[]{:S(2)}, u32[]{:S(2)}) %collective-permute-start.13) | collective-permute-done | bytes 24608 | tf_op jit(solution)/shard_map/ppermute | solution.py:19
  61.3 2.6 %collective-permute-start.14 = (f32[48,256]{1,0:T(8,128)S(1)}, f32[48,256]{1,0:T(8,128)S(1)}, u32[]{:S(2)}, u32[]{:S(2)}) collective-permute-start(f32[48,256]{1,0:T(8,128)S(1)} %pad_add_fusion.5), channel_id=1, source_target_pairs={{0,4},{1,5},{2,6},{3,7},{4,0},{5,1},{6,2},{7,3},{8,12},{9,13},{10,... | collective-permute-start | bytes 147464 | tf_op jit(solution)/shard_map/ppermute | solution.py:19
  63.9 2.4 %collective-permute-done.14 = f32[48,256]{1,0:T(8,128)S(1)} collective-permute-done((f32[48,256]{1,0:T(8,128)S(1)}, f32[48,256]{1,0:T(8,128)S(1)}, u32[]{:S(2)}, u32[]{:S(2)}) %collective-permute-start.14) | collective-permute-done | bytes 49184 | tf_op jit(solution)/shard_map/ppermute | solution.py:19
  66.3 2.0 %collective-permute-start.15 = (f32[96,256]{1,0:T(8,128)S(1)}, f32[96,256]{1,0:T(8,128)S(1)}, u32[]{:S(2)}, u32[]{:S(2)}) collective-permute-start(f32[96,256]{1,0:T(8,128)S(1)} %pad_add_fusion.2.refs_0_), channel_id=1, source_target_pairs={{0,2},{1,3},{2,0},{3,1},{4,6},{5,7},{6,4},{7,5},{8,10},{9,11},{10,... | collective-permute-start | bytes 294920 | tf_op jit(solution)/shard_map/ppermute | solution.py:19
  68.4 1.1 collective-permute-start.20
  70.1 1.2 collective-permute-done.15.refs_1_
  72.2 0.9 collective-permute-start.17
  73.6 3.0 %collective-permute-start.18 = (f32[136,256]{1,0:T(8,128)S(1)}, f32[136,256]{1,0:T(8,128)S(1)}, u32[]{:S(2)}, u32[]{:S(2)}) collective-permute-start(f32[136,256]{1,0:T(8,128)S(1)} %shard_map.94), channel_id=1, source_target_pairs={{0,8},{8,0},{16,24},{24,16},{1,9},{9,1},{17,25},{25,17},{2,10},{10... | collective-permute-start | bytes 417800 | tf_op jit(solution)/shard_map/ppermute | solution.py:19
  76.6 1.0 collective-permute-done.18
  78.0 3.5 %shard_map.96.refs_10_.refs_11_.refs_18_ = f32[1536,128]{1,0:T(8,128)S(1)} custom-call(f32[6]{0:T(128)S(1)} %pad_maximum_fusion.refs_0_.flags, f32[416,256]{1,0:T(8,128)S(1)} %collective-permute-done.refs_4_.near0, f32[416,256]{1,0:T(8,128)S(1)} %collective-permute-done.1.refs_5_.near1, f32[424,256]{1,0:T(8,128)S(1)} %collective-permute-done.2.refs_4_.near2, ...), custom_call_target="tpu_custom_call" | custom-call | flops 1024 | bytes 1024 | tf_op jit(solution)/shard_map/pallas_call | solution.py:342
  81.5 2.9 %collective-permute-done.19 = f32[136,256]{1,0:T(8,128)S(1)} collective-permute-done((f32[136,256]{1,0:T(8,128)S(1)}, f32[136,256]{1,0:T(8,128)S(1)}, u32[]{:S(2)}, u32[]{:S(2)}) %collective-permute-start.19) | collective-permute-done | bytes 139296 | tf_op jit(solution)/shard_map/ppermute | solution.py:19
  85.0 3.7 %shard_map.97 = (f32[384,256]{1,0:T(8,128)S(1)}, f32[384,256]{1,0:T(8,128)S(1)}, f32[384,256]{1,0:T(8,128)S(1)}, f32[384,256]{1,0:T(8,128)S(1)}, f32[1536,256]{1,0:T(8,128)S(1)}) custom-call(f32[6]{0:T(128)S(1)} %pad_maximum_fusion.refs_0_.flags, f32[1536,1536]{1,0:T(8,128)S(1)} %bitcast.19, f32[384,256]{1,0:T(8,128)S(1)} %get-tuple-element.116.refs_2_.refs_8_, ...), custom_call_target="tpu_custom_call" | custom-call | flops 1024 | bytes 1024 | tf_op jit(solution)/shard_map/pallas_call | solution.py:342
  88.8 3.2 %shard_map.98 = (f32[384,256]{1,0:T(8,128)S(1)}, f32[384,256]{1,0:T(8,128)S(1)}, f32[384,256]{1,0:T(8,128)S(1)}, f32[384,256]{1,0:T(8,128)S(1)}, f32[392,256]{1,0:T(8,128)S(1)}, /*index=5*/f32[392,256]{1,0:T(8,128)S(1)}) custom-call(f32[6]{0:T(128)S(1)} %pad_maximum_fusion.refs_0_.flags, f32[1536,1536]{1,0:T(8,128)S(1)} %bitcast.20, ...), custom_call_target="tpu_custom_call" | custom-call | flops 8000000000 | bytes 1024 | tf_op jit(solution)/shard_map/pallas_call | solution.py:342
  92.0 2.5 %collective-permute-start.24 = (f32[392,256]{1,0:T(8,128)S(1)}, f32[392,256]{1,0:T(8,128)S(1)}, u32[]{:S(2)}, u32[]{:S(2)}) collective-permute-start(f32[392,256]{1,0:T(8,128)S(1)} %get-tuple-element.128.refs_6_.refs_2_), channel_id=1, source_target_pairs={{0,1},{1,0},{2,3},{3,2},{4,5},{5,4},{6,7},{7,6},{8,9},{9,8},{10,11... | collective-permute-start | bytes 1204232 | tf_op jit(solution)/shard_map/ppermute | solution.py:19
  95.2 2.0 %shard_map.99 = (f32[384,256]{1,0:T(8,128)S(1)}, f32[384,256]{1,0:T(8,128)S(1)}, f32[1,256]{1,0:T(1,128)S(1)}) custom-call(f32[6]{0:T(128)S(1)} %pad_maximum_fusion.refs_0_.flags, f32[1536,1536]{1,0:T(8,128)S(1)} %bitcast.21, f32[384,256]{1,0:T(8,128)S(1)} %get-tuple-element.121.refs_2_.refs_9_, f32[384,256]{1,0:T(8,128)S(1)} %get-tuple-element.122.refs_3_.refs_10_, ...), custom_call_target="tpu_custom_call" | custom-call | flops 1024 | bytes 1024 | tf_op jit(solution)/shard_map/pallas_call | solution.py:342
  97.2 0.9 collective-permute-start.23
  99.0 3.4 %shard_map.100 = (f32[384,256]{1,0:T(8,128)S(1)}, f32[384,256]{1,0:T(8,128)S(1)}, f32[1536,256]{1,0:T(8,128)S(1)}) custom-call(f32[6]{0:T(128)S(1)} %pad_maximum_fusion.refs_0_.flags, f32[1536,1536]{1,0:T(8,128)S(1)} %bitcast.27, f32[384,256]{1,0:T(8,128)S(1)} %get-tuple-element.130.refs_2_, f32[384,256]{1,0:T(8,128)S(1)} %get-tuple-element.131.refs_3_, ...), custom_call_target="tpu_custom_call" | custom-call | flops 1024 | bytes 1024 | tf_op jit(solution)/shard_map/pallas_call | solution.py:342
  102.4 8.9 %collective-permute-done.24.refs_4_ = f32[392,256]{1,0:T(8,128)S(1)} collective-permute-done((f32[392,256]{1,0:T(8,128)S(1)}, f32[392,256]{1,0:T(8,128)S(1)}, u32[]{:S(2)}, u32[]{:S(2)}) %collective-permute-start.24) | collective-permute-done | bytes 401440 | tf_op jit(solution)/shard_map/ppermute | solution.py:19
  111.3 2.7 %shard_map.101 = (f32[384,256]{1,0:T(8,128)S(1)}, f32[384,256]{1,0:T(8,128)S(1)}, f32[392,256]{1,0:T(8,128)S(1)}, f32[392,256]{1,0:T(8,128)S(1)}) custom-call(f32[6]{0:T(128)S(1)} %pad_maximum_fusion.refs_0_.flags, f32[1536,1536]{1,0:T(8,128)S(1)} %bitcast.28, f32[392,256]{1,0:T(8,128)S(1)} %get-tuple-element.128.refs_6_.refs_2_, ...), custom_call_target="tpu_custom_call" | custom-call | flops 8000000000 | bytes 1024 | tf_op jit(solution)/shard_map/pallas_call | solution.py:342
  114.0 2.5 %shard_map.102 = (f32[384,256]{1,0:T(8,128)S(1)}, f32[384,256]{1,0:T(8,128)S(1)}, f32[24,256]{1,0:T(8,128)S(1)}) custom-call(f32[6]{0:T(128)S(1)} %pad_maximum_fusion.refs_0_.flags, f32[1536,1536]{1,0:T(8,128)S(1)} %bitcast.29, f32[384,256]{1,0:T(8,128)S(1)} %get-tuple-element.132.refs_2_.refs_4_, f32[384,256]{1,0:T(8,128)S(1)} %get-tuple-element.133.refs_3_.refs_5_, ...), custom_call_target="tpu_custom_call" | custom-call | flops 1024 | bytes 1024 | tf_op jit(solution)/shard_map/pallas_call | solution.py:342
  116.5 2.5 %collective-permute-start.26 = (f32[24,256]{1,0:T(8,128)S(1)}, f32[24,256]{1,0:T(8,128)S(1)}, u32[]{:S(2)}, u32[]{:S(2)}) collective-permute-start(f32[24,256]{1,0:T(8,128)S(1)} %get-tuple-element.140), channel_id=1, source_target_pairs={{0,1},{1,0},{2,3},{3,2},{4,5},{5,4},{6,7},{7,6},{8,9},{9,8},{10,11... | collective-permute-start | bytes 73736 | tf_op jit(solution)/shard_map/ppermute | solution.py:19
  119.0 1.8 %collective-permute-done.26 = f32[24,256]{1,0:T(8,128)S(1)} collective-permute-done((f32[24,256]{1,0:T(8,128)S(1)}, f32[24,256]{1,0:T(8,128)S(1)}, u32[]{:S(2)}, u32[]{:S(2)}) %collective-permute-start.26) | collective-permute-done | bytes 24608 | tf_op jit(solution)/shard_map/ppermute | solution.py:19
  120.9 2.9 %collective-permute-start.27 = (f32[48,256]{1,0:T(8,128)S(1)}, f32[48,256]{1,0:T(8,128)S(1)}, u32[]{:S(2)}, u32[]{:S(2)}) collective-permute-start(f32[48,256]{1,0:T(8,128)S(1)} %pad_add_fusion.4), channel_id=1, source_target_pairs={{0,4},{1,5},{2,6},{3,7},{4,0},{5,1},{6,2},{7,3},{8,12},{9,13},{10,... | collective-permute-start | bytes 147464 | tf_op jit(solution)/shard_map/ppermute | solution.py:19
  123.8 2.8 %collective-permute-done.27 = f32[48,256]{1,0:T(8,128)S(1)} collective-permute-done((f32[48,256]{1,0:T(8,128)S(1)}, f32[48,256]{1,0:T(8,128)S(1)}, u32[]{:S(2)}, u32[]{:S(2)}) %collective-permute-start.27) | collective-permute-done | bytes 49184 | tf_op jit(solution)/shard_map/ppermute | solution.py:19
  126.6 2.5 %collective-permute-start.28 = (f32[96,256]{1,0:T(8,128)S(1)}, f32[96,256]{1,0:T(8,128)S(1)}, u32[]{:S(2)}, u32[]{:S(2)}) collective-permute-start(f32[96,256]{1,0:T(8,128)S(1)} %pad_add_fusion.1.refs_0_), channel_id=1, source_target_pairs={{0,2},{1,3},{2,0},{3,1},{4,6},{5,7},{6,4},{7,5},{8,10},{9,11},{10,... | collective-permute-start | bytes 294920 | tf_op jit(solution)/shard_map/ppermute | solution.py:19
  129.1 1.7 %collective-permute-start.33 = (f32[392,256]{1,0:T(8,128)S(1)}, f32[392,256]{1,0:T(8,128)S(1)}, u32[]{:S(2)}, u32[]{:S(2)}) collective-permute-start(f32[392,256]{1,0:T(8,128)S(1)} %get-tuple-element.150.refs_6_.refs_3_), channel_id=1, source_target_pairs={{0,1},{1,0},{2,3},{3,2},{4,5},{5,4},{6,7},{7,6},{8,9},{9,8},{10,11... | collective-permute-start | bytes 1204232 | tf_op jit(solution)/shard_map/ppermute | solution.py:19
  132.9 3.0 %collective-permute-start.29 = (f32[136,256]{1,0:T(8,128)S(1)}, f32[136,256]{1,0:T(8,128)S(1)}, u32[]{:S(2)}, u32[]{:S(2)}) collective-permute-start(f32[136,256]{1,0:T(8,128)S(1)} %shard_map.103), channel_id=1, source_target_pairs={{0,8},{8,0},{16,24},{24,16},{1,9},{9,1},{17,25},{25,17},{2,10},{10... | collective-permute-start | bytes 417800 | tf_op jit(solution)/shard_map/ppermute | solution.py:19
  136.0 1.0 collective-permute-done.29
  137.8 6.6 %collective-permute-done.30 = f32[136,256]{1,0:T(8,128)S(1)} collective-permute-done((f32[136,256]{1,0:T(8,128)S(1)}, f32[136,256]{1,0:T(8,128)S(1)}, u32[]{:S(2)}, u32[]{:S(2)}) %collective-permute-start.30) | collective-permute-done | bytes 139296 | tf_op jit(solution)/shard_map/ppermute | solution.py:19
  145.0 1.2 shard_map.105
  146.5 3.7 %shard_map.106 = f32[1536,256]{1,0:T(8,128)} custom-call(f32[6]{0:T(128)S(1)} %pad_maximum_fusion.refs_0_.flags, f32[384,256]{1,0:T(8,128)S(1)} %get-tuple-element.148.refs_1_, f32[384,256]{1,0:T(8,128)S(1)} %get-tuple-element.149.refs_2_, f32[392,256]{1,0:T(8,128)S(1)} %get-tuple-element.150.refs_6_.refs_3_, ...), custom_call_target="tpu_custom_call" | custom-call | flops 1024 | bytes 1024 | tf_op jit(solution)/shard_map/pallas_call | solution.py:342
  (96 shorter events, 13.1 us)
Async XLA Ops:
  0.6 4.7 %copy-start.3 = (s32[1,1,16]{2,1,0:T(1,128)S(1)}, s32[1,1,16]{2,1,0:T(1,128)}, u32[]{:S(2)}) copy-start(s32[1,1,16]{2,1,0:T(1,128)} %param.11) | copy-start | bytes 196
  0.6 4.7 %copy-start.6 = (f32[4,128]{1,0:T(4,128)S(1)}, f32[4,128]{1,0:T(4,128)}, u32[]{:S(2)}) copy-start(f32[4,128]{1,0:T(4,128)} %inverse) | copy-start | bytes 6148
  5.3 23.1 %slice-start = ((s8[9437184]{0:T(1024)(128)(4,1)}), s8[4194304]{0:T(1024)(128)(4,1)S(1)}, s32[]{:S(2)}) async-start(s8[9437184]{0:T(1024)(128)(4,1)} %bitcast.14), calls=%async_computation | async-start | bytes 8388608
  5.4 3.6 %copy-start.4 = (f32[424,256]{1,0:T(8,128)S(1)}, f32[424,256]{1,0:T(8,128)}, u32[]{:S(2)}) copy-start(f32[424,256]{1,0:T(8,128)} %get-tuple-element.88.refs_2_) | copy-start | bytes 1302532
  5.4 4.1 %copy-start.5 = (f32[424,256]{1,0:T(8,128)S(1)}, f32[424,256]{1,0:T(8,128)}, u32[]{:S(2)}) copy-start(f32[424,256]{1,0:T(8,128)} %get-tuple-element.89.refs_3_) | copy-start | bytes 1302532
  5.4 5.3 %copy-start.2 = (f32[416,256]{1,0:T(8,128)S(1)}, f32[416,256]{1,0:T(8,128)}, u32[]{:S(2)}) copy-start(f32[416,256]{1,0:T(8,128)} %get-tuple-element.83.refs_3_) | copy-start | bytes 1277956
  5.4 6.0 %copy-start = (f32[416,256]{1,0:T(8,128)S(1)}, f32[416,256]{1,0:T(8,128)}, u32[]{:S(2)}) copy-start(f32[416,256]{1,0:T(8,128)} %get-tuple-element.81.refs_2_.sent) | copy-start | bytes 1277956
  5.4 23.0 %slice-start.1 = ((s8[9437184]{0:T(1024)(128)(4,1)}), s8[4194304]{0:T(1024)(128)(4,1)S(1)}, s32[]{:S(2)}) async-start(s8[9437184]{0:T(1024)(128)(4,1)} %bitcast.14), calls=%async_computation.1 | async-start | bytes 8388608
  5.4 23.0 %slice-start.2 = ((s8[9437184]{0:T(1024)(128)(4,1)}), s8[1048576]{0:T(1024)(128)(4,1)S(1)}, s32[]{:S(2)}) async-start(s8[9437184]{0:T(1024)(128)(4,1)} %bitcast.14), calls=%async_computation.2 | async-start | bytes 2097152
  6.0 4.6 %collective-permute-start.4 = (f32[12,128]{1,0:T(8,128)S(1)}, f32[12,128]{1,0:T(8,128)S(1)}, u32[]{:S(2)}, u32[]{:S(2)}) collective-permute-start(f32[12,128]{1,0:T(8,128)S(1)} %shard_map.88), channel_id=1, source_target_pairs={{0,1},{1,0},{2,3},{3,2},{4,5},{5,4},{6,7},{7,6},{8,9},{9,8},{10,11... | collective-permute-start | bytes 18440 | tf_op jit(solution)/shard_map/ppermute | solution.py:19
  9.0 22.9 %collective-permute-start.2 = (f32[424,256]{1,0:T(8,128)S(1)}, f32[424,256]{1,0:T(8,128)S(1)}, u32[]{:S(2)}, u32[]{:S(2)}) collective-permute-start(f32[424,256]{1,0:T(8,128)S(1)} %copy-done.4), channel_id=1, source_target_pairs={{0,1},{1,0},{2,3},{3,2},{4,5},{5,4},{6,7},{7,6},{8,9},{9,8},{10,11... | collective-permute-start | bytes 1302536 | tf_op jit(solution)/shard_map/ppermute | solution.py:19
  9.5 22.4 %collective-permute-start.3 = (f32[424,256]{1,0:T(8,128)S(1)}, f32[424,256]{1,0:T(8,128)S(1)}, u32[]{:S(2)}, u32[]{:S(2)}) collective-permute-start(f32[424,256]{1,0:T(8,128)S(1)} %copy-done.5), channel_id=1, source_target_pairs={{1,2},{2,1},{3,4},{4,3},{5,6},{6,5},{9,10},{10,9},{11,12},{12,11},... | collective-permute-start | bytes 1302536 | tf_op jit(solution)/shard_map/ppermute | solution.py:26
  10.6 4.2 %collective-permute-start.5 = (f32[24,128]{1,0:T(8,128)S(1)}, f32[24,128]{1,0:T(8,128)S(1)}, u32[]{:S(2)}, u32[]{:S(2)}) collective-permute-start(f32[24,128]{1,0:T(8,128)S(1)} %pad_add_fusion.8), channel_id=1, source_target_pairs={{0,8},{8,0},{16,24},{24,16},{1,9},{9,1},{17,25},{25,17},{2,10},{10... | collective-permute-start | bytes 36872 | tf_op jit(solution)/shard_map/ppermute | solution.py:19
  10.7 17.7 %collective-permute-start.1 = (f32[416,256]{1,0:T(8,128)S(1)}, f32[416,256]{1,0:T(8,128)S(1)}, u32[]{:S(2)}, u32[]{:S(2)}) collective-permute-start(f32[416,256]{1,0:T(8,128)S(1)} %copy-done.2), channel_id=1, source_target_pairs={{8,16},{16,8},{9,17},{17,9},{10,18},{18,10},{11,19},{19,11},{12,20... | collective-permute-start | bytes 1277960 | tf_op jit(solution)/shard_map/ppermute | solution.py:26
  11.4 17.0 %collective-permute-start = (f32[416,256]{1,0:T(8,128)S(1)}, f32[416,256]{1,0:T(8,128)S(1)}, u32[]{:S(2)}, u32[]{:S(2)}) collective-permute-start(f32[416,256]{1,0:T(8,128)S(1)} %copy-done), channel_id=1, source_target_pairs={{0,8},{8,0},{16,24},{24,16},{1,9},{9,1},{17,25},{25,17},{2,10},{10... | collective-permute-start | bytes 1277960 | tf_op jit(solution)/shard_map/ppermute | solution.py:19
  14.8 6.5 %collective-permute-start.6 = (f32[48,128]{1,0:T(8,128)S(1)}, f32[48,128]{1,0:T(8,128)S(1)}, u32[]{:S(2)}, u32[]{:S(2)}) collective-permute-start(f32[48,128]{1,0:T(8,128)S(1)} %pad_add_fusion.7), channel_id=1, source_target_pairs={{0,16},{8,24},{16,0},{24,8},{1,17},{9,25},{17,1},{25,9},{2,18},{10... | collective-permute-start | bytes 73736 | tf_op jit(solution)/shard_map/ppermute | solution.py:19
  21.3 7.1 %collective-permute-start.7 = (f32[96,128]{1,0:T(8,128)S(1)}, f32[96,128]{1,0:T(8,128)S(1)}, u32[]{:S(2)}, u32[]{:S(2)}) collective-permute-start(f32[96,128]{1,0:T(8,128)S(1)} %pad_add_fusion.6), channel_id=1, source_target_pairs={{0,4},{1,5},{2,6},{3,7},{4,0},{5,1},{6,2},{7,3},{8,12},{9,13},{10,... | collective-permute-start | bytes 147464 | tf_op jit(solution)/shard_map/ppermute | solution.py:19
  31.9 17.0 %slice-start.3 = ((s8[9437184]{0:T(1024)(128)(4,1)}), s8[4194304]{0:T(1024)(128)(4,1)S(1)}, s32[]{:S(2)}) async-start(s8[9437184]{0:T(1024)(128)(4,1)} %bitcast.22), calls=%async_computation.3 | async-start | bytes 8388608
  31.9 17.0 %slice-start.4 = ((s8[9437184]{0:T(1024)(128)(4,1)}), s8[4194304]{0:T(1024)(128)(4,1)S(1)}, s32[]{:S(2)}) async-start(s8[9437184]{0:T(1024)(128)(4,1)} %bitcast.22), calls=%async_computation.4 | async-start | bytes 8388608
  31.9 17.0 %slice-start.5 = ((s8[9437184]{0:T(1024)(128)(4,1)}), s8[1048576]{0:T(1024)(128)(4,1)S(1)}, s32[]{:S(2)}) async-start(s8[9437184]{0:T(1024)(128)(4,1)} %bitcast.22), calls=%async_computation.5 | async-start | bytes 2097152
  34.6 17.7 %collective-permute-start.11 = (f32[392,256]{1,0:T(8,128)S(1)}, f32[392,256]{1,0:T(8,128)S(1)}, u32[]{:S(2)}, u32[]{:S(2)}) collective-permute-start(f32[392,256]{1,0:T(8,128)S(1)} %get-tuple-element.95.refs_6_.refs_2_), channel_id=1, source_target_pairs={{0,1},{1,0},{2,3},{3,2},{4,5},{5,4},{6,7},{7,6},{8,9},{9,8},{10,11... | collective-permute-start | bytes 1204232 | tf_op jit(solution)/shard_map/ppermute | solution.py:19
  36.7 15.7 %collective-permute-start.12 = (f32[392,256]{1,0:T(8,128)S(1)}, f32[392,256]{1,0:T(8,128)S(1)}, u32[]{:S(2)}, u32[]{:S(2)}) collective-permute-start(f32[392,256]{1,0:T(8,128)S(1)} %get-tuple-element.96.refs_7_.refs_3_), channel_id=1, source_target_pairs={{1,2},{2,1},{3,4},{4,3},{5,6},{6,5},{9,10},{10,9},{11,12},{12,11},... | collective-permute-start | bytes 1204232 | tf_op jit(solution)/shard_map/ppermute | solution.py:26
  39.4 9.5 %collective-permute-start.8 = (f32[384,256]{1,0:T(8,128)S(1)}, f32[384,256]{1,0:T(8,128)S(1)}, u32[]{:S(2)}, u32[]{:S(2)}) collective-permute-start(f32[384,256]{1,0:T(8,128)S(1)} %get-tuple-element.97.refs_2_), channel_id=1, source_target_pairs={{0,8},{8,0},{16,24},{24,16},{1,9},{9,1},{17,25},{25,17},{2,10},{10... | collective-permute-start | bytes 1179656 | tf_op jit(solution)/shard_map/ppermute | solution.py:19
  39.4 9.4 %collective-permute-start.9 = (f32[384,256]{1,0:T(8,128)S(1)}, f32[384,256]{1,0:T(8,128)S(1)}, u32[]{:S(2)}, u32[]{:S(2)}) collective-permute-start(f32[384,256]{1,0:T(8,128)S(1)} %get-tuple-element.98.refs_3_), channel_id=1, source_target_pairs={{8,16},{16,8},{9,17},{17,9},{10,18},{18,10},{11,19},{19,11},{12,20... | collective-permute-start | bytes 1179656 | tf_op jit(solution)/shard_map/ppermute | solution.py:26
  40.3 8.5 %collective-permute-start.10 = (f32[192,128]{1,0:T(8,128)S(1)}, f32[192,128]{1,0:T(8,128)S(1)}, u32[]{:S(2)}, u32[]{:S(2)}) collective-permute-start(f32[192,128]{1,0:T(8,128)S(1)} %pad_add_fusion.3), channel_id=1, source_target_pairs={{0,2},{1,3},{2,0},{3,1},{4,6},{5,7},{6,4},{7,5},{8,10},{9,11},{10,... | collective-permute-start | bytes 294920 | tf_op jit(solution)/shard_map/ppermute | solution.py:19
  52.4 2.7 %copy-start.1 = (f32[1,1,16,1536]{3,2,1,0:T(8,128)S(1)}, f32[1,1,16,1536]{3,2,1,0:T(8,128)}, u32[]{:S(2)}) copy-start(f32[1,1,16,1536]{3,2,1,0:T(8,128)} %param.10) | copy-start | bytes 294916
  57.4 3.9 %collective-permute-start.13 = (f32[24,256]{1,0:T(8,128)S(1)}, f32[24,256]{1,0:T(8,128)S(1)}, u32[]{:S(2)}, u32[]{:S(2)}) collective-permute-start(f32[24,256]{1,0:T(8,128)S(1)} %get-tuple-element.111), channel_id=1, source_target_pairs={{0,1},{1,0},{2,3},{3,2},{4,5},{5,4},{6,7},{7,6},{8,9},{9,8},{10,11... | collective-permute-start | bytes 73736 | tf_op jit(solution)/shard_map/ppermute | solution.py:19
  61.3 5.0 %collective-permute-start.14 = (f32[48,256]{1,0:T(8,128)S(1)}, f32[48,256]{1,0:T(8,128)S(1)}, u32[]{:S(2)}, u32[]{:S(2)}) collective-permute-start(f32[48,256]{1,0:T(8,128)S(1)} %pad_add_fusion.5), channel_id=1, source_target_pairs={{0,4},{1,5},{2,6},{3,7},{4,0},{5,1},{6,2},{7,3},{8,12},{9,13},{10,... | collective-permute-start | bytes 147464 | tf_op jit(solution)/shard_map/ppermute | solution.py:19
  66.3 5.1 %collective-permute-start.15 = (f32[96,256]{1,0:T(8,128)S(1)}, f32[96,256]{1,0:T(8,128)S(1)}, u32[]{:S(2)}, u32[]{:S(2)}) collective-permute-start(f32[96,256]{1,0:T(8,128)S(1)} %pad_add_fusion.2.refs_0_), channel_id=1, source_target_pairs={{0,2},{1,3},{2,0},{3,1},{4,6},{5,7},{6,4},{7,5},{8,10},{9,11},{10,... | collective-permute-start | bytes 294920 | tf_op jit(solution)/shard_map/ppermute | solution.py:19
  68.4 20.4 %collective-permute-start.20 = (f32[392,256]{1,0:T(8,128)S(1)}, f32[392,256]{1,0:T(8,128)S(1)}, u32[]{:S(2)}, u32[]{:S(2)}) collective-permute-start(f32[392,256]{1,0:T(8,128)S(1)} %get-tuple-element.123.refs_6_.refs_2_.refs_10_), channel_id=1, source_target_pairs={{0,1},{1,0},{2,3},{3,2},{4,5},{5,4},{6,7},{7,6},{8,9},{9,8},{10,11... | collective-permute-start | bytes 1204232 | tf_op jit(solution)/shard_map/ppermute | solution.py:19
  69.5 19.3 %collective-permute-start.21 = (f32[392,256]{1,0:T(8,128)S(1)}, f32[392,256]{1,0:T(8,128)S(1)}, u32[]{:S(2)}, u32[]{:S(2)}) collective-permute-start(f32[392,256]{1,0:T(8,128)S(1)} %get-tuple-element.124.refs_7_.refs_3_.refs_11_), channel_id=1, source_target_pairs={{1,2},{2,1},{3,4},{4,3},{5,6},{6,5},{9,10},{10,9},{11,12},{12,11},... | collective-permute-start | bytes 1204232 | tf_op jit(solution)/shard_map/ppermute | solution.py:26
  71.4 13.6 %collective-permute-start.16 = (f32[384,256]{1,0:T(8,128)S(1)}, f32[384,256]{1,0:T(8,128)S(1)}, u32[]{:S(2)}, u32[]{:S(2)}) collective-permute-start(f32[384,256]{1,0:T(8,128)S(1)} %get-tuple-element.116.refs_2_.refs_8_), channel_id=1, source_target_pairs={{0,8},{8,0},{16,24},{24,16},{1,9},{9,1},{17,25},{25,17},{2,10},{10... | collective-permute-start | bytes 1179656 | tf_op jit(solution)/shard_map/ppermute | solution.py:19
  72.2 12.9 %collective-permute-start.17 = (f32[384,256]{1,0:T(8,128)S(1)}, f32[384,256]{1,0:T(8,128)S(1)}, u32[]{:S(2)}, u32[]{:S(2)}) collective-permute-start(f32[384,256]{1,0:T(8,128)S(1)} %get-tuple-element.117.refs_3_.refs_9_), channel_id=1, source_target_pairs={{8,16},{16,8},{9,17},{17,9},{10,18},{18,10},{11,19},{19,11},{12,20... | collective-permute-start | bytes 1179656 | tf_op jit(solution)/shard_map/ppermute | solution.py:26
  73.6 4.0 %collective-permute-start.18 = (f32[136,256]{1,0:T(8,128)S(1)}, f32[136,256]{1,0:T(8,128)S(1)}, u32[]{:S(2)}, u32[]{:S(2)}) collective-permute-start(f32[136,256]{1,0:T(8,128)S(1)} %shard_map.94), channel_id=1, source_target_pairs={{0,8},{8,0},{16,24},{24,16},{1,9},{9,1},{17,25},{25,17},{2,10},{10... | collective-permute-start | bytes 417800 | tf_op jit(solution)/shard_map/ppermute | solution.py:19
  77.6 6.8 %collective-permute-start.19 = (f32[136,256]{1,0:T(8,128)S(1)}, f32[136,256]{1,0:T(8,128)S(1)}, u32[]{:S(2)}, u32[]{:S(2)}) collective-permute-start(f32[136,256]{1,0:T(8,128)S(1)} %add.149), channel_id=1, source_target_pairs={{0,16},{8,24},{16,0},{24,8},{1,17},{9,25},{17,1},{25,9},{2,18},{10... | collective-permute-start | bytes 417800 | tf_op jit(solution)/shard_map/ppermute | solution.py:19
  92.0 19.2 %collective-permute-start.24 = (f32[392,256]{1,0:T(8,128)S(1)}, f32[392,256]{1,0:T(8,128)S(1)}, u32[]{:S(2)}, u32[]{:S(2)}) collective-permute-start(f32[392,256]{1,0:T(8,128)S(1)} %get-tuple-element.128.refs_6_.refs_2_), channel_id=1, source_target_pairs={{0,1},{1,0},{2,3},{3,2},{4,5},{5,4},{6,7},{7,6},{8,9},{9,8},{10,11... | collective-permute-start | bytes 1204232 | tf_op jit(solution)/shard_map/ppermute | solution.py:19
  94.5 16.8 %collective-permute-start.25 = (f32[392,256]{1,0:T(8,128)S(1)}, f32[392,256]{1,0:T(8,128)S(1)}, u32[]{:S(2)}, u32[]{:S(2)}) collective-permute-start(f32[392,256]{1,0:T(8,128)S(1)} %get-tuple-element.129.refs_7_.refs_3_), channel_id=1, source_target_pairs={{1,2},{2,1},{3,4},{4,3},{5,6},{6,5},{9,10},{10,9},{11,12},{12,11},... | collective-permute-start | bytes 1204232 | tf_op jit(solution)/shard_map/ppermute | solution.py:26
  97.2 1.8 %collective-permute-start.22 = (f32[384,256]{1,0:T(8,128)S(1)}, f32[384,256]{1,0:T(8,128)S(1)}, u32[]{:S(2)}, u32[]{:S(2)}) collective-permute-start(f32[384,256]{1,0:T(8,128)S(1)} %get-tuple-element.130.refs_2_), channel_id=1, source_target_pairs={{0,8},{8,0},{16,24},{24,16},{1,9},{9,1},{17,25},{25,17},{2,10},{10... | collective-permute-start | bytes 1179656 | tf_op jit(solution)/shard_map/ppermute | solution.py:19
  97.2 1.7 %collective-permute-start.23 = (f32[384,256]{1,0:T(8,128)S(1)}, f32[384,256]{1,0:T(8,128)S(1)}, u32[]{:S(2)}, u32[]{:S(2)}) collective-permute-start(f32[384,256]{1,0:T(8,128)S(1)} %get-tuple-element.131.refs_3_), channel_id=1, source_target_pairs={{8,16},{16,8},{9,17},{17,9},{10,18},{18,10},{11,19},{19,11},{12,20... | collective-permute-start | bytes 1179656 | tf_op jit(solution)/shard_map/ppermute | solution.py:26
  116.5 4.4 %collective-permute-start.26 = (f32[24,256]{1,0:T(8,128)S(1)}, f32[24,256]{1,0:T(8,128)S(1)}, u32[]{:S(2)}, u32[]{:S(2)}) collective-permute-start(f32[24,256]{1,0:T(8,128)S(1)} %get-tuple-element.140), channel_id=1, source_target_pairs={{0,1},{1,0},{2,3},{3,2},{4,5},{5,4},{6,7},{7,6},{8,9},{9,8},{10,11... | collective-permute-start | bytes 73736 | tf_op jit(solution)/shard_map/ppermute | solution.py:19
  120.9 5.7 %collective-permute-start.27 = (f32[48,256]{1,0:T(8,128)S(1)}, f32[48,256]{1,0:T(8,128)S(1)}, u32[]{:S(2)}, u32[]{:S(2)}) collective-permute-start(f32[48,256]{1,0:T(8,128)S(1)} %pad_add_fusion.4), channel_id=1, source_target_pairs={{0,4},{1,5},{2,6},{3,7},{4,0},{5,1},{6,2},{7,3},{8,12},{9,13},{10,... | collective-permute-start | bytes 147464 | tf_op jit(solution)/shard_map/ppermute | solution.py:19
  126.6 5.1 %collective-permute-start.28 = (f32[96,256]{1,0:T(8,128)S(1)}, f32[96,256]{1,0:T(8,128)S(1)}, u32[]{:S(2)}, u32[]{:S(2)}) collective-permute-start(f32[96,256]{1,0:T(8,128)S(1)} %pad_add_fusion.1.refs_0_), channel_id=1, source_target_pairs={{0,2},{1,3},{2,0},{3,1},{4,6},{5,7},{6,4},{7,5},{8,10},{9,11},{10,... | collective-permute-start | bytes 294920 | tf_op jit(solution)/shard_map/ppermute | solution.py:19
  129.1 17.4 %collective-permute-start.33 = (f32[392,256]{1,0:T(8,128)S(1)}, f32[392,256]{1,0:T(8,128)S(1)}, u32[]{:S(2)}, u32[]{:S(2)}) collective-permute-start(f32[392,256]{1,0:T(8,128)S(1)} %get-tuple-element.150.refs_6_.refs_3_), channel_id=1, source_target_pairs={{0,1},{1,0},{2,3},{3,2},{4,5},{5,4},{6,7},{7,6},{8,9},{9,8},{10,11... | collective-permute-start | bytes 1204232 | tf_op jit(solution)/shard_map/ppermute | solution.py:19
  130.8 15.6 %collective-permute-start.34 = (f32[392,256]{1,0:T(8,128)S(1)}, f32[392,256]{1,0:T(8,128)S(1)}, u32[]{:S(2)}, u32[]{:S(2)}) collective-permute-start(f32[392,256]{1,0:T(8,128)S(1)} %get-tuple-element.151.refs_7_.refs_4_), channel_id=1, source_target_pairs={{1,2},{2,1},{3,4},{4,3},{5,6},{6,5},{9,10},{10,9},{11,12},{12,11},... | collective-permute-start | bytes 1204232 | tf_op jit(solution)/shard_map/ppermute | solution.py:26
  131.7 14.8 %collective-permute-start.31 = (f32[384,256]{1,0:T(8,128)S(1)}, f32[384,256]{1,0:T(8,128)S(1)}, u32[]{:S(2)}, u32[]{:S(2)}) collective-permute-start(f32[384,256]{1,0:T(8,128)S(1)} %get-tuple-element.148.refs_1_), channel_id=1, source_target_pairs={{0,8},{8,0},{16,24},{24,16},{1,9},{9,1},{17,25},{25,17},{2,10},{10... | collective-permute-start | bytes 1179656 | tf_op jit(solution)/shard_map/ppermute | solution.py:19
  131.7 14.8 %collective-permute-start.32 = (f32[384,256]{1,0:T(8,128)S(1)}, f32[384,256]{1,0:T(8,128)S(1)}, u32[]{:S(2)}, u32[]{:S(2)}) collective-permute-start(f32[384,256]{1,0:T(8,128)S(1)} %get-tuple-element.149.refs_2_), channel_id=1, source_target_pairs={{8,16},{16,8},{9,17},{17,9},{10,18},{18,10},{11,19},{19,11},{12,20... | collective-permute-start | bytes 1179656 | tf_op jit(solution)/shard_map/ppermute | solution.py:26
  132.9 4.0 %collective-permute-start.29 = (f32[136,256]{1,0:T(8,128)S(1)}, f32[136,256]{1,0:T(8,128)S(1)}, u32[]{:S(2)}, u32[]{:S(2)}) collective-permute-start(f32[136,256]{1,0:T(8,128)S(1)} %shard_map.103), channel_id=1, source_target_pairs={{0,8},{8,0},{16,24},{24,16},{1,9},{9,1},{17,25},{25,17},{2,10},{10... | collective-permute-start | bytes 417800 | tf_op jit(solution)/shard_map/ppermute | solution.py:19
  137.0 7.5 %collective-permute-start.30 = (f32[136,256]{1,0:T(8,128)S(1)}, f32[136,256]{1,0:T(8,128)S(1)}, u32[]{:S(2)}, u32[]{:S(2)}) collective-permute-start(f32[136,256]{1,0:T(8,128)S(1)} %add.153), channel_id=1, source_target_pairs={{0,16},{8,24},{16,0},{24,8},{1,17},{9,25},{17,1},{25,9},{2,18},{10... | collective-permute-start | bytes 417800 | tf_op jit(solution)/shard_map/ppermute | solution.py:19

commit v5 on v4

--- a/solution.py
+++ b/solution.py
@@ -36,7 +36,7 @@
 
 
 def steps_of():
-    return [("sy", 1)] + [("sx", bit) for bit in bits_of("sx")] + [("sy", bit) for bit in bits_of("sy")[:0:-1]]
+    return [("sy", 1)] + [("sx", bit) for bit in bits_of("sx")[::-1]] + [("sy", bit) for bit in bits_of("sy")[:0:-1]]
 
 
 def stacked_rows(parts):

time: 151 us -> 149 us (0.987)
  waiting for transfers between devices: 46.8 us -> 44.8 us
    ppermute x25, waiting for transfers between devices: 46.8 us -> 44.8 us  [swapped(): lax.ppermute(block, axis, [(i, i ^ bit) for i in range(lax.axis_size(axis...]
  transfers between devices with their start and end apart: 35 -> 35, of which waited for: 17 -> 16; matrix products, arithmetic and copies ran while one was open for 0% -> 0% of each run, Pallas kernels for 17% -> 17%
where the time goes in v5:
time: 149 us; the launch traced here: 148 us
  starting transfers between devices  51.8 us (35%)
  Pallas kernels  48.7 us (33%)
  waiting for transfers between devices  44.8 us (30%)
  between operations  1.51 us (1%)
    pallas_call x21, Pallas kernels, call(): pl.pallas_call(kernel, in_specs=[SMEM_SPEC if i < smem else ANY_SPEC if i...  48.7 us
    ppermute x25, waiting for transfers between devices, swapped(): lax.ppermute(block, axis, [(i, i ^ bit) for i in range(lax.axis_size(axis...  44.8 us
    ppermute x25, starting transfers between devices, swapped(): lax.ppermute(block, axis, [(i, i ^ bit) for i in range(lax.axis_size(axis...  44.3 us
    ppermute x10, starting transfers between devices, swapped_between(): return lax.ppermute(block, axis, route)  7.43 us
  transfers between devices with their start and end apart: 35, of which 16 were waited for; matrix products, arithmetic and copies ran while one was open for 0% of the time, Pallas kernels for 17%

profile of v5, /device:TPU:0, one launch (start us, length us, event | category | flops | bytes accessed | tf_op | source)
XLA Modules:
  0.0 148.2 jit_solution(11933688972088160408)
XLA Ops:
  0.7 1.0 fusion.refs_6_.select.refs_17_
  1.9 3.4 %shard_map.86 = (f32[416,256]{1,0:T(8,128)}, f32[416,256]{1,0:T(8,128)}, f32[424,256]{1,0:T(8,128)}, f32[424,256]{1,0:T(8,128)}) custom-call(s32[16]{0:T(128)} %bitcast.34, f32[1536,256]{1,0:T(8,128)} %bitcast.36, f32[16,1536]{1,0:T(8,128)} %bitcast.30), custom_call_target="tpu_custom_call" | custom-call | flops 1024 | bytes 1024 | tf_op jit(solution)/shard_map/pallas_call | solution.py:342
  6.0 3.0 %collective-permute-start.4 = (f32[12,128]{1,0:T(8,128)S(1)}, f32[12,128]{1,0:T(8,128)S(1)}, u32[]{:S(2)}, u32[]{:S(2)}) collective-permute-start(f32[12,128]{1,0:T(8,128)S(1)} %shard_map.88), channel_id=1, source_target_pairs={{0,1},{1,0},{2,3},{3,2},{4,5},{5,4},{6,7},{7,6},{8,9},{9,8},{10,11... | collective-permute-start | bytes 18440 | tf_op jit(solution)/shard_map/ppermute | solution.py:19
  10.6 2.1 %collective-permute-start.5 = (f32[24,128]{1,0:T(8,128)S(1)}, f32[24,128]{1,0:T(8,128)S(1)}, u32[]{:S(2)}, u32[]{:S(2)}) collective-permute-start(f32[24,128]{1,0:T(8,128)S(1)} %pad_add_fusion.8), channel_id=1, source_target_pairs={{0,16},{8,24},{16,0},{24,8},{1,17},{9,25},{17,1},{25,9},{2,18},{10... | collective-permute-start | bytes 36872 | tf_op jit(solution)/shard_map/ppermute | solution.py:19
  13.4 1.4 collective-permute-start
  14.9 1.3 collective-permute-done.6
  16.3 5.0 %collective-permute-start.7 = (f32[96,128]{1,0:T(8,128)S(1)}, f32[96,128]{1,0:T(8,128)S(1)}, u32[]{:S(2)}, u32[]{:S(2)}) collective-permute-start(f32[96,128]{1,0:T(8,128)S(1)} %pad_add_fusion.6), channel_id=1, source_target_pairs={{0,4},{1,5},{2,6},{3,7},{4,0},{5,1},{6,2},{7,3},{8,12},{9,13},{10,... | collective-permute-start | bytes 147464 | tf_op jit(solution)/shard_map/ppermute | solution.py:19
  21.2 5.2 %collective-permute-done.7 = f32[96,128]{1,0:T(8,128)S(1)} collective-permute-done((f32[96,128]{1,0:T(8,128)S(1)}, f32[96,128]{1,0:T(8,128)S(1)}, u32[]{:S(2)}, u32[]{:S(2)}) %collective-permute-start.7) | collective-permute-done | bytes 49184 | tf_op jit(solution)/shard_map/ppermute | solution.py:19
  26.5 3.4 %shard_map.87 = (f32[384,256]{1,0:T(8,128)S(1)}, f32[384,256]{1,0:T(8,128)S(1)}, f32[1536,256]{1,0:T(8,128)S(1)}) custom-call(f32[6]{0:T(128)S(1)} %pad_maximum_fusion.refs_0_.flags, f32[1536,1536]{1,0:T(8,128)S(1)} %bitcast.16, f32[416,256]{1,0:T(8,128)S(1)} %copy-done, f32[416,256]{1,0:T(8,128)S(1)} %copy-done.2, ...), custom_call_target="tpu_custom_call" | custom-call | flops 1024 | bytes 1024 | tf_op jit(solution)/shard_map/pallas_call | solution.py:342
  30.0 2.7 %shard_map.89 = (f32[384,256]{1,0:T(8,128)S(1)}, f32[384,256]{1,0:T(8,128)S(1)}, f32[392,256]{1,0:T(8,128)S(1)}, f32[392,256]{1,0:T(8,128)S(1)}) custom-call(f32[6]{0:T(128)S(1)} %pad_maximum_fusion.refs_0_.flags, f32[1536,1536]{1,0:T(8,128)S(1)} %bitcast.17, f32[424,256]{1,0:T(8,128)S(1)} %copy-done.4, f32[424,256]{1,0:T(8,128)S(1)} %copy-done.5, ...), custom_call_target="tpu_custom_call" | custom-call | flops 8000000000 | bytes 1024 | tf_op jit(solution)/shard_map/pallas_call | solution.py:342
  34.1 2.0 %shard_map.90 = (f32[384,256]{1,0:T(8,128)S(1)}, f32[384,256]{1,0:T(8,128)S(1)}, f32[1,256]{1,0:T(1,128)S(1)}) custom-call(f32[6]{0:T(128)S(1)} %pad_maximum_fusion.refs_0_.flags, f32[1536,1536]{1,0:T(8,128)S(1)} %bitcast.18, f32[384,256]{1,0:T(8,128)S(1)} %get-tuple-element.86.refs_2_.refs_8_, f32[384,256]{1,0:T(8,128)S(1)} %get-tuple-element.87.refs_3_.refs_9_, ...), custom_call_target="tpu_custom_call" | custom-call | flops 1024 | bytes 1024 | tf_op jit(solution)/shard_map/pallas_call | solution.py:342
  37.0 4.2 %collective-permute-start.10 = (f32[192,128]{1,0:T(8,128)S(1)}, f32[192,128]{1,0:T(8,128)S(1)}, u32[]{:S(2)}, u32[]{:S(2)}) collective-permute-start(f32[192,128]{1,0:T(8,128)S(1)} %pad_add_fusion.3), channel_id=1, source_target_pairs={{0,2},{1,3},{2,0},{3,1},{4,6},{5,7},{6,4},{7,5},{8,10},{9,11},{10,... | collective-permute-start | bytes 294920 | tf_op jit(solution)/shard_map/ppermute | solution.py:19
  41.2 6.0 %collective-permute-done.10 = f32[192,128]{1,0:T(8,128)S(1)} collective-permute-done((f32[192,128]{1,0:T(8,128)S(1)}, f32[192,128]{1,0:T(8,128)S(1)}, u32[]{:S(2)}, u32[]{:S(2)}) %collective-permute-start.10) | collective-permute-done | bytes 98336 | tf_op jit(solution)/shard_map/ppermute | solution.py:19
  47.2 3.4 %shard_map.91 = (f32[384,256]{1,0:T(8,128)S(1)}, f32[384,256]{1,0:T(8,128)S(1)}, f32[1536,256]{1,0:T(8,128)S(1)}) custom-call(f32[6]{0:T(128)S(1)} %pad_maximum_fusion.refs_0_.flags, f32[1536,1536]{1,0:T(8,128)S(1)} %bitcast.24, f32[384,256]{1,0:T(8,128)S(1)} %get-tuple-element.97.refs_2_, f32[384,256]{1,0:T(8,128)S(1)} %get-tuple-element.98.refs_3_, ...), custom_call_target="tpu_custom_call" | custom-call | flops 1024 | bytes 1024 | tf_op jit(solution)/shard_map/pallas_call | solution.py:342
  50.7 2.7 %shard_map.92 = (f32[384,256]{1,0:T(8,128)S(1)}, f32[384,256]{1,0:T(8,128)S(1)}, f32[392,256]{1,0:T(8,128)S(1)}, f32[392,256]{1,0:T(8,128)S(1)}) custom-call(f32[6]{0:T(128)S(1)} %pad_maximum_fusion.refs_0_.flags, f32[1536,1536]{1,0:T(8,128)S(1)} %bitcast.25, f32[392,256]{1,0:T(8,128)S(1)} %get-tuple-element.95.refs_6_.refs_2_, ...), custom_call_target="tpu_custom_call" | custom-call | flops 8000000000 | bytes 1024 | tf_op jit(solution)/shard_map/pallas_call | solution.py:342
  53.4 2.3 %shard_map.93 = (f32[384,256]{1,0:T(8,128)S(1)}, f32[384,256]{1,0:T(8,128)S(1)}, f32[24,256]{1,0:T(8,128)S(1)}) custom-call(f32[6]{0:T(128)S(1)} %pad_maximum_fusion.refs_0_.flags, f32[1536,1536]{1,0:T(8,128)S(1)} %bitcast.26, f32[384,256]{1,0:T(8,128)S(1)} %get-tuple-element.101.refs_2_.refs_0_, f32[384,256]{1,0:T(8,128)S(1)} %get-tuple-element.102.refs_3_.refs_1_, ...), custom_call_target="tpu_custom_call" | custom-call | flops 1024 | bytes 1024 | tf_op jit(solution)/shard_map/pallas_call | solution.py:342
  55.7 1.6 %collective-permute-start.13 = (f32[24,256]{1,0:T(8,128)S(1)}, f32[24,256]{1,0:T(8,128)S(1)}, u32[]{:S(2)}, u32[]{:S(2)}) collective-permute-start(f32[24,256]{1,0:T(8,128)S(1)} %get-tuple-element.111), channel_id=1, source_target_pairs={{0,1},{1,0},{2,3},{3,2},{4,5},{5,4},{6,7},{7,6},{8,9},{9,8},{10,11... | collective-permute-start | bytes 73736 | tf_op jit(solution)/shard_map/ppermute | solution.py:19
  57.3 2.3 %collective-permute-done.13 = f32[24,256]{1,0:T(8,128)S(1)} collective-permute-done((f32[24,256]{1,0:T(8,128)S(1)}, f32[24,256]{1,0:T(8,128)S(1)}, u32[]{:S(2)}, u32[]{:S(2)}) %collective-permute-start.13) | collective-permute-done | bytes 24608 | tf_op jit(solution)/shard_map/ppermute | solution.py:19
  59.6 3.1 %collective-permute-start.14 = (f32[48,256]{1,0:T(8,128)S(1)}, f32[48,256]{1,0:T(8,128)S(1)}, u32[]{:S(2)}, u32[]{:S(2)}) collective-permute-start(f32[48,256]{1,0:T(8,128)S(1)} %pad_add_fusion.5), channel_id=1, source_target_pairs={{0,4},{1,5},{2,6},{3,7},{4,0},{5,1},{6,2},{7,3},{8,12},{9,13},{10,... | collective-permute-start | bytes 147464 | tf_op jit(solution)/shard_map/ppermute | solution.py:19
  62.7 2.1 %collective-permute-done.14 = f32[48,256]{1,0:T(8,128)S(1)} collective-permute-done((f32[48,256]{1,0:T(8,128)S(1)}, f32[48,256]{1,0:T(8,128)S(1)}, u32[]{:S(2)}, u32[]{:S(2)}) %collective-permute-start.14) | collective-permute-done | bytes 49184 | tf_op jit(solution)/shard_map/ppermute | solution.py:19
  64.8 2.0 %collective-permute-start.15 = (f32[96,256]{1,0:T(8,128)S(1)}, f32[96,256]{1,0:T(8,128)S(1)}, u32[]{:S(2)}, u32[]{:S(2)}) collective-permute-start(f32[96,256]{1,0:T(8,128)S(1)} %pad_add_fusion.2.refs_0_), channel_id=1, source_target_pairs={{0,2},{1,3},{2,0},{3,1},{4,6},{5,7},{6,4},{7,5},{8,10},{9,11},{10,... | collective-permute-start | bytes 294920 | tf_op jit(solution)/shard_map/ppermute | solution.py:19
  66.8 1.0 collective-permute-start.20
  70.9 4.5 %collective-permute-start.18 = (f32[136,256]{1,0:T(8,128)S(1)}, f32[136,256]{1,0:T(8,128)S(1)}, u32[]{:S(2)}, u32[]{:S(2)}) collective-permute-start(f32[136,256]{1,0:T(8,128)S(1)} %shard_map.94), channel_id=1, source_target_pairs={{0,8},{8,0},{16,24},{24,16},{1,9},{9,1},{17,25},{25,17},{2,10},{10... | collective-permute-start | bytes 417800 | tf_op jit(solution)/shard_map/ppermute | solution.py:19
  75.4 1.0 collective-permute-done.18
  76.8 3.5 %shard_map.96.refs_10_.refs_11_.refs_18_ = f32[1536,128]{1,0:T(8,128)S(1)} custom-call(f32[6]{0:T(128)S(1)} %pad_maximum_fusion.refs_0_.flags, f32[416,256]{1,0:T(8,128)S(1)} %collective-permute-done.refs_4_.near0, f32[416,256]{1,0:T(8,128)S(1)} %collective-permute-done.1.refs_5_.near1, f32[424,256]{1,0:T(8,128)S(1)} %collective-permute-done.2.refs_4_.near2, ...), custom_call_target="tpu_custom_call" | custom-call | flops 1024 | bytes 1024 | tf_op jit(solution)/shard_map/pallas_call | solution.py:342
  80.3 2.9 %collective-permute-done.19 = f32[136,256]{1,0:T(8,128)S(1)} collective-permute-done((f32[136,256]{1,0:T(8,128)S(1)}, f32[136,256]{1,0:T(8,128)S(1)}, u32[]{:S(2)}, u32[]{:S(2)}) %collective-permute-start.19) | collective-permute-done | bytes 139296 | tf_op jit(solution)/shard_map/ppermute | solution.py:19
  83.8 3.7 %shard_map.97 = (f32[384,256]{1,0:T(8,128)S(1)}, f32[384,256]{1,0:T(8,128)S(1)}, f32[384,256]{1,0:T(8,128)S(1)}, f32[384,256]{1,0:T(8,128)S(1)}, f32[1536,256]{1,0:T(8,128)S(1)}) custom-call(f32[6]{0:T(128)S(1)} %pad_maximum_fusion.refs_0_.flags, f32[1536,1536]{1,0:T(8,128)S(1)} %bitcast.19, f32[384,256]{1,0:T(8,128)S(1)} %get-tuple-element.116.refs_2_.refs_8_, ...), custom_call_target="tpu_custom_call" | custom-call | flops 1024 | bytes 1024 | tf_op jit(solution)/shard_map/pallas_call | solution.py:342
  87.6 3.2 %shard_map.98 = (f32[384,256]{1,0:T(8,128)S(1)}, f32[384,256]{1,0:T(8,128)S(1)}, f32[384,256]{1,0:T(8,128)S(1)}, f32[384,256]{1,0:T(8,128)S(1)}, f32[392,256]{1,0:T(8,128)S(1)}, /*index=5*/f32[392,256]{1,0:T(8,128)S(1)}) custom-call(f32[6]{0:T(128)S(1)} %pad_maximum_fusion.refs_0_.flags, f32[1536,1536]{1,0:T(8,128)S(1)} %bitcast.20, ...), custom_call_target="tpu_custom_call" | custom-call | flops 8000000000 | bytes 1024 | tf_op jit(solution)/shard_map/pallas_call | solution.py:342
  90.8 2.4 %collective-permute-start.24 = (f32[392,256]{1,0:T(8,128)S(1)}, f32[392,256]{1,0:T(8,128)S(1)}, u32[]{:S(2)}, u32[]{:S(2)}) collective-permute-start(f32[392,256]{1,0:T(8,128)S(1)} %get-tuple-element.128.refs_6_.refs_2_), channel_id=1, source_target_pairs={{0,1},{1,0},{2,3},{3,2},{4,5},{5,4},{6,7},{7,6},{8,9},{9,8},{10,11... | collective-permute-start | bytes 1204232 | tf_op jit(solution)/shard_map/ppermute | solution.py:19
  93.9 2.0 %shard_map.99 = (f32[384,256]{1,0:T(8,128)S(1)}, f32[384,256]{1,0:T(8,128)S(1)}, f32[1,256]{1,0:T(1,128)S(1)}) custom-call(f32[6]{0:T(128)S(1)} %pad_maximum_fusion.refs_0_.flags, f32[1536,1536]{1,0:T(8,128)S(1)} %bitcast.21, f32[384,256]{1,0:T(8,128)S(1)} %get-tuple-element.121.refs_2_.refs_9_, f32[384,256]{1,0:T(8,128)S(1)} %get-tuple-element.122.refs_3_.refs_10_, ...), custom_call_target="tpu_custom_call" | custom-call | flops 1024 | bytes 1024 | tf_op jit(solution)/shard_map/pallas_call | solution.py:342
  95.9 0.9 collective-permute-start.23
  97.7 3.4 %shard_map.100 = (f32[384,256]{1,0:T(8,128)S(1)}, f32[384,256]{1,0:T(8,128)S(1)}, f32[1536,256]{1,0:T(8,128)S(1)}) custom-call(f32[6]{0:T(128)S(1)} %pad_maximum_fusion.refs_0_.flags, f32[1536,1536]{1,0:T(8,128)S(1)} %bitcast.27, f32[384,256]{1,0:T(8,128)S(1)} %get-tuple-element.130.refs_2_, f32[384,256]{1,0:T(8,128)S(1)} %get-tuple-element.131.refs_3_, ...), custom_call_target="tpu_custom_call" | custom-call | flops 1024 | bytes 1024 | tf_op jit(solution)/shard_map/pallas_call | solution.py:342
  101.1 8.0 %collective-permute-done.24.refs_4_ = f32[392,256]{1,0:T(8,128)S(1)} collective-permute-done((f32[392,256]{1,0:T(8,128)S(1)}, f32[392,256]{1,0:T(8,128)S(1)}, u32[]{:S(2)}, u32[]{:S(2)}) %collective-permute-start.24) | collective-permute-done | bytes 401440 | tf_op jit(solution)/shard_map/ppermute | solution.py:19
  109.0 2.7 %shard_map.101 = (f32[384,256]{1,0:T(8,128)S(1)}, f32[384,256]{1,0:T(8,128)S(1)}, f32[392,256]{1,0:T(8,128)S(1)}, f32[392,256]{1,0:T(8,128)S(1)}) custom-call(f32[6]{0:T(128)S(1)} %pad_maximum_fusion.refs_0_.flags, f32[1536,1536]{1,0:T(8,128)S(1)} %bitcast.28, f32[392,256]{1,0:T(8,128)S(1)} %get-tuple-element.128.refs_6_.refs_2_, ...), custom_call_target="tpu_custom_call" | custom-call | flops 8000000000 | bytes 1024 | tf_op jit(solution)/shard_map/pallas_call | solution.py:342
  111.7 2.5 %shard_map.102 = (f32[384,256]{1,0:T(8,128)S(1)}, f32[384,256]{1,0:T(8,128)S(1)}, f32[24,256]{1,0:T(8,128)S(1)}) custom-call(f32[6]{0:T(128)S(1)} %pad_maximum_fusion.refs_0_.flags, f32[1536,1536]{1,0:T(8,128)S(1)} %bitcast.29, f32[384,256]{1,0:T(8,128)S(1)} %get-tuple-element.132.refs_2_.refs_4_, f32[384,256]{1,0:T(8,128)S(1)} %get-tuple-element.133.refs_3_.refs_5_, ...), custom_call_target="tpu_custom_call" | custom-call | flops 1024 | bytes 1024 | tf_op jit(solution)/shard_map/pallas_call | solution.py:342
  114.3 2.5 %collective-permute-start.26 = (f32[24,256]{1,0:T(8,128)S(1)}, f32[24,256]{1,0:T(8,128)S(1)}, u32[]{:S(2)}, u32[]{:S(2)}) collective-permute-start(f32[24,256]{1,0:T(8,128)S(1)} %get-tuple-element.140), channel_id=1, source_target_pairs={{0,1},{1,0},{2,3},{3,2},{4,5},{5,4},{6,7},{7,6},{8,9},{9,8},{10,11... | collective-permute-start | bytes 73736 | tf_op jit(solution)/shard_map/ppermute | solution.py:19
  116.8 1.8 %collective-permute-done.26 = f32[24,256]{1,0:T(8,128)S(1)} collective-permute-done((f32[24,256]{1,0:T(8,128)S(1)}, f32[24,256]{1,0:T(8,128)S(1)}, u32[]{:S(2)}, u32[]{:S(2)}) %collective-permute-start.26) | collective-permute-done | bytes 24608 | tf_op jit(solution)/shard_map/ppermute | solution.py:19
  118.6 3.1 %collective-permute-start.27 = (f32[48,256]{1,0:T(8,128)S(1)}, f32[48,256]{1,0:T(8,128)S(1)}, u32[]{:S(2)}, u32[]{:S(2)}) collective-permute-start(f32[48,256]{1,0:T(8,128)S(1)} %pad_add_fusion.4), channel_id=1, source_target_pairs={{0,4},{1,5},{2,6},{3,7},{4,0},{5,1},{6,2},{7,3},{8,12},{9,13},{10,... | collective-permute-start | bytes 147464 | tf_op jit(solution)/shard_map/ppermute | solution.py:19
  121.7 3.1 %collective-permute-done.27 = f32[48,256]{1,0:T(8,128)S(1)} collective-permute-done((f32[48,256]{1,0:T(8,128)S(1)}, f32[48,256]{1,0:T(8,128)S(1)}, u32[]{:S(2)}, u32[]{:S(2)}) %collective-permute-start.27) | collective-permute-done | bytes 49184 | tf_op jit(solution)/shard_map/ppermute | solution.py:19
  124.8 1.3 collective-permute-start.28
  126.1 1.6 %collective-permute-start.33 = (f32[392,256]{1,0:T(8,128)S(1)}, f32[392,256]{1,0:T(8,128)S(1)}, u32[]{:S(2)}, u32[]{:S(2)}) collective-permute-start(f32[392,256]{1,0:T(8,128)S(1)} %get-tuple-element.150.refs_6_.refs_3_), channel_id=1, source_target_pairs={{0,1},{1,0},{2,3},{3,2},{4,5},{5,4},{6,7},{7,6},{8,9},{9,8},{10,11... | collective-permute-start | bytes 1204232 | tf_op jit(solution)/shard_map/ppermute | solution.py:19
  128.4 1.3 collective-permute-done.28.refs_1_
  130.9 2.2 %collective-permute-start.29 = (f32[136,256]{1,0:T(8,128)S(1)}, f32[136,256]{1,0:T(8,128)S(1)}, u32[]{:S(2)}, u32[]{:S(2)}) collective-permute-start(f32[136,256]{1,0:T(8,128)S(1)} %shard_map.103), channel_id=1, source_target_pairs={{0,8},{8,0},{16,24},{24,16},{1,9},{9,1},{17,25},{25,17},{2,10},{10... | collective-permute-start | bytes 417800 | tf_op jit(solution)/shard_map/ppermute | solution.py:19
  133.2 1.0 collective-permute-done.29
  134.2 1.7 %collective-permute-start.30 = (f32[136,256]{1,0:T(8,128)S(1)}, f32[136,256]{1,0:T(8,128)S(1)}, u32[]{:S(2)}, u32[]{:S(2)}) collective-permute-start(f32[136,256]{1,0:T(8,128)S(1)} %add.153), channel_id=1, source_target_pairs={{0,16},{8,24},{16,0},{24,8},{1,17},{9,25},{17,1},{25,9},{2,18},{10... | collective-permute-start | bytes 417800 | tf_op jit(solution)/shard_map/ppermute | solution.py:19
  135.8 6.6 %collective-permute-done.30 = f32[136,256]{1,0:T(8,128)S(1)} collective-permute-done((f32[136,256]{1,0:T(8,128)S(1)}, f32[136,256]{1,0:T(8,128)S(1)}, u32[]{:S(2)}, u32[]{:S(2)}) %collective-permute-start.30) | collective-permute-done | bytes 139296 | tf_op jit(solution)/shard_map/ppermute | solution.py:19
  143.0 1.2 shard_map.105
  144.3 3.7 %shard_map.106 = f32[1536,256]{1,0:T(8,128)} custom-call(f32[6]{0:T(128)S(1)} %pad_maximum_fusion.refs_0_.flags, f32[384,256]{1,0:T(8,128)S(1)} %get-tuple-element.148.refs_1_, f32[384,256]{1,0:T(8,128)S(1)} %get-tuple-element.149.refs_2_, f32[392,256]{1,0:T(8,128)S(1)} %get-tuple-element.150.refs_6_.refs_3_, ...), custom_call_target="tpu_custom_call" | custom-call | flops 1024 | bytes 1024 | tf_op jit(solution)/shard_map/pallas_call | solution.py:342
  (96 shorter events, 13.7 us)
Async XLA Ops:
  0.6 4.7 %copy-start.3 = (s32[1,1,16]{2,1,0:T(1,128)S(1)}, s32[1,1,16]{2,1,0:T(1,128)}, u32[]{:S(2)}) copy-start(s32[1,1,16]{2,1,0:T(1,128)} %param.11) | copy-start | bytes 196
  0.6 4.7 %copy-start.6 = (f32[4,128]{1,0:T(4,128)S(1)}, f32[4,128]{1,0:T(4,128)}, u32[]{:S(2)}) copy-start(f32[4,128]{1,0:T(4,128)} %inverse) | copy-start | bytes 6148
  5.3 21.1 %slice-start = ((s8[9437184]{0:T(1024)(128)(4,1)}), s8[4194304]{0:T(1024)(128)(4,1)S(1)}, s32[]{:S(2)}) async-start(s8[9437184]{0:T(1024)(128)(4,1)} %bitcast.14), calls=%async_computation | async-start | bytes 8388608
  5.4 3.6 %copy-start.4 = (f32[424,256]{1,0:T(8,128)S(1)}, f32[424,256]{1,0:T(8,128)}, u32[]{:S(2)}) copy-start(f32[424,256]{1,0:T(8,128)} %get-tuple-element.88.refs_2_) | copy-start | bytes 1302532
  5.4 4.1 %copy-start.5 = (f32[424,256]{1,0:T(8,128)S(1)}, f32[424,256]{1,0:T(8,128)}, u32[]{:S(2)}) copy-start(f32[424,256]{1,0:T(8,128)} %get-tuple-element.89.refs_3_) | copy-start | bytes 1302532
  5.4 7.3 %copy-start.2 = (f32[416,256]{1,0:T(8,128)S(1)}, f32[416,256]{1,0:T(8,128)}, u32[]{:S(2)}) copy-start(f32[416,256]{1,0:T(8,128)} %get-tuple-element.83.refs_3_) | copy-start | bytes 1277956
  5.4 8.0 %copy-start = (f32[416,256]{1,0:T(8,128)S(1)}, f32[416,256]{1,0:T(8,128)}, u32[]{:S(2)}) copy-start(f32[416,256]{1,0:T(8,128)} %get-tuple-element.81.refs_2_.sent) | copy-start | bytes 1277956
  5.4 21.1 %slice-start.1 = ((s8[9437184]{0:T(1024)(128)(4,1)}), s8[4194304]{0:T(1024)(128)(4,1)S(1)}, s32[]{:S(2)}) async-start(s8[9437184]{0:T(1024)(128)(4,1)} %bitcast.14), calls=%async_computation.1 | async-start | bytes 8388608
  5.4 21.1 %slice-start.2 = ((s8[9437184]{0:T(1024)(128)(4,1)}), s8[1048576]{0:T(1024)(128)(4,1)S(1)}, s32[]{:S(2)}) async-start(s8[9437184]{0:T(1024)(128)(4,1)} %bitcast.14), calls=%async_computation.2 | async-start | bytes 2097152
  6.0 4.6 %collective-permute-start.4 = (f32[12,128]{1,0:T(8,128)S(1)}, f32[12,128]{1,0:T(8,128)S(1)}, u32[]{:S(2)}, u32[]{:S(2)}) collective-permute-start(f32[12,128]{1,0:T(8,128)S(1)} %shard_map.88), channel_id=1, source_target_pairs={{0,1},{1,0},{2,3},{3,2},{4,5},{5,4},{6,7},{7,6},{8,9},{9,8},{10,11... | collective-permute-start | bytes 18440 | tf_op jit(solution)/shard_map/ppermute | solution.py:19
  9.0 20.9 %collective-permute-start.2 = (f32[424,256]{1,0:T(8,128)S(1)}, f32[424,256]{1,0:T(8,128)S(1)}, u32[]{:S(2)}, u32[]{:S(2)}) collective-permute-start(f32[424,256]{1,0:T(8,128)S(1)} %copy-done.4), channel_id=1, source_target_pairs={{0,1},{1,0},{2,3},{3,2},{4,5},{5,4},{6,7},{7,6},{8,9},{9,8},{10,11... | collective-permute-start | bytes 1302536 | tf_op jit(solution)/shard_map/ppermute | solution.py:19
  9.5 20.5 %collective-permute-start.3 = (f32[424,256]{1,0:T(8,128)S(1)}, f32[424,256]{1,0:T(8,128)S(1)}, u32[]{:S(2)}, u32[]{:S(2)}) collective-permute-start(f32[424,256]{1,0:T(8,128)S(1)} %copy-done.5), channel_id=1, source_target_pairs={{1,2},{2,1},{3,4},{4,3},{5,6},{6,5},{9,10},{10,9},{11,12},{12,11},... | collective-permute-start | bytes 1302536 | tf_op jit(solution)/shard_map/ppermute | solution.py:26
  10.6 4.2 %collective-permute-start.5 = (f32[24,128]{1,0:T(8,128)S(1)}, f32[24,128]{1,0:T(8,128)S(1)}, u32[]{:S(2)}, u32[]{:S(2)}) collective-permute-start(f32[24,128]{1,0:T(8,128)S(1)} %pad_add_fusion.8), channel_id=1, source_target_pairs={{0,16},{8,24},{16,0},{24,8},{1,17},{9,25},{17,1},{25,9},{2,18},{10... | collective-permute-start | bytes 36872 | tf_op jit(solution)/shard_map/ppermute | solution.py:19
  12.7 13.8 %collective-permute-start.1 = (f32[416,256]{1,0:T(8,128)S(1)}, f32[416,256]{1,0:T(8,128)S(1)}, u32[]{:S(2)}, u32[]{:S(2)}) collective-permute-start(f32[416,256]{1,0:T(8,128)S(1)} %copy-done.2), channel_id=1, source_target_pairs={{8,16},{16,8},{9,17},{17,9},{10,18},{18,10},{11,19},{19,11},{12,20... | collective-permute-start | bytes 1277960 | tf_op jit(solution)/shard_map/ppermute | solution.py:26
  13.4 13.1 %collective-permute-start = (f32[416,256]{1,0:T(8,128)S(1)}, f32[416,256]{1,0:T(8,128)S(1)}, u32[]{:S(2)}, u32[]{:S(2)}) collective-permute-start(f32[416,256]{1,0:T(8,128)S(1)} %copy-done), channel_id=1, source_target_pairs={{0,8},{8,0},{16,24},{24,16},{1,9},{9,1},{17,25},{25,17},{2,10},{10... | collective-permute-start | bytes 1277960 | tf_op jit(solution)/shard_map/ppermute | solution.py:19
  14.8 1.4 collective-permute-start.6
  16.3 10.2 %collective-permute-start.7 = (f32[96,128]{1,0:T(8,128)S(1)}, f32[96,128]{1,0:T(8,128)S(1)}, u32[]{:S(2)}, u32[]{:S(2)}) collective-permute-start(f32[96,128]{1,0:T(8,128)S(1)} %pad_add_fusion.6), channel_id=1, source_target_pairs={{0,4},{1,5},{2,6},{3,7},{4,0},{5,1},{6,2},{7,3},{8,12},{9,13},{10,... | collective-permute-start | bytes 147464 | tf_op jit(solution)/shard_map/ppermute | solution.py:19
  30.0 17.2 %slice-start.3 = ((s8[9437184]{0:T(1024)(128)(4,1)}), s8[4194304]{0:T(1024)(128)(4,1)S(1)}, s32[]{:S(2)}) async-start(s8[9437184]{0:T(1024)(128)(4,1)} %bitcast.22), calls=%async_computation.3 | async-start | bytes 8388608
  30.0 17.2 %slice-start.4 = ((s8[9437184]{0:T(1024)(128)(4,1)}), s8[4194304]{0:T(1024)(128)(4,1)S(1)}, s32[]{:S(2)}) async-start(s8[9437184]{0:T(1024)(128)(4,1)} %bitcast.22), calls=%async_computation.4 | async-start | bytes 8388608
  30.0 17.2 %slice-start.5 = ((s8[9437184]{0:T(1024)(128)(4,1)}), s8[1048576]{0:T(1024)(128)(4,1)S(1)}, s32[]{:S(2)}) async-start(s8[9437184]{0:T(1024)(128)(4,1)} %bitcast.22), calls=%async_computation.5 | async-start | bytes 2097152
  32.7 18.0 %collective-permute-start.11 = (f32[392,256]{1,0:T(8,128)S(1)}, f32[392,256]{1,0:T(8,128)S(1)}, u32[]{:S(2)}, u32[]{:S(2)}) collective-permute-start(f32[392,256]{1,0:T(8,128)S(1)} %get-tuple-element.95.refs_6_.refs_2_), channel_id=1, source_target_pairs={{0,1},{1,0},{2,3},{3,2},{4,5},{5,4},{6,7},{7,6},{8,9},{9,8},{10,11... | collective-permute-start | bytes 1204232 | tf_op jit(solution)/shard_map/ppermute | solution.py:19
  33.4 17.3 %collective-permute-start.12 = (f32[392,256]{1,0:T(8,128)S(1)}, f32[392,256]{1,0:T(8,128)S(1)}, u32[]{:S(2)}, u32[]{:S(2)}) collective-permute-start(f32[392,256]{1,0:T(8,128)S(1)} %get-tuple-element.96.refs_7_.refs_3_), channel_id=1, source_target_pairs={{1,2},{2,1},{3,4},{4,3},{5,6},{6,5},{9,10},{10,9},{11,12},{12,11},... | collective-permute-start | bytes 1204232 | tf_op jit(solution)/shard_map/ppermute | solution.py:26
  36.0 11.1 %collective-permute-start.8 = (f32[384,256]{1,0:T(8,128)S(1)}, f32[384,256]{1,0:T(8,128)S(1)}, u32[]{:S(2)}, u32[]{:S(2)}) collective-permute-start(f32[384,256]{1,0:T(8,128)S(1)} %get-tuple-element.97.refs_2_), channel_id=1, source_target_pairs={{0,8},{8,0},{16,24},{24,16},{1,9},{9,1},{17,25},{25,17},{2,10},{10... | collective-permute-start | bytes 1179656 | tf_op jit(solution)/shard_map/ppermute | solution.py:19
  36.1 11.1 %collective-permute-start.9 = (f32[384,256]{1,0:T(8,128)S(1)}, f32[384,256]{1,0:T(8,128)S(1)}, u32[]{:S(2)}, u32[]{:S(2)}) collective-permute-start(f32[384,256]{1,0:T(8,128)S(1)} %get-tuple-element.98.refs_3_), channel_id=1, source_target_pairs={{8,16},{16,8},{9,17},{17,9},{10,18},{18,10},{11,19},{19,11},{12,20... | collective-permute-start | bytes 1179656 | tf_op jit(solution)/shard_map/ppermute | solution.py:26
  37.0 10.1 %collective-permute-start.10 = (f32[192,128]{1,0:T(8,128)S(1)}, f32[192,128]{1,0:T(8,128)S(1)}, u32[]{:S(2)}, u32[]{:S(2)}) collective-permute-start(f32[192,128]{1,0:T(8,128)S(1)} %pad_add_fusion.3), channel_id=1, source_target_pairs={{0,2},{1,3},{2,0},{3,1},{4,6},{5,7},{6,4},{7,5},{8,10},{9,11},{10,... | collective-permute-start | bytes 294920 | tf_op jit(solution)/shard_map/ppermute | solution.py:19
  50.7 2.7 %copy-start.1 = (f32[1,1,16,1536]{3,2,1,0:T(8,128)S(1)}, f32[1,1,16,1536]{3,2,1,0:T(8,128)}, u32[]{:S(2)}) copy-start(f32[1,1,16,1536]{3,2,1,0:T(8,128)} %param.10) | copy-start | bytes 294916
  55.7 3.9 %collective-permute-start.13 = (f32[24,256]{1,0:T(8,128)S(1)}, f32[24,256]{1,0:T(8,128)S(1)}, u32[]{:S(2)}, u32[]{:S(2)}) collective-permute-start(f32[24,256]{1,0:T(8,128)S(1)} %get-tuple-element.111), channel_id=1, source_target_pairs={{0,1},{1,0},{2,3},{3,2},{4,5},{5,4},{6,7},{7,6},{8,9},{9,8},{10,11... | collective-permute-start | bytes 73736 | tf_op jit(solution)/shard_map/ppermute | solution.py:19
  59.6 5.1 %collective-permute-start.14 = (f32[48,256]{1,0:T(8,128)S(1)}, f32[48,256]{1,0:T(8,128)S(1)}, u32[]{:S(2)}, u32[]{:S(2)}) collective-permute-start(f32[48,256]{1,0:T(8,128)S(1)} %pad_add_fusion.5), channel_id=1, source_target_pairs={{0,4},{1,5},{2,6},{3,7},{4,0},{5,1},{6,2},{7,3},{8,12},{9,13},{10,... | collective-permute-start | bytes 147464 | tf_op jit(solution)/shard_map/ppermute | solution.py:19
  64.8 4.7 %collective-permute-start.15 = (f32[96,256]{1,0:T(8,128)S(1)}, f32[96,256]{1,0:T(8,128)S(1)}, u32[]{:S(2)}, u32[]{:S(2)}) collective-permute-start(f32[96,256]{1,0:T(8,128)S(1)} %pad_add_fusion.2.refs_0_), channel_id=1, source_target_pairs={{0,2},{1,3},{2,0},{3,1},{4,6},{5,7},{6,4},{7,5},{8,10},{9,11},{10,... | collective-permute-start | bytes 294920 | tf_op jit(solution)/shard_map/ppermute | solution.py:19
  66.8 20.7 %collective-permute-start.20 = (f32[392,256]{1,0:T(8,128)S(1)}, f32[392,256]{1,0:T(8,128)S(1)}, u32[]{:S(2)}, u32[]{:S(2)}) collective-permute-start(f32[392,256]{1,0:T(8,128)S(1)} %get-tuple-element.123.refs_6_.refs_2_.refs_10_), channel_id=1, source_target_pairs={{0,1},{1,0},{2,3},{3,2},{4,5},{5,4},{6,7},{7,6},{8,9},{9,8},{10,11... | collective-permute-start | bytes 1204232 | tf_op jit(solution)/shard_map/ppermute | solution.py:19
  67.8 19.7 %collective-permute-start.21 = (f32[392,256]{1,0:T(8,128)S(1)}, f32[392,256]{1,0:T(8,128)S(1)}, u32[]{:S(2)}, u32[]{:S(2)}) collective-permute-start(f32[392,256]{1,0:T(8,128)S(1)} %get-tuple-element.124.refs_7_.refs_3_.refs_11_), channel_id=1, source_target_pairs={{1,2},{2,1},{3,4},{4,3},{5,6},{6,5},{9,10},{10,9},{11,12},{12,11},... | collective-permute-start | bytes 1204232 | tf_op jit(solution)/shard_map/ppermute | solution.py:26
  69.4 14.3 %collective-permute-start.16 = (f32[384,256]{1,0:T(8,128)S(1)}, f32[384,256]{1,0:T(8,128)S(1)}, u32[]{:S(2)}, u32[]{:S(2)}) collective-permute-start(f32[384,256]{1,0:T(8,128)S(1)} %get-tuple-element.116.refs_2_.refs_8_), channel_id=1, source_target_pairs={{0,8},{8,0},{16,24},{24,16},{1,9},{9,1},{17,25},{25,17},{2,10},{10... | collective-permute-start | bytes 1179656 | tf_op jit(solution)/shard_map/ppermute | solution.py:19
  69.4 14.3 %collective-permute-start.17 = (f32[384,256]{1,0:T(8,128)S(1)}, f32[384,256]{1,0:T(8,128)S(1)}, u32[]{:S(2)}, u32[]{:S(2)}) collective-permute-start(f32[384,256]{1,0:T(8,128)S(1)} %get-tuple-element.117.refs_3_.refs_9_), channel_id=1, source_target_pairs={{8,16},{16,8},{9,17},{17,9},{10,18},{18,10},{11,19},{19,11},{12,20... | collective-permute-start | bytes 1179656 | tf_op jit(solution)/shard_map/ppermute | solution.py:26
  70.9 5.5 %collective-permute-start.18 = (f32[136,256]{1,0:T(8,128)S(1)}, f32[136,256]{1,0:T(8,128)S(1)}, u32[]{:S(2)}, u32[]{:S(2)}) collective-permute-start(f32[136,256]{1,0:T(8,128)S(1)} %shard_map.94), channel_id=1, source_target_pairs={{0,8},{8,0},{16,24},{24,16},{1,9},{9,1},{17,25},{25,17},{2,10},{10... | collective-permute-start | bytes 417800 | tf_op jit(solution)/shard_map/ppermute | solution.py:19
  76.5 6.7 %collective-permute-start.19 = (f32[136,256]{1,0:T(8,128)S(1)}, f32[136,256]{1,0:T(8,128)S(1)}, u32[]{:S(2)}, u32[]{:S(2)}) collective-permute-start(f32[136,256]{1,0:T(8,128)S(1)} %add.149), channel_id=1, source_target_pairs={{0,16},{8,24},{16,0},{24,8},{1,17},{9,25},{17,1},{25,9},{2,18},{10... | collective-permute-start | bytes 417800 | tf_op jit(solution)/shard_map/ppermute | solution.py:19
  90.8 18.2 %collective-permute-start.24 = (f32[392,256]{1,0:T(8,128)S(1)}, f32[392,256]{1,0:T(8,128)S(1)}, u32[]{:S(2)}, u32[]{:S(2)}) collective-permute-start(f32[392,256]{1,0:T(8,128)S(1)} %get-tuple-element.128.refs_6_.refs_2_), channel_id=1, source_target_pairs={{0,1},{1,0},{2,3},{3,2},{4,5},{5,4},{6,7},{7,6},{8,9},{9,8},{10,11... | collective-permute-start | bytes 1204232 | tf_op jit(solution)/shard_map/ppermute | solution.py:19
  93.2 15.9 %collective-permute-start.25 = (f32[392,256]{1,0:T(8,128)S(1)}, f32[392,256]{1,0:T(8,128)S(1)}, u32[]{:S(2)}, u32[]{:S(2)}) collective-permute-start(f32[392,256]{1,0:T(8,128)S(1)} %get-tuple-element.129.refs_7_.refs_3_), channel_id=1, source_target_pairs={{1,2},{2,1},{3,4},{4,3},{5,6},{6,5},{9,10},{10,9},{11,12},{12,11},... | collective-permute-start | bytes 1204232 | tf_op jit(solution)/shard_map/ppermute | solution.py:26
  95.9 1.8 %collective-permute-start.22 = (f32[384,256]{1,0:T(8,128)S(1)}, f32[384,256]{1,0:T(8,128)S(1)}, u32[]{:S(2)}, u32[]{:S(2)}) collective-permute-start(f32[384,256]{1,0:T(8,128)S(1)} %get-tuple-element.130.refs_2_), channel_id=1, source_target_pairs={{0,8},{8,0},{16,24},{24,16},{1,9},{9,1},{17,25},{25,17},{2,10},{10... | collective-permute-start | bytes 1179656 | tf_op jit(solution)/shard_map/ppermute | solution.py:19
  95.9 1.7 %collective-permute-start.23 = (f32[384,256]{1,0:T(8,128)S(1)}, f32[384,256]{1,0:T(8,128)S(1)}, u32[]{:S(2)}, u32[]{:S(2)}) collective-permute-start(f32[384,256]{1,0:T(8,128)S(1)} %get-tuple-element.131.refs_3_), channel_id=1, source_target_pairs={{8,16},{16,8},{9,17},{17,9},{10,18},{18,10},{11,19},{19,11},{12,20... | collective-permute-start | bytes 1179656 | tf_op jit(solution)/shard_map/ppermute | solution.py:26
  114.3 4.4 %collective-permute-start.26 = (f32[24,256]{1,0:T(8,128)S(1)}, f32[24,256]{1,0:T(8,128)S(1)}, u32[]{:S(2)}, u32[]{:S(2)}) collective-permute-start(f32[24,256]{1,0:T(8,128)S(1)} %get-tuple-element.140), channel_id=1, source_target_pairs={{0,1},{1,0},{2,3},{3,2},{4,5},{5,4},{6,7},{7,6},{8,9},{9,8},{10,11... | collective-permute-start | bytes 73736 | tf_op jit(solution)/shard_map/ppermute | solution.py:19
  118.6 6.2 %collective-permute-start.27 = (f32[48,256]{1,0:T(8,128)S(1)}, f32[48,256]{1,0:T(8,128)S(1)}, u32[]{:S(2)}, u32[]{:S(2)}) collective-permute-start(f32[48,256]{1,0:T(8,128)S(1)} %pad_add_fusion.4), channel_id=1, source_target_pairs={{0,4},{1,5},{2,6},{3,7},{4,0},{5,1},{6,2},{7,3},{8,12},{9,13},{10,... | collective-permute-start | bytes 147464 | tf_op jit(solution)/shard_map/ppermute | solution.py:19
  124.8 4.9 %collective-permute-start.28 = (f32[96,256]{1,0:T(8,128)S(1)}, f32[96,256]{1,0:T(8,128)S(1)}, u32[]{:S(2)}, u32[]{:S(2)}) collective-permute-start(f32[96,256]{1,0:T(8,128)S(1)} %pad_add_fusion.1.refs_0_), channel_id=1, source_target_pairs={{0,2},{1,3},{2,0},{3,1},{4,6},{5,7},{6,4},{7,5},{8,10},{9,11},{10,... | collective-permute-start | bytes 294920 | tf_op jit(solution)/shard_map/ppermute | solution.py:19
  126.1 18.2 %collective-permute-start.33 = (f32[392,256]{1,0:T(8,128)S(1)}, f32[392,256]{1,0:T(8,128)S(1)}, u32[]{:S(2)}, u32[]{:S(2)}) collective-permute-start(f32[392,256]{1,0:T(8,128)S(1)} %get-tuple-element.150.refs_6_.refs_3_), channel_id=1, source_target_pairs={{0,1},{1,0},{2,3},{3,2},{4,5},{5,4},{6,7},{7,6},{8,9},{9,8},{10,11... | collective-permute-start | bytes 1204232 | tf_op jit(solution)/shard_map/ppermute | solution.py:19
  127.7 16.6 %collective-permute-start.34 = (f32[392,256]{1,0:T(8,128)S(1)}, f32[392,256]{1,0:T(8,128)S(1)}, u32[]{:S(2)}, u32[]{:S(2)}) collective-permute-start(f32[392,256]{1,0:T(8,128)S(1)} %get-tuple-element.151.refs_7_.refs_4_), channel_id=1, source_target_pairs={{1,2},{2,1},{3,4},{4,3},{5,6},{6,5},{9,10},{10,9},{11,12},{12,11},... | collective-permute-start | bytes 1204232 | tf_op jit(solution)/shard_map/ppermute | solution.py:26
  129.7 14.6 %collective-permute-start.31 = (f32[384,256]{1,0:T(8,128)S(1)}, f32[384,256]{1,0:T(8,128)S(1)}, u32[]{:S(2)}, u32[]{:S(2)}) collective-permute-start(f32[384,256]{1,0:T(8,128)S(1)} %get-tuple-element.148.refs_1_), channel_id=1, source_target_pairs={{0,8},{8,0},{16,24},{24,16},{1,9},{9,1},{17,25},{25,17},{2,10},{10... | collective-permute-start | bytes 1179656 | tf_op jit(solution)/shard_map/ppermute | solution.py:19
  129.7 14.6 %collective-permute-start.32 = (f32[384,256]{1,0:T(8,128)S(1)}, f32[384,256]{1,0:T(8,128)S(1)}, u32[]{:S(2)}, u32[]{:S(2)}) collective-permute-start(f32[384,256]{1,0:T(8,128)S(1)} %get-tuple-element.149.refs_2_), channel_id=1, source_target_pairs={{8,16},{16,8},{9,17},{17,9},{10,18},{18,10},{11,19},{19,11},{12,20... | collective-permute-start | bytes 1179656 | tf_op jit(solution)/shard_map/ppermute | solution.py:26
  130.9 3.2 %collective-permute-start.29 = (f32[136,256]{1,0:T(8,128)S(1)}, f32[136,256]{1,0:T(8,128)S(1)}, u32[]{:S(2)}, u32[]{:S(2)}) collective-permute-start(f32[136,256]{1,0:T(8,128)S(1)} %shard_map.103), channel_id=1, source_target_pairs={{0,8},{8,0},{16,24},{24,16},{1,9},{9,1},{17,25},{25,17},{2,10},{10... | collective-permute-start | bytes 417800 | tf_op jit(solution)/shard_map/ppermute | solution.py:19
  134.2 8.3 %collective-permute-start.30 = (f32[136,256]{1,0:T(8,128)S(1)}, f32[136,256]{1,0:T(8,128)S(1)}, u32[]{:S(2)}, u32[]{:S(2)}) collective-permute-start(f32[136,256]{1,0:T(8,128)S(1)} %add.153), channel_id=1, source_target_pairs={{0,16},{8,24},{16,0},{24,8},{1,17},{9,25},{17,1},{25,9},{2,18},{10... | collective-permute-start | bytes 417800 | tf_op jit(solution)/shard_map/ppermute | solution.py:19

commit v6 on v5

--- a/solution.py
+++ b/solution.py
@@ -208,7 +208,10 @@
         rows = slice((f - 2) * size, (f - 1) * size)
         high[rows], low[rows] = split(flags[f] * values[f][...])
     value = partial[: 2 * size] + product(mat[: 2 * size, 2 * size :], high[...], low[...])
-    slots[1][...], slots[0][...] = pair(flags[4], value[size:], value[:size])
+    slots[1][:size], slots[0][...] = pair(flags[4], value[size:], value[:size])
+    rest = slots[1].shape[0] - size
+    if rest:
+        slots[1][size:] = jnp.zeros((rest, slots[1].shape[1]), F32)
     return faces_of(flags, [slot[:size] for slot in slots])
 
 
@@ -379,7 +382,7 @@
     within = coarse_ids % (ncoarse // (n_sx * n_sy))
     order = (origin * (ncoarse // (n_sx * n_sy)) + within)[None, :] == coarse_ids[:, None]
     order = order.astype(BF16)
-    one_face, far_face = (face, width), (face + FAR_ROWS, width)
+    one_face = (face, width)
     parts = [pltpu.VMEM((half, width), BF16)] * 2
     one, select, order, flags = lax.optimization_barrier((jnp.ones((1, width), F32), select, order, flags))
     half_one = jnp.full((1, width), 0.5, F32)
@@ -392,6 +395,7 @@
         return fields[:2], fields[2:], partial
 
     def crit(matrix, owns, nears, coef, partial, bases, lifts):
+        far_face = (face + (2 if matrix is flex_mat else 1) * FAR_ROWS, width)
         operands = [flags, matrix, *owns, *nears, select, coef, partial, *bases, *lifts]
         shapes = [one_face] * (4 if lifts else 2) + [far_face] * 2
         kernel = functools.partial(crit_kernel, bool(bases), bool(lifts))
@@ -414,7 +418,7 @@
     def flex_late(values, a23, partial, carried, other=()):
         operands = [flags, flex_mat, *values, *a23, *other, partial, coupling_mat, carried]
         kernel = functools.partial(flex_late_kernel, int(bool(other)))
-        a0, a1, sums = call(kernel, operands, [one_face, one_face, (ncl + 8, width)], parts, smem=1)
+        a0, a1, sums = call(kernel, operands, [one_face, (face + FAR_ROWS, width), (ncl + 8, width)], parts, smem=1)
         return (a0, a1, *a23), sums
 
     def solved(kernel, sums, faces, more):

time: 149 us -> 148 us (level)
  starting transfers between devices: 51.8 us -> 50.3 us
  transfers between devices with their start and end apart: 35 -> 35, of which waited for: 16 -> 17; matrix products, arithmetic and copies ran while one was open for 0% -> 0% of each run, Pallas kernels for 17% -> 17%
where the time goes in v6:
time: 148 us
  starting transfers between devices  50.3 us (34%)
  Pallas kernels  48.7 us (33%)
  waiting for transfers between devices  45.9 us (31%)
  between operations  1.48 us (1%)
    pallas_call x21, Pallas kernels, call(): pl.pallas_call(kernel, in_specs=[SMEM_SPEC if i < smem else ANY_SPEC if i...  48.7 us
    ppermute x25, waiting for transfers between devices, swapped(): lax.ppermute(block, axis, [(i, i ^ bit) for i in range(lax.axis_size(axis...  45.9 us
    ppermute x25, starting transfers between devices, swapped(): lax.ppermute(block, axis, [(i, i ^ bit) for i in range(lax.axis_size(axis...  42.9 us
    ppermute x10, starting transfers between devices, swapped_between(): return lax.ppermute(block, axis, route)  7.43 us
  transfers between devices with their start and end apart: 35, of which 17 were waited for; matrix products, arithmetic and copies ran while one was open for 0% of the time, Pallas kernels for 17%

profile of v6, /device:TPU:0, one launch (start us, length us, event | category | flops | bytes accessed | tf_op | source)
XLA Modules:
  0.0 147.8 jit_solution(2978334128401938085)
XLA Ops:
  0.7 1.0 fusion.refs_6_.select.refs_17_
  1.9 3.4 %shard_map.86 = (f32[416,256]{1,0:T(8,128)}, f32[416,256]{1,0:T(8,128)}, f32[424,256]{1,0:T(8,128)}, f32[424,256]{1,0:T(8,128)}) custom-call(s32[16]{0:T(128)} %bitcast.34, f32[1536,256]{1,0:T(8,128)} %bitcast.36, f32[16,1536]{1,0:T(8,128)} %bitcast.30), custom_call_target="tpu_custom_call" | custom-call | flops 1024 | bytes 1024 | tf_op jit(solution)/shard_map/pallas_call | solution.py:345
  6.0 3.0 %collective-permute-start.4 = (f32[12,128]{1,0:T(8,128)S(1)}, f32[12,128]{1,0:T(8,128)S(1)}, u32[]{:S(2)}, u32[]{:S(2)}) collective-permute-start(f32[12,128]{1,0:T(8,128)S(1)} %shard_map.88), channel_id=1, source_target_pairs={{0,1},{1,0},{2,3},{3,2},{4,5},{5,4},{6,7},{7,6},{8,9},{9,8},{10,11... | collective-permute-start | bytes 18440 | tf_op jit(solution)/shard_map/ppermute | solution.py:19
  10.6 2.1 %collective-permute-start.5 = (f32[24,128]{1,0:T(8,128)S(1)}, f32[24,128]{1,0:T(8,128)S(1)}, u32[]{:S(2)}, u32[]{:S(2)}) collective-permute-start(f32[24,128]{1,0:T(8,128)S(1)} %pad_add_fusion.8), channel_id=1, source_target_pairs={{0,16},{8,24},{16,0},{24,8},{1,17},{9,25},{17,1},{25,9},{2,18},{10... | collective-permute-start | bytes 36872 | tf_op jit(solution)/shard_map/ppermute | solution.py:19
  13.4 1.4 collective-permute-start
  14.9 1.3 collective-permute-done.6
  16.3 5.0 %collective-permute-start.7 = (f32[96,128]{1,0:T(8,128)S(1)}, f32[96,128]{1,0:T(8,128)S(1)}, u32[]{:S(2)}, u32[]{:S(2)}) collective-permute-start(f32[96,128]{1,0:T(8,128)S(1)} %pad_add_fusion.6), channel_id=1, source_target_pairs={{0,4},{1,5},{2,6},{3,7},{4,0},{5,1},{6,2},{7,3},{8,12},{9,13},{10,... | collective-permute-start | bytes 147464 | tf_op jit(solution)/shard_map/ppermute | solution.py:19
  21.2 5.2 %collective-permute-done.7 = f32[96,128]{1,0:T(8,128)S(1)} collective-permute-done((f32[96,128]{1,0:T(8,128)S(1)}, f32[96,128]{1,0:T(8,128)S(1)}, u32[]{:S(2)}, u32[]{:S(2)}) %collective-permute-start.7) | collective-permute-done | bytes 49184 | tf_op jit(solution)/shard_map/ppermute | solution.py:19
  26.5 3.4 %shard_map.87 = (f32[384,256]{1,0:T(8,128)S(1)}, f32[384,256]{1,0:T(8,128)S(1)}, f32[1536,256]{1,0:T(8,128)S(1)}) custom-call(f32[6]{0:T(128)S(1)} %pad_maximum_fusion.refs_0_.flags, f32[1536,1536]{1,0:T(8,128)S(1)} %bitcast.16, f32[416,256]{1,0:T(8,128)S(1)} %copy-done, f32[416,256]{1,0:T(8,128)S(1)} %copy-done.2, ...), custom_call_target="tpu_custom_call" | custom-call | flops 1024 | bytes 1024 | tf_op jit(solution)/shard_map/pallas_call | solution.py:345
  30.0 2.7 %shard_map.89 = (f32[384,256]{1,0:T(8,128)S(1)}, f32[384,256]{1,0:T(8,128)S(1)}, f32[392,256]{1,0:T(8,128)S(1)}, f32[392,256]{1,0:T(8,128)S(1)}) custom-call(f32[6]{0:T(128)S(1)} %pad_maximum_fusion.refs_0_.flags, f32[1536,1536]{1,0:T(8,128)S(1)} %bitcast.17, f32[424,256]{1,0:T(8,128)S(1)} %copy-done.4, f32[424,256]{1,0:T(8,128)S(1)} %copy-done.5, ...), custom_call_target="tpu_custom_call" | custom-call | flops 8000000000 | bytes 1024 | tf_op jit(solution)/shard_map/pallas_call | solution.py:345
  34.1 2.0 %shard_map.90 = (f32[384,256]{1,0:T(8,128)S(1)}, f32[384,256]{1,0:T(8,128)S(1)}, f32[1,256]{1,0:T(1,128)S(1)}) custom-call(f32[6]{0:T(128)S(1)} %pad_maximum_fusion.refs_0_.flags, f32[1536,1536]{1,0:T(8,128)S(1)} %bitcast.18, f32[384,256]{1,0:T(8,128)S(1)} %get-tuple-element.86.refs_2_.refs_8_, f32[384,256]{1,0:T(8,128)S(1)} %get-tuple-element.87.refs_3_.refs_9_, ...), custom_call_target="tpu_custom_call" | custom-call | flops 1024 | bytes 1024 | tf_op jit(solution)/shard_map/pallas_call | solution.py:345
  37.0 4.2 %collective-permute-start.10 = (f32[192,128]{1,0:T(8,128)S(1)}, f32[192,128]{1,0:T(8,128)S(1)}, u32[]{:S(2)}, u32[]{:S(2)}) collective-permute-start(f32[192,128]{1,0:T(8,128)S(1)} %pad_add_fusion.3), channel_id=1, source_target_pairs={{0,2},{1,3},{2,0},{3,1},{4,6},{5,7},{6,4},{7,5},{8,10},{9,11},{10,... | collective-permute-start | bytes 294920 | tf_op jit(solution)/shard_map/ppermute | solution.py:19
  41.2 6.0 %collective-permute-done.10 = f32[192,128]{1,0:T(8,128)S(1)} collective-permute-done((f32[192,128]{1,0:T(8,128)S(1)}, f32[192,128]{1,0:T(8,128)S(1)}, u32[]{:S(2)}, u32[]{:S(2)}) %collective-permute-start.10) | collective-permute-done | bytes 98336 | tf_op jit(solution)/shard_map/ppermute | solution.py:19
  47.2 3.4 %shard_map.91 = (f32[384,256]{1,0:T(8,128)S(1)}, f32[384,256]{1,0:T(8,128)S(1)}, f32[1536,256]{1,0:T(8,128)S(1)}) custom-call(f32[6]{0:T(128)S(1)} %pad_maximum_fusion.refs_0_.flags, f32[1536,1536]{1,0:T(8,128)S(1)} %bitcast.24, f32[384,256]{1,0:T(8,128)S(1)} %get-tuple-element.97.refs_2_, f32[384,256]{1,0:T(8,128)S(1)} %get-tuple-element.98.refs_3_, ...), custom_call_target="tpu_custom_call" | custom-call | flops 1024 | bytes 1024 | tf_op jit(solution)/shard_map/pallas_call | solution.py:345
  50.7 2.7 %shard_map.92 = (f32[384,256]{1,0:T(8,128)S(1)}, f32[384,256]{1,0:T(8,128)S(1)}, f32[400,256]{1,0:T(8,128)S(1)}, f32[400,256]{1,0:T(8,128)S(1)}) custom-call(f32[6]{0:T(128)S(1)} %pad_maximum_fusion.refs_0_.flags, f32[1536,1536]{1,0:T(8,128)S(1)} %bitcast.25, f32[392,256]{1,0:T(8,128)S(1)} %get-tuple-element.95.refs_6_.refs_2_, ...), custom_call_target="tpu_custom_call" | custom-call | flops 8000000000 | bytes 1024 | tf_op jit(solution)/shard_map/pallas_call | solution.py:345
  53.4 2.3 %shard_map.93 = (f32[384,256]{1,0:T(8,128)S(1)}, f32[392,256]{1,0:T(8,128)S(1)}, f32[24,256]{1,0:T(8,128)S(1)}) custom-call(f32[6]{0:T(128)S(1)} %pad_maximum_fusion.refs_0_.flags, f32[1536,1536]{1,0:T(8,128)S(1)} %bitcast.26, f32[384,256]{1,0:T(8,128)S(1)} %get-tuple-element.101.refs_2_.refs_0_, f32[384,256]{1,0:T(8,128)S(1)} %get-tuple-element.102.refs_3_.refs_1_, ...), custom_call_target="tpu_custom_call" | custom-call | flops 1024 | bytes 1024 | tf_op jit(solution)/shard_map/pallas_call | solution.py:345
  55.7 1.6 %collective-permute-start.13 = (f32[24,256]{1,0:T(8,128)S(1)}, f32[24,256]{1,0:T(8,128)S(1)}, u32[]{:S(2)}, u32[]{:S(2)}) collective-permute-start(f32[24,256]{1,0:T(8,128)S(1)} %get-tuple-element.111), channel_id=1, source_target_pairs={{0,1},{1,0},{2,3},{3,2},{4,5},{5,4},{6,7},{7,6},{8,9},{9,8},{10,11... | collective-permute-start | bytes 73736 | tf_op jit(solution)/shard_map/ppermute | solution.py:19
  57.3 2.3 %collective-permute-done.13 = f32[24,256]{1,0:T(8,128)S(1)} collective-permute-done((f32[24,256]{1,0:T(8,128)S(1)}, f32[24,256]{1,0:T(8,128)S(1)}, u32[]{:S(2)}, u32[]{:S(2)}) %collective-permute-start.13) | collective-permute-done | bytes 24608 | tf_op jit(solution)/shard_map/ppermute | solution.py:19
  59.6 3.1 %collective-permute-start.14 = (f32[48,256]{1,0:T(8,128)S(1)}, f32[48,256]{1,0:T(8,128)S(1)}, u32[]{:S(2)}, u32[]{:S(2)}) collective-permute-start(f32[48,256]{1,0:T(8,128)S(1)} %pad_add_fusion.5), channel_id=1, source_target_pairs={{0,4},{1,5},{2,6},{3,7},{4,0},{5,1},{6,2},{7,3},{8,12},{9,13},{10,... | collective-permute-start | bytes 147464 | tf_op jit(solution)/shard_map/ppermute | solution.py:19
  62.7 2.1 %collective-permute-done.14 = f32[48,256]{1,0:T(8,128)S(1)} collective-permute-done((f32[48,256]{1,0:T(8,128)S(1)}, f32[48,256]{1,0:T(8,128)S(1)}, u32[]{:S(2)}, u32[]{:S(2)}) %collective-permute-start.14) | collective-permute-done | bytes 49184 | tf_op jit(solution)/shard_map/ppermute | solution.py:19
  64.7 2.0 %collective-permute-start.15 = (f32[96,256]{1,0:T(8,128)S(1)}, f32[96,256]{1,0:T(8,128)S(1)}, u32[]{:S(2)}, u32[]{:S(2)}) collective-permute-start(f32[96,256]{1,0:T(8,128)S(1)} %pad_add_fusion.2.refs_0_), channel_id=1, source_target_pairs={{0,2},{1,3},{2,0},{3,1},{4,6},{5,7},{6,4},{7,5},{8,10},{9,11},{10,... | collective-permute-start | bytes 294920 | tf_op jit(solution)/shard_map/ppermute | solution.py:19
  66.8 1.0 collective-permute-start.20
  68.5 0.9 collective-permute-done.15.refs_1_
  70.3 4.5 %collective-permute-start.16 = (f32[384,256]{1,0:T(8,128)S(1)}, f32[384,256]{1,0:T(8,128)S(1)}, u32[]{:S(2)}, u32[]{:S(2)}) collective-permute-start(f32[384,256]{1,0:T(8,128)S(1)} %get-tuple-element.116.refs_2_.refs_8_), channel_id=1, source_target_pairs={{0,8},{8,0},{16,24},{24,16},{1,9},{9,1},{17,25},{25,17},{2,10},{10... | collective-permute-start | bytes 1179656 | tf_op jit(solution)/shard_map/ppermute | solution.py:19
  75.5 1.3 collective-permute-done.18
  77.0 3.5 %shard_map.96.refs_10_.refs_11_.refs_18_ = f32[1536,128]{1,0:T(8,128)S(1)} custom-call(f32[6]{0:T(128)S(1)} %pad_maximum_fusion.refs_0_.flags, f32[416,256]{1,0:T(8,128)S(1)} %collective-permute-done.refs_4_.near0, f32[416,256]{1,0:T(8,128)S(1)} %collective-permute-done.1.refs_5_.near1, f32[424,256]{1,0:T(8,128)S(1)} %collective-permute-done.2.refs_4_.near2, ...), custom_call_target="tpu_custom_call" | custom-call | flops 1024 | bytes 1024 | tf_op jit(solution)/shard_map/pallas_call | solution.py:345
  80.5 2.8 %collective-permute-done.19 = f32[136,256]{1,0:T(8,128)S(1)} collective-permute-done((f32[136,256]{1,0:T(8,128)S(1)}, f32[136,256]{1,0:T(8,128)S(1)}, u32[]{:S(2)}, u32[]{:S(2)}) %collective-permute-start.19) | collective-permute-done | bytes 139296 | tf_op jit(solution)/shard_map/ppermute | solution.py:19
  83.9 3.8 %shard_map.97 = (f32[384,256]{1,0:T(8,128)S(1)}, f32[384,256]{1,0:T(8,128)S(1)}, f32[384,256]{1,0:T(8,128)S(1)}, f32[384,256]{1,0:T(8,128)S(1)}, f32[1536,256]{1,0:T(8,128)S(1)}) custom-call(f32[6]{0:T(128)S(1)} %pad_maximum_fusion.refs_0_.flags, f32[1536,1536]{1,0:T(8,128)S(1)} %bitcast.19, f32[384,256]{1,0:T(8,128)S(1)} %get-tuple-element.116.refs_2_.refs_8_, ...), custom_call_target="tpu_custom_call" | custom-call | flops 1024 | bytes 1024 | tf_op jit(solution)/shard_map/pallas_call | solution.py:345
  87.6 3.2 %shard_map.98 = (f32[384,256]{1,0:T(8,128)S(1)}, f32[384,256]{1,0:T(8,128)S(1)}, f32[384,256]{1,0:T(8,128)S(1)}, f32[384,256]{1,0:T(8,128)S(1)}, f32[392,256]{1,0:T(8,128)S(1)}, /*index=5*/f32[392,256]{1,0:T(8,128)S(1)}) custom-call(f32[6]{0:T(128)S(1)} %pad_maximum_fusion.refs_0_.flags, f32[1536,1536]{1,0:T(8,128)S(1)} %bitcast.20, ...), custom_call_target="tpu_custom_call" | custom-call | flops 8000000000 | bytes 1024 | tf_op jit(solution)/shard_map/pallas_call | solution.py:345
  90.9 1.4 collective-permute-start.24
  93.0 2.0 %shard_map.99 = (f32[384,256]{1,0:T(8,128)S(1)}, f32[384,256]{1,0:T(8,128)S(1)}, f32[1,256]{1,0:T(1,128)S(1)}) custom-call(f32[6]{0:T(128)S(1)} %pad_maximum_fusion.refs_0_.flags, f32[1536,1536]{1,0:T(8,128)S(1)} %bitcast.21, f32[384,256]{1,0:T(8,128)S(1)} %get-tuple-element.121.refs_2_.refs_9_, f32[384,256]{1,0:T(8,128)S(1)} %get-tuple-element.122.refs_3_.refs_10_, ...), custom_call_target="tpu_custom_call" | custom-call | flops 1024 | bytes 1024 | tf_op jit(solution)/shard_map/pallas_call | solution.py:345
  95.0 0.9 collective-permute-start.23
  96.8 3.4 %shard_map.100 = (f32[384,256]{1,0:T(8,128)S(1)}, f32[384,256]{1,0:T(8,128)S(1)}, f32[1536,256]{1,0:T(8,128)S(1)}) custom-call(f32[6]{0:T(128)S(1)} %pad_maximum_fusion.refs_0_.flags, f32[1536,1536]{1,0:T(8,128)S(1)} %bitcast.27, f32[384,256]{1,0:T(8,128)S(1)} %get-tuple-element.130.refs_2_, f32[384,256]{1,0:T(8,128)S(1)} %get-tuple-element.131.refs_3_, ...), custom_call_target="tpu_custom_call" | custom-call | flops 1024 | bytes 1024 | tf_op jit(solution)/shard_map/pallas_call | solution.py:345
  100.2 9.0 %collective-permute-done.24.refs_4_ = f32[392,256]{1,0:T(8,128)S(1)} collective-permute-done((f32[392,256]{1,0:T(8,128)S(1)}, f32[392,256]{1,0:T(8,128)S(1)}, u32[]{:S(2)}, u32[]{:S(2)}) %collective-permute-start.24) | collective-permute-done | bytes 401440 | tf_op jit(solution)/shard_map/ppermute | solution.py:19
  109.2 2.7 %shard_map.101 = (f32[384,256]{1,0:T(8,128)S(1)}, f32[384,256]{1,0:T(8,128)S(1)}, f32[400,256]{1,0:T(8,128)S(1)}, f32[400,256]{1,0:T(8,128)S(1)}) custom-call(f32[6]{0:T(128)S(1)} %pad_maximum_fusion.refs_0_.flags, f32[1536,1536]{1,0:T(8,128)S(1)} %bitcast.28, f32[392,256]{1,0:T(8,128)S(1)} %get-tuple-element.128.refs_6_.refs_2_, ...), custom_call_target="tpu_custom_call" | custom-call | flops 8000000000 | bytes 1024 | tf_op jit(solution)/shard_map/pallas_call | solution.py:345
  111.9 2.5 %shard_map.102 = (f32[384,256]{1,0:T(8,128)S(1)}, f32[392,256]{1,0:T(8,128)S(1)}, f32[24,256]{1,0:T(8,128)S(1)}) custom-call(f32[6]{0:T(128)S(1)} %pad_maximum_fusion.refs_0_.flags, f32[1536,1536]{1,0:T(8,128)S(1)} %bitcast.29, f32[384,256]{1,0:T(8,128)S(1)} %get-tuple-element.132.refs_2_.refs_4_, f32[384,256]{1,0:T(8,128)S(1)} %get-tuple-element.133.refs_3_.refs_5_, ...), custom_call_target="tpu_custom_call" | custom-call | flops 1024 | bytes 1024 | tf_op jit(solution)/shard_map/pallas_call | solution.py:345
  114.4 2.5 %collective-permute-start.26 = (f32[24,256]{1,0:T(8,128)S(1)}, f32[24,256]{1,0:T(8,128)S(1)}, u32[]{:S(2)}, u32[]{:S(2)}) collective-permute-start(f32[24,256]{1,0:T(8,128)S(1)} %get-tuple-element.140), channel_id=1, source_target_pairs={{0,1},{1,0},{2,3},{3,2},{4,5},{5,4},{6,7},{7,6},{8,9},{9,8},{10,11... | collective-permute-start | bytes 73736 | tf_op jit(solution)/shard_map/ppermute | solution.py:19
  116.9 1.8 %collective-permute-done.26 = f32[24,256]{1,0:T(8,128)S(1)} collective-permute-done((f32[24,256]{1,0:T(8,128)S(1)}, f32[24,256]{1,0:T(8,128)S(1)}, u32[]{:S(2)}, u32[]{:S(2)}) %collective-permute-start.26) | collective-permute-done | bytes 24608 | tf_op jit(solution)/shard_map/ppermute | solution.py:19
  118.7 3.2 %collective-permute-start.27 = (f32[48,256]{1,0:T(8,128)S(1)}, f32[48,256]{1,0:T(8,128)S(1)}, u32[]{:S(2)}, u32[]{:S(2)}) collective-permute-start(f32[48,256]{1,0:T(8,128)S(1)} %pad_add_fusion.4), channel_id=1, source_target_pairs={{0,4},{1,5},{2,6},{3,7},{4,0},{5,1},{6,2},{7,3},{8,12},{9,13},{10,... | collective-permute-start | bytes 147464 | tf_op jit(solution)/shard_map/ppermute | solution.py:19
  121.9 2.5 %collective-permute-done.27 = f32[48,256]{1,0:T(8,128)S(1)} collective-permute-done((f32[48,256]{1,0:T(8,128)S(1)}, f32[48,256]{1,0:T(8,128)S(1)}, u32[]{:S(2)}, u32[]{:S(2)}) %collective-permute-start.27) | collective-permute-done | bytes 49184 | tf_op jit(solution)/shard_map/ppermute | solution.py:19
  124.4 1.7 %collective-permute-start.28 = (f32[96,256]{1,0:T(8,128)S(1)}, f32[96,256]{1,0:T(8,128)S(1)}, u32[]{:S(2)}, u32[]{:S(2)}) collective-permute-start(f32[96,256]{1,0:T(8,128)S(1)} %pad_add_fusion.1.refs_0_), channel_id=1, source_target_pairs={{0,2},{1,3},{2,0},{3,1},{4,6},{5,7},{6,4},{7,5},{8,10},{9,11},{10,... | collective-permute-start | bytes 294920 | tf_op jit(solution)/shard_map/ppermute | solution.py:19
  126.2 1.7 %collective-permute-start.33 = (f32[400,256]{1,0:T(8,128)S(1)}, f32[400,256]{1,0:T(8,128)S(1)}, u32[]{:S(2)}, u32[]{:S(2)}) collective-permute-start(f32[400,256]{1,0:T(8,128)S(1)} %get-tuple-element.150.refs_6_.refs_3_), channel_id=1, source_target_pairs={{0,1},{1,0},{2,3},{3,2},{4,5},{5,4},{6,7},{7,6},{8,9},{9,8},{10,11... | collective-permute-start | bytes 1228808 | tf_op jit(solution)/shard_map/ppermute | solution.py:19
  129.8 2.7 %collective-permute-start.31 = (f32[384,256]{1,0:T(8,128)S(1)}, f32[384,256]{1,0:T(8,128)S(1)}, u32[]{:S(2)}, u32[]{:S(2)}) collective-permute-start(f32[384,256]{1,0:T(8,128)S(1)} %get-tuple-element.148.refs_1_), channel_id=1, source_target_pairs={{0,8},{8,0},{16,24},{24,16},{1,9},{9,1},{17,25},{25,17},{2,10},{10... | collective-permute-start | bytes 1179656 | tf_op jit(solution)/shard_map/ppermute | solution.py:19
  133.2 1.3 collective-permute-done.29
  134.7 6.5 %collective-permute-done.30 = f32[136,256]{1,0:T(8,128)S(1)} collective-permute-done((f32[136,256]{1,0:T(8,128)S(1)}, f32[136,256]{1,0:T(8,128)S(1)}, u32[]{:S(2)}, u32[]{:S(2)}) %collective-permute-start.30) | collective-permute-done | bytes 139296 | tf_op jit(solution)/shard_map/ppermute | solution.py:19
  141.8 1.2 shard_map.105
  143.0 0.9 collective-permute-done.33.refs_7_
  144.0 3.7 %shard_map.106 = f32[1536,256]{1,0:T(8,128)} custom-call(f32[6]{0:T(128)S(1)} %pad_maximum_fusion.refs_0_.flags, f32[384,256]{1,0:T(8,128)S(1)} %get-tuple-element.148.refs_1_, f32[392,256]{1,0:T(8,128)S(1)} %get-tuple-element.149.refs_2_, f32[400,256]{1,0:T(8,128)S(1)} %get-tuple-element.150.refs_6_.refs_3_, ...), custom_call_target="tpu_custom_call" | custom-call | flops 1024 | bytes 1024 | tf_op jit(solution)/shard_map/pallas_call | solution.py:345
  (96 shorter events, 13.4 us)
Async XLA Ops:
  0.6 4.7 %copy-start.3 = (s32[1,1,16]{2,1,0:T(1,128)S(1)}, s32[1,1,16]{2,1,0:T(1,128)}, u32[]{:S(2)}) copy-start(s32[1,1,16]{2,1,0:T(1,128)} %param.11) | copy-start | bytes 196
  0.6 4.7 %copy-start.6 = (f32[4,128]{1,0:T(4,128)S(1)}, f32[4,128]{1,0:T(4,128)}, u32[]{:S(2)}) copy-start(f32[4,128]{1,0:T(4,128)} %inverse) | copy-start | bytes 6148
  5.3 21.1 %slice-start = ((s8[9437184]{0:T(1024)(128)(4,1)}), s8[4194304]{0:T(1024)(128)(4,1)S(1)}, s32[]{:S(2)}) async-start(s8[9437184]{0:T(1024)(128)(4,1)} %bitcast.14), calls=%async_computation | async-start | bytes 8388608
  5.4 3.6 %copy-start.4 = (f32[424,256]{1,0:T(8,128)S(1)}, f32[424,256]{1,0:T(8,128)}, u32[]{:S(2)}) copy-start(f32[424,256]{1,0:T(8,128)} %get-tuple-element.88.refs_2_) | copy-start | bytes 1302532
  5.4 4.1 %copy-start.5 = (f32[424,256]{1,0:T(8,128)S(1)}, f32[424,256]{1,0:T(8,128)}, u32[]{:S(2)}) copy-start(f32[424,256]{1,0:T(8,128)} %get-tuple-element.89.refs_3_) | copy-start | bytes 1302532
  5.4 7.3 %copy-start.2 = (f32[416,256]{1,0:T(8,128)S(1)}, f32[416,256]{1,0:T(8,128)}, u32[]{:S(2)}) copy-start(f32[416,256]{1,0:T(8,128)} %get-tuple-element.83.refs_3_) | copy-start | bytes 1277956
  5.4 8.0 %copy-start = (f32[416,256]{1,0:T(8,128)S(1)}, f32[416,256]{1,0:T(8,128)}, u32[]{:S(2)}) copy-start(f32[416,256]{1,0:T(8,128)} %get-tuple-element.81.refs_2_.sent) | copy-start | bytes 1277956
  5.4 21.1 %slice-start.1 = ((s8[9437184]{0:T(1024)(128)(4,1)}), s8[4194304]{0:T(1024)(128)(4,1)S(1)}, s32[]{:S(2)}) async-start(s8[9437184]{0:T(1024)(128)(4,1)} %bitcast.14), calls=%async_computation.1 | async-start | bytes 8388608
  5.4 21.1 %slice-start.2 = ((s8[9437184]{0:T(1024)(128)(4,1)}), s8[1048576]{0:T(1024)(128)(4,1)S(1)}, s32[]{:S(2)}) async-start(s8[9437184]{0:T(1024)(128)(4,1)} %bitcast.14), calls=%async_computation.2 | async-start | bytes 2097152
  6.0 4.6 %collective-permute-start.4 = (f32[12,128]{1,0:T(8,128)S(1)}, f32[12,128]{1,0:T(8,128)S(1)}, u32[]{:S(2)}, u32[]{:S(2)}) collective-permute-start(f32[12,128]{1,0:T(8,128)S(1)} %shard_map.88), channel_id=1, source_target_pairs={{0,1},{1,0},{2,3},{3,2},{4,5},{5,4},{6,7},{7,6},{8,9},{9,8},{10,11... | collective-permute-start | bytes 18440 | tf_op jit(solution)/shard_map/ppermute | solution.py:19
  9.0 21.0 %collective-permute-start.2 = (f32[424,256]{1,0:T(8,128)S(1)}, f32[424,256]{1,0:T(8,128)S(1)}, u32[]{:S(2)}, u32[]{:S(2)}) collective-permute-start(f32[424,256]{1,0:T(8,128)S(1)} %copy-done.4), channel_id=1, source_target_pairs={{0,1},{1,0},{2,3},{3,2},{4,5},{5,4},{6,7},{7,6},{8,9},{9,8},{10,11... | collective-permute-start | bytes 1302536 | tf_op jit(solution)/shard_map/ppermute | solution.py:19
  9.5 20.5 %collective-permute-start.3 = (f32[424,256]{1,0:T(8,128)S(1)}, f32[424,256]{1,0:T(8,128)S(1)}, u32[]{:S(2)}, u32[]{:S(2)}) collective-permute-start(f32[424,256]{1,0:T(8,128)S(1)} %copy-done.5), channel_id=1, source_target_pairs={{1,2},{2,1},{3,4},{4,3},{5,6},{6,5},{9,10},{10,9},{11,12},{12,11},... | collective-permute-start | bytes 1302536 | tf_op jit(solution)/shard_map/ppermute | solution.py:26
  10.6 4.2 %collective-permute-start.5 = (f32[24,128]{1,0:T(8,128)S(1)}, f32[24,128]{1,0:T(8,128)S(1)}, u32[]{:S(2)}, u32[]{:S(2)}) collective-permute-start(f32[24,128]{1,0:T(8,128)S(1)} %pad_add_fusion.8), channel_id=1, source_target_pairs={{0,16},{8,24},{16,0},{24,8},{1,17},{9,25},{17,1},{25,9},{2,18},{10... | collective-permute-start | bytes 36872 | tf_op jit(solution)/shard_map/ppermute | solution.py:19
  12.7 13.8 %collective-permute-start.1 = (f32[416,256]{1,0:T(8,128)S(1)}, f32[416,256]{1,0:T(8,128)S(1)}, u32[]{:S(2)}, u32[]{:S(2)}) collective-permute-start(f32[416,256]{1,0:T(8,128)S(1)} %copy-done.2), channel_id=1, source_target_pairs={{8,16},{16,8},{9,17},{17,9},{10,18},{18,10},{11,19},{19,11},{12,20... | collective-permute-start | bytes 1277960 | tf_op jit(solution)/shard_map/ppermute | solution.py:26
  13.4 13.1 %collective-permute-start = (f32[416,256]{1,0:T(8,128)S(1)}, f32[416,256]{1,0:T(8,128)S(1)}, u32[]{:S(2)}, u32[]{:S(2)}) collective-permute-start(f32[416,256]{1,0:T(8,128)S(1)} %copy-done), channel_id=1, source_target_pairs={{0,8},{8,0},{16,24},{24,16},{1,9},{9,1},{17,25},{25,17},{2,10},{10... | collective-permute-start | bytes 1277960 | tf_op jit(solution)/shard_map/ppermute | solution.py:19
  14.8 1.4 collective-permute-start.6
  16.3 10.2 %collective-permute-start.7 = (f32[96,128]{1,0:T(8,128)S(1)}, f32[96,128]{1,0:T(8,128)S(1)}, u32[]{:S(2)}, u32[]{:S(2)}) collective-permute-start(f32[96,128]{1,0:T(8,128)S(1)} %pad_add_fusion.6), channel_id=1, source_target_pairs={{0,4},{1,5},{2,6},{3,7},{4,0},{5,1},{6,2},{7,3},{8,12},{9,13},{10,... | collective-permute-start | bytes 147464 | tf_op jit(solution)/shard_map/ppermute | solution.py:19
  30.0 17.2 %slice-start.3 = ((s8[9437184]{0:T(1024)(128)(4,1)}), s8[4194304]{0:T(1024)(128)(4,1)S(1)}, s32[]{:S(2)}) async-start(s8[9437184]{0:T(1024)(128)(4,1)} %bitcast.22), calls=%async_computation.3 | async-start | bytes 8388608
  30.0 17.2 %slice-start.4 = ((s8[9437184]{0:T(1024)(128)(4,1)}), s8[4194304]{0:T(1024)(128)(4,1)S(1)}, s32[]{:S(2)}) async-start(s8[9437184]{0:T(1024)(128)(4,1)} %bitcast.22), calls=%async_computation.4 | async-start | bytes 8388608
  30.0 17.2 %slice-start.5 = ((s8[9437184]{0:T(1024)(128)(4,1)}), s8[1048576]{0:T(1024)(128)(4,1)S(1)}, s32[]{:S(2)}) async-start(s8[9437184]{0:T(1024)(128)(4,1)} %bitcast.22), calls=%async_computation.5 | async-start | bytes 2097152
  32.7 17.9 %collective-permute-start.11 = (f32[392,256]{1,0:T(8,128)S(1)}, f32[392,256]{1,0:T(8,128)S(1)}, u32[]{:S(2)}, u32[]{:S(2)}) collective-permute-start(f32[392,256]{1,0:T(8,128)S(1)} %get-tuple-element.95.refs_6_.refs_2_), channel_id=1, source_target_pairs={{0,1},{1,0},{2,3},{3,2},{4,5},{5,4},{6,7},{7,6},{8,9},{9,8},{10,11... | collective-permute-start | bytes 1204232 | tf_op jit(solution)/shard_map/ppermute | solution.py:19
  33.4 17.3 %collective-permute-start.12 = (f32[392,256]{1,0:T(8,128)S(1)}, f32[392,256]{1,0:T(8,128)S(1)}, u32[]{:S(2)}, u32[]{:S(2)}) collective-permute-start(f32[392,256]{1,0:T(8,128)S(1)} %get-tuple-element.96.refs_7_.refs_3_), channel_id=1, source_target_pairs={{1,2},{2,1},{3,4},{4,3},{5,6},{6,5},{9,10},{10,9},{11,12},{12,11},... | collective-permute-start | bytes 1204232 | tf_op jit(solution)/shard_map/ppermute | solution.py:26
  36.1 11.1 %collective-permute-start.8 = (f32[384,256]{1,0:T(8,128)S(1)}, f32[384,256]{1,0:T(8,128)S(1)}, u32[]{:S(2)}, u32[]{:S(2)}) collective-permute-start(f32[384,256]{1,0:T(8,128)S(1)} %get-tuple-element.97.refs_2_), channel_id=1, source_target_pairs={{0,8},{8,0},{16,24},{24,16},{1,9},{9,1},{17,25},{25,17},{2,10},{10... | collective-permute-start | bytes 1179656 | tf_op jit(solution)/shard_map/ppermute | solution.py:19
  36.1 11.0 %collective-permute-start.9 = (f32[384,256]{1,0:T(8,128)S(1)}, f32[384,256]{1,0:T(8,128)S(1)}, u32[]{:S(2)}, u32[]{:S(2)}) collective-permute-start(f32[384,256]{1,0:T(8,128)S(1)} %get-tuple-element.98.refs_3_), channel_id=1, source_target_pairs={{8,16},{16,8},{9,17},{17,9},{10,18},{18,10},{11,19},{19,11},{12,20... | collective-permute-start | bytes 1179656 | tf_op jit(solution)/shard_map/ppermute | solution.py:26
  37.0 10.1 %collective-permute-start.10 = (f32[192,128]{1,0:T(8,128)S(1)}, f32[192,128]{1,0:T(8,128)S(1)}, u32[]{:S(2)}, u32[]{:S(2)}) collective-permute-start(f32[192,128]{1,0:T(8,128)S(1)} %pad_add_fusion.3), channel_id=1, source_target_pairs={{0,2},{1,3},{2,0},{3,1},{4,6},{5,7},{6,4},{7,5},{8,10},{9,11},{10,... | collective-permute-start | bytes 294920 | tf_op jit(solution)/shard_map/ppermute | solution.py:19
  50.7 2.7 %copy-start.1 = (f32[1,1,16,1536]{3,2,1,0:T(8,128)S(1)}, f32[1,1,16,1536]{3,2,1,0:T(8,128)}, u32[]{:S(2)}) copy-start(f32[1,1,16,1536]{3,2,1,0:T(8,128)} %param.10) | copy-start | bytes 294916
  55.7 3.9 %collective-permute-start.13 = (f32[24,256]{1,0:T(8,128)S(1)}, f32[24,256]{1,0:T(8,128)S(1)}, u32[]{:S(2)}, u32[]{:S(2)}) collective-permute-start(f32[24,256]{1,0:T(8,128)S(1)} %get-tuple-element.111), channel_id=1, source_target_pairs={{0,1},{1,0},{2,3},{3,2},{4,5},{5,4},{6,7},{7,6},{8,9},{9,8},{10,11... | collective-permute-start | bytes 73736 | tf_op jit(solution)/shard_map/ppermute | solution.py:19
  59.6 5.1 %collective-permute-start.14 = (f32[48,256]{1,0:T(8,128)S(1)}, f32[48,256]{1,0:T(8,128)S(1)}, u32[]{:S(2)}, u32[]{:S(2)}) collective-permute-start(f32[48,256]{1,0:T(8,128)S(1)} %pad_add_fusion.5), channel_id=1, source_target_pairs={{0,4},{1,5},{2,6},{3,7},{4,0},{5,1},{6,2},{7,3},{8,12},{9,13},{10,... | collective-permute-start | bytes 147464 | tf_op jit(solution)/shard_map/ppermute | solution.py:19
  64.7 4.7 %collective-permute-start.15 = (f32[96,256]{1,0:T(8,128)S(1)}, f32[96,256]{1,0:T(8,128)S(1)}, u32[]{:S(2)}, u32[]{:S(2)}) collective-permute-start(f32[96,256]{1,0:T(8,128)S(1)} %pad_add_fusion.2.refs_0_), channel_id=1, source_target_pairs={{0,2},{1,3},{2,0},{3,1},{4,6},{5,7},{6,4},{7,5},{8,10},{9,11},{10,... | collective-permute-start | bytes 294920 | tf_op jit(solution)/shard_map/ppermute | solution.py:19
  66.8 20.9 %collective-permute-start.20 = (f32[400,256]{1,0:T(8,128)S(1)}, f32[400,256]{1,0:T(8,128)S(1)}, u32[]{:S(2)}, u32[]{:S(2)}) collective-permute-start(f32[400,256]{1,0:T(8,128)S(1)} %get-tuple-element.123.refs_6_.refs_2_.refs_10_), channel_id=1, source_target_pairs={{0,1},{1,0},{2,3},{3,2},{4,5},{5,4},{6,7},{7,6},{8,9},{9,8},{10,11... | collective-permute-start | bytes 1228808 | tf_op jit(solution)/shard_map/ppermute | solution.py:19
  67.8 19.8 %collective-permute-start.21 = (f32[400,256]{1,0:T(8,128)S(1)}, f32[400,256]{1,0:T(8,128)S(1)}, u32[]{:S(2)}, u32[]{:S(2)}) collective-permute-start(f32[400,256]{1,0:T(8,128)S(1)} %get-tuple-element.124.refs_7_.refs_3_.refs_11_), channel_id=1, source_target_pairs={{1,2},{2,1},{3,4},{4,3},{5,6},{6,5},{9,10},{10,9},{11,12},{12,11},... | collective-permute-start | bytes 1228808 | tf_op jit(solution)/shard_map/ppermute | solution.py:26
  69.4 14.4 %collective-permute-start.17 = (f32[392,256]{1,0:T(8,128)S(1)}, f32[392,256]{1,0:T(8,128)S(1)}, u32[]{:S(2)}, u32[]{:S(2)}) collective-permute-start(f32[392,256]{1,0:T(8,128)S(1)} %get-tuple-element.117.refs_3_.refs_9_), channel_id=1, source_target_pairs={{8,16},{16,8},{9,17},{17,9},{10,18},{18,10},{11,19},{19,11},{12,20... | collective-permute-start | bytes 1204232 | tf_op jit(solution)/shard_map/ppermute | solution.py:26
  70.3 13.5 %collective-permute-start.16 = (f32[384,256]{1,0:T(8,128)S(1)}, f32[384,256]{1,0:T(8,128)S(1)}, u32[]{:S(2)}, u32[]{:S(2)}) collective-permute-start(f32[384,256]{1,0:T(8,128)S(1)} %get-tuple-element.116.refs_2_.refs_8_), channel_id=1, source_target_pairs={{0,8},{8,0},{16,24},{24,16},{1,9},{9,1},{17,25},{25,17},{2,10},{10... | collective-permute-start | bytes 1179656 | tf_op jit(solution)/shard_map/ppermute | solution.py:19
  75.4 1.4 collective-permute-start.18
  76.8 6.4 %collective-permute-start.19 = (f32[136,256]{1,0:T(8,128)S(1)}, f32[136,256]{1,0:T(8,128)S(1)}, u32[]{:S(2)}, u32[]{:S(2)}) collective-permute-start(f32[136,256]{1,0:T(8,128)S(1)} %add.149), channel_id=1, source_target_pairs={{0,16},{8,24},{16,0},{24,8},{1,17},{9,25},{17,1},{25,9},{2,18},{10... | collective-permute-start | bytes 417800 | tf_op jit(solution)/shard_map/ppermute | solution.py:19
  90.9 18.3 %collective-permute-start.24 = (f32[392,256]{1,0:T(8,128)S(1)}, f32[392,256]{1,0:T(8,128)S(1)}, u32[]{:S(2)}, u32[]{:S(2)}) collective-permute-start(f32[392,256]{1,0:T(8,128)S(1)} %get-tuple-element.128.refs_6_.refs_2_), channel_id=1, source_target_pairs={{0,1},{1,0},{2,3},{3,2},{4,5},{5,4},{6,7},{7,6},{8,9},{9,8},{10,11... | collective-permute-start | bytes 1204232 | tf_op jit(solution)/shard_map/ppermute | solution.py:19
  92.3 16.9 %collective-permute-start.25 = (f32[392,256]{1,0:T(8,128)S(1)}, f32[392,256]{1,0:T(8,128)S(1)}, u32[]{:S(2)}, u32[]{:S(2)}) collective-permute-start(f32[392,256]{1,0:T(8,128)S(1)} %get-tuple-element.129.refs_7_.refs_3_), channel_id=1, source_target_pairs={{1,2},{2,1},{3,4},{4,3},{5,6},{6,5},{9,10},{10,9},{11,12},{12,11},... | collective-permute-start | bytes 1204232 | tf_op jit(solution)/shard_map/ppermute | solution.py:26
  95.0 1.8 %collective-permute-start.22 = (f32[384,256]{1,0:T(8,128)S(1)}, f32[384,256]{1,0:T(8,128)S(1)}, u32[]{:S(2)}, u32[]{:S(2)}) collective-permute-start(f32[384,256]{1,0:T(8,128)S(1)} %get-tuple-element.130.refs_2_), channel_id=1, source_target_pairs={{0,8},{8,0},{16,24},{24,16},{1,9},{9,1},{17,25},{25,17},{2,10},{10... | collective-permute-start | bytes 1179656 | tf_op jit(solution)/shard_map/ppermute | solution.py:19
  95.0 1.7 %collective-permute-start.23 = (f32[384,256]{1,0:T(8,128)S(1)}, f32[384,256]{1,0:T(8,128)S(1)}, u32[]{:S(2)}, u32[]{:S(2)}) collective-permute-start(f32[384,256]{1,0:T(8,128)S(1)} %get-tuple-element.131.refs_3_), channel_id=1, source_target_pairs={{8,16},{16,8},{9,17},{17,9},{10,18},{18,10},{11,19},{19,11},{12,20... | collective-permute-start | bytes 1179656 | tf_op jit(solution)/shard_map/ppermute | solution.py:26
  114.4 4.4 %collective-permute-start.26 = (f32[24,256]{1,0:T(8,128)S(1)}, f32[24,256]{1,0:T(8,128)S(1)}, u32[]{:S(2)}, u32[]{:S(2)}) collective-permute-start(f32[24,256]{1,0:T(8,128)S(1)} %get-tuple-element.140), channel_id=1, source_target_pairs={{0,1},{1,0},{2,3},{3,2},{4,5},{5,4},{6,7},{7,6},{8,9},{9,8},{10,11... | collective-permute-start | bytes 73736 | tf_op jit(solution)/shard_map/ppermute | solution.py:19
  118.7 5.7 %collective-permute-start.27 = (f32[48,256]{1,0:T(8,128)S(1)}, f32[48,256]{1,0:T(8,128)S(1)}, u32[]{:S(2)}, u32[]{:S(2)}) collective-permute-start(f32[48,256]{1,0:T(8,128)S(1)} %pad_add_fusion.4), channel_id=1, source_target_pairs={{0,4},{1,5},{2,6},{3,7},{4,0},{5,1},{6,2},{7,3},{8,12},{9,13},{10,... | collective-permute-start | bytes 147464 | tf_op jit(solution)/shard_map/ppermute | solution.py:19
  124.4 4.7 %collective-permute-start.28 = (f32[96,256]{1,0:T(8,128)S(1)}, f32[96,256]{1,0:T(8,128)S(1)}, u32[]{:S(2)}, u32[]{:S(2)}) collective-permute-start(f32[96,256]{1,0:T(8,128)S(1)} %pad_add_fusion.1.refs_0_), channel_id=1, source_target_pairs={{0,2},{1,3},{2,0},{3,1},{4,6},{5,7},{6,4},{7,5},{8,10},{9,11},{10,... | collective-permute-start | bytes 294920 | tf_op jit(solution)/shard_map/ppermute | solution.py:19
  126.2 17.8 %collective-permute-start.33 = (f32[400,256]{1,0:T(8,128)S(1)}, f32[400,256]{1,0:T(8,128)S(1)}, u32[]{:S(2)}, u32[]{:S(2)}) collective-permute-start(f32[400,256]{1,0:T(8,128)S(1)} %get-tuple-element.150.refs_6_.refs_3_), channel_id=1, source_target_pairs={{0,1},{1,0},{2,3},{3,2},{4,5},{5,4},{6,7},{7,6},{8,9},{9,8},{10,11... | collective-permute-start | bytes 1228808 | tf_op jit(solution)/shard_map/ppermute | solution.py:19
  127.9 16.1 %collective-permute-start.34 = (f32[400,256]{1,0:T(8,128)S(1)}, f32[400,256]{1,0:T(8,128)S(1)}, u32[]{:S(2)}, u32[]{:S(2)}) collective-permute-start(f32[400,256]{1,0:T(8,128)S(1)} %get-tuple-element.151.refs_7_.refs_4_), channel_id=1, source_target_pairs={{1,2},{2,1},{3,4},{4,3},{5,6},{6,5},{9,10},{10,9},{11,12},{12,11},... | collective-permute-start | bytes 1228808 | tf_op jit(solution)/shard_map/ppermute | solution.py:26
  129.2 14.8 %collective-permute-start.32 = (f32[392,256]{1,0:T(8,128)S(1)}, f32[392,256]{1,0:T(8,128)S(1)}, u32[]{:S(2)}, u32[]{:S(2)}) collective-permute-start(f32[392,256]{1,0:T(8,128)S(1)} %get-tuple-element.149.refs_2_), channel_id=1, source_target_pairs={{8,16},{16,8},{9,17},{17,9},{10,18},{18,10},{11,19},{19,11},{12,20... | collective-permute-start | bytes 1204232 | tf_op jit(solution)/shard_map/ppermute | solution.py:26
  129.8 14.1 %collective-permute-start.31 = (f32[384,256]{1,0:T(8,128)S(1)}, f32[384,256]{1,0:T(8,128)S(1)}, u32[]{:S(2)}, u32[]{:S(2)}) collective-permute-start(f32[384,256]{1,0:T(8,128)S(1)} %get-tuple-element.148.refs_1_), channel_id=1, source_target_pairs={{0,8},{8,0},{16,24},{24,16},{1,9},{9,1},{17,25},{25,17},{2,10},{10... | collective-permute-start | bytes 1179656 | tf_op jit(solution)/shard_map/ppermute | solution.py:19
  133.1 1.4 collective-permute-start.29
  134.6 6.6 %collective-permute-start.30 = (f32[136,256]{1,0:T(8,128)S(1)}, f32[136,256]{1,0:T(8,128)S(1)}, u32[]{:S(2)}, u32[]{:S(2)}) collective-permute-start(f32[136,256]{1,0:T(8,128)S(1)} %add.153), channel_id=1, source_target_pairs={{0,16},{8,24},{16,0},{24,8},{1,17},{9,25},{17,1},{25,9},{2,18},{10... | collective-permute-start | bytes 417800 | tf_op jit(solution)/shard_map/ppermute | solution.py:19

commit v7 on v6

--- a/solution.py
+++ b/solution.py
@@ -310,10 +310,13 @@
 
 
 def tail_kernel(*refs):
-    (flags,), owns, nears, residuals, images, (select, lift, sol, steps, out, values, sems) = take(
-        refs, 1, 4, 4, 4, 4
-    )
+    (flags,), owns, nears, residuals, images, firsts, seconds, rest = take(refs, 1, 4, 4, 4, 4, 4, 4)
+    select, lift, sol, steps, weighted_out, out, weighted, values, weighted_sems, sems = rest
+    weighted_stores = stored(weighted, weighted_out, weighted_sems)
     stores = stored(values, out, sems)
+    for f in range(4):
+        weighted[f] = steps[2:3] * firsts[f][...] + steps[3:4] * seconds[f][...]
+        weighted_stores[f].start()
     parts = split(sol[...])
     size = values.shape[1]
     owns = faces_of(flags, [own[:size] for own in owns])
@@ -322,17 +325,7 @@
         image = owns[f] - permuted(select[f], nears[f]) + product(lift[f * size : (f + 1) * size], *parts)
         values[f] = residuals[f][...] + steps[0:1] * image + steps[1:2] * images[f][...]
         stores[f].start()
-    for copy in stores:
-        copy.wait()
-
-
-def weighted_kernel(*refs):
-    firsts, seconds, (steps, out, values, sems) = take(refs, 4, 4)
-    stores = stored(values, out, sems)
-    for f in range(4):
-        values[f] = steps[2:3] * firsts[f][...] + steps[3:4] * seconds[f][...]
-        stores[f].start()
-    for copy in stores:
+    for copy in weighted_stores + stores:
         copy.wait()
 
 
@@ -485,13 +478,9 @@
     near, _, result1 = solved(second_step_kernel, sums, fine1, [total0, result0])
     sol1, steps1 = result1[:ncoarse], result1[ncoarse:]
 
-    def final(kernel, operands, smem=0):
-        ends = [pltpu.VMEM((4, face, width), F32), pltpu.SemaphoreType.DMA((4,))]
-        return call(kernel, operands, [(ni, width)], ends, smem=smem, out_spec=ANY_SPEC)[0]
-
-    multipliers = final(weighted_kernel, [*direction0, *precond, steps1])
-    operands = [flags, *fine1, *near, *residual1, *image0, select, lift, sol1, steps1]
-    residual2 = final(tail_kernel, operands, smem=1)
+    ends = [pltpu.VMEM((4, face, width), F32)] * 2 + [pltpu.SemaphoreType.DMA((4,))] * 2
+    operands = [flags, *fine1, *near, *residual1, *image0, *direction0, *precond, select, lift, sol1, steps1]
+    multipliers, residual2 = call(tail_kernel, operands, [(ni, width)] * 2, ends, smem=1, out_spec=ANY_SPEC)
     return multipliers[None, None], residual2[None, None]
 
 

time: 148 us -> 149 us (level)
    pallas_call x21 -> x20, Pallas kernels: 48.7 us -> 48.1 us  [call(): pl.pallas_call(kernel, in_specs=[SMEM_SPEC if i < smem else ANY_SPEC if i...]
  transfers between devices with their start and end apart: 35 -> 35, of which waited for: 17 -> 17; matrix products, arithmetic and copies ran while one was open for 0% -> 0% of each run, Pallas kernels for 17% -> 16%
where the time goes in v7:
time: 149 us
  starting transfers between devices  50.3 us (34%)
  Pallas kernels  48.1 us (32%)
  waiting for transfers between devices  47.2 us (32%)
    pallas_call x20, Pallas kernels, call(): pl.pallas_call(kernel, in_specs=[SMEM_SPEC if i < smem else ANY_SPEC if i...  48.1 us
    ppermute x25, waiting for transfers between devices, swapped(): lax.ppermute(block, axis, [(i, i ^ bit) for i in range(lax.axis_size(axis...  47.2 us
    ppermute x25, starting transfers between devices, swapped(): lax.ppermute(block, axis, [(i, i ^ bit) for i in range(lax.axis_size(axis...  42.8 us
    ppermute x10, starting transfers between devices, swapped_between(): return lax.ppermute(block, axis, route)  7.43 us
  transfers between devices with their start and end apart: 35, of which 17 were waited for; matrix products, arithmetic and copies ran while one was open for 0% of the time, Pallas kernels for 16%

profile of v7, /device:TPU:0, one launch (start us, length us, event | category | flops | bytes accessed | tf_op | source)
XLA Modules:
  0.0 148.5 jit_solution(10940196704566458402)
XLA Ops:
  0.7 1.0 fusion.refs_6_.select.refs_25_
  1.9 3.4 %shard_map.86 = (f32[416,256]{1,0:T(8,128)}, f32[416,256]{1,0:T(8,128)}, f32[424,256]{1,0:T(8,128)}, f32[424,256]{1,0:T(8,128)}) custom-call(s32[16]{0:T(128)} %bitcast.34, f32[1536,256]{1,0:T(8,128)} %bitcast.36, f32[16,1536]{1,0:T(8,128)} %bitcast.30), custom_call_target="tpu_custom_call" | custom-call | flops 1024 | bytes 1024 | tf_op jit(solution)/shard_map/pallas_call | solution.py:338
  6.0 3.0 %collective-permute-start.4 = (f32[12,128]{1,0:T(8,128)S(1)}, f32[12,128]{1,0:T(8,128)S(1)}, u32[]{:S(2)}, u32[]{:S(2)}) collective-permute-start(f32[12,128]{1,0:T(8,128)S(1)} %shard_map.88), channel_id=1, source_target_pairs={{0,1},{1,0},{2,3},{3,2},{4,5},{5,4},{6,7},{7,6},{8,9},{9,8},{10,11... | collective-permute-start | bytes 18440 | tf_op jit(solution)/shard_map/ppermute | solution.py:19
  10.6 2.1 %collective-permute-start.5 = (f32[24,128]{1,0:T(8,128)S(1)}, f32[24,128]{1,0:T(8,128)S(1)}, u32[]{:S(2)}, u32[]{:S(2)}) collective-permute-start(f32[24,128]{1,0:T(8,128)S(1)} %pad_add_fusion.8), channel_id=1, source_target_pairs={{0,16},{8,24},{16,0},{24,8},{1,17},{9,25},{17,1},{25,9},{2,18},{10... | collective-permute-start | bytes 36872 | tf_op jit(solution)/shard_map/ppermute | solution.py:19
  13.4 1.4 collective-permute-start
  14.9 1.3 collective-permute-done.6
  16.3 5.0 %collective-permute-start.7 = (f32[96,128]{1,0:T(8,128)S(1)}, f32[96,128]{1,0:T(8,128)S(1)}, u32[]{:S(2)}, u32[]{:S(2)}) collective-permute-start(f32[96,128]{1,0:T(8,128)S(1)} %pad_add_fusion.6), channel_id=1, source_target_pairs={{0,4},{1,5},{2,6},{3,7},{4,0},{5,1},{6,2},{7,3},{8,12},{9,13},{10,... | collective-permute-start | bytes 147464 | tf_op jit(solution)/shard_map/ppermute | solution.py:19
  21.2 5.2 %collective-permute-done.7 = f32[96,128]{1,0:T(8,128)S(1)} collective-permute-done((f32[96,128]{1,0:T(8,128)S(1)}, f32[96,128]{1,0:T(8,128)S(1)}, u32[]{:S(2)}, u32[]{:S(2)}) %collective-permute-start.7) | collective-permute-done | bytes 49184 | tf_op jit(solution)/shard_map/ppermute | solution.py:19
  26.5 3.4 %shard_map.87 = (f32[384,256]{1,0:T(8,128)S(1)}, f32[384,256]{1,0:T(8,128)S(1)}, f32[1536,256]{1,0:T(8,128)S(1)}) custom-call(f32[6]{0:T(128)S(1)} %pad_maximum_fusion.refs_0_.flags, f32[1536,1536]{1,0:T(8,128)S(1)} %bitcast.16, f32[416,256]{1,0:T(8,128)S(1)} %copy-done, f32[416,256]{1,0:T(8,128)S(1)} %copy-done.2, ...), custom_call_target="tpu_custom_call" | custom-call | flops 1024 | bytes 1024 | tf_op jit(solution)/shard_map/pallas_call | solution.py:338
  30.0 2.7 %shard_map.89 = (f32[384,256]{1,0:T(8,128)S(1)}, f32[384,256]{1,0:T(8,128)S(1)}, f32[392,256]{1,0:T(8,128)S(1)}, f32[392,256]{1,0:T(8,128)S(1)}) custom-call(f32[6]{0:T(128)S(1)} %pad_maximum_fusion.refs_0_.flags, f32[1536,1536]{1,0:T(8,128)S(1)} %bitcast.17, f32[424,256]{1,0:T(8,128)S(1)} %copy-done.4, f32[424,256]{1,0:T(8,128)S(1)} %copy-done.5, ...), custom_call_target="tpu_custom_call" | custom-call | flops 8000000000 | bytes 1024 | tf_op jit(solution)/shard_map/pallas_call | solution.py:338
  34.1 2.0 %shard_map.90 = (f32[384,256]{1,0:T(8,128)S(1)}, f32[384,256]{1,0:T(8,128)S(1)}, f32[1,256]{1,0:T(1,128)S(1)}) custom-call(f32[6]{0:T(128)S(1)} %pad_maximum_fusion.refs_0_.flags, f32[1536,1536]{1,0:T(8,128)S(1)} %bitcast.18, f32[384,256]{1,0:T(8,128)S(1)} %get-tuple-element.88.refs_2_.refs_8_, f32[384,256]{1,0:T(8,128)S(1)} %get-tuple-element.89.refs_3_.refs_9_, ...), custom_call_target="tpu_custom_call" | custom-call | flops 1024 | bytes 1024 | tf_op jit(solution)/shard_map/pallas_call | solution.py:338
  37.0 4.2 %collective-permute-start.10 = (f32[192,128]{1,0:T(8,128)S(1)}, f32[192,128]{1,0:T(8,128)S(1)}, u32[]{:S(2)}, u32[]{:S(2)}) collective-permute-start(f32[192,128]{1,0:T(8,128)S(1)} %pad_add_fusion.3), channel_id=1, source_target_pairs={{0,2},{1,3},{2,0},{3,1},{4,6},{5,7},{6,4},{7,5},{8,10},{9,11},{10,... | collective-permute-start | bytes 294920 | tf_op jit(solution)/shard_map/ppermute | solution.py:19
  41.2 6.0 %collective-permute-done.10 = f32[192,128]{1,0:T(8,128)S(1)} collective-permute-done((f32[192,128]{1,0:T(8,128)S(1)}, f32[192,128]{1,0:T(8,128)S(1)}, u32[]{:S(2)}, u32[]{:S(2)}) %collective-permute-start.10) | collective-permute-done | bytes 98336 | tf_op jit(solution)/shard_map/ppermute | solution.py:19
  47.2 3.4 %shard_map.91 = (f32[384,256]{1,0:T(8,128)S(1)}, f32[384,256]{1,0:T(8,128)S(1)}, f32[1536,256]{1,0:T(8,128)S(1)}) custom-call(f32[6]{0:T(128)S(1)} %pad_maximum_fusion.refs_0_.flags, f32[1536,1536]{1,0:T(8,128)S(1)} %bitcast.24, f32[384,256]{1,0:T(8,128)S(1)} %get-tuple-element.99.refs_2_, f32[384,256]{1,0:T(8,128)S(1)} %get-tuple-element.100.refs_3_, ...), custom_call_target="tpu_custom_call" | custom-call | flops 1024 | bytes 1024 | tf_op jit(solution)/shard_map/pallas_call | solution.py:338
  50.7 2.7 %shard_map.92 = (f32[384,256]{1,0:T(8,128)S(1)}, f32[384,256]{1,0:T(8,128)S(1)}, f32[400,256]{1,0:T(8,128)S(1)}, f32[400,256]{1,0:T(8,128)S(1)}) custom-call(f32[6]{0:T(128)S(1)} %pad_maximum_fusion.refs_0_.flags, f32[1536,1536]{1,0:T(8,128)S(1)} %bitcast.25, f32[392,256]{1,0:T(8,128)S(1)} %get-tuple-element.97.refs_6_.refs_2_, ...), custom_call_target="tpu_custom_call" | custom-call | flops 8000000000 | bytes 1024 | tf_op jit(solution)/shard_map/pallas_call | solution.py:338
  53.4 2.3 %shard_map.93 = (f32[384,256]{1,0:T(8,128)S(1)}, f32[392,256]{1,0:T(8,128)S(1)}, f32[24,256]{1,0:T(8,128)S(1)}) custom-call(f32[6]{0:T(128)S(1)} %pad_maximum_fusion.refs_0_.flags, f32[1536,1536]{1,0:T(8,128)S(1)} %bitcast.26, f32[384,256]{1,0:T(8,128)S(1)} %get-tuple-element.103.refs_2_.refs_17_, f32[384,256]{1,0:T(8,128)S(1)} %get-tuple-element.104.refs_3_.refs_18_, ...), custom_call_target="tpu_custom_call" | custom-call | flops 1024 | bytes 1024 | tf_op jit(solution)/shard_map/pallas_call | solution.py:338
  55.7 1.6 %collective-permute-start.13 = (f32[24,256]{1,0:T(8,128)S(1)}, f32[24,256]{1,0:T(8,128)S(1)}, u32[]{:S(2)}, u32[]{:S(2)}) collective-permute-start(f32[24,256]{1,0:T(8,128)S(1)} %get-tuple-element.113), channel_id=1, source_target_pairs={{0,1},{1,0},{2,3},{3,2},{4,5},{5,4},{6,7},{7,6},{8,9},{9,8},{10,11... | collective-permute-start | bytes 73736 | tf_op jit(solution)/shard_map/ppermute | solution.py:19
  57.3 2.3 %collective-permute-done.13 = f32[24,256]{1,0:T(8,128)S(1)} collective-permute-done((f32[24,256]{1,0:T(8,128)S(1)}, f32[24,256]{1,0:T(8,128)S(1)}, u32[]{:S(2)}, u32[]{:S(2)}) %collective-permute-start.13) | collective-permute-done | bytes 24608 | tf_op jit(solution)/shard_map/ppermute | solution.py:19
  59.6 3.1 %collective-permute-start.14 = (f32[48,256]{1,0:T(8,128)S(1)}, f32[48,256]{1,0:T(8,128)S(1)}, u32[]{:S(2)}, u32[]{:S(2)}) collective-permute-start(f32[48,256]{1,0:T(8,128)S(1)} %pad_add_fusion.5), channel_id=1, source_target_pairs={{0,4},{1,5},{2,6},{3,7},{4,0},{5,1},{6,2},{7,3},{8,12},{9,13},{10,... | collective-permute-start | bytes 147464 | tf_op jit(solution)/shard_map/ppermute | solution.py:19
  62.7 2.1 %collective-permute-done.14 = f32[48,256]{1,0:T(8,128)S(1)} collective-permute-done((f32[48,256]{1,0:T(8,128)S(1)}, f32[48,256]{1,0:T(8,128)S(1)}, u32[]{:S(2)}, u32[]{:S(2)}) %collective-permute-start.14) | collective-permute-done | bytes 49184 | tf_op jit(solution)/shard_map/ppermute | solution.py:19
  64.8 2.0 %collective-permute-start.15 = (f32[96,256]{1,0:T(8,128)S(1)}, f32[96,256]{1,0:T(8,128)S(1)}, u32[]{:S(2)}, u32[]{:S(2)}) collective-permute-start(f32[96,256]{1,0:T(8,128)S(1)} %pad_add_fusion.2.refs_0_), channel_id=1, source_target_pairs={{0,2},{1,3},{2,0},{3,1},{4,6},{5,7},{6,4},{7,5},{8,10},{9,11},{10,... | collective-permute-start | bytes 294920 | tf_op jit(solution)/shard_map/ppermute | solution.py:19
  66.8 1.0 collective-permute-start.20
  68.5 0.9 collective-permute-done.15.refs_1_
  69.4 0.9 collective-permute-start.17
  70.3 4.4 %collective-permute-start.16 = (f32[384,256]{1,0:T(8,128)S(1)}, f32[384,256]{1,0:T(8,128)S(1)}, u32[]{:S(2)}, u32[]{:S(2)}) collective-permute-start(f32[384,256]{1,0:T(8,128)S(1)} %get-tuple-element.118.refs_2_.refs_8_), channel_id=1, source_target_pairs={{0,8},{8,0},{16,24},{24,16},{1,9},{9,1},{17,25},{25,17},{2,10},{10... | collective-permute-start | bytes 1179656 | tf_op jit(solution)/shard_map/ppermute | solution.py:19
  75.4 1.3 collective-permute-done.18
  76.9 3.5 %shard_map.96.refs_10_.refs_11_.refs_26_ = f32[1536,128]{1,0:T(8,128)S(1)} custom-call(f32[6]{0:T(128)S(1)} %pad_maximum_fusion.refs_0_.flags, f32[416,256]{1,0:T(8,128)S(1)} %collective-permute-done.refs_4_.near0, f32[416,256]{1,0:T(8,128)S(1)} %collective-permute-done.1.refs_5_.near1, f32[424,256]{1,0:T(8,128)S(1)} %collective-permute-done.2.refs_4_.near2, ...), custom_call_target="tpu_custom_call" | custom-call | flops 1024 | bytes 1024 | tf_op jit(solution)/shard_map/pallas_call | solution.py:338
  80.4 2.8 %collective-permute-done.19 = f32[136,256]{1,0:T(8,128)S(1)} collective-permute-done((f32[136,256]{1,0:T(8,128)S(1)}, f32[136,256]{1,0:T(8,128)S(1)}, u32[]{:S(2)}, u32[]{:S(2)}) %collective-permute-start.19) | collective-permute-done | bytes 139296 | tf_op jit(solution)/shard_map/ppermute | solution.py:19
  83.8 3.7 %shard_map.97 = (f32[384,256]{1,0:T(8,128)S(1)}, f32[384,256]{1,0:T(8,128)S(1)}, f32[384,256]{1,0:T(8,128)S(1)}, f32[384,256]{1,0:T(8,128)S(1)}, f32[1536,256]{1,0:T(8,128)S(1)}) custom-call(f32[6]{0:T(128)S(1)} %pad_maximum_fusion.refs_0_.flags, f32[1536,1536]{1,0:T(8,128)S(1)} %bitcast.19, f32[384,256]{1,0:T(8,128)S(1)} %get-tuple-element.118.refs_2_.refs_8_, ...), custom_call_target="tpu_custom_call" | custom-call | flops 1024 | bytes 1024 | tf_op jit(solution)/shard_map/pallas_call | solution.py:338
  87.6 3.2 %shard_map.98 = (f32[384,256]{1,0:T(8,128)S(1)}, f32[384,256]{1,0:T(8,128)S(1)}, f32[384,256]{1,0:T(8,128)S(1)}, f32[384,256]{1,0:T(8,128)S(1)}, f32[392,256]{1,0:T(8,128)S(1)}, /*index=5*/f32[392,256]{1,0:T(8,128)S(1)}) custom-call(f32[6]{0:T(128)S(1)} %pad_maximum_fusion.refs_0_.flags, f32[1536,1536]{1,0:T(8,128)S(1)} %bitcast.20, ...), custom_call_target="tpu_custom_call" | custom-call | flops 8000000000 | bytes 1024 | tf_op jit(solution)/shard_map/pallas_call | solution.py:338
  90.8 1.5 %collective-permute-start.24 = (f32[392,256]{1,0:T(8,128)S(1)}, f32[392,256]{1,0:T(8,128)S(1)}, u32[]{:S(2)}, u32[]{:S(2)}) collective-permute-start(f32[392,256]{1,0:T(8,128)S(1)} %get-tuple-element.130.refs_6_.refs_2_), channel_id=1, source_target_pairs={{0,1},{1,0},{2,3},{3,2},{4,5},{5,4},{6,7},{7,6},{8,9},{9,8},{10,11... | collective-permute-start | bytes 1204232 | tf_op jit(solution)/shard_map/ppermute | solution.py:19
  93.0 2.0 %shard_map.99 = (f32[384,256]{1,0:T(8,128)S(1)}, f32[384,256]{1,0:T(8,128)S(1)}, f32[1,256]{1,0:T(1,128)S(1)}) custom-call(f32[6]{0:T(128)S(1)} %pad_maximum_fusion.refs_0_.flags, f32[1536,1536]{1,0:T(8,128)S(1)} %bitcast.21, f32[384,256]{1,0:T(8,128)S(1)} %get-tuple-element.123.refs_2_.refs_9_, f32[384,256]{1,0:T(8,128)S(1)} %get-tuple-element.124.refs_3_.refs_10_, ...), custom_call_target="tpu_custom_call" | custom-call | flops 1024 | bytes 1024 | tf_op jit(solution)/shard_map/pallas_call | solution.py:338
  95.1 0.9 collective-permute-start.23
  96.8 3.4 %shard_map.100 = (f32[384,256]{1,0:T(8,128)S(1)}, f32[384,256]{1,0:T(8,128)S(1)}, f32[1536,256]{1,0:T(8,128)S(1)}) custom-call(f32[6]{0:T(128)S(1)} %pad_maximum_fusion.refs_0_.flags, f32[1536,1536]{1,0:T(8,128)S(1)} %bitcast.27, f32[384,256]{1,0:T(8,128)S(1)} %get-tuple-element.132.refs_2_, f32[384,256]{1,0:T(8,128)S(1)} %get-tuple-element.133.refs_3_, ...), custom_call_target="tpu_custom_call" | custom-call | flops 1024 | bytes 1024 | tf_op jit(solution)/shard_map/pallas_call | solution.py:338
  100.2 9.0 %collective-permute-done.24.refs_4_ = f32[392,256]{1,0:T(8,128)S(1)} collective-permute-done((f32[392,256]{1,0:T(8,128)S(1)}, f32[392,256]{1,0:T(8,128)S(1)}, u32[]{:S(2)}, u32[]{:S(2)}) %collective-permute-start.24) | collective-permute-done | bytes 401440 | tf_op jit(solution)/shard_map/ppermute | solution.py:19
  109.2 2.7 %shard_map.101 = (f32[384,256]{1,0:T(8,128)S(1)}, f32[384,256]{1,0:T(8,128)S(1)}, f32[400,256]{1,0:T(8,128)S(1)}, f32[400,256]{1,0:T(8,128)S(1)}) custom-call(f32[6]{0:T(128)S(1)} %pad_maximum_fusion.refs_0_.flags, f32[1536,1536]{1,0:T(8,128)S(1)} %bitcast.28, f32[392,256]{1,0:T(8,128)S(1)} %get-tuple-element.130.refs_6_.refs_2_, ...), custom_call_target="tpu_custom_call" | custom-call | flops 8000000000 | bytes 1024 | tf_op jit(solution)/shard_map/pallas_call | solution.py:338
  111.9 2.5 %shard_map.102 = (f32[384,256]{1,0:T(8,128)S(1)}, f32[392,256]{1,0:T(8,128)S(1)}, f32[24,256]{1,0:T(8,128)S(1)}) custom-call(f32[6]{0:T(128)S(1)} %pad_maximum_fusion.refs_0_.flags, f32[1536,1536]{1,0:T(8,128)S(1)} %bitcast.29, f32[384,256]{1,0:T(8,128)S(1)} %get-tuple-element.134.refs_2_.refs_21_, f32[384,256]{1,0:T(8,128)S(1)} %get-tuple-element.135.refs_3_.refs_22_, ...), custom_call_target="tpu_custom_call" | custom-call | flops 1024 | bytes 1024 | tf_op jit(solution)/shard_map/pallas_call | solution.py:338
  114.4 2.5 %collective-permute-start.26 = (f32[24,256]{1,0:T(8,128)S(1)}, f32[24,256]{1,0:T(8,128)S(1)}, u32[]{:S(2)}, u32[]{:S(2)}) collective-permute-start(f32[24,256]{1,0:T(8,128)S(1)} %get-tuple-element.144), channel_id=1, source_target_pairs={{0,1},{1,0},{2,3},{3,2},{4,5},{5,4},{6,7},{7,6},{8,9},{9,8},{10,11... | collective-permute-start | bytes 73736 | tf_op jit(solution)/shard_map/ppermute | solution.py:19
  116.9 1.8 %collective-permute-done.26 = f32[24,256]{1,0:T(8,128)S(1)} collective-permute-done((f32[24,256]{1,0:T(8,128)S(1)}, f32[24,256]{1,0:T(8,128)S(1)}, u32[]{:S(2)}, u32[]{:S(2)}) %collective-permute-start.26) | collective-permute-done | bytes 24608 | tf_op jit(solution)/shard_map/ppermute | solution.py:19
  118.7 3.1 %collective-permute-start.27 = (f32[48,256]{1,0:T(8,128)S(1)}, f32[48,256]{1,0:T(8,128)S(1)}, u32[]{:S(2)}, u32[]{:S(2)}) collective-permute-start(f32[48,256]{1,0:T(8,128)S(1)} %pad_add_fusion.4), channel_id=1, source_target_pairs={{0,4},{1,5},{2,6},{3,7},{4,0},{5,1},{6,2},{7,3},{8,12},{9,13},{10,... | collective-permute-start | bytes 147464 | tf_op jit(solution)/shard_map/ppermute | solution.py:19
  121.9 2.5 %collective-permute-done.27 = f32[48,256]{1,0:T(8,128)S(1)} collective-permute-done((f32[48,256]{1,0:T(8,128)S(1)}, f32[48,256]{1,0:T(8,128)S(1)}, u32[]{:S(2)}, u32[]{:S(2)}) %collective-permute-start.27) | collective-permute-done | bytes 49184 | tf_op jit(solution)/shard_map/ppermute | solution.py:19
  124.4 1.7 %collective-permute-start.28 = (f32[96,256]{1,0:T(8,128)S(1)}, f32[96,256]{1,0:T(8,128)S(1)}, u32[]{:S(2)}, u32[]{:S(2)}) collective-permute-start(f32[96,256]{1,0:T(8,128)S(1)} %pad_add_fusion.1.refs_0_), channel_id=1, source_target_pairs={{0,2},{1,3},{2,0},{3,1},{4,6},{5,7},{6,4},{7,5},{8,10},{9,11},{10,... | collective-permute-start | bytes 294920 | tf_op jit(solution)/shard_map/ppermute | solution.py:19
  126.1 1.7 %collective-permute-start.31 = (f32[400,256]{1,0:T(8,128)S(1)}, f32[400,256]{1,0:T(8,128)S(1)}, u32[]{:S(2)}, u32[]{:S(2)}) collective-permute-start(f32[400,256]{1,0:T(8,128)S(1)} %get-tuple-element.151.refs_6_.refs_3_), channel_id=1, source_target_pairs={{0,1},{1,0},{2,3},{3,2},{4,5},{5,4},{6,7},{7,6},{8,9},{9,8},{10,11... | collective-permute-start | bytes 1228808 | tf_op jit(solution)/shard_map/ppermute | solution.py:19
  129.8 2.6 %collective-permute-start.29 = (f32[384,256]{1,0:T(8,128)S(1)}, f32[384,256]{1,0:T(8,128)S(1)}, u32[]{:S(2)}, u32[]{:S(2)}) collective-permute-start(f32[384,256]{1,0:T(8,128)S(1)} %get-tuple-element.149.refs_1_), channel_id=1, source_target_pairs={{0,8},{8,0},{16,24},{24,16},{1,9},{9,1},{17,25},{25,17},{2,10},{10... | collective-permute-start | bytes 1179656 | tf_op jit(solution)/shard_map/ppermute | solution.py:19
  133.1 1.3 collective-permute-done.33
  134.6 6.5 %collective-permute-done.34 = f32[136,256]{1,0:T(8,128)S(1)} collective-permute-done((f32[136,256]{1,0:T(8,128)S(1)}, f32[136,256]{1,0:T(8,128)S(1)}, u32[]{:S(2)}, u32[]{:S(2)}) %collective-permute-start.34) | collective-permute-done | bytes 139296 | tf_op jit(solution)/shard_map/ppermute | solution.py:19
  141.7 2.2 %collective-permute-done.31.refs_7_ = f32[400,256]{1,0:T(8,128)S(1)} collective-permute-done((f32[400,256]{1,0:T(8,128)S(1)}, f32[400,256]{1,0:T(8,128)S(1)}, u32[]{:S(2)}, u32[]{:S(2)}) %collective-permute-start.31) | collective-permute-done | bytes 409632 | tf_op jit(solution)/shard_map/ppermute | solution.py:19
  144.0 4.3 %shard_map.105 = (f32[1536,256]{1,0:T(8,128)}, f32[1536,256]{1,0:T(8,128)}) custom-call(f32[6]{0:T(128)S(1)} %pad_maximum_fusion.refs_0_.flags, f32[384,256]{1,0:T(8,128)S(1)} %get-tuple-element.149.refs_1_, f32[392,256]{1,0:T(8,128)S(1)} %get-tuple-element.150.refs_2_, f32[400,256]{1,0:T(8,128)S(1)} %get-tuple-element.151.refs_6_.refs_3_, ...), custom_call_target="tpu_custom_call" | custom-call | flops 1024 | bytes 1024 | tf_op jit(solution)/shard_map/pallas_call | solution.py:338
  (95 shorter events, 12.5 us)
Async XLA Ops:
  0.6 4.7 %copy-start.3 = (s32[1,1,16]{2,1,0:T(1,128)S(1)}, s32[1,1,16]{2,1,0:T(1,128)}, u32[]{:S(2)}) copy-start(s32[1,1,16]{2,1,0:T(1,128)} %param.11) | copy-start | bytes 196
  0.6 4.7 %copy-start.6 = (f32[4,128]{1,0:T(4,128)S(1)}, f32[4,128]{1,0:T(4,128)}, u32[]{:S(2)}) copy-start(f32[4,128]{1,0:T(4,128)} %inverse) | copy-start | bytes 6148
  5.3 21.1 %slice-start = ((s8[9437184]{0:T(1024)(128)(4,1)}), s8[4194304]{0:T(1024)(128)(4,1)S(1)}, s32[]{:S(2)}) async-start(s8[9437184]{0:T(1024)(128)(4,1)} %bitcast.14), calls=%async_computation | async-start | bytes 8388608
  5.4 3.6 %copy-start.4 = (f32[424,256]{1,0:T(8,128)S(1)}, f32[424,256]{1,0:T(8,128)}, u32[]{:S(2)}) copy-start(f32[424,256]{1,0:T(8,128)} %get-tuple-element.90.refs_2_) | copy-start | bytes 1302532
  5.4 4.1 %copy-start.5 = (f32[424,256]{1,0:T(8,128)S(1)}, f32[424,256]{1,0:T(8,128)}, u32[]{:S(2)}) copy-start(f32[424,256]{1,0:T(8,128)} %get-tuple-element.91.refs_3_) | copy-start | bytes 1302532
  5.4 7.3 %copy-start.2 = (f32[416,256]{1,0:T(8,128)S(1)}, f32[416,256]{1,0:T(8,128)}, u32[]{:S(2)}) copy-start(f32[416,256]{1,0:T(8,128)} %get-tuple-element.85.refs_3_) | copy-start | bytes 1277956
  5.4 8.0 %copy-start = (f32[416,256]{1,0:T(8,128)S(1)}, f32[416,256]{1,0:T(8,128)}, u32[]{:S(2)}) copy-start(f32[416,256]{1,0:T(8,128)} %get-tuple-element.83.refs_2_.sent) | copy-start | bytes 1277956
  5.4 21.1 %slice-start.1 = ((s8[9437184]{0:T(1024)(128)(4,1)}), s8[4194304]{0:T(1024)(128)(4,1)S(1)}, s32[]{:S(2)}) async-start(s8[9437184]{0:T(1024)(128)(4,1)} %bitcast.14), calls=%async_computation.1 | async-start | bytes 8388608
  5.4 21.1 %slice-start.2 = ((s8[9437184]{0:T(1024)(128)(4,1)}), s8[1048576]{0:T(1024)(128)(4,1)S(1)}, s32[]{:S(2)}) async-start(s8[9437184]{0:T(1024)(128)(4,1)} %bitcast.14), calls=%async_computation.2 | async-start | bytes 2097152
  6.0 4.6 %collective-permute-start.4 = (f32[12,128]{1,0:T(8,128)S(1)}, f32[12,128]{1,0:T(8,128)S(1)}, u32[]{:S(2)}, u32[]{:S(2)}) collective-permute-start(f32[12,128]{1,0:T(8,128)S(1)} %shard_map.88), channel_id=1, source_target_pairs={{0,1},{1,0},{2,3},{3,2},{4,5},{5,4},{6,7},{7,6},{8,9},{9,8},{10,11... | collective-permute-start | bytes 18440 | tf_op jit(solution)/shard_map/ppermute | solution.py:19
  9.0 20.9 %collective-permute-start.2 = (f32[424,256]{1,0:T(8,128)S(1)}, f32[424,256]{1,0:T(8,128)S(1)}, u32[]{:S(2)}, u32[]{:S(2)}) collective-permute-start(f32[424,256]{1,0:T(8,128)S(1)} %copy-done.4), channel_id=1, source_target_pairs={{0,1},{1,0},{2,3},{3,2},{4,5},{5,4},{6,7},{7,6},{8,9},{9,8},{10,11... | collective-permute-start | bytes 1302536 | tf_op jit(solution)/shard_map/ppermute | solution.py:19
  9.5 20.5 %collective-permute-start.3 = (f32[424,256]{1,0:T(8,128)S(1)}, f32[424,256]{1,0:T(8,128)S(1)}, u32[]{:S(2)}, u32[]{:S(2)}) collective-permute-start(f32[424,256]{1,0:T(8,128)S(1)} %copy-done.5), channel_id=1, source_target_pairs={{1,2},{2,1},{3,4},{4,3},{5,6},{6,5},{9,10},{10,9},{11,12},{12,11},... | collective-permute-start | bytes 1302536 | tf_op jit(solution)/shard_map/ppermute | solution.py:26
  10.6 4.2 %collective-permute-start.5 = (f32[24,128]{1,0:T(8,128)S(1)}, f32[24,128]{1,0:T(8,128)S(1)}, u32[]{:S(2)}, u32[]{:S(2)}) collective-permute-start(f32[24,128]{1,0:T(8,128)S(1)} %pad_add_fusion.8), channel_id=1, source_target_pairs={{0,16},{8,24},{16,0},{24,8},{1,17},{9,25},{17,1},{25,9},{2,18},{10... | collective-permute-start | bytes 36872 | tf_op jit(solution)/shard_map/ppermute | solution.py:19
  12.7 13.8 %collective-permute-start.1 = (f32[416,256]{1,0:T(8,128)S(1)}, f32[416,256]{1,0:T(8,128)S(1)}, u32[]{:S(2)}, u32[]{:S(2)}) collective-permute-start(f32[416,256]{1,0:T(8,128)S(1)} %copy-done.2), channel_id=1, source_target_pairs={{8,16},{16,8},{9,17},{17,9},{10,18},{18,10},{11,19},{19,11},{12,20... | collective-permute-start | bytes 1277960 | tf_op jit(solution)/shard_map/ppermute | solution.py:26
  13.4 13.1 %collective-permute-start = (f32[416,256]{1,0:T(8,128)S(1)}, f32[416,256]{1,0:T(8,128)S(1)}, u32[]{:S(2)}, u32[]{:S(2)}) collective-permute-start(f32[416,256]{1,0:T(8,128)S(1)} %copy-done), channel_id=1, source_target_pairs={{0,8},{8,0},{16,24},{24,16},{1,9},{9,1},{17,25},{25,17},{2,10},{10... | collective-permute-start | bytes 1277960 | tf_op jit(solution)/shard_map/ppermute | solution.py:19
  14.8 1.4 collective-permute-start.6
  16.3 10.2 %collective-permute-start.7 = (f32[96,128]{1,0:T(8,128)S(1)}, f32[96,128]{1,0:T(8,128)S(1)}, u32[]{:S(2)}, u32[]{:S(2)}) collective-permute-start(f32[96,128]{1,0:T(8,128)S(1)} %pad_add_fusion.6), channel_id=1, source_target_pairs={{0,4},{1,5},{2,6},{3,7},{4,0},{5,1},{6,2},{7,3},{8,12},{9,13},{10,... | collective-permute-start | bytes 147464 | tf_op jit(solution)/shard_map/ppermute | solution.py:19
  30.0 17.2 %slice-start.3 = ((s8[9437184]{0:T(1024)(128)(4,1)}), s8[4194304]{0:T(1024)(128)(4,1)S(1)}, s32[]{:S(2)}) async-start(s8[9437184]{0:T(1024)(128)(4,1)} %bitcast.22), calls=%async_computation.3 | async-start | bytes 8388608
  30.0 17.2 %slice-start.4 = ((s8[9437184]{0:T(1024)(128)(4,1)}), s8[4194304]{0:T(1024)(128)(4,1)S(1)}, s32[]{:S(2)}) async-start(s8[9437184]{0:T(1024)(128)(4,1)} %bitcast.22), calls=%async_computation.4 | async-start | bytes 8388608
  30.0 17.2 %slice-start.5 = ((s8[9437184]{0:T(1024)(128)(4,1)}), s8[1048576]{0:T(1024)(128)(4,1)S(1)}, s32[]{:S(2)}) async-start(s8[9437184]{0:T(1024)(128)(4,1)} %bitcast.22), calls=%async_computation.5 | async-start | bytes 2097152
  32.7 18.0 %collective-permute-start.11 = (f32[392,256]{1,0:T(8,128)S(1)}, f32[392,256]{1,0:T(8,128)S(1)}, u32[]{:S(2)}, u32[]{:S(2)}) collective-permute-start(f32[392,256]{1,0:T(8,128)S(1)} %get-tuple-element.97.refs_6_.refs_2_), channel_id=1, source_target_pairs={{0,1},{1,0},{2,3},{3,2},{4,5},{5,4},{6,7},{7,6},{8,9},{9,8},{10,11... | collective-permute-start | bytes 1204232 | tf_op jit(solution)/shard_map/ppermute | solution.py:19
  33.4 17.3 %collective-permute-start.12 = (f32[392,256]{1,0:T(8,128)S(1)}, f32[392,256]{1,0:T(8,128)S(1)}, u32[]{:S(2)}, u32[]{:S(2)}) collective-permute-start(f32[392,256]{1,0:T(8,128)S(1)} %get-tuple-element.98.refs_7_.refs_3_), channel_id=1, source_target_pairs={{1,2},{2,1},{3,4},{4,3},{5,6},{6,5},{9,10},{10,9},{11,12},{12,11},... | collective-permute-start | bytes 1204232 | tf_op jit(solution)/shard_map/ppermute | solution.py:26
  36.1 11.1 %collective-permute-start.8 = (f32[384,256]{1,0:T(8,128)S(1)}, f32[384,256]{1,0:T(8,128)S(1)}, u32[]{:S(2)}, u32[]{:S(2)}) collective-permute-start(f32[384,256]{1,0:T(8,128)S(1)} %get-tuple-element.99.refs_2_), channel_id=1, source_target_pairs={{0,8},{8,0},{16,24},{24,16},{1,9},{9,1},{17,25},{25,17},{2,10},{10... | collective-permute-start | bytes 1179656 | tf_op jit(solution)/shard_map/ppermute | solution.py:19
  36.1 11.0 %collective-permute-start.9 = (f32[384,256]{1,0:T(8,128)S(1)}, f32[384,256]{1,0:T(8,128)S(1)}, u32[]{:S(2)}, u32[]{:S(2)}) collective-permute-start(f32[384,256]{1,0:T(8,128)S(1)} %get-tuple-element.100.refs_3_), channel_id=1, source_target_pairs={{8,16},{16,8},{9,17},{17,9},{10,18},{18,10},{11,19},{19,11},{12,20... | collective-permute-start | bytes 1179656 | tf_op jit(solution)/shard_map/ppermute | solution.py:26
  37.0 10.1 %collective-permute-start.10 = (f32[192,128]{1,0:T(8,128)S(1)}, f32[192,128]{1,0:T(8,128)S(1)}, u32[]{:S(2)}, u32[]{:S(2)}) collective-permute-start(f32[192,128]{1,0:T(8,128)S(1)} %pad_add_fusion.3), channel_id=1, source_target_pairs={{0,2},{1,3},{2,0},{3,1},{4,6},{5,7},{6,4},{7,5},{8,10},{9,11},{10,... | collective-permute-start | bytes 294920 | tf_op jit(solution)/shard_map/ppermute | solution.py:19
  50.7 2.7 %copy-start.1 = (f32[1,1,16,1536]{3,2,1,0:T(8,128)S(1)}, f32[1,1,16,1536]{3,2,1,0:T(8,128)}, u32[]{:S(2)}) copy-start(f32[1,1,16,1536]{3,2,1,0:T(8,128)} %param.10) | copy-start | bytes 294916
  55.7 3.9 %collective-permute-start.13 = (f32[24,256]{1,0:T(8,128)S(1)}, f32[24,256]{1,0:T(8,128)S(1)}, u32[]{:S(2)}, u32[]{:S(2)}) collective-permute-start(f32[24,256]{1,0:T(8,128)S(1)} %get-tuple-element.113), channel_id=1, source_target_pairs={{0,1},{1,0},{2,3},{3,2},{4,5},{5,4},{6,7},{7,6},{8,9},{9,8},{10,11... | collective-permute-start | bytes 73736 | tf_op jit(solution)/shard_map/ppermute | solution.py:19
  59.6 5.1 %collective-permute-start.14 = (f32[48,256]{1,0:T(8,128)S(1)}, f32[48,256]{1,0:T(8,128)S(1)}, u32[]{:S(2)}, u32[]{:S(2)}) collective-permute-start(f32[48,256]{1,0:T(8,128)S(1)} %pad_add_fusion.5), channel_id=1, source_target_pairs={{0,4},{1,5},{2,6},{3,7},{4,0},{5,1},{6,2},{7,3},{8,12},{9,13},{10,... | collective-permute-start | bytes 147464 | tf_op jit(solution)/shard_map/ppermute | solution.py:19
  64.8 4.7 %collective-permute-start.15 = (f32[96,256]{1,0:T(8,128)S(1)}, f32[96,256]{1,0:T(8,128)S(1)}, u32[]{:S(2)}, u32[]{:S(2)}) collective-permute-start(f32[96,256]{1,0:T(8,128)S(1)} %pad_add_fusion.2.refs_0_), channel_id=1, source_target_pairs={{0,2},{1,3},{2,0},{3,1},{4,6},{5,7},{6,4},{7,5},{8,10},{9,11},{10,... | collective-permute-start | bytes 294920 | tf_op jit(solution)/shard_map/ppermute | solution.py:19
  66.8 20.8 %collective-permute-start.20 = (f32[400,256]{1,0:T(8,128)S(1)}, f32[400,256]{1,0:T(8,128)S(1)}, u32[]{:S(2)}, u32[]{:S(2)}) collective-permute-start(f32[400,256]{1,0:T(8,128)S(1)} %get-tuple-element.125.refs_6_.refs_2_.refs_10_), channel_id=1, source_target_pairs={{0,1},{1,0},{2,3},{3,2},{4,5},{5,4},{6,7},{7,6},{8,9},{9,8},{10,11... | collective-permute-start | bytes 1228808 | tf_op jit(solution)/shard_map/ppermute | solution.py:19
  67.8 19.7 %collective-permute-start.21 = (f32[400,256]{1,0:T(8,128)S(1)}, f32[400,256]{1,0:T(8,128)S(1)}, u32[]{:S(2)}, u32[]{:S(2)}) collective-permute-start(f32[400,256]{1,0:T(8,128)S(1)} %get-tuple-element.126.refs_7_.refs_3_.refs_11_), channel_id=1, source_target_pairs={{1,2},{2,1},{3,4},{4,3},{5,6},{6,5},{9,10},{10,9},{11,12},{12,11},... | collective-permute-start | bytes 1228808 | tf_op jit(solution)/shard_map/ppermute | solution.py:26
  69.4 14.3 %collective-permute-start.17 = (f32[392,256]{1,0:T(8,128)S(1)}, f32[392,256]{1,0:T(8,128)S(1)}, u32[]{:S(2)}, u32[]{:S(2)}) collective-permute-start(f32[392,256]{1,0:T(8,128)S(1)} %get-tuple-element.119.refs_3_.refs_9_), channel_id=1, source_target_pairs={{8,16},{16,8},{9,17},{17,9},{10,18},{18,10},{11,19},{19,11},{12,20... | collective-permute-start | bytes 1204232 | tf_op jit(solution)/shard_map/ppermute | solution.py:26
  70.3 13.4 %collective-permute-start.16 = (f32[384,256]{1,0:T(8,128)S(1)}, f32[384,256]{1,0:T(8,128)S(1)}, u32[]{:S(2)}, u32[]{:S(2)}) collective-permute-start(f32[384,256]{1,0:T(8,128)S(1)} %get-tuple-element.118.refs_2_.refs_8_), channel_id=1, source_target_pairs={{0,8},{8,0},{16,24},{24,16},{1,9},{9,1},{17,25},{25,17},{2,10},{10... | collective-permute-start | bytes 1179656 | tf_op jit(solution)/shard_map/ppermute | solution.py:19
  75.3 1.4 collective-permute-start.18
  76.8 6.4 %collective-permute-start.19 = (f32[136,256]{1,0:T(8,128)S(1)}, f32[136,256]{1,0:T(8,128)S(1)}, u32[]{:S(2)}, u32[]{:S(2)}) collective-permute-start(f32[136,256]{1,0:T(8,128)S(1)} %add.149), channel_id=1, source_target_pairs={{0,16},{8,24},{16,0},{24,8},{1,17},{9,25},{17,1},{25,9},{2,18},{10... | collective-permute-start | bytes 417800 | tf_op jit(solution)/shard_map/ppermute | solution.py:19
  90.8 18.4 %collective-permute-start.24 = (f32[392,256]{1,0:T(8,128)S(1)}, f32[392,256]{1,0:T(8,128)S(1)}, u32[]{:S(2)}, u32[]{:S(2)}) collective-permute-start(f32[392,256]{1,0:T(8,128)S(1)} %get-tuple-element.130.refs_6_.refs_2_), channel_id=1, source_target_pairs={{0,1},{1,0},{2,3},{3,2},{4,5},{5,4},{6,7},{7,6},{8,9},{9,8},{10,11... | collective-permute-start | bytes 1204232 | tf_op jit(solution)/shard_map/ppermute | solution.py:19
  92.3 16.9 %collective-permute-start.25 = (f32[392,256]{1,0:T(8,128)S(1)}, f32[392,256]{1,0:T(8,128)S(1)}, u32[]{:S(2)}, u32[]{:S(2)}) collective-permute-start(f32[392,256]{1,0:T(8,128)S(1)} %get-tuple-element.131.refs_7_.refs_3_), channel_id=1, source_target_pairs={{1,2},{2,1},{3,4},{4,3},{5,6},{6,5},{9,10},{10,9},{11,12},{12,11},... | collective-permute-start | bytes 1204232 | tf_op jit(solution)/shard_map/ppermute | solution.py:26
  95.0 1.8 %collective-permute-start.22 = (f32[384,256]{1,0:T(8,128)S(1)}, f32[384,256]{1,0:T(8,128)S(1)}, u32[]{:S(2)}, u32[]{:S(2)}) collective-permute-start(f32[384,256]{1,0:T(8,128)S(1)} %get-tuple-element.132.refs_2_), channel_id=1, source_target_pairs={{0,8},{8,0},{16,24},{24,16},{1,9},{9,1},{17,25},{25,17},{2,10},{10... | collective-permute-start | bytes 1179656 | tf_op jit(solution)/shard_map/ppermute | solution.py:19
  95.1 1.7 %collective-permute-start.23 = (f32[384,256]{1,0:T(8,128)S(1)}, f32[384,256]{1,0:T(8,128)S(1)}, u32[]{:S(2)}, u32[]{:S(2)}) collective-permute-start(f32[384,256]{1,0:T(8,128)S(1)} %get-tuple-element.133.refs_3_), channel_id=1, source_target_pairs={{8,16},{16,8},{9,17},{17,9},{10,18},{18,10},{11,19},{19,11},{12,20... | collective-permute-start | bytes 1179656 | tf_op jit(solution)/shard_map/ppermute | solution.py:26
  114.4 4.4 %collective-permute-start.26 = (f32[24,256]{1,0:T(8,128)S(1)}, f32[24,256]{1,0:T(8,128)S(1)}, u32[]{:S(2)}, u32[]{:S(2)}) collective-permute-start(f32[24,256]{1,0:T(8,128)S(1)} %get-tuple-element.144), channel_id=1, source_target_pairs={{0,1},{1,0},{2,3},{3,2},{4,5},{5,4},{6,7},{7,6},{8,9},{9,8},{10,11... | collective-permute-start | bytes 73736 | tf_op jit(solution)/shard_map/ppermute | solution.py:19
  118.7 5.7 %collective-permute-start.27 = (f32[48,256]{1,0:T(8,128)S(1)}, f32[48,256]{1,0:T(8,128)S(1)}, u32[]{:S(2)}, u32[]{:S(2)}) collective-permute-start(f32[48,256]{1,0:T(8,128)S(1)} %pad_add_fusion.4), channel_id=1, source_target_pairs={{0,4},{1,5},{2,6},{3,7},{4,0},{5,1},{6,2},{7,3},{8,12},{9,13},{10,... | collective-permute-start | bytes 147464 | tf_op jit(solution)/shard_map/ppermute | solution.py:19
  124.4 4.7 %collective-permute-start.28 = (f32[96,256]{1,0:T(8,128)S(1)}, f32[96,256]{1,0:T(8,128)S(1)}, u32[]{:S(2)}, u32[]{:S(2)}) collective-permute-start(f32[96,256]{1,0:T(8,128)S(1)} %pad_add_fusion.1.refs_0_), channel_id=1, source_target_pairs={{0,2},{1,3},{2,0},{3,1},{4,6},{5,7},{6,4},{7,5},{8,10},{9,11},{10,... | collective-permute-start | bytes 294920 | tf_op jit(solution)/shard_map/ppermute | solution.py:19
  126.1 17.8 %collective-permute-start.31 = (f32[400,256]{1,0:T(8,128)S(1)}, f32[400,256]{1,0:T(8,128)S(1)}, u32[]{:S(2)}, u32[]{:S(2)}) collective-permute-start(f32[400,256]{1,0:T(8,128)S(1)} %get-tuple-element.151.refs_6_.refs_3_), channel_id=1, source_target_pairs={{0,1},{1,0},{2,3},{3,2},{4,5},{5,4},{6,7},{7,6},{8,9},{9,8},{10,11... | collective-permute-start | bytes 1228808 | tf_op jit(solution)/shard_map/ppermute | solution.py:19
  127.9 16.1 %collective-permute-start.32 = (f32[400,256]{1,0:T(8,128)S(1)}, f32[400,256]{1,0:T(8,128)S(1)}, u32[]{:S(2)}, u32[]{:S(2)}) collective-permute-start(f32[400,256]{1,0:T(8,128)S(1)} %get-tuple-element.152.refs_7_.refs_4_), channel_id=1, source_target_pairs={{1,2},{2,1},{3,4},{4,3},{5,6},{6,5},{9,10},{10,9},{11,12},{12,11},... | collective-permute-start | bytes 1228808 | tf_op jit(solution)/shard_map/ppermute | solution.py:26
  129.2 14.8 %collective-permute-start.30 = (f32[392,256]{1,0:T(8,128)S(1)}, f32[392,256]{1,0:T(8,128)S(1)}, u32[]{:S(2)}, u32[]{:S(2)}) collective-permute-start(f32[392,256]{1,0:T(8,128)S(1)} %get-tuple-element.150.refs_2_), channel_id=1, source_target_pairs={{8,16},{16,8},{9,17},{17,9},{10,18},{18,10},{11,19},{19,11},{12,20... | collective-permute-start | bytes 1204232 | tf_op jit(solution)/shard_map/ppermute | solution.py:26
  129.8 14.1 %collective-permute-start.29 = (f32[384,256]{1,0:T(8,128)S(1)}, f32[384,256]{1,0:T(8,128)S(1)}, u32[]{:S(2)}, u32[]{:S(2)}) collective-permute-start(f32[384,256]{1,0:T(8,128)S(1)} %get-tuple-element.149.refs_1_), channel_id=1, source_target_pairs={{0,8},{8,0},{16,24},{24,16},{1,9},{9,1},{17,25},{25,17},{2,10},{10... | collective-permute-start | bytes 1179656 | tf_op jit(solution)/shard_map/ppermute | solution.py:19
  133.0 1.4 collective-permute-start.33
  134.5 6.6 %collective-permute-start.34 = (f32[136,256]{1,0:T(8,128)S(1)}, f32[136,256]{1,0:T(8,128)S(1)}, u32[]{:S(2)}, u32[]{:S(2)}) collective-permute-start(f32[136,256]{1,0:T(8,128)S(1)} %add.153), channel_id=1, source_target_pairs={{0,16},{8,24},{16,0},{24,8},{1,17},{9,25},{17,1},{25,9},{2,18},{10... | collective-permute-start | bytes 417800 | tf_op jit(solution)/shard_map/ppermute | solution.py:19
